TPU v7x, 32 devices: a whole 2x2x4 slice. The times are simulated.
32 devices in a mesh: tm: 8 (over y, x, core), chan: 4 (over z).
Axes of the slice: x: 2, y: 2, z: 4, core: 2. Of those that a mesh axis runs over, the one named last changes fastest.
Arguments:
- signal: bfloat16 [16384, 512], P('tm', 'chan'), may hold values from -6 to 6
- segment_ids: int32 [16384], replicated, may hold values from 0 to 8, as said below
- v_section: bfloat16 [256, 16, 512], P('chan'), may hold values from -6 to 6
- g_section: bfloat16 [512], replicated, may hold values from 1.5 to 3
- b_section: bfloat16 [256], P('chan'), may hold values from -2 to 2
- v_dilated: bfloat16 [3, 256, 3, 256], P(None, 'chan'), may hold values from -6 to 6
- g_dilated: bfloat16 [3, 256], P(None, 'chan'), may hold values from 0.59765625 to 1.3984375
- b_dilated: bfloat16 [3, 256], P(None, 'chan'), may hold values from -2 to 2
- v_mix: bfloat16 [3, 256, 256], P(None, 'chan'), may hold values from -6 to 6
- g_mix: bfloat16 [3, 256], P(None, 'chan'), may hold values from 0.59765625 to 1.3984375
- b_mix: bfloat16 [3, 256], P(None, 'chan'), may hold values from -2 to 2
- v_skip: bfloat16 [3, 256, 256], P(None, 'chan'), may hold values from -6 to 6
- g_skip: bfloat16 [3, 256], P(None, 'chan'), may hold values from 0.59765625 to 1.3984375
- b_skip: bfloat16 [3, 256], P(None, 'chan'), may hold values from -2 to 2
- cotangent: bfloat16 [256, 131072], P('chan', 'tm'), may hold values from -6 to 6
Outputs:
- output: bfloat16 [256, 131072], P('chan', 'tm')
- signal_grad: bfloat16 [16384, 512], P('tm', 'chan')
- v_section_grad: float32 [256, 16, 512], P('chan')
- g_section_grad: float32 [512], replicated
- b_section_grad: float32 [256], P('chan')
- v_dilated_grad: float32 [3, 256, 3, 256], P(None, 'chan')
- g_dilated_grad: float32 [3, 256], P(None, 'chan')
- b_dilated_grad: float32 [3, 256], P(None, 'chan')
- v_mix_grad: float32 [3, 256, 256], P(None, 'chan')
- g_mix_grad: float32 [3, 256], P(None, 'chan')
- b_mix_grad: float32 [3, 256], P(None, 'chan')
- v_skip_grad: float32 [3, 256, 256], P(None, 'chan')
- g_skip_grad: float32 [3, 256], P(None, 'chan')
- b_skip_grad: float32 [3, 256], P(None, 'chan')
Inputs may be any that keep to these rules, and one draw needn't show every extreme that they name: `segment_ids`: ids never fall; they rise by one at exactly one frame inside each aligned block of 2048 frames, never at a block's first frame.
All inputs are finite; a program needn't handle non-finite values.
Results may differ from a plain program's by a relative error of at most 0.014.
Values may be sent and summed in bfloat16 or wider, within the bound.
No kernel may reach another device: no remote copies, remote signals or barrier semaphores. Data moves between devices by JAX's collectives and lax.ppermute only.
A program may use at most 256 MiB of HBM per device.

v0:
```python
import jax
import jax.numpy as jnp
from jax import lax
from jax.sharding import PartitionSpec as P

EPSILON = 1e-06


def extended(block, sides, width):
    for axis, dim in sides:
        count = lax.axis_size(axis)
        forward = [(i, i + 1) for i in range(count - 1)]
        backward = [(target, source) for source, target in forward]
        low = lax.ppermute(
            lax.slice_in_dim(block, block.shape[dim] - width, None, axis=dim), axis, forward
        )
        high = lax.ppermute(lax.slice_in_dim(block, 0, width, axis=dim), axis, backward)
        block = jnp.concatenate([low, block, high], axis=dim)
    return block


def silu_grad(values):
    sigmoid_value = jax.nn.sigmoid(values)
    return sigmoid_value * (1.0 + values * (1.0 - sigmoid_value))


def matmul(left_side, right_side):
    return jnp.dot(left_side, right_side, preferred_element_type=jnp.float32)


def contract_rows(left_side, right_side):
    return lax.dot_general(
        left_side, right_side, (((0,), (0,)), ((), ())), preferred_element_type=jnp.float32
    )


def contract_cols(left_side, right_side):
    return lax.dot_general(
        left_side, right_side, (((1,), (1,)), ((), ())), preferred_element_type=jnp.float32
    )


def widen(values, span_width):
    if span_width > 0:
        values = extended(values, (("tm", 0),), span_width)
    return lax.all_gather(values, "chan", axis=1, tiled=True)


def grad_rim(values, span_width):
    return extended(values, (("tm", 0),), span_width)


def channel_sum(values):
    return lax.psum_scatter(values, "chan", scatter_dimension=1, tiled=True)


def tap_mask(frame_ids, offset, frames):
    centre_ids = frame_ids[16 : 16 + frames]
    shifted_ids = frame_ids[16 + offset : 16 + offset + frames]
    return (centre_ids == shifted_ids).astype(jnp.float32)[:, None]


def normed(v_values, gain_values, sum_axes):
    norm_values = jnp.sqrt(jnp.sum(v_values * v_values, axis=sum_axes, keepdims=True) + EPSILON)
    return (gain_values * v_values / norm_values, norm_values)


def norm_back(grad_w, v_values, gain_values, norm_values, sum_axes):
    grad_g = jnp.sum(grad_w * v_values, axis=sum_axes, keepdims=True) / norm_values
    grad_v = gain_values / norm_values * (grad_w - grad_g / norm_values * v_values)
    return (grad_v, grad_g)


def body(
    signal,
    segment_ids,
    v_section,
    g_section,
    b_section,
    v_dilated,
    g_dilated,
    b_dilated,
    v_mix,
    g_mix,
    b_mix,
    v_skip,
    g_skip,
    b_skip,
    cotangent,
):
    row_start = lax.axis_index("tm") * signal.shape[0]
    cotangent = cotangent.T
    v_section = jnp.transpose(v_section, (1, 2, 0))
    v_dilated = jnp.transpose(v_dilated, (0, 2, 3, 1))
    v_mix = jnp.transpose(v_mix, (0, 2, 1))
    v_skip = jnp.transpose(v_skip, (0, 2, 1))
    in_rows = signal.shape[0]
    frames = 8 * in_rows
    padded = jnp.pad(segment_ids, 2, constant_values=-1)
    nearby = lax.dynamic_slice_in_dim(padded, row_start, in_rows + 4)
    same_prev = (nearby[2:-2] == nearby[1:-3]).astype(jnp.float32)[:, None]
    same_next = (nearby[2:-2] == nearby[3:-1]).astype(jnp.float32)[:, None]
    frame_ids = jnp.repeat(nearby, 8)
    section_v = v_section.astype(jnp.float32)
    section_gain = g_section.astype(jnp.float32)[None, :, None]
    squares = jnp.sum(section_v * section_v, axis=(0, 2))
    squares = lax.psum(squares, "chan")
    section_norm = jnp.sqrt(squares + EPSILON)[None, :, None]
    w_section = (section_gain * section_v / section_norm).astype(jnp.bfloat16)
    in_width = section_v.shape[1]
    out_width = section_v.shape[2]
    centre_w = jnp.transpose(w_section[4:12], (1, 0, 2)).reshape(in_width, 8 * out_width)
    before_w = jnp.transpose(w_section[12:16], (1, 0, 2)).reshape(in_width, 4 * out_width)
    after_w = jnp.transpose(w_section[0:4], (1, 0, 2)).reshape(in_width, 4 * out_width)
    signal_full = widen(signal, 1)
    activated = jax.nn.silu(signal_full.astype(jnp.float32)).astype(jnp.bfloat16)
    early_sum = same_prev * matmul(activated[:-2], before_w)
    late_sum = same_next * matmul(activated[2:], after_w)
    section_sum = matmul(activated[1:-1], centre_w) + jnp.concatenate([early_sum, late_sum], axis=1)
    hidden = (section_sum.reshape(frames, out_width) + b_section.astype(jnp.float32)).astype(
        jnp.bfloat16
    )
    kept_values = []
    kept_norms = []
    for block_index in range(3):
        dilate = 3**block_index
        three_v = v_dilated[block_index].astype(jnp.float32)
        three_g = g_dilated[block_index].astype(jnp.float32)
        w_three, three_norm = normed(three_v, three_g, (0, 1))
        mix_v = v_mix[block_index].astype(jnp.float32)
        mix_g = g_mix[block_index].astype(jnp.float32)
        w_mix, mix_norm = normed(mix_v, mix_g, (0,))
        skip_v = v_skip[block_index].astype(jnp.float32)
        skip_g = g_skip[block_index].astype(jnp.float32)
        w_skip, skip_norm = normed(skip_v, skip_g, (0,))
        w_three = w_three.astype(jnp.bfloat16)
        w_mix = w_mix.astype(jnp.bfloat16)
        w_skip = w_skip.astype(jnp.bfloat16)
        widened = widen(hidden, dilate)
        act_rows = jax.nn.silu(widened.astype(jnp.float32)).astype(jnp.bfloat16)
        inner_sum = b_dilated[block_index].astype(jnp.float32)
        for tap_index in range(3):
            row_first = tap_index * dilate
            inner_sum = inner_sum + tap_mask(frame_ids, (tap_index - 1) * dilate, frames) * matmul(
                act_rows[row_first : row_first + frames], w_three[tap_index]
            )
        mixed_rows = widen(jax.nn.silu(inner_sum).astype(jnp.bfloat16), 0)
        centre_rows = widened[dilate : dilate + frames]
        mixed_sum = (
            matmul(mixed_rows, w_mix)
            + b_mix[block_index].astype(jnp.float32)
            + matmul(centre_rows, w_skip)
            + b_skip[block_index].astype(jnp.float32)
        )
        hidden = mixed_sum.astype(jnp.bfloat16)
        kept_values.append((widened, act_rows, inner_sum, mixed_rows, w_three, w_mix, w_skip))
        kept_norms.append(
            (three_v, three_g, three_norm, mix_v, mix_g, mix_norm, skip_v, skip_g, skip_norm)
        )
    output = hidden
    upstream = cotangent
    grads_by_block = [None, None, None]
    for block_index in (2, 1, 0):
        dilate = 3**block_index
        widened, act_rows, inner_sum, mixed_rows, w_three, w_mix, w_skip = kept_values[block_index]
        centre_rows = widened[dilate : dilate + frames]
        grad_mix = contract_rows(mixed_rows, upstream)
        grad_skip = contract_rows(centre_rows, upstream)
        grad_bias = jnp.sum(upstream.astype(jnp.float32), axis=0)
        inner_grad = (channel_sum(contract_cols(upstream, w_mix)) * silu_grad(inner_sum)).astype(
            jnp.bfloat16
        )
        grad_three = jnp.stack(
            [
                contract_rows(
                    act_rows[tap_index * dilate : tap_index * dilate + frames],
                    inner_grad
                    * tap_mask(frame_ids, (tap_index - 1) * dilate, frames).astype(jnp.bfloat16),
                )
                for tap_index in range(3)
            ]
        )
        grad_inner_bias = jnp.sum(inner_grad.astype(jnp.float32), axis=0)
        inner_rim = grad_rim(inner_grad, dilate)
        back_sum = contract_cols(upstream, w_skip)
        through = jnp.zeros_like(back_sum)
        for tap_index in range(3):
            row_first = (2 - tap_index) * dilate
            through = through + tap_mask(
                frame_ids, (1 - tap_index) * dilate, frames
            ) * contract_cols(inner_rim[row_first : row_first + frames], w_three[tap_index])
        back_sum = back_sum + silu_grad(centre_rows.astype(jnp.float32)) * through
        upstream = channel_sum(back_sum).astype(jnp.bfloat16)
        grads_by_block[block_index] = (grad_three, grad_inner_bias, grad_mix, grad_skip, grad_bias)
    grad_rows = upstream.reshape(in_rows, 8 * out_width)
    grad_centre = contract_rows(activated[1:-1], grad_rows).reshape(in_width, 8, out_width)
    grad_before = contract_rows(
        activated[:-2], grad_rows[:, : 4 * out_width] * same_prev.astype(jnp.bfloat16)
    ).reshape(in_width, 4, out_width)
    grad_after = contract_rows(
        activated[2:], grad_rows[:, 4 * out_width :] * same_next.astype(jnp.bfloat16)
    ).reshape(in_width, 4, out_width)
    grad_section = jnp.transpose(
        jnp.concatenate([grad_after, grad_centre, grad_before], axis=1), (1, 0, 2)
    )
    grad_section_bias = jnp.sum(upstream.astype(jnp.float32), axis=0)
    section_rim = grad_rim(grad_rows, 1)
    back_sum = (
        contract_cols(section_rim[1:-1], centre_w)
        + same_next * contract_cols(section_rim[2:, : 4 * out_width], before_w)
        + same_prev * contract_cols(section_rim[:-2, 4 * out_width :], after_w)
    )
    signal_grad = channel_sum(back_sum * silu_grad(signal_full[1:-1].astype(jnp.float32))).astype(
        jnp.bfloat16
    )
    grad_three_all = jnp.stack([entry[0] for entry in grads_by_block])
    three_bias_all = jnp.stack([entry[1] for entry in grads_by_block])
    grad_mix_all = jnp.stack([entry[2] for entry in grads_by_block])
    grad_skip_all = jnp.stack([entry[3] for entry in grads_by_block])
    bias_all = jnp.stack([entry[4] for entry in grads_by_block])
    summed = lax.psum(
        (
            grad_section,
            grad_section_bias,
            grad_three_all,
            three_bias_all,
            grad_mix_all,
            grad_skip_all,
            bias_all,
        ),
        "tm",
    )
    (
        grad_section,
        grad_section_bias,
        grad_three_all,
        three_bias_all,
        grad_mix_all,
        grad_skip_all,
        bias_all,
    ) = summed
    gain_part = jnp.sum(grad_section * section_v, axis=(0, 2)) / section_norm[0, :, 0]
    section_gain_grad = lax.psum(gain_part, "chan")
    section_v_grad = (
        section_gain
        / section_norm
        * (grad_section - section_gain_grad[None, :, None] / section_norm * section_v)
    )
    three_v_list, three_g_list, mix_v_list, mix_g_list, skip_v_list, skip_g_list = (
        [],
        [],
        [],
        [],
        [],
        [],
    )
    for block_index in range(3):
        three_v, three_g, three_norm, mix_v, mix_g, mix_norm, skip_v, skip_g, skip_norm = (
            kept_norms[block_index]
        )
        grad_v, grad_g = norm_back(
            grad_three_all[block_index], three_v, three_g, three_norm, (0, 1)
        )
        three_v_list.append(grad_v)
        three_g_list.append(grad_g.reshape(-1))
        grad_v, grad_g = norm_back(grad_mix_all[block_index], mix_v, mix_g, mix_norm, (0,))
        mix_v_list.append(grad_v)
        mix_g_list.append(grad_g.reshape(-1))
        grad_v, grad_g = norm_back(grad_skip_all[block_index], skip_v, skip_g, skip_norm, (0,))
        skip_v_list.append(grad_v)
        skip_g_list.append(grad_g.reshape(-1))
    channel_results = [
        section_v_grad,
        grad_section_bias,
        jnp.stack(three_v_list),
        jnp.stack(three_g_list),
        three_bias_all,
        jnp.stack(mix_v_list),
        jnp.stack(mix_g_list),
        bias_all,
        jnp.stack(skip_v_list),
        jnp.stack(skip_g_list),
    ]
    output = output.T
    (
        section_v_grad,
        grad_section_bias,
        dilated_v_grad,
        dilated_g_grad,
        three_bias_all,
        mix_v_grad,
        mix_g_grad,
        bias_all,
        skip_v_grad,
        skip_g_grad,
    ) = channel_results
    section_v_grad = jnp.transpose(section_v_grad, (2, 0, 1))
    dilated_v_grad = jnp.transpose(dilated_v_grad, (0, 3, 1, 2))
    mix_v_grad = jnp.transpose(mix_v_grad, (0, 2, 1))
    skip_v_grad = jnp.transpose(skip_v_grad, (0, 2, 1))
    return (
        output,
        signal_grad,
        section_v_grad,
        section_gain_grad,
        grad_section_bias,
        dilated_v_grad,
        dilated_g_grad,
        three_bias_all,
        mix_v_grad,
        mix_g_grad,
        bias_all,
        skip_v_grad,
        skip_g_grad,
        bias_all,
    )


def solution(mesh):
    return jax.shard_map(
        body,
        mesh=mesh,
        in_specs=(
            P("tm", "chan"),
            P(),
            P("chan", None, None),
            P(),
            P("chan"),
            P(None, "chan", None, None),
            P(None, "chan"),
            P(None, "chan"),
            P(None, "chan", None),
            P(None, "chan"),
            P(None, "chan"),
            P(None, "chan", None),
            P(None, "chan"),
            P(None, "chan"),
            P("chan", "tm"),
        ),
        out_specs=(
            P("chan", "tm"),
            P("tm", "chan"),
            P("chan", None, None),
            P(),
            P("chan"),
            P(None, "chan", None, None),
            P(None, "chan"),
            P(None, "chan"),
            P(None, "chan", None),
            P(None, "chan"),
            P(None, "chan"),
            P(None, "chan", None),
            P(None, "chan"),
            P(None, "chan"),
        ),
        check_vma=False,
    )
```

profile of v0, /device:TPU:9, one launch (start us, length us, event | category | flops | bytes accessed | tf_op | source)
XLA Modules:
  0.0 3082.4 jit_solution(8734164508046547350)
XLA Ops:
  16.5 5.6 concatenate.46
  24.6 7.0 psum.63
  35.6 32.1 %all-gather.8.cloned.1.call-done = bf16[2050,512]{1,0:T(8,128)(2,1)} async-done(((bf16[2050,128]{1,0:T(8,128)(2,1)}), bf16[2050,512]{1,0:T(8,128)(2,1)}) %all-gather.8.cloned.1.call-update) | async-done | bytes 2099216 | tf_op jit(solution)/shard_map/all_gather | solution.py:46
  75.5 7.0 reshape.576
  82.5 6.8 copy.46
  106.9 145.2 %all-gather.10.cloned.1.call-done = bf16[16386,256]{0,1:T(8,128)(2,1)} async-done(((bf16[16386,64]{0,1:T(8,128)(2,1)}), bf16[16386,256]{0,1:T(8,128)(2,1)}) %all-gather.10.cloned.1.call-update) | async-done | bytes 8389648 | tf_op jit(solution)/shard_map/all_gather | solution.py:46
  252.1 6.6 fusion.27
  263.5 5.4 multiply_convert_fusion.5
  271.0 146.0 %all-gather.12.cloned.1.call-done = bf16[16384,256]{0,1:T(8,128)(2,1)} async-done(((bf16[16384,64]{0,1:T(8,128)(2,1)}), bf16[16384,256]{0,1:T(8,128)(2,1)}) %all-gather.12.cloned.1.call-update) | async-done | bytes 8388624 | tf_op jit(solution)/shard_map/all_gather | solution.py:46
  422.1 6.6 fusion.22
  442.3 148.0 %all-gather.14.cloned.1.call-done = bf16[16390,256]{0,1:T(8,128)(2,1)} async-done(((bf16[16390,64]{0,1:T(8,128)(2,1)}), bf16[16390,256]{0,1:T(8,128)(2,1)}) %all-gather.14.cloned.1.call-update) | async-done | bytes 8391696 | tf_op jit(solution)/shard_map/all_gather | solution.py:46
  590.3 6.6 fusion.31
  601.7 5.5 multiply_convert_fusion.4
  607.3 147.9 %all-gather.16.cloned.1.call-done = bf16[16384,256]{0,1:T(8,128)(2,1)} async-done(((bf16[16384,64]{0,1:T(8,128)(2,1)}), bf16[16384,256]{0,1:T(8,128)(2,1)}) %all-gather.16.cloned.1.call-update) | async-done | bytes 8388624 | tf_op jit(solution)/shard_map/all_gather | solution.py:46
  760.2 6.6 fusion.21
  777.1 6.5 concatenate.50
  783.8 8.6 convolution_bitcast_fusion
  792.5 8.7 convolution_bitcast_fusion.1
  801.3 130.9 %all-gather.18.cloned.1.call-done = bf16[16402,256]{0,1:T(8,128)(2,1)} async-done(((bf16[16402,64]{0,1:T(8,128)(2,1)}), bf16[16402,256]{0,1:T(8,128)(2,1)}) %all-gather.18.cloned.1.call-update) | async-done | bytes 8397840 | tf_op jit(solution)/shard_map/all_gather | solution.py:46
  932.2 6.6 fusion.35
  947.7 265.2 %reduce-scatter.8.cloned.1.call-done = f32[16384,64]{0,1:T(8,128)} async-done(((f32[16384,256]{0,1:T(8,128)}), f32[16384,64]{0,1:T(8,128)}) %reduce-scatter.8.cloned.1.call-update) | async-done | bytes 4194320 | tf_op jit(solution)/shard_map/reduce_scatter | solution.py:54
  1212.9 14.6 convert_reduce_fusion.3
  1236.0 9.9 fusion.5
  1245.9 22.4 fusion.11
  1268.9 280.0 %reduce-scatter.10.cloned.1.call-done = f32[16384,64]{0,1:T(8,128)} async-done(((f32[16384,256]{0,1:T(8,128)}), f32[16384,64]{0,1:T(8,128)}) %reduce-scatter.10.cloned.1.call-update) | async-done | bytes 4194320 | tf_op jit(solution)/shard_map/reduce_scatter | solution.py:54
  1552.0 8.2 fusion.310
  1560.3 8.3 fusion.307
  1568.6 272.8 %reduce-scatter.12.cloned.1.call-done = f32[16384,64]{0,1:T(8,128)} async-done(((f32[16384,256]{0,1:T(8,128)}), f32[16384,64]{0,1:T(8,128)}) %reduce-scatter.12.cloned.1.call-update) | async-done | bytes 4194320 | tf_op jit(solution)/shard_map/reduce_scatter | solution.py:54
  1854.9 9.9 fusion.3
  1864.8 22.5 fusion.10
  1887.4 280.4 %reduce-scatter.14.cloned.1.call-done = f32[16384,64]{0,1:T(8,128)} async-done(((f32[16384,256]{0,1:T(8,128)}), f32[16384,64]{0,1:T(8,128)}) %reduce-scatter.14.cloned.1.call-update) | async-done | bytes 4194320 | tf_op jit(solution)/shard_map/reduce_scatter | solution.py:54
  2170.9 8.2 fusion.316
  2180.0 8.3 fusion.313
  2188.3 272.0 %reduce-scatter.16.cloned.1.call-done = f32[16384,64]{0,1:T(8,128)} async-done(((f32[16384,256]{0,1:T(8,128)}), f32[16384,64]{0,1:T(8,128)}) %reduce-scatter.16.cloned.1.call-update) | async-done | bytes 4194320 | tf_op jit(solution)/shard_map/reduce_scatter | solution.py:54
  2473.9 10.4 fusion.1
  2484.3 22.8 fusion.9
  2508.7 7.4 fusion.166
  2516.2 6.2 fusion.161
  2530.6 82.4 %all-gather.20.cloned.1.call-done = bf16[16384,256]{0,1:T(8,128)(2,1)} async-done(((bf16[16384,64]{0,1:T(8,128)(2,1)}), bf16[16384,256]{0,1:T(8,128)(2,1)}) %all-gather.20.cloned.1.call-update) | async-done | bytes 8388624 | tf_op jit(solution)/shard_map/all_gather | solution.py:46
  2613.0 6.6 convolution_bitcast_fusion.2
  2619.7 6.2 convolution_bitcast_fusion.3
  2625.9 7.4 fusion.129
  2664.1 229.7 %reduce-scatter.18.cloned.1.call-done = f32[16384,64]{0,1:T(8,128)} async-done(((f32[16384,256]{0,1:T(8,128)}), f32[16384,64]{0,1:T(8,128)}) %reduce-scatter.18.cloned.1.call-update) | async-done | bytes 4194320 | tf_op jit(solution)/shard_map/reduce_scatter | solution.py:54
  2940.7 8.2 fusion.23
  2948.9 12.9 all-reduce.1
  2961.8 32.0 %all-reduce.5.cloned.1.call-done = (f32[16,512,64]{1,2,0:T(8,128)}, f32[3,3,256,64]{2,3,1,0:T(8,128)}, f32[3,256,64]{1,2,0:T(8,128)}, f32[3,256,64]{1,2,0:T(8,128)}) async-done(((f32[16,512,64]{1,2,0:T(8,128)}, f32[3,3,256,64]{2,3,1,0:T(8,128)}, f32[3,256,64]{1,2,0:T(8,128)}, f32[3,256,64]{1,2,0:T(8,128)}), (f32[16,512,64]{1,2,0:T(8,128)}, f32[3,3,256,64]{2,3,1,0:T(8,128)}, f32[3,256,64]{1,2,0:T(8,128)}, ...) | async-done | bytes 3080208 | tf_op jit(solution)/shard_map/psum | solution.py:221
  2996.2 7.1 psum.65
  3011.4 61.6 %reduce-scatter.20.cloned.1.call-done = f32[2048,128]{1,0:T(8,128)} async-done(((f32[2048,512]{1,0:T(8,128)}), f32[2048,128]{1,0:T(8,128)}) %reduce-scatter.20.cloned.1.call-update) | async-done | bytes 1048592 | tf_op jit(solution)/shard_map/reduce_scatter | solution.py:54
  (455 shorter events, 237.7 us)
Async XLA Ops:
  7.2 60.5 %all-gather.8.cloned.1.call-start = ((), (), s32[]{:S(2)}) async-start(), calls=%async_computation.7 | async-start | bytes 2631680 | tf_op jit(solution)/shard_map/all_gather | solution.py:46
  8.0 5.6 collective-permute-start
  11.6 4.9 collective-permute-start.1
  22.1 230.0 %all-gather.10.cloned.1.call-start = ((), (), s32[]{:S(2)}) async-start(), calls=%async_computation.8 | async-start | bytes 10567680 | tf_op jit(solution)/shard_map/all_gather | solution.py:46
  91.9 4.4 collective-permute-start.2
  94.4 5.1 collective-permute-start.3
  103.6 313.4 %all-gather.12.cloned.1.call-start = ((), (), s32[]{:S(2)}) async-start(), calls=%async_computation.9 | async-start | bytes 10485760 | tf_op jit(solution)/shard_map/all_gather | solution.py:46
  105.8 153.0 %copy-start.99 = (f32[64]{0:T(128)}, f32[64]{0:T(128)S(1)}, u32[]{:S(2)}) copy-start(f32[64]{0:T(128)S(1)} %get-tuple-element.65) | copy-start | bytes 772
  105.8 153.0 %copy-start.101 = (f32[64]{0:T(128)}, f32[64]{0:T(128)S(1)}, u32[]{:S(2)}) copy-start(f32[64]{0:T(128)S(1)} %get-tuple-element.66) | copy-start | bytes 772
  105.8 153.0 %copy-start.103 = (f32[64]{0:T(128)}, f32[64]{0:T(128)S(1)}, u32[]{:S(2)}) copy-start(f32[64]{0:T(128)S(1)} %get-tuple-element.67) | copy-start | bytes 772
  106.0 157.4 %copy-start.39 = (bf16[3,256,64]{1,2,0:T(8,128)(2,1)}, bf16[3,256,64]{1,2,0:T(8,128)(2,1)S(1)}, u32[]{:S(2)}) copy-start(bf16[3,256,64]{1,2,0:T(8,128)(2,1)S(1)} %get-tuple-element.140) | copy-start | bytes 294916
  106.9 155.0 %copy-start.41 = (f32[16384]{0:T(1024)}, f32[16384]{0:T(1024)S(1)}, u32[]{:S(2)}) copy-start(f32[16384]{0:T(1024)S(1)} %get-tuple-element.148) | copy-start | bytes 196612
  106.9 493.2 %copy-start.43 = (f32[16384]{0:T(1024)}, f32[16384]{0:T(1024)S(1)}, u32[]{:S(2)}) copy-start(f32[16384]{0:T(1024)S(1)} %get-tuple-element.150) | copy-start | bytes 196612
  269.0 321.3 %all-gather.14.cloned.1.call-start = ((), (), s32[]{:S(2)}) async-start(), calls=%async_computation.10 | async-start | bytes 10567680 | tf_op jit(solution)/shard_map/all_gather | solution.py:46
  269.2 338.0 %copy-start.82 = (f32[64]{0:T(128)}, f32[64]{0:T(128)S(1)}, u32[]{:S(2)}) copy-start(f32[64]{0:T(128)S(1)} %get-tuple-element.72) | copy-start | bytes 772
  269.2 514.5 %copy-start.80 = (f32[64]{0:T(128)}, f32[64]{0:T(128)S(1)}, u32[]{:S(2)}) copy-start(f32[64]{0:T(128)S(1)} %get-tuple-element.71) | copy-start | bytes 772
  269.4 337.8 %copy-start.86 = (f32[64]{0:T(128)}, f32[64]{0:T(128)S(1)}, u32[]{:S(2)}) copy-start(f32[64]{0:T(128)S(1)} %get-tuple-element.70) | copy-start | bytes 772
  269.4 523.0 %copy-start.84 = (f32[64]{0:T(128)}, f32[64]{0:T(128)S(1)}, u32[]{:S(2)}) copy-start(f32[64]{0:T(128)S(1)} %get-tuple-element.68) | copy-start | bytes 772
  269.4 152.6 %copy-start.88 = (f32[64]{0:T(128)}, f32[64]{0:T(128)S(1)}, u32[]{:S(2)}) copy-start(f32[64]{0:T(128)S(1)} %fusion.288) | copy-start | bytes 772
  269.9 152.2 %copy-start.78 = (f32[64]{0:T(128)}, f32[64]{0:T(128)S(1)}, u32[]{:S(2)}) copy-start(f32[64]{0:T(128)S(1)} %fusion.289) | copy-start | bytes 772
  269.9 152.1 %copy-start.76 = (f32[64]{0:T(128)}, f32[64]{0:T(128)S(1)}, u32[]{:S(2)}) copy-start(f32[64]{0:T(128)S(1)} %get-tuple-element.176) | copy-start | bytes 772
  269.9 513.8 %copy-start.57 = (f32[64]{0:T(128)}, f32[64]{0:T(128)S(1)}, u32[]{:S(2)}) copy-start(f32[64]{0:T(128)S(1)} %get-tuple-element.174) | copy-start | bytes 772
  270.5 522.0 %copy-start.55 = (f32[64]{0:T(128)}, f32[64]{0:T(128)S(1)}, u32[]{:S(2)}) copy-start(f32[64]{0:T(128)S(1)} %get-tuple-element.168) | copy-start | bytes 772
  428.8 5.7 collective-permute-start.4
  432.5 5.1 collective-permute-start.5
  441.8 313.3 %all-gather.16.cloned.1.call-start = ((), (), s32[]{:S(2)}) async-start(), calls=%async_computation.11 | async-start | bytes 10485760 | tf_op jit(solution)/shard_map/all_gather | solution.py:46
  607.2 325.0 %all-gather.18.cloned.1.call-start = ((), (), s32[]{:S(2)}) async-start(), calls=%async_computation.12 | async-start | bytes 10567680 | tf_op jit(solution)/shard_map/all_gather | solution.py:46
  768.2 6.0 collective-permute-start.6
  772.1 5.1 collective-permute-start.7
  783.7 429.2 %reduce-scatter.8.cloned.1.call-start = ((), (), s32[]{:S(2)}) async-start(), calls=%async_computation.14 | async-start | bytes 20971520 | tf_op jit(solution)/shard_map/reduce_scatter | solution.py:54
  792.4 756.5 %reduce-scatter.10.cloned.1.call-start = ((), (), s32[]{:S(2)}) async-start(), calls=%async_computation.15 | async-start | bytes 20971520 | tf_op jit(solution)/shard_map/reduce_scatter | solution.py:54
  1227.6 8.4 collective-permute-start.8
  1232.6 13.3 collective-permute-start.9
  1268.4 573.0 %reduce-scatter.12.cloned.1.call-start = ((), (), s32[]{:S(2)}) async-start(), calls=%async_computation.16 | async-start | bytes 20971520 | tf_op jit(solution)/shard_map/reduce_scatter | solution.py:54
  1560.2 607.5 %reduce-scatter.14.cloned.1.call-start = ((), (), s32[]{:S(2)}) async-start(), calls=%async_computation.17 | async-start | bytes 20971520 | tf_op jit(solution)/shard_map/reduce_scatter | solution.py:54
  1846.4 8.5 collective-permute-start.10
  1851.2 13.6 collective-permute-start.11
  1887.3 283.6 %copy-start.77 = (f32[64]{0:T(128)S(1)}, f32[64]{0:T(128)}, u32[]{:S(2)}) copy-start(f32[64]{0:T(128)} %copy-done.76) | copy-start | bytes 772
  1887.3 283.6 %copy-start.89 = (f32[64]{0:T(128)S(1)}, f32[64]{0:T(128)}, u32[]{:S(2)}) copy-start(f32[64]{0:T(128)} %copy-done.88) | copy-start | bytes 772
  1887.3 573.0 %reduce-scatter.16.cloned.1.call-start = ((), (), s32[]{:S(2)}) async-start(), calls=%async_computation.18 | async-start | bytes 20971520 | tf_op jit(solution)/shard_map/reduce_scatter | solution.py:54
  2179.1 433.9 %all-gather.20.cloned.1.call-start = ((), (), s32[]{:S(2)}) async-start(), calls=%async_computation.13 | async-start | bytes 10485760 | tf_op jit(solution)/shard_map/all_gather | solution.py:46
  2179.7 714.1 %reduce-scatter.18.cloned.1.call-start = ((), (), s32[]{:S(2)}) async-start(), calls=%async_computation.19 | async-start | bytes 20971520 | tf_op jit(solution)/shard_map/reduce_scatter | solution.py:54
  2465.4 8.5 collective-permute-start.12
  2470.4 14.0 collective-permute-start.13
  2507.1 486.7 %all-reduce.5.cloned.1.call-start = ((), (), s32[]{:S(2)}) async-start(), calls=%async_computation.21 | async-start | bytes 6160384 | tf_op jit(solution)/shard_map/psum | solution.py:221
  2915.3 12.7 collective-permute-start.14
  2920.7 152.3 %reduce-scatter.20.cloned.1.call-start = ((), (), s32[]{:S(2)}) async-start(), calls=%async_computation.20 | async-start | bytes 5242880 | tf_op jit(solution)/shard_map/reduce_scatter | solution.py:54
  2924.2 4.6 collective-permute-start.15
  (115 other events, 1478.3 us)
Sparse Core Ops, SparseCore 0:
  22.2 45.4 all-gather.7
  103.8 148.2 all-gather.9
  269.1 147.8 all-gather.11
  442.0 148.3 all-gather.13
  607.3 147.8 all-gather.15
  783.8 148.3 all-gather.17
  934.5 278.3 reduce-scatter.7
  1268.5 280.3 reduce-scatter.9
  1560.3 281.0 reduce-scatter.11
  1887.4 280.2 reduce-scatter.13
  2179.2 281.0 reduce-scatter.15
  2462.4 150.5 all-gather.19
  2615.5 278.3 reduce-scatter.17
  2920.8 72.9 all-reduce.4
  2995.9 77.0 reduce-scatter.19
where the time goes:
time: 3090 us; the launch traced here: 3080 us
  waiting for transfers between devices  2540 us (82%)
  matrix products  327 us (11%)
  other arithmetic  67.3 us (2%)
  local copies, waits for them, and re-layouts  57.3 us (2%)
  starting transfers between devices  48.3 us (2%)
    reduce_scatter x7, waiting for transfers between devices, channel_sum(): return lax.psum_scatter(values, 'chan', scatter_dimension=1, tiled=True)  1660 us
    all_gather x7, waiting for transfers between devices, widen(): return lax.all_gather(values, 'chan', axis=1, tiled=True)  833 us
    dot_general x18, matrix products, contract_cols(): lax.dot_general(left_side, right_side, (((1,), (1,)), ((), ())), preferre...  164 us
    dot_general x18, matrix products, matmul(): return jnp.dot(left_side, right_side, preferred_element_type=jnp.float32)  85.3 us
    dot_general x18, matrix products, contract_rows(): lax.dot_general(left_side, right_side, (((0,), (0,)), ((), ())), preferre...  77.8 us
  transfers between devices with their start and end apart: 31, of which 19 were waited for; matrix products, arithmetic and copies ran while one was open for 8% of the time, Pallas kernels for 0%

commit v1 on v0

v1 whole, which is shorter than its diff:
```python
import jax
import jax.numpy as jnp
from jax import lax
from jax.experimental import pallas as pl
from jax.experimental.pallas import tpu as pltpu
from jax.sharding import PartitionSpec as P

EPSILON = 1e-06
F32 = jnp.float32
BF16 = jnp.bfloat16
HALO = 8
VMEM_BYTES = 60 * 1024 * 1024


def xor_pairs(axis, bit):
    return [(i, i ^ bit) for i in range(lax.axis_size(axis))]


def swap(values, axis, bit):
    return lax.ppermute(values, axis, xor_pairs(axis, bit))


def spread(piece):
    half = piece.shape[0] // 2
    by_x = swap(piece, "tm", 2)
    by_y = swap(piece, "tm", 4)
    far_a = swap(by_y[:half], "tm", 2)
    far_b = swap(by_x[half:], "tm", 4)
    near = [piece, by_x, by_y, far_a, far_b]
    return near + [swap(entry, "tm", 1) for entry in near]


SPREAD_PLACES = [(0, 0, 2), (2, 0, 2), (4, 0, 2), (6, 0, 1), (6, 1, 1)]
SPREAD_PLACES = SPREAD_PLACES + [(a + 1, first, count) for a, first, count in SPREAD_PLACES]


def edges(block, dim, width):
    count = lax.axis_size("tm")
    forward = [(i, i + 1) for i in range(count - 1)]
    backward = [(target, source) for source, target in forward]
    size = block.shape[dim]
    low = lax.ppermute(lax.slice_in_dim(block, size - width, None, axis=dim), "tm", forward)
    high = lax.ppermute(lax.slice_in_dim(block, 0, width, axis=dim), "tm", backward)
    return low, high


def nt(left, right):
    return lax.dot_general(left, right, (((1,), (1,)), ((), ())), preferred_element_type=F32)


def nn(left, right):
    return lax.dot_general(left, right, (((1,), (0,)), ((), ())), preferred_element_type=F32)


def tn(left, right):
    return lax.dot_general(left, right, (((0,), (0,)), ((), ())), preferred_element_type=F32)


def sigmoid(values):
    return 0.5 * jnp.tanh(0.5 * values) + 0.5


def doubled(mask):
    return jnp.concatenate([mask, mask], axis=1)


def moved(values, rows):
    return pltpu.roll(values, (-rows) % values.shape[0], 0)


def spread_phases(store, mask_ref, phase, values, dilate):
    def masked(rows, mask_index):
        return (moved(values, rows) * doubled(mask_ref[mask_index])).astype(BF16)

    store[9 + phase] = values.astype(BF16)

    @pl.when(phase >= 8 - min(dilate, 8))
    def _():
        store[1 + phase] = masked(-1, 0)

    @pl.when(phase <= min(dilate, 8) - 1)
    def _():
        store[17 + phase] = masked(1, 1)

    if dilate > 8:

        @pl.when(phase == 7)
        def _():
            store[0] = masked(-2, 2)

        @pl.when(phase == 0)
        def _():
            store[25] = masked(2, 3)


def weight_copies(places, refs, wsec, wblk, sem):
    turn, chan = places[0], places[1]
    copies = []
    for ref, (place, first, _) in zip(refs, SPREAD_PLACES, strict=True):
        pair = 2 * (turn ^ place)
        for k in range(ref.shape[0]):
            rows = pl.ds(pl.multiple_of(64 * (chan ^ (2 * first + k)), 64), 64)
            copies.append(
                pltpu.make_async_copy(
                    ref.at[k, :, :, 0:512], wsec.at[pl.ds(pair, 2), rows, :], sem
                )
            )
            copies.append(
                pltpu.make_async_copy(
                    ref.at[k, :, :, 512:768], wblk.at[pl.ds(pair, 2), rows, :], sem
                )
            )
    return copies


def forward_kernel(
    places,
    sig0,
    sig1,
    sig2,
    sig3,
    mask_ref,
    gain_ref,
    *rest,
):
    pieces = rest[:10]
    hid_out, act_out, mix_out, dsi_out, dsh_out = rest[10:15]
    sact_out, dsig_out, stat_out = rest[15:18]
    outs = rest[18:22]
    wsec, wblk, cat, bias, hid, mix, dsi, dsh, act, wide, turned, wsem, ssem, osem = rest[22:]
    chan = places[1]
    rows = sig0.shape[0]
    own = rows - 2 * HALO
    loads = weight_copies(places, pieces, wsec, wblk, wsem)
    for copy in loads:
        copy.start()
    for k, ref in enumerate((sig0, sig1, sig2, sig3)):
        lanes = pl.ds(pl.multiple_of(128 * (chan ^ k), 128), 128)
        values = ref[...].astype(F32)
        s = sigmoid(values)
        a = values * s
        sact_out[:, lanes] = a.astype(BF16)
        dsig_out[:, lanes] = (s + a * (1.0 - s))[:own]
    for copy in loads:
        copy.wait()

    def square(k, total):
        part = wsec[k].astype(F32)
        return total + jnp.sum((part * part).reshape(32, 8, 512), axis=0)

    total = lax.fori_loop(0, 16, square, jnp.zeros((8, 512), F32))
    norm = jnp.sqrt(jnp.sum(total, axis=0, keepdims=True) + EPSILON)
    scale = gain_ref[...] / norm
    stat_out[...] = jnp.concatenate([norm, scale, jnp.zeros((6, 512), F32)], axis=0)
    bias[...] = jnp.transpose(wblk[15].astype(F32))[:16]
    scaled = sact_out[...].astype(F32) * scale
    cat[0] = scaled.astype(BF16)
    cat[1] = (moved(scaled, -1) * doubled(doubled(mask_ref[0]))).astype(BF16)
    cat[2] = (moved(scaled, 1) * doubled(doubled(mask_ref[1]))).astype(BF16)

    def section(r, carry):
        total = nt(cat[0], wsec[r + 4]) + nt(cat[1 + r // 4], wsec[lax.rem(r + 12, 16)])
        hid[0, r] = (total + bias[0:1]).astype(BF16)
        return carry

    lax.fori_loop(0, 8, section, 0)

    def save(b, r, part, whole, out):
        pltpu.make_async_copy(part, whole, out).start()

    for b in range(3):
        dilate = 3**b

        def widen(p, carry):
            h = hid[b, p].astype(F32)
            s = sigmoid(h)
            a = h * s
            dsh[b, p] = (s + a * (1.0 - s)).astype(BF16)
            spread_phases(act, mask_ref, p, a, dilate)
            pltpu.make_async_copy(hid.at[b, p], hid_out.at[b, p], ssem).start()
            pltpu.make_async_copy(dsh.at[b, p], dsh_out.at[b, p], ssem).start()
            pltpu.make_async_copy(act.at[9 + p], act_out.at[b, p], osem).start()
            return carry

        lax.fori_loop(0, 8, widen, 0)

        def block(r, carry):
            inner = (
                nt(act[9 + r - dilate], wblk[5 * b])
                + nt(act[9 + r], wblk[5 * b + 1])
                + nt(act[9 + r + dilate], wblk[5 * b + 2])
                + bias[1 + b : 2 + b]
            )
            s = sigmoid(inner)
            m = inner * s
            mixed = m.astype(BF16)
            mix[b, r] = mixed
            dsi[b, r] = (s + m * (1.0 - s)).astype(BF16)
            pltpu.make_async_copy(mix.at[b, r], mix_out.at[b, r], ssem).start()
            pltpu.make_async_copy(dsi.at[b, r], dsi_out.at[b, r], ssem).start()
            after = nt(mixed, wblk[5 * b + 3]) + nt(hid[b, r], wblk[5 * b + 4])
            after = after + (bias[4 + b : 5 + b] + bias[7 + b : 8 + b])
            if b < 2:
                hid[b + 1, r] = after.astype(BF16)
            else:
                for half in range(2):
                    wide[half, pl.ds(r, own, stride=8), :] = after[:own, 128 * half : 128 * half + 128]
            return carry

        lax.fori_loop(0, 8, block, 0)
        for p in range(8):
            pltpu.make_async_copy(act.at[9 + p], act_out.at[b, p], osem).wait()

    def turn(q, carry):
        frames = pl.ds(pl.multiple_of(128 * q, 128), 128)
        for half in range(2):
            part = wide[half, frames, :]
            turned[128 * half : 128 * half + 128, frames] = jnp.transpose(part).astype(BF16)
        return carry

    lax.fori_loop(0, 8 * own // 128, turn, 0)
    final = []
    for k, out in enumerate(outs):
        part = turned.at[pl.ds(pl.multiple_of(64 * (chan ^ k), 64), 64), :]
        final.append(pltpu.make_async_copy(part, out, osem))
    for copy in final:
        copy.start()
    for source, out in ((hid, hid_out), (dsh, dsh_out), (mix, mix_out), (dsi, dsi_out)):
        for b in range(3):
            for p in range(8):
                pltpu.make_async_copy(source.at[b, p], out.at[b, p], ssem).wait()
    for copy in final:
        copy.wait()


def backward_kernel(
    places,
    cot0,
    cot1,
    cot2,
    cot3,
    mask_ref,
    sact_ref,
    dsig_ref,
    stat_ref,
    hid_in,
    act_in,
    mix_in,
    dsi_in,
    dsh_in,
    *rest,
):
    pieces = rest[:10]
    even_out, odd_out = rest[10:12]
    sgrads = rest[12:16]
    (wsec, wblk, turned, wide, grad, inner, both, act, dsi, dsh) = rest[16:26]
    (acc_one, acc_three, through, sums, staged, wsem, csem, bsem, osem) = rest[26:]
    turn_index, chan = places[0], places[1]
    rows = mask_ref.shape[1]
    own = rows - 2 * HALO

    loads = weight_copies(places, pieces, wsec, wblk, wsem)
    cots = []
    for k, ref in enumerate((cot0, cot1, cot2, cot3)):
        part = turned.at[pl.ds(pl.multiple_of(64 * (chan ^ k), 64), 64), :]
        cots.append(pltpu.make_async_copy(ref, part, csem))

    def kept(b):
        slot = b % 2
        return [
            pltpu.make_async_copy(mix_in.at[b, :, 0:own], both.at[slot, :, :, 0:256], bsem.at[slot]),
            pltpu.make_async_copy(hid_in.at[b, :, 0:own], both.at[slot, :, :, 256:512], bsem.at[slot]),
            pltpu.make_async_copy(act_in.at[b, :, 0:own], act.at[slot], bsem.at[slot]),
            pltpu.make_async_copy(dsi_in.at[b], dsi.at[slot], bsem.at[slot]),
            pltpu.make_async_copy(dsh_in.at[b], dsh.at[slot], bsem.at[slot]),
        ]

    for copy in cots + loads + kept(2) + kept(1):
        copy.start()
    for copy in cots:
        copy.wait()

    def turn(q, carry):
        frames = pl.ds(pl.multiple_of(128 * q, 128), 128)
        for half in range(2):
            part = turned[128 * half : 128 * half + 128, frames].astype(F32)
            wide[half, frames, :] = jnp.transpose(part)
        return carry

    lax.fori_loop(0, 8 * rows // 128, turn, 0)

    def phases(r, carry):
        for half in range(2):
            part = wide[half, pl.ds(r, rows, stride=8), :]
            grad[r, :, 128 * half : 128 * half + 128] = part.astype(BF16)
        return carry

    lax.fori_loop(0, 8, phases, 0)
    for copy in loads:
        copy.wait()
    sums[...] = jnp.zeros_like(sums)

    def own_sum(values):
        return jnp.sum(values[:own].reshape(own // 8, 8, 256), axis=0)

    for b in (2, 1, 0):
        dilate = 3**b
        slot = b % 2
        for copy in kept(b):
            copy.wait()
        acc_one[...] = jnp.zeros_like(acc_one)
        acc_three[...] = jnp.zeros_like(acc_three)

        def first(r, carry):
            g = grad[r]
            down = nn(g, wblk[5 * b + 3])
            ig = down * dsi[slot, r].astype(F32)
            spread_phases(inner, mask_ref, r, ig, dilate)
            acc_one[...] += tn(g[:own], both[slot, r])
            sums[1 + b] += own_sum(ig)
            sums[4 + b] += own_sum(g.astype(F32))
            return carry

        lax.fori_loop(0, 8, first, 0)

        def second(r, carry):
            low, mid, high = inner[9 + r - dilate], inner[9 + r], inner[9 + r + dilate]
            deep = nn(high, wblk[5 * b]) + nn(mid, wblk[5 * b + 1]) + nn(low, wblk[5 * b + 2])
            back = nn(grad[r], wblk[5 * b + 4]) + dsh[slot, r].astype(F32) * deep
            grad[r] = back.astype(BF16)
            a = act[slot, r]
            acc_three[:, 0:256] += tn(a, high[:own])
            acc_three[:, 256:512] += tn(a, mid[:own])
            acc_three[:, 512:768] += tn(a, low[:own])
            return carry

        lax.fori_loop(0, 8, second, 0)
        for tap in range(3):
            part = jnp.transpose(acc_three[:, 256 * tap : 256 * tap + 256])
            staged[5 * b + tap, :, 512:768] = part.astype(BF16)
        staged[5 * b + 3, :, 512:768] = acc_one[:, 0:256].astype(BF16)
        staged[5 * b + 4, :, 512:768] = acc_one[:, 256:512].astype(BF16)
        if b == 2:
            for copy in kept(0):
                copy.start()

    def taps(r, carry):
        g = grad[r].astype(F32)
        sums[0] += own_sum(g)
        inner[r + 4] = grad[r]
        early = r < 4
        nearby = jnp.where(early, moved(g, 1), moved(g, -1))
        mask = jnp.where(early, mask_ref[1], mask_ref[0])
        inner[lax.rem(r + 12, 16)] = (nearby * doubled(mask)).astype(BF16)
        return carry

    lax.fori_loop(0, 8, taps, 0)
    through[...] = jnp.zeros_like(through)

    def collect(k, carry):
        through[...] += nn(inner[k, 0:own], wsec[k])
        return carry

    lax.fori_loop(0, 16, collect, 0)
    deep = through[...]
    sact = sact_ref[0:own]
    gains = jnp.sum(sact.astype(F32) * deep, axis=0, keepdims=True)
    signal_grad = deep * stat_ref[1:2] * dsig_ref[...]
    through[...] = signal_grad
    for k, out in enumerate(sgrads):
        lanes = pl.ds(pl.multiple_of(128 * (chan ^ k), 128), 128)
        out[...] = through[:, lanes].astype(BF16)
    biases = jnp.concatenate(
        [jnp.sum(sums[index], axis=0, keepdims=True) for index in range(8)]
        + [jnp.zeros((120, 256), F32)],
        axis=0,
    )
    staged[15, :, 512:640] = jnp.transpose(biases).astype(BF16)
    gain_rows = jnp.concatenate(
        [gains[:, 128 * q : 128 * q + 128] for q in range(4)] + [jnp.zeros((60, 128), F32)], axis=0
    ).astype(BF16)
    for part in range(4):
        staged[15, 64 * part : 64 * part + 64, 640:768] = gain_rows

    def finish(pair, carry):
        for tap in range(2):
            k = 2 * pair + tap
            staged[k, :, 0:512] = tn(inner[k, 0:own], sact).astype(BF16)
        place = pair ^ turn_index
        source = staged.at[pl.ds(2 * pair, 2)]

        @pl.when(lax.rem(place, 2) == 0)
        def _():
            pltpu.make_async_copy(source, even_out.at[place // 2], osem).start()

        @pl.when(lax.rem(place, 2) == 1)
        def _():
            pltpu.make_async_copy(source, odd_out.at[place // 2], osem).start()

        return carry

    lax.fori_loop(0, 8, finish, 0)
    for pair in range(8):
        pltpu.make_async_copy(staged.at[pl.ds(2 * pair, 2)], even_out.at[0], osem).wait()


def shape_of(shape, kind=BF16):
    return jax.ShapeDtypeStruct(shape, kind)


SPEC_VMEM = pl.BlockSpec(memory_space=pltpu.VMEM)
SPEC_ANY = pl.BlockSpec(memory_space=pl.ANY)
SPEC_SMEM = pl.BlockSpec(memory_space=pltpu.SMEM)


def run_forward(places, signals, masks, gain, pieces):
    rows = masks.shape[1]
    own = rows - 2 * HALO
    kept = shape_of((3, 8, rows, 256))
    out_shape = [kept] * 5 + [
        shape_of((rows, 512)),
        shape_of((own, 512), F32),
        shape_of((8, 512), F32),
    ]
    out_shape = out_shape + [shape_of((64, 8 * own))] * 4
    return pl.pallas_call(
        forward_kernel,
        out_shape=out_shape,
        in_specs=[SPEC_SMEM] + [SPEC_VMEM] * 6 + [SPEC_ANY] * 10,
        out_specs=[SPEC_ANY] * 5 + [SPEC_VMEM] * 3 + [SPEC_ANY] * 4,
        scratch_shapes=[
            pltpu.VMEM((16, 256, 512), BF16),
            pltpu.VMEM((16, 256, 256), BF16),
            pltpu.VMEM((3, rows, 512), BF16),
            pltpu.VMEM((16, 256), F32),
            pltpu.VMEM((3, 8, rows, 256), BF16),
            pltpu.VMEM((3, 8, rows, 256), BF16),
            pltpu.VMEM((3, 8, rows, 256), BF16),
            pltpu.VMEM((3, 8, rows, 256), BF16),
            pltpu.VMEM((26, rows, 256), BF16),
            pltpu.VMEM((2, 8 * own, 128), F32),
            pltpu.VMEM((256, 8 * own), BF16),
            pltpu.SemaphoreType.DMA,
            pltpu.SemaphoreType.DMA,
            pltpu.SemaphoreType.DMA,
        ],
        compiler_params=pltpu.CompilerParams(vmem_limit_bytes=VMEM_BYTES),
        name="forward_blocks",
    )(places, *signals, masks, gain, *pieces)


def run_backward(places, cotangents, masks, sact, dsig, stat, kept, pieces):
    rows = masks.shape[1]
    own = rows - 2 * HALO
    return pl.pallas_call(
        backward_kernel,
        out_shape=[shape_of((4, 2, 256, 768))] * 2 + [shape_of((own, 128))] * 4,
        in_specs=[SPEC_SMEM]
        + [SPEC_ANY] * 4
        + [SPEC_VMEM] * 4
        + [SPEC_ANY] * 5
        + [SPEC_ANY] * 10,
        out_specs=[SPEC_ANY] * 2 + [SPEC_VMEM] * 4,
        scratch_shapes=[
            pltpu.VMEM((16, 256, 512), BF16),
            pltpu.VMEM((16, 256, 256), BF16),
            pltpu.VMEM((256, 8 * rows), BF16),
            pltpu.VMEM((2, 8 * rows, 128), F32),
            pltpu.VMEM((8, rows, 256), BF16),
            pltpu.VMEM((26, rows, 256), BF16),
            pltpu.VMEM((2, 8, own, 512), BF16),
            pltpu.VMEM((2, 8, own, 256), BF16),
            pltpu.VMEM((2, 8, rows, 256), BF16),
            pltpu.VMEM((2, 8, rows, 256), BF16),
            pltpu.VMEM((256, 512), F32),
            pltpu.VMEM((256, 768), F32),
            pltpu.VMEM((own, 512), F32),
            pltpu.VMEM((8, 8, 256), F32),
            pltpu.VMEM((16, 256, 768), BF16),
            pltpu.SemaphoreType.DMA,
            pltpu.SemaphoreType.DMA,
            pltpu.SemaphoreType.DMA((2,)),
            pltpu.SemaphoreType.DMA,
        ],
        compiler_params=pltpu.CompilerParams(vmem_limit_bytes=VMEM_BYTES),
        name="backward_blocks",
    )(places, *cotangents, masks, sact, dsig, stat, *kept, *pieces)


def exchange(values, axis, cut):
    me = lax.axis_index(axis)
    parts = [cut(me)]
    for k in (1, 2, 3):
        parts.append(swap(cut(me ^ k), axis, k))
    return parts


def normed(v_values, gain_values, sum_axes):
    norm_values = jnp.sqrt(jnp.sum(v_values * v_values, axis=sum_axes, keepdims=True) + EPSILON)
    return gain_values * v_values / norm_values, norm_values


def norm_back(grad_w, v_values, gain_values, norm_values, sum_axes):
    grad_g = jnp.sum(grad_w * v_values, axis=sum_axes, keepdims=True) / norm_values
    grad_v = gain_values / norm_values * (grad_w - grad_g / norm_values * v_values)
    return grad_v, grad_g


def body(
    signal,
    segment_ids,
    v_section,
    g_section,
    b_section,
    v_dilated,
    g_dilated,
    b_dilated,
    v_mix,
    g_mix,
    b_mix,
    v_skip,
    g_skip,
    b_skip,
    cotangent,
):
    tm_index, chan = lax.axis_index("tm"), lax.axis_index("chan")
    turn = tm_index % 8
    places = jnp.stack([turn, chan]).astype(jnp.int32)
    own = signal.shape[0] // 4
    rows = own + 2 * HALO
    start = tm_index * signal.shape[0] + chan * own

    padded = jnp.pad(segment_ids, HALO + 2, constant_values=-1)
    nearby = lax.dynamic_slice_in_dim(padded, start, rows + 4)

    def same(offset):
        flags = (nearby[2 : 2 + rows] == nearby[2 + offset : 2 + offset + rows]).astype(F32)
        flags = jnp.concatenate([flags[HALO:], flags[:HALO]])
        return jnp.broadcast_to(flags[:, None], (rows, 128))

    masks = jnp.stack([same(-1), same(1), same(-2), same(2)])

    low, high = edges(signal, 0, HALO)
    longer = jnp.concatenate([low, signal, high], axis=0)

    def cut_signal(place):
        block = lax.dynamic_slice_in_dim(longer, place * own, rows, axis=0)
        return jnp.concatenate([block[HALO:], block[:HALO]], axis=0)

    signals = exchange(longer, "chan", cut_signal)

    three_v, three_g = v_dilated.astype(F32), g_dilated.astype(F32)[:, :, None, None]
    mix_v, mix_g = v_mix.astype(F32), g_mix.astype(F32)[:, :, None]
    skip_v, skip_g = v_skip.astype(F32), g_skip.astype(F32)[:, :, None]
    w_three, three_norm = normed(three_v, three_g, (2, 3))
    w_mix, mix_norm = normed(mix_v, mix_g, (2,))
    w_skip, skip_norm = normed(skip_v, skip_g, (2,))
    matrices = jnp.concatenate(
        [jnp.transpose(w_three, (0, 2, 1, 3)), w_mix[:, None], w_skip[:, None]], axis=1
    ).astype(BF16)
    matrices = matrices.reshape(15, 64, 256)
    small = jnp.concatenate([b_section[None], b_dilated, b_mix, b_skip], axis=0).T
    small = jnp.pad(small, ((0, 0), (0, 246)))
    matrices = jnp.concatenate([matrices, small[None]], axis=0)
    piece = jnp.concatenate(
        [
            jnp.transpose(lax.dynamic_slice_in_dim(v_section, 2 * turn, 2, axis=1), (1, 0, 2)),
            lax.dynamic_slice_in_dim(matrices, 2 * turn, 2, axis=0),
        ],
        axis=2,
    )
    column = jnp.stack([piece] + [swap(piece, "chan", k) for k in (1, 2, 3)])
    pieces = spread(column)

    frames = 8 * own
    rim = 8 * HALO
    low, high = edges(cotangent, 1, rim)

    def cut_cotangent(place):
        main = lax.dynamic_slice_in_dim(cotangent, place * frames, frames, axis=1)
        after_start = jnp.minimum((place + 1) * frames, 3 * frames)
        before_start = jnp.maximum(place * frames - rim, 0)
        after = lax.dynamic_slice_in_dim(cotangent, after_start, rim, axis=1)
        before = lax.dynamic_slice_in_dim(cotangent, before_start, rim, axis=1)
        after = jnp.where(place == 3, high, after)
        before = jnp.where(place == 0, low, before)
        return jnp.concatenate([main, after, before], axis=1)

    cotangents = exchange(cotangent, "chan", cut_cotangent)

    section_gain = g_section.astype(F32)
    results = run_forward(places, signals, masks, section_gain[None], pieces)
    kept, sact, dsig, stat, outs = results[:5], results[5], results[6], results[7], results[8:]

    received = [outs[0]] + [swap(outs[k], "chan", k) for k in (1, 2, 3)]
    output = jnp.zeros((64, 4 * frames), BF16)
    for k in range(4):
        output = lax.dynamic_update_slice_in_dim(output, received[k], (chan ^ k) * frames, axis=1)

    results = run_backward(places, cotangents, masks, sact, dsig, stat, kept, pieces)
    even, odd, sgrads = results[0], results[1], results[2:]

    received = [sgrads[0]] + [swap(sgrads[k], "chan", k) for k in (1, 2, 3)]
    signal_grad = jnp.zeros((4 * own, 128), BF16)
    for k in range(4):
        signal_grad = lax.dynamic_update_slice_in_dim(
            signal_grad, received[k], (chan ^ k) * own, axis=0
        )

    quarter = even + swap(odd, "tm", 1)
    far_a = swap(quarter[3, :1], "tm", 2)
    far_b = swap(quarter[3, 1:], "tm", 4)
    for_y = jnp.concatenate([quarter[2, :1] + far_a, quarter[2, 1:]], axis=0)
    for_x = jnp.concatenate([quarter[1, :1], quarter[1, 1:] + far_b], axis=0)
    summed = quarter[0] + swap(for_x, "tm", 2) + swap(for_y, "tm", 4)

    def cut_rows(place):
        return lax.dynamic_slice_in_dim(summed, place * 64, 64, axis=1)

    parts = exchange(summed, "chan", cut_rows)
    mine = parts[0] + parts[1] + parts[2] + parts[3]
    bit = 8
    while bit < lax.axis_size("tm"):
        mine = mine + swap(mine, "tm", bit)
        bit = 2 * bit
    gathered = spread(mine)
    slots = [None] * 8
    for a in (0, 1):
        base = gathered[5 * a : 5 * a + 5]
        slots[a], slots[2 + a], slots[4 + a] = base[0], base[1], base[2]
        slots[6 + a] = jnp.concatenate([base[3], base[4]], axis=0)
    slots = jnp.stack(slots)
    slots = jnp.take(slots, jnp.arange(8) ^ turn, axis=0).reshape(16, 64, 768).astype(F32)

    grad_section = jnp.transpose(slots[:, :, 0:512], (1, 0, 2))
    grad_blocks = slots[:15, :, 512:768].reshape(3, 5, 64, 256)
    aux = slots[15, :, 512:768]
    section_norm = stat[0]
    section_gain_grad = aux[0:4, 128:256].reshape(512) / section_norm
    section_v_grad = (
        section_gain
        / section_norm
        * (grad_section - section_gain_grad / section_norm * v_section.astype(F32))
    )
    bias_grads = aux[:, 0:7].T
    three_v_grad, three_g_grad = norm_back(
        jnp.transpose(grad_blocks[:, 0:3], (0, 2, 1, 3)), three_v, three_g, three_norm, (2, 3)
    )
    mix_v_grad, mix_g_grad = norm_back(grad_blocks[:, 3], mix_v, mix_g, mix_norm, (2,))
    skip_v_grad, skip_g_grad = norm_back(grad_blocks[:, 4], skip_v, skip_g, skip_norm, (2,))
    return (
        output,
        signal_grad,
        section_v_grad,
        section_gain_grad,
        bias_grads[0],
        three_v_grad,
        three_g_grad.reshape(3, 64),
        bias_grads[1:4],
        mix_v_grad,
        mix_g_grad.reshape(3, 64),
        bias_grads[4:7],
        skip_v_grad,
        skip_g_grad.reshape(3, 64),
        bias_grads[4:7],
    )


def solution(mesh):
    return jax.shard_map(
        body,
        mesh=mesh,
        in_specs=(
            P("tm", "chan"),
            P(),
            P("chan", None, None),
            P(),
            P("chan"),
            P(None, "chan", None, None),
            P(None, "chan"),
            P(None, "chan"),
            P(None, "chan", None),
            P(None, "chan"),
            P(None, "chan"),
            P(None, "chan", None),
            P(None, "chan"),
            P(None, "chan"),
            P("chan", "tm"),
        ),
        out_specs=(
            P("chan", "tm"),
            P("tm", "chan"),
            P("chan", None, None),
            P(),
            P("chan"),
            P(None, "chan", None, None),
            P(None, "chan"),
            P(None, "chan"),
            P(None, "chan", None),
            P(None, "chan"),
            P(None, "chan"),
            P(None, "chan", None),
            P(None, "chan"),
            P(None, "chan"),
        ),
        check_vma=False,
    )
```

time: 3090 us -> 307 us (0.10)
  waiting for transfers between devices: 2540 us -> 89.5 us
  matrix products: 327 us -> 0 us
  Pallas kernels: 0 us -> 95.8 us
  other arithmetic: 67.3 us -> 28.4 us
    reduce_scatter x7 -> x0, waiting for transfers between devices: 1660 us -> none  [channel_sum(): return lax.psum_scatter(values, 'chan', scatter_dimension=1, tiled=True)]
    all_gather x7 -> x0, waiting for transfers between devices: 833 us -> none  [widen(): return lax.all_gather(values, 'chan', axis=1, tiled=True)]
    dot_general x54 -> x0, matrix products: 327 us -> none  [the longest x18 164 us: contract_cols(): lax.dot_general(left_side, right_side, (((1,), (1,)), ((), ())), preferre...]
    pallas_call x0 -> x2, Pallas kernels: none -> 95.8 us  [the longest x1 56.3 us: run_backward(): pl.pallas_call(backward_kernel, out_shape=[shape_of((4, 2, 256, 768))] *...]
    ppermute x16 -> x45, waiting for transfers between devices: 12.1 us -> 89.5 us  [the longest x41 87 us: swap(): return lax.ppermute(values, axis, xor_pairs(axis, bit))]
    psum x1 -> x0, waiting for transfers between devices: 32 us -> none  [body(): lax.psum((grad_section, grad_section_bias, grad_three_all, three_bias_all...]
  transfers between devices with their start and end apart: 31 -> 45, of which waited for: 19 -> 18; matrix products, arithmetic and copies ran while one was open for 8% -> 13% of each run, Pallas kernels for 0% -> 13%
where the time goes in v1:
time: 307 us; the launch traced here: 305 us
  Pallas kernels  95.8 us (31%)
  waiting for transfers between devices  89.5 us (29%)
  starting transfers between devices  56 us (18%)
  local copies, waits for them, and re-layouts  34 us (11%)
  other arithmetic  28.4 us (9%)
    ppermute x41, waiting for transfers between devices, swap(): return lax.ppermute(values, axis, xor_pairs(axis, bit))  87 us
    pallas_call x1, Pallas kernels, run_backward(): pl.pallas_call(backward_kernel, out_shape=[shape_of((4, 2, 256, 768))] *...  56.3 us
    ppermute x41, starting transfers between devices, swap(): return lax.ppermute(values, axis, xor_pairs(axis, bit))  44 us
    pallas_call x1, Pallas kernels, run_forward(): pl.pallas_call(forward_kernel, out_shape=out_shape, in_specs=[SPEC_SMEM]...  39.5 us
    unnamed x88, local copies, waits for them, and re-layouts  10.2 us
    ppermute x2, starting transfers between devices, edges(): lax.ppermute(lax.slice_in_dim(block, size - width, None, axis=dim), 'tm',...  8.14 us
    concatenate x4, local copies, waits for them, and re-layouts, cut_cotangent(): return jnp.concatenate([main, after, before], axis=1)  6.72 us
  transfers between devices with their start and end apart: 45, of which 18 were waited for; matrix products, arithmetic and copies ran while one was open for 13% of the time, Pallas kernels for 13%

profile of v1, /device:TPU:9, one launch (start us, length us, event | category | flops | bytes accessed | tf_op | source)
XLA Modules:
  0.0 305.3 jit_solution(8298536505792232084)
XLA Ops:
  7.4 2.8 copy.64
  11.8 2.5 collective-permute-start.6
  14.5 1.3 fusion.38
  15.8 4.5 %collective-permute-start = (bf16[8,128]{1,0:T(8,128)(2,1)}, bf16[8,128]{1,0:T(8,128)(2,1)}, u32[]{:S(2)}, u32[]{:S(2)}) collective-permute-start(bf16[8,128]{1,0:T(8,128)(2,1)} %get-tuple-element.143), channel_id=1, source_target_pairs={{0,4},{4,8},{8,12},{12,16},{16,20},{20,24},{24,28},{1,5},{5,9},{9,... | collective-permute-start | bytes 6152 | tf_op jit(solution)/shard_map/ppermute | solution.py:42
  20.3 1.9 collective-permute-start.1
  23.0 1.3 constant_dynamic-slice_fusion.7
  26.3 3.6 %collective-permute-start.21 = (bf16[64,64]{1,0:T(8,128)(2,1)S(1)}, bf16[64,64]{1,0:T(8,128)(2,1)S(1)}, u32[]{:S(2)}, u32[]{:S(2)}) collective-permute-start(bf16[64,64]{1,0:T(8,128)(2,1)S(1)} %slice.174), channel_id=1, source_target_pairs={{0,4},{4,8},{8,12},{12,16},{16,20},{20,24},{24,28},{1,5},{5,9},{9,... | collective-permute-start | bytes 24584 | tf_op jit(solution)/shard_map/ppermute | solution.py:42
  30.0 1.2 collective-permute-done.7
  31.3 1.3 collective-permute-start.9
  32.6 1.2 collective-permute-start.8
  37.7 10.9 %collective-permute-done.9.rest_2_ = bf16[4,2,64,768]{3,2,1,0:T(8,128)(2,1)S(1)} collective-permute-done((bf16[4,2,64,768]{3,2,1,0:T(8,128)(2,1)S(1)}, bf16[4,2,64,768]{3,2,1,0:T(8,128)(2,1)S(1)}, u32[]{:S(2)}, u32[]{:S(2)}) %collective-permute-start.9) | collective-permute-done | bytes 786464 | tf_op jit(solution)/shard_map/ppermute | solution.py:20
  48.6 1.3 collective-permute-start.10
  49.9 1.3 collective-permute-start.11
  51.9 3.3 %collective-permute-start.12 = (bf16[4,2,64,768]{3,2,1,0:T(8,128)(2,1)S(1)}, bf16[4,2,64,768]{3,2,1,0:T(8,128)(2,1)S(1)}, u32[]{:S(2)}, u32[]{:S(2)}) collective-permute-start(bf16[4,2,64,768]{3,2,1,0:T(8,128)(2,1)S(1)} %pad_maximum_fusion.1.rest_0_), channel_id=1, source_target_pairs={{0,4},{4,0},{8,12},{12,8},{16,20},{20,16},{24,28},{28,24},{1,5},{5... | collective-permute-start | bytes 2359304 | tf_op jit(solution)/shard_map/ppermute | solution.py:20
  55.2 1.5 dynamic-slice_select_fusion
  56.7 1.9 collective-permute-start.20
  59.3 2.5 collective-permute-done.20
  61.8 2.4 collective-permute-start.3
  69.2 1.3 convert_element_type.50
  70.4 1.4 pad_maximum_fusion.13
  72.3 2.0 collective-permute-done.4.sig3
  74.3 1.5 dynamic-slice_select_fusion.1
  75.9 2.0 concatenate.78
  77.9 1.9 concatenate.79
  79.8 1.9 concatenate.80
  81.8 3.1 %collective-permute-start.23 = (bf16[64,4224]{1,0:T(8,128)(2,1)}, bf16[64,4224]{1,0:T(8,128)(2,1)}, u32[]{:S(2)}, u32[]{:S(2)}) collective-permute-start(bf16[64,4224]{1,0:T(8,128)(2,1)} %concatenate.79), channel_id=1, source_target_pairs={{0,2},{1,3},{2,0},{3,1},{4,6},{5,7},{6,4},{7,5},{8,10},{9,11},{10,... | collective-permute-start | bytes 1622024 | tf_op jit(solution)/shard_map/ppermute | solution.py:20
  91.6 39.5 %forward_blocks.1 = (bf16[3,8,528,256]{3,2,1,0:T(8,128)(2,1)}, bf16[3,8,528,256]{3,2,1,0:T(8,128)(2,1)}, bf16[3,8,528,256]{3,2,1,0:T(8,128)(2,1)}, bf16[3,8,528,...) custom-call(s32[2]{0:T(128)} %pad_add_fusion.places, ...), custom_call_target="tpu_custom_call" | custom-call | tf_op jit(solution)/shard_map/forward_blocks/pallas_call | solution.py:426
  131.2 56.3 %backward_blocks.1 = (bf16[4,2,256,768]{3,2,1,0:T(8,128)(2,1)}, bf16[4,2,256,768]{3,2,1,0:T(8,128)(2,1)}, bf16[512,128]{1,0:T(8,128)(2,1)}, bf16[512,128]{1,0:T(...) custom-call(s32[2]{0:T(128)} %pad_add_fusion.places, bf16[64,4224]{1,0:T(8,128)(2,1)} %concatenate.77.cot0, ...), custom_call_target="tpu_custom_call" | custom-call | tf_op jit(solution)/shard_map/backward_blocks/pallas_call | solution.py:455
  187.5 1.7 collective-permute-start.28
  190.7 2.5 collective-permute-start.26
  194.8 3.6 %add.212 = bf16[4,2,256,768]{3,2,1,0:T(8,128)(2,1)S(1)} add(bf16[4,2,256,768]{3,2,1,0:T(8,128)(2,1)} %get-tuple-element.48, bf16[4,2,256,768]{3,2,1,0:T(8,128)(2,1)} %collective-permute-done.28) | non-fusion elementwise | flops 1572864 | bytes 9437184 | tf_op jit(solution)/shard_map/add | solution.py:610
  198.6 3.0 collective-permute-start.29
  201.8 9.0 %collective-permute-done.29 = bf16[1,256,768]{2,1,0:T(8,128)(2,1)S(1)} collective-permute-done((bf16[1,256,768]{2,1,0:T(8,128)(2,1)S(1)}, bf16[1,256,768]{2,1,0:T(8,128)(2,1)S(1)}, u32[]{:S(2)}, u32[]{:S(2)}) %collective-permute-start.29) | collective-permute-done | bytes 393248 | tf_op jit(solution)/shard_map/ppermute | solution.py:20
  213.5 2.4 collective-permute-start.18
  216.0 15.0 %collective-permute-done.17 = bf16[64,4096]{1,0:T(8,128)(2,1)S(1)} collective-permute-done((bf16[64,4096]{1,0:T(8,128)(2,1)S(1)}, bf16[64,4096]{1,0:T(8,128)(2,1)S(1)}, u32[]{:S(2)}, u32[]{:S(2)}) %collective-permute-start.17) | collective-permute-done | bytes 524320 | tf_op jit(solution)/shard_map/ppermute | solution.py:20
  231.3 2.3 collective-permute-start.33
  233.6 1.3 collective-permute-start.35
  234.8 12.9 %collective-permute-done.18 = bf16[64,4096]{1,0:T(8,128)(2,1)S(1)} collective-permute-done((bf16[64,4096]{1,0:T(8,128)(2,1)S(1)}, bf16[64,4096]{1,0:T(8,128)(2,1)S(1)}, u32[]{:S(2)}, u32[]{:S(2)}) %collective-permute-start.18) | collective-permute-done | bytes 524320 | tf_op jit(solution)/shard_map/ppermute | solution.py:20
  247.8 2.3 collective-permute-done.33
  250.1 21.7 %collective-permute-done.34 = bf16[2,64,768]{2,1,0:T(8,128)(2,1)S(1)} collective-permute-done((bf16[2,64,768]{2,1,0:T(8,128)(2,1)S(1)}, bf16[2,64,768]{2,1,0:T(8,128)(2,1)S(1)}, u32[]{:S(2)}, u32[]{:S(2)}) %collective-permute-start.34) | collective-permute-done | bytes 196640 | tf_op jit(solution)/shard_map/ppermute | solution.py:20
  271.8 4.2 %collective-permute-done.35 = bf16[2,64,768]{2,1,0:T(8,128)(2,1)S(1)} collective-permute-done((bf16[2,64,768]{2,1,0:T(8,128)(2,1)S(1)}, bf16[2,64,768]{2,1,0:T(8,128)(2,1)S(1)}, u32[]{:S(2)}, u32[]{:S(2)}) %collective-permute-start.35) | collective-permute-done | bytes 196640 | tf_op jit(solution)/shard_map/ppermute | solution.py:20
  276.1 2.9 collective-permute-start.36
  279.1 1.2 collective-permute-start.37
  281.1 5.4 %collective-permute-done.39 = bf16[2,64,768]{2,1,0:T(8,128)(2,1)S(1)} collective-permute-done((bf16[2,64,768]{2,1,0:T(8,128)(2,1)S(1)}, bf16[2,64,768]{2,1,0:T(8,128)(2,1)S(1)}, u32[]{:S(2)}, u32[]{:S(2)}) %collective-permute-start.39) | collective-permute-done | bytes 196640 | tf_op jit(solution)/shard_map/ppermute | solution.py:20
  286.8 1.2 collective-permute-start.42
  288.0 1.7 collective-permute-start.38
  290.0 2.3 collective-permute-start.43
  299.5 2.5 copy.69
  (234 shorter events, 47.0 us)
Async XLA Ops:
  11.8 14.5 %collective-permute-start.5 = (bf16[2,64,768]{2,1,0:T(8,128)(2,1)S(1)}, bf16[2,64,768]{2,1,0:T(8,128)(2,1)S(1)}, u32[]{:S(2)}, u32[]{:S(2)}) collective-permute-start(bf16[2,64,768]{2,1,0:T(8,128)(2,1)S(1)} %get-tuple-element.145), channel_id=1, source_target_pairs={{0,1},{1,0},{2,3},{3,2},{4,5},{5,4},{6,7},{7,6},{8,9},{9,8},{10,11... | collective-permute-start | bytes 589832 | tf_op jit(solution)/shard_map/ppermute | solution.py:20
  11.8 18.1 %collective-permute-start.6 = (bf16[2,64,768]{2,1,0:T(8,128)(2,1)S(1)}, bf16[2,64,768]{2,1,0:T(8,128)(2,1)S(1)}, u32[]{:S(2)}, u32[]{:S(2)}) collective-permute-start(bf16[2,64,768]{2,1,0:T(8,128)(2,1)S(1)} %get-tuple-element.145), channel_id=1, source_target_pairs={{0,2},{1,3},{2,0},{3,1},{4,6},{5,7},{6,4},{7,5},{8,10},{9,11},{10,... | collective-permute-start | bytes 589832 | tf_op jit(solution)/shard_map/ppermute | solution.py:20
  14.3 16.9 %collective-permute-start.7 = (bf16[2,64,768]{2,1,0:T(8,128)(2,1)S(1)}, bf16[2,64,768]{2,1,0:T(8,128)(2,1)S(1)}, u32[]{:S(2)}, u32[]{:S(2)}) collective-permute-start(bf16[2,64,768]{2,1,0:T(8,128)(2,1)S(1)} %get-tuple-element.145), channel_id=1, source_target_pairs={{0,3},{1,2},{2,1},{3,0},{4,7},{5,6},{6,5},{7,4},{8,11},{9,10},{10,... | collective-permute-start | bytes 589832 | tf_op jit(solution)/shard_map/ppermute | solution.py:20
  15.8 18.1 %collective-permute-start = (bf16[8,128]{1,0:T(8,128)(2,1)}, bf16[8,128]{1,0:T(8,128)(2,1)}, u32[]{:S(2)}, u32[]{:S(2)}) collective-permute-start(bf16[8,128]{1,0:T(8,128)(2,1)} %get-tuple-element.143), channel_id=1, source_target_pairs={{0,4},{4,8},{8,12},{12,16},{16,20},{20,24},{24,28},{1,5},{5,9},{9,... | collective-permute-start | bytes 6152 | tf_op jit(solution)/shard_map/ppermute | solution.py:42
  20.3 15.4 %collective-permute-start.1 = (bf16[8,128]{1,0:T(8,128)(2,1)}, bf16[8,128]{1,0:T(8,128)(2,1)}, u32[]{:S(2)}, u32[]{:S(2)}) collective-permute-start(bf16[8,128]{1,0:T(8,128)(2,1)} %get-tuple-element.142), channel_id=1, source_target_pairs={{4,0},{8,4},{12,8},{16,12},{20,16},{24,20},{28,24},{5,1},{9,5},{13... | collective-permute-start | bytes 6152 | tf_op jit(solution)/shard_map/ppermute | solution.py:43
  26.3 28.9 %collective-permute-start.21 = (bf16[64,64]{1,0:T(8,128)(2,1)S(1)}, bf16[64,64]{1,0:T(8,128)(2,1)S(1)}, u32[]{:S(2)}, u32[]{:S(2)}) collective-permute-start(bf16[64,64]{1,0:T(8,128)(2,1)S(1)} %slice.174), channel_id=1, source_target_pairs={{0,4},{4,8},{8,12},{12,16},{16,20},{20,24},{24,28},{1,5},{5,9},{9,... | collective-permute-start | bytes 24584 | tf_op jit(solution)/shard_map/ppermute | solution.py:42
  31.3 17.3 %collective-permute-start.9 = (bf16[4,2,64,768]{3,2,1,0:T(8,128)(2,1)S(1)}, bf16[4,2,64,768]{3,2,1,0:T(8,128)(2,1)S(1)}, u32[]{:S(2)}, u32[]{:S(2)}) collective-permute-start(bf16[4,2,64,768]{3,2,1,0:T(8,128)(2,1)S(1)} %pad_maximum_fusion.1.rest_0_), channel_id=1, source_target_pairs={{0,16},{4,20},{8,24},{12,28},{16,0},{20,4},{24,8},{28,12},{1,17},{... | collective-permute-start | bytes 2359304 | tf_op jit(solution)/shard_map/ppermute | solution.py:20
  32.6 17.3 %collective-permute-start.8 = (bf16[4,2,64,768]{3,2,1,0:T(8,128)(2,1)S(1)}, bf16[4,2,64,768]{3,2,1,0:T(8,128)(2,1)S(1)}, u32[]{:S(2)}, u32[]{:S(2)}) collective-permute-start(bf16[4,2,64,768]{3,2,1,0:T(8,128)(2,1)S(1)} %pad_maximum_fusion.1.rest_0_), channel_id=1, source_target_pairs={{0,8},{4,12},{8,0},{12,4},{16,24},{20,28},{24,16},{28,20},{1,9},{5... | collective-permute-start | bytes 2359304 | tf_op jit(solution)/shard_map/ppermute | solution.py:20
  35.7 32.3 %copy-start.24 = (f32[528]{0:T(1024)S(1)}, f32[528]{0:T(1024)}, u32[]{:S(2)}) copy-start(f32[528]{0:T(1024)} %get-tuple-element.158) | copy-start | bytes 6340
  37.7 26.6 %collective-permute-start.2 = (bf16[528,128]{1,0:T(8,128)(2,1)S(1)}, bf16[528,128]{1,0:T(8,128)(2,1)S(1)}, u32[]{:S(2)}, u32[]{:S(2)}) collective-permute-start(bf16[528,128]{1,0:T(8,128)(2,1)S(1)} %pad_maximum_fusion.7), channel_id=1, source_target_pairs={{0,1},{1,0},{2,3},{3,2},{4,5},{5,4},{6,7},{7,6},{8,9},{9,8},{10,11... | collective-permute-start | bytes 405512 | tf_op jit(solution)/shard_map/ppermute | solution.py:20
  48.6 31.2 %copy-start.1 = (bf16[4,2,64,768]{3,2,1,0:T(8,128)(2,1)}, bf16[4,2,64,768]{3,2,1,0:T(8,128)(2,1)S(1)}, u32[]{:S(2)}) copy-start(bf16[4,2,64,768]{3,2,1,0:T(8,128)(2,1)S(1)} %collective-permute-done.9.rest_2_) | copy-start | bytes 2359300
  48.6 15.6 %collective-permute-start.10 = (bf16[2,2,64,768]{3,2,1,0:T(8,128)(2,1)S(1)}, bf16[2,2,64,768]{3,2,1,0:T(8,128)(2,1)}, u32[]{:S(2)}, u32[]{:S(2)}) collective-permute-start(bf16[2,2,64,768]{3,2,1,0:T(8,128)(2,1)S(1)} %slice.198), channel_id=1, source_target_pairs={{0,8},{4,12},{8,0},{12,4},{16,24},{20,28},{24,16},{28,20},{1,9},{5... | collective-permute-start | bytes 1179656 | tf_op jit(solution)/shard_map/ppermute | solution.py:20
  49.9 31.8 %copy-start.2 = (bf16[4,2,64,768]{3,2,1,0:T(8,128)(2,1)}, bf16[4,2,64,768]{3,2,1,0:T(8,128)(2,1)S(1)}, u32[]{:S(2)}) copy-start(bf16[4,2,64,768]{3,2,1,0:T(8,128)(2,1)S(1)} %collective-permute-done.8.rest_1_) | copy-start | bytes 2359300
  49.9 14.4 %collective-permute-start.11 = (bf16[2,2,64,768]{3,2,1,0:T(8,128)(2,1)S(1)}, bf16[2,2,64,768]{3,2,1,0:T(8,128)(2,1)}, u32[]{:S(2)}, u32[]{:S(2)}) collective-permute-start(bf16[2,2,64,768]{3,2,1,0:T(8,128)(2,1)S(1)} %slice.199), channel_id=1, source_target_pairs={{0,16},{4,20},{8,24},{12,28},{16,0},{20,4},{24,8},{28,12},{1,17},{... | collective-permute-start | bytes 1179656 | tf_op jit(solution)/shard_map/ppermute | solution.py:20
  51.9 29.8 %collective-permute-start.12 = (bf16[4,2,64,768]{3,2,1,0:T(8,128)(2,1)S(1)}, bf16[4,2,64,768]{3,2,1,0:T(8,128)(2,1)S(1)}, u32[]{:S(2)}, u32[]{:S(2)}) collective-permute-start(bf16[4,2,64,768]{3,2,1,0:T(8,128)(2,1)S(1)} %pad_maximum_fusion.1.rest_0_), channel_id=1, source_target_pairs={{0,4},{4,0},{8,12},{12,8},{16,20},{20,16},{24,28},{28,24},{1,5},{5... | collective-permute-start | bytes 2359304 | tf_op jit(solution)/shard_map/ppermute | solution.py:20
  56.7 5.0 %collective-permute-start.20 = (bf16[64,64]{1,0:T(8,128)(2,1)S(1)}, bf16[64,64]{1,0:T(8,128)(2,1)S(1)}, u32[]{:S(2)}, u32[]{:S(2)}) collective-permute-start(bf16[64,64]{1,0:T(8,128)(2,1)S(1)} %get-tuple-element.124), channel_id=1, source_target_pairs={{4,0},{8,4},{12,8},{16,12},{20,16},{24,20},{28,24},{5,1},{9,5},{13... | collective-permute-start | bytes 24584 | tf_op jit(solution)/shard_map/ppermute | solution.py:43
  61.8 10.4 %collective-permute-start.3 = (bf16[528,128]{1,0:T(8,128)(2,1)}, bf16[528,128]{1,0:T(8,128)(2,1)}, u32[]{:S(2)}, u32[]{:S(2)}) collective-permute-start(bf16[528,128]{1,0:T(8,128)(2,1)} %pad_maximum_fusion.8), channel_id=1, source_target_pairs={{0,2},{1,3},{2,0},{3,1},{4,6},{5,7},{6,4},{7,5},{8,10},{9,11},{10,... | collective-permute-start | bytes 405512 | tf_op jit(solution)/shard_map/ppermute | solution.py:20
  64.2 10.1 %collective-permute-start.4 = (bf16[528,128]{1,0:T(8,128)(2,1)}, bf16[528,128]{1,0:T(8,128)(2,1)}, u32[]{:S(2)}, u32[]{:S(2)}) collective-permute-start(bf16[528,128]{1,0:T(8,128)(2,1)} %pad_maximum_fusion.9), channel_id=1, source_target_pairs={{0,3},{1,2},{2,1},{3,0},{4,7},{5,6},{6,5},{7,4},{8,11},{9,10},{10,... | collective-permute-start | bytes 405512 | tf_op jit(solution)/shard_map/ppermute | solution.py:20
  64.2 17.6 %collective-permute-start.15 = (bf16[2,2,64,768]{3,2,1,0:T(8,128)(2,1)}, bf16[2,2,64,768]{3,2,1,0:T(8,128)(2,1)}, u32[]{:S(2)}, u32[]{:S(2)}) collective-permute-start(bf16[2,2,64,768]{3,2,1,0:T(8,128)(2,1)} %collective-permute-done.10.rest_3_), channel_id=1, source_target_pairs={{0,4},{4,0},{8,12},{12,8},{16,20},{20,16},{24,28},{28,24},{1,5},{5... | collective-permute-start | bytes 1179656 | tf_op jit(solution)/shard_map/ppermute | solution.py:20
  64.9 20.0 %collective-permute-start.16 = (bf16[2,2,64,768]{3,2,1,0:T(8,128)(2,1)}, bf16[2,2,64,768]{3,2,1,0:T(8,128)(2,1)}, u32[]{:S(2)}, u32[]{:S(2)}) collective-permute-start(bf16[2,2,64,768]{3,2,1,0:T(8,128)(2,1)} %collective-permute-done.11.rest_4_), channel_id=1, source_target_pairs={{0,4},{4,0},{8,12},{12,8},{16,20},{20,16},{24,28},{28,24},{1,5},{5... | collective-permute-start | bytes 1179656 | tf_op jit(solution)/shard_map/ppermute | solution.py:20
  72.1 19.4 %collective-permute-start.13 = (bf16[4,2,64,768]{3,2,1,0:T(8,128)(2,1)S(1)}, bf16[4,2,64,768]{3,2,1,0:T(8,128)(2,1)}, u32[]{:S(2)}, u32[]{:S(2)}) collective-permute-start(bf16[4,2,64,768]{3,2,1,0:T(8,128)(2,1)S(1)} %collective-permute-done.8.rest_1_), channel_id=1, source_target_pairs={{0,4},{4,0},{8,12},{12,8},{16,20},{20,16},{24,28},{28,24},{1,5},{5... | collective-permute-start | bytes 2359304 | tf_op jit(solution)/shard_map/ppermute | solution.py:20
  74.3 17.2 %collective-permute-start.14 = (bf16[4,2,64,768]{3,2,1,0:T(8,128)(2,1)S(1)}, bf16[4,2,64,768]{3,2,1,0:T(8,128)(2,1)}, u32[]{:S(2)}, u32[]{:S(2)}) collective-permute-start(bf16[4,2,64,768]{3,2,1,0:T(8,128)(2,1)S(1)} %collective-permute-done.9.rest_2_), channel_id=1, source_target_pairs={{0,4},{4,0},{8,12},{12,8},{16,20},{20,16},{24,28},{28,24},{1,5},{5... | collective-permute-start | bytes 2359304 | tf_op jit(solution)/shard_map/ppermute | solution.py:20
  81.7 49.3 %collective-permute-start.22 = (bf16[64,4224]{1,0:T(8,128)(2,1)}, bf16[64,4224]{1,0:T(8,128)(2,1)}, u32[]{:S(2)}, u32[]{:S(2)}) collective-permute-start(bf16[64,4224]{1,0:T(8,128)(2,1)} %concatenate.78), channel_id=1, source_target_pairs={{0,1},{1,0},{2,3},{3,2},{4,5},{5,4},{6,7},{7,6},{8,9},{9,8},{10,11... | collective-permute-start | bytes 1622024 | tf_op jit(solution)/shard_map/ppermute | solution.py:20
  81.8 49.2 %collective-permute-start.23 = (bf16[64,4224]{1,0:T(8,128)(2,1)}, bf16[64,4224]{1,0:T(8,128)(2,1)}, u32[]{:S(2)}, u32[]{:S(2)}) collective-permute-start(bf16[64,4224]{1,0:T(8,128)(2,1)} %concatenate.79), channel_id=1, source_target_pairs={{0,2},{1,3},{2,0},{3,1},{4,6},{5,7},{6,4},{7,5},{8,10},{9,11},{10,... | collective-permute-start | bytes 1622024 | tf_op jit(solution)/shard_map/ppermute | solution.py:20
  84.9 46.3 %collective-permute-start.24 = (bf16[64,4224]{1,0:T(8,128)(2,1)}, bf16[64,4224]{1,0:T(8,128)(2,1)}, u32[]{:S(2)}, u32[]{:S(2)}) collective-permute-start(bf16[64,4224]{1,0:T(8,128)(2,1)} %concatenate.80), channel_id=1, source_target_pairs={{0,3},{1,2},{2,1},{3,0},{4,7},{5,6},{6,5},{7,4},{8,11},{9,10},{10,... | collective-permute-start | bytes 1622024 | tf_op jit(solution)/shard_map/ppermute | solution.py:20
  187.5 7.3 %collective-permute-start.28 = (bf16[4,2,256,768]{3,2,1,0:T(8,128)(2,1)}, bf16[4,2,256,768]{3,2,1,0:T(8,128)(2,1)}, u32[]{:S(2)}, u32[]{:S(2)}) collective-permute-start(bf16[4,2,256,768]{3,2,1,0:T(8,128)(2,1)} %get-tuple-element.49), channel_id=1, source_target_pairs={{0,4},{4,0},{8,12},{12,8},{16,20},{20,16},{24,28},{28,24},{1,5},{5... | collective-permute-start | bytes 9437192 | tf_op jit(solution)/shard_map/ppermute | solution.py:20
  190.1 22.2 %collective-permute-start.25 = (bf16[512,128]{1,0:T(8,128)(2,1)}, bf16[512,128]{1,0:T(8,128)(2,1)S(1)}, u32[]{:S(2)}, u32[]{:S(2)}) collective-permute-start(bf16[512,128]{1,0:T(8,128)(2,1)} %get-tuple-element.45), channel_id=1, source_target_pairs={{0,1},{1,0},{2,3},{3,2},{4,5},{5,4},{6,7},{7,6},{8,9},{9,8},{10,11... | collective-permute-start | bytes 393224 | tf_op jit(solution)/shard_map/ppermute | solution.py:20
  190.7 22.7 %collective-permute-start.26 = (bf16[512,128]{1,0:T(8,128)(2,1)}, bf16[512,128]{1,0:T(8,128)(2,1)S(1)}, u32[]{:S(2)}, u32[]{:S(2)}) collective-permute-start(bf16[512,128]{1,0:T(8,128)(2,1)} %get-tuple-element.46), channel_id=1, source_target_pairs={{0,2},{1,3},{2,0},{3,1},{4,6},{5,7},{6,4},{7,5},{8,10},{9,11},{10,... | collective-permute-start | bytes 393224 | tf_op jit(solution)/shard_map/ppermute | solution.py:20
  193.2 22.7 %collective-permute-start.27 = (bf16[512,128]{1,0:T(8,128)(2,1)}, bf16[512,128]{1,0:T(8,128)(2,1)S(1)}, u32[]{:S(2)}, u32[]{:S(2)}) collective-permute-start(bf16[512,128]{1,0:T(8,128)(2,1)} %get-tuple-element.47), channel_id=1, source_target_pairs={{0,3},{1,2},{2,1},{3,0},{4,7},{5,6},{6,5},{7,4},{8,11},{9,10},{10,... | collective-permute-start | bytes 393224 | tf_op jit(solution)/shard_map/ppermute | solution.py:20
  198.6 12.2 %collective-permute-start.29 = (bf16[1,256,768]{2,1,0:T(8,128)(2,1)S(1)}, bf16[1,256,768]{2,1,0:T(8,128)(2,1)S(1)}, u32[]{:S(2)}, u32[]{:S(2)}) collective-permute-start(bf16[1,256,768]{2,1,0:T(8,128)(2,1)S(1)} %get-tuple-element.113), channel_id=1, source_target_pairs={{0,16},{4,20},{8,24},{12,28},{16,0},{20,4},{24,8},{28,12},{1,17},{... | collective-permute-start | bytes 1179656 | tf_op jit(solution)/shard_map/ppermute | solution.py:20
  201.6 10.0 %collective-permute-start.31 = (bf16[1,256,768]{2,1,0:T(8,128)(2,1)S(1)}, bf16[1,256,768]{2,1,0:T(8,128)(2,1)S(1)}, u32[]{:S(2)}, u32[]{:S(2)}) collective-permute-start(bf16[1,256,768]{2,1,0:T(8,128)(2,1)S(1)} %get-tuple-element.112), channel_id=1, source_target_pairs={{0,8},{4,12},{8,0},{12,4},{16,24},{20,28},{24,16},{28,20},{1,9},{5... | collective-permute-start | bytes 1179656 | tf_op jit(solution)/shard_map/ppermute | solution.py:20
  210.8 20.3 %collective-permute-start.17 = (bf16[64,4096]{1,0:T(8,128)(2,1)S(1)}, bf16[64,4096]{1,0:T(8,128)(2,1)S(1)}, u32[]{:S(2)}, u32[]{:S(2)}) collective-permute-start(bf16[64,4096]{1,0:T(8,128)(2,1)S(1)} %copy-done.37), channel_id=1, source_target_pairs={{0,1},{1,0},{2,3},{3,2},{4,5},{5,4},{6,7},{7,6},{8,9},{9,8},{10,11... | collective-permute-start | bytes 1572872 | tf_op jit(solution)/shard_map/ppermute | solution.py:20
  211.8 19.3 %collective-permute-start.30 = (bf16[2,256,768]{2,1,0:T(8,128)(2,1)S(1)}, bf16[2,256,768]{2,1,0:T(8,128)(2,1)S(1)}, u32[]{:S(2)}, u32[]{:S(2)}) collective-permute-start(bf16[2,256,768]{2,1,0:T(8,128)(2,1)S(1)} %pad_maximum_fusion.2), channel_id=1, source_target_pairs={{0,8},{4,12},{8,0},{12,4},{16,24},{20,28},{24,16},{28,20},{1,9},{5... | collective-permute-start | bytes 2359304 | tf_op jit(solution)/shard_map/ppermute | solution.py:20
  212.3 18.8 %collective-permute-start.32 = (bf16[2,256,768]{2,1,0:T(8,128)(2,1)S(1)}, bf16[2,256,768]{2,1,0:T(8,128)(2,1)S(1)}, u32[]{:S(2)}, u32[]{:S(2)}) collective-permute-start(bf16[2,256,768]{2,1,0:T(8,128)(2,1)S(1)} %pad_maximum_fusion.3), channel_id=1, source_target_pairs={{0,16},{4,20},{8,24},{12,28},{16,0},{20,4},{24,8},{28,12},{1,17},{... | collective-permute-start | bytes 2359304 | tf_op jit(solution)/shard_map/ppermute | solution.py:20
  213.5 34.3 %collective-permute-start.18 = (bf16[64,4096]{1,0:T(8,128)(2,1)S(1)}, bf16[64,4096]{1,0:T(8,128)(2,1)S(1)}, u32[]{:S(2)}, u32[]{:S(2)}) collective-permute-start(bf16[64,4096]{1,0:T(8,128)(2,1)S(1)} %copy-done.36), channel_id=1, source_target_pairs={{0,2},{1,3},{2,0},{3,1},{4,6},{5,7},{6,4},{7,5},{8,10},{9,11},{10,... | collective-permute-start | bytes 1572872 | tf_op jit(solution)/shard_map/ppermute | solution.py:20
  215.9 65.1 %collective-permute-start.19 = (bf16[64,4096]{1,0:T(8,128)(2,1)S(1)}, bf16[64,4096]{1,0:T(8,128)(2,1)S(1)}, u32[]{:S(2)}, u32[]{:S(2)}) collective-permute-start(bf16[64,4096]{1,0:T(8,128)(2,1)S(1)} %copy-done.35), channel_id=1, source_target_pairs={{0,3},{1,2},{2,1},{3,0},{4,7},{5,6},{6,5},{7,4},{8,11},{9,10},{10,... | collective-permute-start | bytes 1572872 | tf_op jit(solution)/shard_map/ppermute | solution.py:20
  231.3 18.8 %collective-permute-start.33 = (bf16[2,64,768]{2,1,0:T(8,128)(2,1)S(1)}, bf16[2,64,768]{2,1,0:T(8,128)(2,1)S(1)}, u32[]{:S(2)}, u32[]{:S(2)}) collective-permute-start(bf16[2,64,768]{2,1,0:T(8,128)(2,1)S(1)} %get-tuple-element.131), channel_id=1, source_target_pairs={{0,1},{1,0},{2,3},{3,2},{4,5},{5,4},{6,7},{7,6},{8,9},{9,8},{10,11... | collective-permute-start | bytes 589832 | tf_op jit(solution)/shard_map/ppermute | solution.py:20
  233.6 38.2 %collective-permute-start.34 = (bf16[2,64,768]{2,1,0:T(8,128)(2,1)S(1)}, bf16[2,64,768]{2,1,0:T(8,128)(2,1)S(1)}, u32[]{:S(2)}, u32[]{:S(2)}) collective-permute-start(bf16[2,64,768]{2,1,0:T(8,128)(2,1)S(1)} %get-tuple-element.133), channel_id=1, source_target_pairs={{0,2},{1,3},{2,0},{3,1},{4,6},{5,7},{6,4},{7,5},{8,10},{9,11},{10,... | collective-permute-start | bytes 589832 | tf_op jit(solution)/shard_map/ppermute | solution.py:20
  233.6 42.4 %collective-permute-start.35 = (bf16[2,64,768]{2,1,0:T(8,128)(2,1)S(1)}, bf16[2,64,768]{2,1,0:T(8,128)(2,1)S(1)}, u32[]{:S(2)}, u32[]{:S(2)}) collective-permute-start(bf16[2,64,768]{2,1,0:T(8,128)(2,1)S(1)} %get-tuple-element.132), channel_id=1, source_target_pairs={{0,3},{1,2},{2,1},{3,0},{4,7},{5,6},{6,5},{7,4},{8,11},{9,10},{10,... | collective-permute-start | bytes 589832 | tf_op jit(solution)/shard_map/ppermute | solution.py:20
  276.1 13.6 %collective-permute-start.36 = (bf16[2,64,768]{2,1,0:T(8,128)(2,1)S(1)}, bf16[2,64,768]{2,1,0:T(8,128)(2,1)S(1)}, u32[]{:S(2)}, u32[]{:S(2)}) collective-permute-start(bf16[2,64,768]{2,1,0:T(8,128)(2,1)S(1)} %get-tuple-element.109), channel_id=1, source_target_pairs={{0,4},{4,0},{8,12},{12,8},{16,20},{20,16},{24,28},{28,24},{1,5},{5... | collective-permute-start | bytes 589832 | tf_op jit(solution)/shard_map/ppermute | solution.py:20
  279.1 7.7 %collective-permute-start.37 = (bf16[2,64,768]{2,1,0:T(8,128)(2,1)S(1)}, bf16[2,64,768]{2,1,0:T(8,128)(2,1)S(1)}, u32[]{:S(2)}, u32[]{:S(2)}) collective-permute-start(bf16[2,64,768]{2,1,0:T(8,128)(2,1)S(1)} %get-tuple-element.109), channel_id=1, source_target_pairs={{0,8},{4,12},{8,0},{12,4},{16,24},{20,28},{24,16},{28,20},{1,9},{5... | collective-permute-start | bytes 589832 | tf_op jit(solution)/shard_map/ppermute | solution.py:20
  280.3 6.1 %collective-permute-start.39 = (bf16[2,64,768]{2,1,0:T(8,128)(2,1)S(1)}, bf16[2,64,768]{2,1,0:T(8,128)(2,1)S(1)}, u32[]{:S(2)}, u32[]{:S(2)}) collective-permute-start(bf16[2,64,768]{2,1,0:T(8,128)(2,1)S(1)} %get-tuple-element.109), channel_id=1, source_target_pairs={{0,16},{4,20},{8,24},{12,28},{16,0},{20,4},{24,8},{28,12},{1,17},{... | collective-permute-start | bytes 589832 | tf_op jit(solution)/shard_map/ppermute | solution.py:20
  286.5 3.5 %collective-permute-start.41 = (bf16[1,64,768]{2,1,0:T(8,128)(2,1)S(1)}, bf16[1,64,768]{2,1,0:T(8,128)(2,1)S(1)}, u32[]{:S(2)}, u32[]{:S(2)}) collective-permute-start(bf16[1,64,768]{2,1,0:T(8,128)(2,1)S(1)} %slice.207), channel_id=1, source_target_pairs={{0,8},{4,12},{8,0},{12,4},{16,24},{20,28},{24,16},{28,20},{1,9},{5... | collective-permute-start | bytes 294920 | tf_op jit(solution)/shard_map/ppermute | solution.py:20
  286.8 5.5 %collective-permute-start.42 = (bf16[1,64,768]{2,1,0:T(8,128)(2,1)S(1)}, bf16[1,64,768]{2,1,0:T(8,128)(2,1)S(1)}, u32[]{:S(2)}, u32[]{:S(2)}) collective-permute-start(bf16[1,64,768]{2,1,0:T(8,128)(2,1)S(1)} %slice.208), channel_id=1, source_target_pairs={{0,16},{4,20},{8,24},{12,28},{16,0},{20,4},{24,8},{28,12},{1,17},{... | collective-permute-start | bytes 294920 | tf_op jit(solution)/shard_map/ppermute | solution.py:20
  288.0 4.9 %collective-permute-start.38 = (bf16[2,64,768]{2,1,0:T(8,128)(2,1)S(1)}, bf16[2,64,768]{2,1,0:T(8,128)(2,1)S(1)}, u32[]{:S(2)}, u32[]{:S(2)}) collective-permute-start(bf16[2,64,768]{2,1,0:T(8,128)(2,1)S(1)} %collective-permute-done.37), channel_id=1, source_target_pairs={{0,4},{4,0},{8,12},{12,8},{16,20},{20,16},{24,28},{28,24},{1,5},{5... | collective-permute-start | bytes 589832 | tf_op jit(solution)/shard_map/ppermute | solution.py:20
  289.7 3.2 %collective-permute-start.40 = (bf16[2,64,768]{2,1,0:T(8,128)(2,1)S(1)}, bf16[2,64,768]{2,1,0:T(8,128)(2,1)S(1)}, u32[]{:S(2)}, u32[]{:S(2)}) collective-permute-start(bf16[2,64,768]{2,1,0:T(8,128)(2,1)S(1)} %collective-permute-done.39), channel_id=1, source_target_pairs={{0,4},{4,0},{8,12},{12,8},{16,20},{20,16},{24,28},{28,24},{1,5},{5... | collective-permute-start | bytes 589832 | tf_op jit(solution)/shard_map/ppermute | solution.py:20
  290.0 3.3 %collective-permute-start.43 = (bf16[1,64,768]{2,1,0:T(8,128)(2,1)S(1)}, bf16[1,64,768]{2,1,0:T(8,128)(2,1)S(1)}, u32[]{:S(2)}, u32[]{:S(2)}) collective-permute-start(bf16[1,64,768]{2,1,0:T(8,128)(2,1)S(1)} %collective-permute-done.41), channel_id=1, source_target_pairs={{0,4},{4,0},{8,12},{12,8},{16,20},{20,16},{24,28},{28,24},{1,5},{5... | collective-permute-start | bytes 294920 | tf_op jit(solution)/shard_map/ppermute | solution.py:20
  292.3 1.5 collective-permute-start.44
  (35 other events, 307.7 us)

commit v2 on v1

--- a/solution.py
+++ b/solution.py
@@ -10,6 +10,7 @@
 BF16 = jnp.bfloat16
 HALO = 8
 VMEM_BYTES = 60 * 1024 * 1024
+MIB = 1024 * 1024
 
 
 def xor_pairs(axis, bit):
@@ -34,16 +35,6 @@
 SPREAD_PLACES = SPREAD_PLACES + [(a + 1, first, count) for a, first, count in SPREAD_PLACES]
 
 
-def edges(block, dim, width):
-    count = lax.axis_size("tm")
-    forward = [(i, i + 1) for i in range(count - 1)]
-    backward = [(target, source) for source, target in forward]
-    size = block.shape[dim]
-    low = lax.ppermute(lax.slice_in_dim(block, size - width, None, axis=dim), "tm", forward)
-    high = lax.ppermute(lax.slice_in_dim(block, 0, width, axis=dim), "tm", backward)
-    return low, high
-
-
 def nt(left, right):
     return lax.dot_general(left, right, (((1,), (1,)), ((), ())), preferred_element_type=F32)
 
@@ -66,6 +57,153 @@
 
 def moved(values, rows):
     return pltpu.roll(values, (-rows) % values.shape[0], 0)
+
+
+def fill_masks(ids_ref, mask_ref):
+    rows = mask_ref.shape[1]
+    for index, step in enumerate((-1, 1, -2, 2)):
+        inside = ids_ref[16 : 8 + rows] == ids_ref[16 + step : 8 + rows + step]
+        before = ids_ref[8:16] == ids_ref[8 + step : 16 + step]
+        mask_ref[index, 0 : rows - 8] = inside.astype(F32)
+        mask_ref[index, rows - 8 : rows] = before.astype(F32)
+
+
+def edge_tile(chan, tile, edge, dim):
+    half = tile.shape[dim] // 2
+    after = lax.broadcasted_iota(jnp.int32, tile.shape, dim) < half
+    is_last = jnp.where(chan == 3, 1, 0)
+    is_first = jnp.where(chan == 0, 1, 0)
+    return jnp.where(jnp.where(after, is_last, is_first) == 1, edge, tile)
+
+
+def pack_weights_kernel(
+    places, sec_ref, three_ref, mix_ref, skip_ref, bs, bt, bm, bk, gt, gm, gk, out, wide, rows, mats
+):
+    turn = places[0]
+    for q in range(4):
+        part = sec_ref[:, :, 128 * q : 128 * q + 128].astype(F32)
+        wide[q] = part.reshape(1024, 128)
+    rows[...] = jnp.zeros_like(rows)
+    rows[0:1, 0:64] = bs[...].astype(F32)
+    for index, ref in enumerate((bt, bm, bk, gt, gm, gk)):
+        rows[1 + 3 * index : 4 + 3 * index, 0:64] = ref[...].astype(F32)
+    columns = jnp.transpose(rows[...])[0:64]
+    for b in range(3):
+        three = three_ref[b].astype(F32)
+        gain = columns[:, 10 + b : 11 + b]
+        total = jnp.sum(jnp.sum(three * three, axis=0), axis=1, keepdims=True)
+        scale = gain / jnp.sqrt(total + EPSILON)
+        for tap in range(3):
+            mats[5 * b + tap] = (three[tap] * scale).astype(BF16)
+        for index, ref in ((3, mix_ref), (4, skip_ref)):
+            part = ref[b].astype(F32)
+            gain = columns[:, 3 * index + 4 + b : 3 * index + 5 + b]
+            total = jnp.sum(part * part, axis=1, keepdims=True)
+            mats[5 * b + index] = (part * (gain / jnp.sqrt(total + EPSILON))).astype(BF16)
+    mats[15, :, 0:128] = columns.astype(BF16)
+    mats[15, :, 128:256] = jnp.zeros((64, 128), BF16)
+    for tap in range(2):
+        for q in range(4):
+            part = wide[q, pl.ds(2 * turn + tap, 64, stride=16), :]
+            out[tap, :, 128 * q : 128 * q + 128] = part.astype(BF16)
+        out[tap, :, 512:768] = mats[2 * turn + tap]
+
+
+def pack_frames_kernel(places, piece, signal, cotangent, *rest):
+    sigs, edges, cots = rest[0:4], rest[4:8], rest[8:12]
+    chan = places[1]
+    own = signal.shape[0] // 4
+    frames = 8 * own
+    lower = lax.broadcasted_iota(jnp.int32, (16, 128), 0) < HALO
+    for k in range(4):
+        dest = chan ^ k
+        sigs[k][0:own] = signal[pl.ds(pl.multiple_of(dest * own, own), own)]
+        after = pl.multiple_of(jnp.minimum(dest + 1, 3) * own, 16)
+        before = pl.multiple_of(jnp.maximum(dest * own - 16, 0), 16)
+        tile = jnp.where(
+            lower, signal[pl.ds(after, 16)].astype(F32), signal[pl.ds(before, 16)].astype(F32)
+        )
+        sigs[k][own : own + 16] = tile.astype(BF16)
+        first = signal[0:16].astype(F32)
+        last = signal[4 * own - 16 : 4 * own].astype(F32)
+        edges[k][0:16] = jnp.where(dest == 3, first, last).astype(BF16)
+    lower = lax.broadcasted_iota(jnp.int32, (64, 128), 1) < 8 * HALO
+    for k in range(4):
+        dest = chan ^ k
+        lanes = pl.ds(pl.multiple_of(dest * frames, frames), frames)
+        cots[k][:, 0:frames] = cotangent[:, lanes]
+        after = pl.multiple_of(jnp.minimum(dest + 1, 3) * frames, 128)
+        before = pl.multiple_of(jnp.maximum(dest * frames - 128, 0), 128)
+        tile = jnp.where(
+            lower,
+            cotangent[:, pl.ds(after, 128)].astype(F32),
+            cotangent[:, pl.ds(before, 128)].astype(F32),
+        )
+        cots[k][:, frames : frames + 128] = tile.astype(BF16)
+        first = cotangent[:, 0:128].astype(F32)
+        last = cotangent[:, 4 * frames - 128 : 4 * frames].astype(F32)
+        edges[k][16:80] = jnp.where(dest == 3, first, last).astype(BF16)
+
+
+def finish_kernel(places, sec_ref, three_ref, mix_ref, skip_ref, gt, gm, gk, stat, *rest):
+    pieces = rest[:10]
+    sec_out, gain_out, bs, three_out, gt_out, bt, mix_out, gm_out, bm, skip_out, gk_out, bk = rest[10:22]
+    wide, rows, mats = rest[22:]
+    turn = places[0]
+    for ref, (place, first, _) in zip(pieces, SPREAD_PLACES, strict=True):
+        pair = 2 * (turn ^ place)
+        taps = 1 if place >= 6 else 2
+        for tap in range(taps):
+            k = pair + tap + first
+            part = ref[tap].astype(F32)
+            for q in range(4):
+                wide[q, pl.ds(k, 64, stride=16), :] = part[:, 128 * q : 128 * q + 128]
+            mats[k] = part[:, 512:768]
+    aux = mats[15]
+    norm, scale = stat[0:1], stat[1:2]
+    gains = jnp.concatenate([aux[q : q + 1, 128:256] for q in range(4)], axis=1) / norm
+    gain_out[...] = gains
+    ratio = gains / norm
+    for q in range(4):
+        lanes = slice(128 * q, 128 * q + 128)
+        part = sec_ref[:, :, lanes].astype(F32).reshape(1024, 128)
+        grad = scale[:, lanes] * (wide[q] - ratio[:, lanes] * part)
+        sec_out[:, :, lanes] = grad.reshape(64, 16, 128)
+    rows[...] = jnp.zeros_like(rows)
+    for index, ref in enumerate((gt, gm, gk)):
+        rows[3 * index : 3 * index + 3, 0:64] = ref[...].astype(F32)
+    columns = jnp.transpose(rows[...])[0:64]
+    results = []
+    for b in range(3):
+        three = three_ref[b].astype(F32)
+        norm = jnp.sqrt(jnp.sum(jnp.sum(three * three, axis=0), axis=1, keepdims=True) + EPSILON)
+        total = mats[5 * b] * three[0] + mats[5 * b + 1] * three[1] + mats[5 * b + 2] * three[2]
+        gain = jnp.sum(total, axis=1, keepdims=True) / norm
+        results.append(gain)
+        for tap in range(3):
+            grad = mats[5 * b + tap] - gain / norm * three[tap]
+            three_out[b, tap] = columns[:, b : b + 1] / norm * grad
+    for index, (ref, out) in enumerate(((mix_ref, mix_out), (skip_ref, skip_out))):
+        for b in range(3):
+            part = ref[b].astype(F32)
+            grad = mats[5 * b + 3 + index]
+            norm = jnp.sqrt(jnp.sum(part * part, axis=1, keepdims=True) + EPSILON)
+            gain = jnp.sum(grad * part, axis=1, keepdims=True) / norm
+            results.append(gain)
+            place = 3 + 3 * index + b
+            out[b] = columns[:, place : place + 1] / norm * (grad - gain / norm * part)
+    lane = lax.broadcasted_iota(jnp.int32, (64, 128), 1)
+    table = jnp.where(lane < 7, aux[:, 0:128], 0.0)
+    for index, gain in enumerate(results):
+        table = jnp.where(lane == 8 + index, gain, table)
+    rows[:, 0:64] = jnp.transpose(table)
+    bs[...] = rows[0:1, 0:64]
+    bt[...] = rows[1:4, 0:64]
+    bm[...] = rows[4:7, 0:64]
+    bk[...] = rows[4:7, 0:64]
+    gt_out[...] = rows[8:11, 0:64]
+    gm_out[...] = rows[11:14, 0:64]
+    gk_out[...] = rows[14:17, 0:64]
 
 
 def spread_phases(store, mask_ref, phase, values, dilate):
@@ -119,7 +257,11 @@
     sig1,
     sig2,
     sig3,
-    mask_ref,
+    edge0,
+    edge1,
+    edge2,
+    edge3,
+    ids_ref,
     gain_ref,
     *rest,
 ):
@@ -127,20 +269,24 @@
     hid_out, act_out, mix_out, dsi_out, dsh_out = rest[10:15]
     sact_out, dsig_out, stat_out = rest[15:18]
     outs = rest[18:22]
-    wsec, wblk, cat, bias, hid, mix, dsi, dsh, act, wide, turned, wsem, ssem, osem = rest[22:]
+    wsec, wblk, cat, bias, hid, mix, dsi, dsh, act, wide, turned, mask_ref, wsem, ssem, osem = rest[22:]
     chan = places[1]
     rows = sig0.shape[0]
     own = rows - 2 * HALO
     loads = weight_copies(places, pieces, wsec, wblk, wsem)
     for copy in loads:
         copy.start()
-    for k, ref in enumerate((sig0, sig1, sig2, sig3)):
+    fill_masks(ids_ref, mask_ref)
+    pairs = ((sig0, edge0), (sig1, edge1), (sig2, edge2), (sig3, edge3))
+    for k, (ref, edge) in enumerate(pairs):
         lanes = pl.ds(pl.multiple_of(128 * (chan ^ k), 128), 128)
-        values = ref[...].astype(F32)
+        values = ref[0:own].astype(F32)
         s = sigmoid(values)
         a = values * s
-        sact_out[:, lanes] = a.astype(BF16)
-        dsig_out[:, lanes] = (s + a * (1.0 - s))[:own]
+        sact_out[0:own, lanes] = a.astype(BF16)
+        dsig_out[:, lanes] = s + a * (1.0 - s)
+        tile = edge_tile(chan, ref[own:rows].astype(F32), edge[0:16].astype(F32), 0)
+        sact_out[own:rows, lanes] = (tile * sigmoid(tile)).astype(BF16)
     for copy in loads:
         copy.wait()
 
@@ -239,7 +385,11 @@
     cot1,
     cot2,
     cot3,
-    mask_ref,
+    edge0,
+    edge1,
+    edge2,
+    edge3,
+    ids_ref,
     sact_ref,
     dsig_ref,
     stat_ref,
@@ -254,7 +404,7 @@
     even_out, odd_out = rest[10:12]
     sgrads = rest[12:16]
     (wsec, wblk, turned, wide, grad, inner, both, act, dsi, dsh) = rest[16:26]
-    (acc_one, acc_three, through, sums, staged, wsem, csem, bsem, osem) = rest[26:]
+    (acc_one, acc_three, through, sums, staged, mask_ref, wsem, csem, bsem, osem) = rest[26:]
     turn_index, chan = places[0], places[1]
     rows = mask_ref.shape[1]
     own = rows - 2 * HALO
@@ -277,8 +427,14 @@
 
     for copy in cots + loads + kept(2) + kept(1):
         copy.start()
+    fill_masks(ids_ref, mask_ref)
     for copy in cots:
         copy.wait()
+    for k, edge in enumerate((edge0, edge1, edge2, edge3)):
+        part = pl.ds(pl.multiple_of(64 * (chan ^ k), 64), 64)
+        tile = turned[part, 8 * own : 8 * rows].astype(F32)
+        tile = edge_tile(chan, tile, edge[16:80].astype(F32), 1)
+        turned[part, 8 * own : 8 * rows] = tile.astype(BF16)
 
     def turn(q, carry):
         frames = pl.ds(pl.multiple_of(128 * q, 128), 128)
@@ -413,8 +569,81 @@
 SPEC_SMEM = pl.BlockSpec(memory_space=pltpu.SMEM)
 
 
-def run_forward(places, signals, masks, gain, pieces):
-    rows = masks.shape[1]
+def params():
+    return pltpu.CompilerParams(vmem_limit_bytes=VMEM_BYTES)
+
+
+def cost(flops, moved_bytes):
+    return pl.CostEstimate(flops=int(flops), bytes_accessed=int(moved_bytes), transcendentals=0)
+
+
+def run_pack_weights(places, *arrays):
+    return pl.pallas_call(
+        pack_weights_kernel,
+        out_shape=shape_of((2, 64, 768)),
+        in_specs=[SPEC_SMEM] + [SPEC_VMEM] * 11,
+        out_specs=SPEC_VMEM,
+        scratch_shapes=[
+            pltpu.VMEM((4, 1024, 128), F32),
+            pltpu.VMEM((128, 128), F32),
+            pltpu.VMEM((16, 64, 256), BF16),
+        ],
+        compiler_params=params(),
+        cost_estimate=cost(2e7, 3e6),
+        name="pack_weights",
+    )(places, *arrays)
+
+
+def run_pack_frames(places, piece, signal, cotangent):
+    own = signal.shape[0] // 4
+    rows = own + 2 * HALO
+    out_shape = [shape_of((rows, 128))] * 4 + [shape_of((80, 128))] * 4
+    out_shape = out_shape + [shape_of((64, 8 * rows))] * 4
+    return pl.pallas_call(
+        pack_frames_kernel,
+        out_shape=out_shape,
+        in_specs=[SPEC_SMEM, SPEC_ANY, SPEC_VMEM, SPEC_VMEM],
+        out_specs=[SPEC_VMEM] * 12,
+        compiler_params=params(),
+        cost_estimate=cost(1e6, 6e6),
+        name="pack_frames",
+    )(places, piece, signal, cotangent)
+
+
+def run_finish(places, v_section, three, v_mix, v_skip, g_dilated, g_mix, g_skip, stat, pieces):
+    small = shape_of((3, 64), F32)
+    out_shape = [
+        shape_of((64, 16, 512), F32),
+        shape_of((1, 512), F32),
+        shape_of((1, 64), F32),
+        shape_of((3, 3, 64, 256), F32),
+        small,
+        small,
+        shape_of((3, 64, 256), F32),
+        small,
+        small,
+        shape_of((3, 64, 256), F32),
+        small,
+        small,
+    ]
+    return pl.pallas_call(
+        finish_kernel,
+        out_shape=out_shape,
+        in_specs=[SPEC_SMEM] + [SPEC_VMEM] * 18,
+        out_specs=[SPEC_VMEM] * 12,
+        scratch_shapes=[
+            pltpu.VMEM((4, 1024, 128), F32),
+            pltpu.VMEM((128, 128), F32),
+            pltpu.VMEM((16, 64, 256), F32),
+        ],
+        compiler_params=params(),
+        cost_estimate=cost(2e7, 8e6),
+        name="finish_weights",
+    )(places, v_section, three, v_mix, v_skip, g_dilated, g_mix, g_skip, stat, *pieces)
+
+
+def run_forward(places, signals, edges, ids, gain, pieces):
+    rows = signals[0].shape[0]
     own = rows - 2 * HALO
     kept = shape_of((3, 8, rows, 256))
     out_shape = [kept] * 5 + [
@@ -426,7 +655,7 @@
     return pl.pallas_call(
         forward_kernel,
         out_shape=out_shape,
-        in_specs=[SPEC_SMEM] + [SPEC_VMEM] * 6 + [SPEC_ANY] * 10,
+        in_specs=[SPEC_SMEM] + [SPEC_VMEM] * 10 + [SPEC_ANY] * 10,
         out_specs=[SPEC_ANY] * 5 + [SPEC_VMEM] * 3 + [SPEC_ANY] * 4,
         scratch_shapes=[
             pltpu.VMEM((16, 256, 512), BF16),
@@ -440,24 +669,26 @@
             pltpu.VMEM((26, rows, 256), BF16),
             pltpu.VMEM((2, 8 * own, 128), F32),
             pltpu.VMEM((256, 8 * own), BF16),
+            pltpu.VMEM((4, rows, 128), F32),
             pltpu.SemaphoreType.DMA,
             pltpu.SemaphoreType.DMA,
             pltpu.SemaphoreType.DMA,
         ],
-        compiler_params=pltpu.CompilerParams(vmem_limit_bytes=VMEM_BYTES),
+        compiler_params=params(),
+        cost_estimate=cost(2 * 1245184 * 8 * rows, 50e6),
         name="forward_blocks",
-    )(places, *signals, masks, gain, *pieces)
-
-
-def run_backward(places, cotangents, masks, sact, dsig, stat, kept, pieces):
-    rows = masks.shape[1]
+    )(places, *signals, *edges, ids, gain, *pieces)
+
+
+def run_backward(places, cotangents, edges, ids, sact, dsig, stat, kept, pieces):
+    rows = sact.shape[0]
     own = rows - 2 * HALO
     return pl.pallas_call(
         backward_kernel,
         out_shape=[shape_of((4, 2, 256, 768))] * 2 + [shape_of((own, 128))] * 4,
         in_specs=[SPEC_SMEM]
         + [SPEC_ANY] * 4
-        + [SPEC_VMEM] * 4
+        + [SPEC_VMEM] * 8
         + [SPEC_ANY] * 5
         + [SPEC_ANY] * 10,
         out_specs=[SPEC_ANY] * 2 + [SPEC_VMEM] * 4,
@@ -477,14 +708,16 @@
             pltpu.VMEM((own, 512), F32),
             pltpu.VMEM((8, 8, 256), F32),
             pltpu.VMEM((16, 256, 768), BF16),
+            pltpu.VMEM((4, rows, 128), F32),
             pltpu.SemaphoreType.DMA,
             pltpu.SemaphoreType.DMA,
             pltpu.SemaphoreType.DMA((2,)),
             pltpu.SemaphoreType.DMA,
         ],
-        compiler_params=pltpu.CompilerParams(vmem_limit_bytes=VMEM_BYTES),
+        compiler_params=params(),
+        cost_estimate=cost(2 * 2490368 * 8 * rows, 60e6),
         name="backward_blocks",
-    )(places, *cotangents, masks, sact, dsig, stat, *kept, *pieces)
+    )(places, *cotangents, *edges, ids, sact, dsig, stat, *kept, *pieces)
 
 
 def exchange(values, axis, cut):
@@ -493,17 +726,6 @@
     for k in (1, 2, 3):
         parts.append(swap(cut(me ^ k), axis, k))
     return parts
-
-
-def normed(v_values, gain_values, sum_axes):
-    norm_values = jnp.sqrt(jnp.sum(v_values * v_values, axis=sum_axes, keepdims=True) + EPSILON)
-    return gain_values * v_values / norm_values, norm_values
-
-
-def norm_back(grad_w, v_values, gain_values, norm_values, sum_axes):
-    grad_g = jnp.sum(grad_w * v_values, axis=sum_axes, keepdims=True) / norm_values
-    grad_v = gain_values / norm_values * (grad_w - grad_g / norm_values * v_values)
-    return grad_v, grad_g
 
 
 def body(
@@ -524,81 +746,79 @@
     cotangent,
 ):
     tm_index, chan = lax.axis_index("tm"), lax.axis_index("chan")
+    tm_size = lax.axis_size("tm")
     turn = tm_index % 8
     places = jnp.stack([turn, chan]).astype(jnp.int32)
     own = signal.shape[0] // 4
     rows = own + 2 * HALO
     start = tm_index * signal.shape[0] + chan * own
 
-    padded = jnp.pad(segment_ids, HALO + 2, constant_values=-1)
-    nearby = lax.dynamic_slice_in_dim(padded, start, rows + 4)
-
-    def same(offset):
-        flags = (nearby[2 : 2 + rows] == nearby[2 + offset : 2 + offset + rows]).astype(F32)
-        flags = jnp.concatenate([flags[HALO:], flags[:HALO]])
-        return jnp.broadcast_to(flags[:, None], (rows, 128))
-
-    masks = jnp.stack([same(-1), same(1), same(-2), same(2)])
-
-    low, high = edges(signal, 0, HALO)
-    longer = jnp.concatenate([low, signal, high], axis=0)
-
-    def cut_signal(place):
-        block = lax.dynamic_slice_in_dim(longer, place * own, rows, axis=0)
-        return jnp.concatenate([block[HALO:], block[:HALO]], axis=0)
-
-    signals = exchange(longer, "chan", cut_signal)
-
-    three_v, three_g = v_dilated.astype(F32), g_dilated.astype(F32)[:, :, None, None]
-    mix_v, mix_g = v_mix.astype(F32), g_mix.astype(F32)[:, :, None]
-    skip_v, skip_g = v_skip.astype(F32), g_skip.astype(F32)[:, :, None]
-    w_three, three_norm = normed(three_v, three_g, (2, 3))
-    w_mix, mix_norm = normed(mix_v, mix_g, (2,))
-    w_skip, skip_norm = normed(skip_v, skip_g, (2,))
-    matrices = jnp.concatenate(
-        [jnp.transpose(w_three, (0, 2, 1, 3)), w_mix[:, None], w_skip[:, None]], axis=1
-    ).astype(BF16)
-    matrices = matrices.reshape(15, 64, 256)
-    small = jnp.concatenate([b_section[None], b_dilated, b_mix, b_skip], axis=0).T
-    small = jnp.pad(small, ((0, 0), (0, 246)))
-    matrices = jnp.concatenate([matrices, small[None]], axis=0)
-    piece = jnp.concatenate(
-        [
-            jnp.transpose(lax.dynamic_slice_in_dim(v_section, 2 * turn, 2, axis=1), (1, 0, 2)),
-            lax.dynamic_slice_in_dim(matrices, 2 * turn, 2, axis=0),
-        ],
-        axis=2,
+    three_v = jnp.transpose(v_dilated, (0, 2, 1, 3))
+    piece = run_pack_weights(
+        places,
+        v_section,
+        three_v,
+        v_mix,
+        v_skip,
+        b_section[None],
+        b_dilated,
+        b_mix,
+        b_skip,
+        g_dilated,
+        g_mix,
+        g_skip,
     )
-    column = jnp.stack([piece] + [swap(piece, "chan", k) for k in (1, 2, 3)])
-    pieces = spread(column)
+    by_chan = [piece] + [swap(piece, "chan", k) for k in (1, 2, 3)]
+
+    packed = run_pack_frames(places, piece, signal, cotangent)
+    signals, edges, cotangents = list(packed[0:4]), list(packed[4:8]), list(packed[8:12])
+    by_chan, _ = lax.optimization_barrier((by_chan, packed[0]))
+    pieces = spread(jnp.stack(by_chan))
+    for k in (1, 2, 3):
+        signals[k] = swap(signals[k], "chan", k)
+    for k in range(4):
+        pairs = []
+        for m in range(tm_size):
+            if m > 0:
+                pairs.append((4 * m + (3 ^ k), 4 * m - 1))
+            if m < tm_size - 1:
+                pairs.append((4 * m + k, 4 * m + 4))
+        edges[k] = lax.ppermute(edges[k], ("tm", "chan"), pairs)
+    for k in (1, 2, 3):
+        cotangents[k] = swap(cotangents[k], "chan", k)
+    padded = jnp.pad(segment_ids, 16, constant_values=-1)
+    nearby = lax.dynamic_slice_in_dim(padded, start, own + 32)
+    ids = jnp.broadcast_to(nearby[:, None], (own + 32, 128))
 
     frames = 8 * own
-    rim = 8 * HALO
-    low, high = edges(cotangent, 1, rim)
-
-    def cut_cotangent(place):
-        main = lax.dynamic_slice_in_dim(cotangent, place * frames, frames, axis=1)
-        after_start = jnp.minimum((place + 1) * frames, 3 * frames)
-        before_start = jnp.maximum(place * frames - rim, 0)
-        after = lax.dynamic_slice_in_dim(cotangent, after_start, rim, axis=1)
-        before = lax.dynamic_slice_in_dim(cotangent, before_start, rim, axis=1)
-        after = jnp.where(place == 3, high, after)
-        before = jnp.where(place == 0, low, before)
-        return jnp.concatenate([main, after, before], axis=1)
-
-    cotangents = exchange(cotangent, "chan", cut_cotangent)
-
-    section_gain = g_section.astype(F32)
-    results = run_forward(places, signals, masks, section_gain[None], pieces)
+    results = run_forward(places, signals, edges, ids, g_section[None].astype(F32), pieces)
     kept, sact, dsig, stat, outs = results[:5], results[5], results[6], results[7], results[8:]
 
     received = [outs[0]] + [swap(outs[k], "chan", k) for k in (1, 2, 3)]
+    results = run_backward(places, cotangents, edges, ids, sact, dsig, stat, kept, pieces)
+    even, odd, sgrads = results[0], results[1], results[2:]
+    odd, received = lax.optimization_barrier((odd, received))
     output = jnp.zeros((64, 4 * frames), BF16)
     for k in range(4):
         output = lax.dynamic_update_slice_in_dim(output, received[k], (chan ^ k) * frames, axis=1)
 
-    results = run_backward(places, cotangents, masks, sact, dsig, stat, kept, pieces)
-    even, odd, sgrads = results[0], results[1], results[2:]
+    quarter = even + swap(odd, "tm", 1)
+    far_a = swap(quarter[3, :1], "tm", 2)
+    far_b = swap(quarter[3, 1:], "tm", 4)
+    for_y = jnp.concatenate([quarter[2, :1] + far_a, quarter[2, 1:]], axis=0)
+    for_x = jnp.concatenate([quarter[1, :1], quarter[1, 1:] + far_b], axis=0)
+    summed = quarter[0] + swap(for_x, "tm", 2) + swap(for_y, "tm", 4)
+
+    def cut_rows(place):
+        return lax.dynamic_slice_in_dim(summed, place * 64, 64, axis=1)
+
+    parts = exchange(summed, "chan", cut_rows)
+    mine = parts[0] + parts[1] + parts[2] + parts[3]
+    bit = 8
+    while bit < tm_size:
+        mine = mine + swap(mine, "tm", bit)
+        bit = 2 * bit
+    gathered = spread(mine)
 
     received = [sgrads[0]] + [swap(sgrads[k], "chan", k) for k in (1, 2, 3)]
     signal_grad = jnp.zeros((4 * own, 128), BF16)
@@ -606,63 +826,24 @@
         signal_grad = lax.dynamic_update_slice_in_dim(
             signal_grad, received[k], (chan ^ k) * own, axis=0
         )
-
-    quarter = even + swap(odd, "tm", 1)
-    far_a = swap(quarter[3, :1], "tm", 2)
-    far_b = swap(quarter[3, 1:], "tm", 4)
-    for_y = jnp.concatenate([quarter[2, :1] + far_a, quarter[2, 1:]], axis=0)
-    for_x = jnp.concatenate([quarter[1, :1], quarter[1, 1:] + far_b], axis=0)
-    summed = quarter[0] + swap(for_x, "tm", 2) + swap(for_y, "tm", 4)
-
-    def cut_rows(place):
-        return lax.dynamic_slice_in_dim(summed, place * 64, 64, axis=1)
-
-    parts = exchange(summed, "chan", cut_rows)
-    mine = parts[0] + parts[1] + parts[2] + parts[3]
-    bit = 8
-    while bit < lax.axis_size("tm"):
-        mine = mine + swap(mine, "tm", bit)
-        bit = 2 * bit
-    gathered = spread(mine)
-    slots = [None] * 8
-    for a in (0, 1):
-        base = gathered[5 * a : 5 * a + 5]
-        slots[a], slots[2 + a], slots[4 + a] = base[0], base[1], base[2]
-        slots[6 + a] = jnp.concatenate([base[3], base[4]], axis=0)
-    slots = jnp.stack(slots)
-    slots = jnp.take(slots, jnp.arange(8) ^ turn, axis=0).reshape(16, 64, 768).astype(F32)
-
-    grad_section = jnp.transpose(slots[:, :, 0:512], (1, 0, 2))
-    grad_blocks = slots[:15, :, 512:768].reshape(3, 5, 64, 256)
-    aux = slots[15, :, 512:768]
-    section_norm = stat[0]
-    section_gain_grad = aux[0:4, 128:256].reshape(512) / section_norm
-    section_v_grad = (
-        section_gain
-        / section_norm
-        * (grad_section - section_gain_grad / section_norm * v_section.astype(F32))
+    (sec, gain, bs, three, gt, bt, mix, gm, bm, skip, gk, bk) = run_finish(
+        places, v_section, three_v, v_mix, v_skip, g_dilated, g_mix, g_skip, stat, gathered
     )
-    bias_grads = aux[:, 0:7].T
-    three_v_grad, three_g_grad = norm_back(
-        jnp.transpose(grad_blocks[:, 0:3], (0, 2, 1, 3)), three_v, three_g, three_norm, (2, 3)
-    )
-    mix_v_grad, mix_g_grad = norm_back(grad_blocks[:, 3], mix_v, mix_g, mix_norm, (2,))
-    skip_v_grad, skip_g_grad = norm_back(grad_blocks[:, 4], skip_v, skip_g, skip_norm, (2,))
     return (
         output,
         signal_grad,
-        section_v_grad,
-        section_gain_grad,
-        bias_grads[0],
-        three_v_grad,
-        three_g_grad.reshape(3, 64),
-        bias_grads[1:4],
-        mix_v_grad,
-        mix_g_grad.reshape(3, 64),
-        bias_grads[4:7],
-        skip_v_grad,
-        skip_g_grad.reshape(3, 64),
-        bias_grads[4:7],
+        sec,
+        gain.reshape(512),
+        bs.reshape(64),
+        jnp.transpose(three, (0, 2, 1, 3)),
+        gt,
+        bt,
+        mix,
+        gm,
+        bm,
+        skip,
+        gk,
+        bk,
     )
 
 

time: 307 us -> 259 us (0.84)
  local copies, waits for them, and re-layouts: 34 us -> 3.06 us
  other arithmetic: 28.4 us -> 7.69 us
  waiting for transfers between devices: 89.5 us -> 72.1 us
  Pallas kernels: 95.8 us -> 108 us
  starting transfers between devices: 56 us -> 65.5 us
    ppermute x41, waiting for transfers between devices: 87 us -> 72.1 us  [swap(): return lax.ppermute(values, axis, xor_pairs(axis, bit))]
    ppermute x41, starting transfers between devices: 44 us -> 58.7 us  [swap(): return lax.ppermute(values, axis, xor_pairs(axis, bit))]
    pallas_call x0 -> x3, Pallas kernels: none -> 12.9 us  [the longest x1 6.21 us: run_finish(): pl.pallas_call(finish_kernel, out_shape=out_shape, in_specs=[SPEC_SMEM] +...]
    slice x16 -> x0, local copies, waits for them, and re-layouts: 8.92 us -> none  [the longest x8 4.78 us: same(): flags = jnp.concatenate([flags[HALO:], flags[:HALO]])]
    unnamed x88 -> x70, local copies, waits for them, and re-layouts: 10.2 us -> 1.44 us
    concatenate x6 -> x0, local copies, waits for them, and re-layouts: 7.51 us -> none  [the longest x4 6.72 us: cut_cotangent(): return jnp.concatenate([main, after, before], axis=1)]
    concatenate x11 -> x0, other arithmetic: 6.37 us -> none  [the longest x4 3.54 us: same(): flags = jnp.concatenate([flags[HALO:], flags[:HALO]])]
    ppermute x4, starting transfers between devices: 12 us -> 6.76 us  [body(): edges[k] = lax.ppermute(edges[k], ('tm', 'chan'), pairs)]
  transfers between devices with their start and end apart: 45 -> 45, of which waited for: 18 -> 20; matrix products, arithmetic and copies ran while one was open for 13% -> 1% of each run, Pallas kernels for 13% -> 38%
where the time goes in v2:
time: 259 us; the launch traced here: 258 us
  Pallas kernels  108 us (42%)
  waiting for transfers between devices  72.1 us (28%)
  starting transfers between devices  65.5 us (25%)
  other arithmetic  7.69 us (3%)
  local copies, waits for them, and re-layouts  3.06 us (1%)
    ppermute x41, waiting for transfers between devices, swap(): return lax.ppermute(values, axis, xor_pairs(axis, bit))  72.1 us
    ppermute x41, starting transfers between devices, swap(): return lax.ppermute(values, axis, xor_pairs(axis, bit))  58.7 us
    pallas_call x1, Pallas kernels, run_backward(): pl.pallas_call(backward_kernel, out_shape=[shape_of((4, 2, 256, 768))] *...  56.1 us
    pallas_call x1, Pallas kernels, run_forward(): pl.pallas_call(forward_kernel, out_shape=out_shape, in_specs=[SPEC_SMEM]...  39.3 us
    ppermute x4, starting transfers between devices, body(): edges[k] = lax.ppermute(edges[k], ('tm', 'chan'), pairs)  6.76 us
    pallas_call x1, Pallas kernels, run_finish(): pl.pallas_call(finish_kernel, out_shape=out_shape, in_specs=[SPEC_SMEM] +...  6.21 us
  transfers between devices with their start and end apart: 45, of which 20 were waited for; matrix products, arithmetic and copies ran while one was open for 1% of the time, Pallas kernels for 38%

profile of v2, /device:TPU:9, one launch (start us, length us, event | category | flops | bytes accessed | tf_op | source)
XLA Modules:
  0.0 258.1 jit_solution(1868528374418251486)
XLA Ops:
  1.3 3.3 %pack_weights.1.piece = bf16[2,64,768]{2,1,0:T(8,128)(2,1)} custom-call(s32[2]{0:T(128)} %pad_add_fusion.places, bf16[64,16,512]{2,1,0:T(8,128)(2,1)} %sec_ref.3, bf16[3,3,64,256]{3,2,1,0:T(8,128)(2,1)} %bitcast.35, bf16[3,64,256]{2,1,0:T(8,128)(2,1)} %mix_ref.3, bf16[3,64,256]{2,1,0:T(8,128)(2,1)} %skip_ref.3, bf16[1,64]{1,0:T(2,128)(2,1)} %bitcast.41, ...), custom_call_target="tpu_custom_call" | custom-call | flops 20000000 | bytes 3000000 | tf_op jit(solution)/shard_map/pack_weights/pallas_call | solution.py:581
  4.6 2.5 collective-permute-start.11
  7.3 3.4 %pack_frames.1 = (bf16[528,128]{1,0:T(8,128)(2,1)}, bf16[528,128]{1,0:T(8,128)(2,1)}, bf16[528,128]{1,0:T(8,128)(2,1)}, bf16[528,128]{1,0:T(8,128)(2,1)}, bf16[8...) custom-call(s32[2]{0:T(128)} %pad_add_fusion.places, ...), custom_call_target="tpu_custom_call" | custom-call | flops 1000000 | bytes 6000000 | tf_op jit(solution)/shard_map/pack_frames/pallas_call | solution.py:602
  10.7 1.1 collective-permute-done.10
  11.8 4.1 %collective-permute-done.11 = bf16[2,64,768]{2,1,0:T(8,128)(2,1)S(1)} collective-permute-done((bf16[2,64,768]{2,1,0:T(8,128)(2,1)}, bf16[2,64,768]{2,1,0:T(8,128)(2,1)S(1)}, u32[]{:S(2)}, u32[]{:S(2)}) %collective-permute-start.11) | collective-permute-done | bytes 196640 | tf_op jit(solution)/shard_map/ppermute | solution.py:21
  15.9 8.4 %collective-permute-done.12 = bf16[2,64,768]{2,1,0:T(8,128)(2,1)S(1)} collective-permute-done((bf16[2,64,768]{2,1,0:T(8,128)(2,1)}, bf16[2,64,768]{2,1,0:T(8,128)(2,1)S(1)}, u32[]{:S(2)}, u32[]{:S(2)}) %collective-permute-start.12) | collective-permute-done | bytes 196640 | tf_op jit(solution)/shard_map/ppermute | solution.py:21
  24.3 1.3 collective-permute-start.14
  25.6 1.2 collective-permute-start.13
  27.5 3.8 %collective-permute-start.4 = (bf16[80,128]{1,0:T(8,128)(2,1)}, bf16[80,128]{1,0:T(8,128)(2,1)S(1)}, u32[]{:S(2)}, u32[]{:S(2)}) collective-permute-start(bf16[80,128]{1,0:T(8,128)(2,1)} %get-tuple-element.70), channel_id=1, source_target_pairs={{1,4},{6,3},{5,8},{10,7},{9,12},{14,11},{13,16},{18,15},{17,20},{2... | collective-permute-start | bytes 61448 | tf_op jit(solution)/shard_map/ppermute | solution.py:786
  31.3 1.7 collective-permute-start.5
  33.0 5.2 %collective-permute-start.7 = (bf16[528,128]{1,0:T(8,128)(2,1)}, bf16[528,128]{1,0:T(8,128)(2,1)S(1)}, u32[]{:S(2)}, u32[]{:S(2)}) collective-permute-start(bf16[528,128]{1,0:T(8,128)(2,1)} %get-tuple-element.74), channel_id=1, source_target_pairs={{0,1},{1,0},{2,3},{3,2},{4,5},{5,4},{6,7},{7,6},{8,9},{9,8},{10,11... | collective-permute-start | bytes 405512 | tf_op jit(solution)/shard_map/ppermute | solution.py:21
  38.2 4.7 %collective-permute-start.8 = (bf16[528,128]{1,0:T(8,128)(2,1)}, bf16[528,128]{1,0:T(8,128)(2,1)S(1)}, u32[]{:S(2)}, u32[]{:S(2)}) collective-permute-start(bf16[528,128]{1,0:T(8,128)(2,1)} %get-tuple-element.75), channel_id=1, source_target_pairs={{0,2},{1,3},{2,0},{3,1},{4,6},{5,7},{6,4},{7,5},{8,10},{9,11},{10,... | collective-permute-start | bytes 405512 | tf_op jit(solution)/shard_map/ppermute | solution.py:21
  43.9 1.2 collective-permute-start.17
  45.2 1.2 collective-permute-start.15
  46.4 1.3 collective-permute-start.16
  48.4 2.5 collective-permute-done.9.sig3
  50.9 4.6 %collective-permute-done.15.rest_3_ = bf16[2,2,64,768]{3,2,1,0:T(8,128)(2,1)} collective-permute-done((bf16[2,2,64,768]{3,2,1,0:T(8,128)(2,1)S(1)}, bf16[2,2,64,768]{3,2,1,0:T(8,128)(2,1)}, u32[]{:S(2)}, u32[]{:S(2)}) %collective-permute-start.15) | collective-permute-done | bytes 393248 | tf_op jit(solution)/shard_map/ppermute | solution.py:21
  55.5 1.3 collective-permute-start.20
  56.8 1.3 collective-permute-start.21
  58.8 8.3 %collective-permute-start = (bf16[64,4224]{1,0:T(8,128)(2,1)}, bf16[64,4224]{1,0:T(8,128)(2,1)}, u32[]{:S(2)}, u32[]{:S(2)}) collective-permute-start(bf16[64,4224]{1,0:T(8,128)(2,1)} %get-tuple-element.66), channel_id=1, source_target_pairs={{0,1},{1,0},{2,3},{3,2},{4,5},{5,4},{6,7},{7,6},{8,9},{9,8},{10,11... | collective-permute-start | bytes 1622024 | tf_op jit(solution)/shard_map/ppermute | solution.py:21
  67.1 1.8 collective-permute-start.1
  70.0 39.3 %forward_blocks.1 = (bf16[3,8,528,256]{3,2,1,0:T(8,128)(2,1)}, bf16[3,8,528,256]{3,2,1,0:T(8,128)(2,1)}, bf16[3,8,528,256]{3,2,1,0:T(8,128)(2,1)}, bf16[3,8,528,...) custom-call(s32[2]{0:T(128)} %pad_add_fusion.places, ...), custom_call_target="tpu_custom_call" | custom-call | flops 10519314432 | bytes 50000000 | tf_op jit(solution)/shard_map/forward_blocks/pallas_call | solution.py:655
  109.4 1.9 collective-permute-start.22
  111.2 1.4 collective-permute-start.23
  112.9 3.7 %collective-permute-done.2.cot3 = bf16[64,4224]{1,0:T(8,128)(2,1)} collective-permute-done((bf16[64,4224]{1,0:T(8,128)(2,1)}, bf16[64,4224]{1,0:T(8,128)(2,1)}, u32[]{:S(2)}, u32[]{:S(2)}) %collective-permute-start.2) | collective-permute-done | bytes 540704 | tf_op jit(solution)/shard_map/ppermute | solution.py:21
  116.6 56.1 %backward_blocks.1 = (bf16[4,2,256,768]{3,2,1,0:T(8,128)(2,1)}, bf16[4,2,256,768]{3,2,1,0:T(8,128)(2,1)}, bf16[512,128]{1,0:T(8,128)(2,1)}, bf16[512,128]{1,0:T(...) custom-call(s32[2]{0:T(128)} %pad_add_fusion.places, bf16[64,4224]{1,0:T(8,128)(2,1)} %get-tuple-element.65.cot0, ...), custom_call_target="tpu_custom_call" | custom-call | flops 21038628864 | bytes 60000000 | tf_op jit(solution)/shard_map/backward_blocks/pallas_call | solution.py:686
  172.8 1.3 collective-permute-start.28
  174.1 5.5 %collective-permute-done.28 = bf16[4,2,256,768]{3,2,1,0:T(8,128)(2,1)S(1)} collective-permute-done((bf16[4,2,256,768]{3,2,1,0:T(8,128)(2,1)}, bf16[4,2,256,768]{3,2,1,0:T(8,128)(2,1)S(1)}, u32[]{:S(2)}, u32[]{:S(2)}) %collective-permute-start.28) | collective-permute-done | bytes 3145760 | tf_op jit(solution)/shard_map/ppermute | solution.py:21
  179.6 2.8 %add.83 = bf16[4,2,256,768]{3,2,1,0:T(8,128)(2,1)S(1)} add(bf16[4,2,256,768]{3,2,1,0:T(8,128)(2,1)} %get-tuple-element.102, bf16[4,2,256,768]{3,2,1,0:T(8,128)(2,1)S(1)} %collective-permute-done.28) | non-fusion elementwise | flops 1572864 | bytes 9437184 | tf_op jit(solution)/shard_map/add | solution.py:805
  182.5 1.8 collective-permute-start.29
  184.6 8.8 %collective-permute-done.29 = bf16[1,256,768]{2,1,0:T(8,128)(2,1)S(1)} collective-permute-done((bf16[1,256,768]{2,1,0:T(8,128)(2,1)S(1)}, bf16[1,256,768]{2,1,0:T(8,128)(2,1)S(1)}, u32[]{:S(2)}, u32[]{:S(2)}) %collective-permute-start.29) | collective-permute-done | bytes 393248 | tf_op jit(solution)/shard_map/ppermute | solution.py:21
  196.9 2.8 %collective-permute-start.26 = (bf16[512,128]{1,0:T(8,128)(2,1)}, bf16[512,128]{1,0:T(8,128)(2,1)S(1)}, u32[]{:S(2)}, u32[]{:S(2)}) collective-permute-start(bf16[512,128]{1,0:T(8,128)(2,1)} %get-tuple-element.100), channel_id=1, source_target_pairs={{0,2},{1,3},{2,0},{3,1},{4,6},{5,7},{6,4},{7,5},{8,10},{9,11},{10,... | collective-permute-start | bytes 393224 | tf_op jit(solution)/shard_map/ppermute | solution.py:21
  199.8 1.5 collective-permute-done.25
  201.4 6.2 %collective-permute-done.26 = bf16[512,128]{1,0:T(8,128)(2,1)S(1)} collective-permute-done((bf16[512,128]{1,0:T(8,128)(2,1)}, bf16[512,128]{1,0:T(8,128)(2,1)S(1)}, u32[]{:S(2)}, u32[]{:S(2)}) %collective-permute-start.26) | collective-permute-done | bytes 131104 | tf_op jit(solution)/shard_map/ppermute | solution.py:21
  207.6 3.1 %collective-permute-done.27 = bf16[512,128]{1,0:T(8,128)(2,1)S(1)} collective-permute-done((bf16[512,128]{1,0:T(8,128)(2,1)S(1)}, bf16[512,128]{1,0:T(8,128)(2,1)S(1)}, u32[]{:S(2)}, u32[]{:S(2)}) %collective-permute-start.27) | collective-permute-done | bytes 131104 | tf_op jit(solution)/shard_map/ppermute | solution.py:21
  210.8 2.4 collective-permute-done.30
  213.1 1.0 collective-permute-done.32
  214.1 1.5 fusion.1
  215.8 2.4 collective-permute-start.34
  218.6 1.6 collective-permute-done.33
  220.3 4.3 %collective-permute-done.34 = bf16[2,64,768]{2,1,0:T(8,128)(2,1)S(1)} collective-permute-done((bf16[2,64,768]{2,1,0:T(8,128)(2,1)S(1)}, bf16[2,64,768]{2,1,0:T(8,128)(2,1)S(1)}, u32[]{:S(2)}, u32[]{:S(2)}) %collective-permute-start.34) | collective-permute-done | bytes 196640 | tf_op jit(solution)/shard_map/ppermute | solution.py:21
  224.6 9.3 %collective-permute-done.35 = bf16[2,64,768]{2,1,0:T(8,128)(2,1)S(1)} collective-permute-done((bf16[2,64,768]{2,1,0:T(8,128)(2,1)S(1)}, bf16[2,64,768]{2,1,0:T(8,128)(2,1)S(1)}, u32[]{:S(2)}, u32[]{:S(2)}) %collective-permute-start.35) | collective-permute-done | bytes 196640 | tf_op jit(solution)/shard_map/ppermute | solution.py:21
  234.8 2.1 collective-permute-start.36
  237.0 1.6 collective-permute-done.37.rest_2_
  238.6 2.0 collective-permute-start.38
  241.7 4.3 %collective-permute-start.40 = (bf16[2,64,768]{2,1,0:T(8,128)(2,1)S(1)}, bf16[2,64,768]{2,1,0:T(8,128)(2,1)S(1)}, u32[]{:S(2)}, u32[]{:S(2)}) collective-permute-start(bf16[2,64,768]{2,1,0:T(8,128)(2,1)S(1)} %add_add_fusion.rest_0_), channel_id=1, source_target_pairs={{0,4},{4,0},{8,12},{12,8},{16,20},{20,16},{24,28},{28,24},{1,5},{5... | collective-permute-start | bytes 589832 | tf_op jit(solution)/shard_map/ppermute | solution.py:21
  247.5 1.9 collective-permute-start.44
  251.7 6.2 %finish_weights.1 = (f32[64,16,512]{2,1,0:T(8,128)}, f32[1,512]{1,0:T(1,128)}, f32[1,64]{1,0:T(1,128)}, f32[3,3,64,256]{3,2,1,0:T(8,128)}, f32[3,64]{1,0:T(4,128...) custom-call(s32[2]{0:T(128)} %pad_add_fusion.places, ...), custom_call_target="tpu_custom_call" | custom-call | flops 20000000 | bytes 8000000 | tf_op jit(solution)/shard_map/finish_weights/pallas_call | solution.py:629
  (144 shorter events, 15.7 us)
Async XLA Ops:
  4.6 7.2 %collective-permute-start.10 = (bf16[2,64,768]{2,1,0:T(8,128)(2,1)}, bf16[2,64,768]{2,1,0:T(8,128)(2,1)S(1)}, u32[]{:S(2)}, u32[]{:S(2)}) collective-permute-start(bf16[2,64,768]{2,1,0:T(8,128)(2,1)} %pack_weights.1.piece), channel_id=1, source_target_pairs={{0,1},{1,0},{2,3},{3,2},{4,5},{5,4},{6,7},{7,6},{8,9},{9,8},{10,11... | collective-permute-start | bytes 589832 | tf_op jit(solution)/shard_map/ppermute | solution.py:21
  4.6 11.2 %collective-permute-start.11 = (bf16[2,64,768]{2,1,0:T(8,128)(2,1)}, bf16[2,64,768]{2,1,0:T(8,128)(2,1)S(1)}, u32[]{:S(2)}, u32[]{:S(2)}) collective-permute-start(bf16[2,64,768]{2,1,0:T(8,128)(2,1)} %pack_weights.1.piece), channel_id=1, source_target_pairs={{0,2},{1,3},{2,0},{3,1},{4,6},{5,7},{6,4},{7,5},{8,10},{9,11},{10,... | collective-permute-start | bytes 589832 | tf_op jit(solution)/shard_map/ppermute | solution.py:21
  7.1 17.1 %collective-permute-start.12 = (bf16[2,64,768]{2,1,0:T(8,128)(2,1)}, bf16[2,64,768]{2,1,0:T(8,128)(2,1)S(1)}, u32[]{:S(2)}, u32[]{:S(2)}) collective-permute-start(bf16[2,64,768]{2,1,0:T(8,128)(2,1)} %pack_weights.1.piece), channel_id=1, source_target_pairs={{0,3},{1,2},{2,1},{3,0},{4,7},{5,6},{6,5},{7,4},{8,11},{9,10},{10,... | collective-permute-start | bytes 589832 | tf_op jit(solution)/shard_map/ppermute | solution.py:21
  10.7 47.4 %copy-start.25 = (bf16[512]{0:T(512)(128)(2,1)S(1)}, bf16[512]{0:T(512)(128)(2,1)}, u32[]{:S(2)}) copy-start(bf16[512]{0:T(512)(128)(2,1)} %param.18) | copy-start | bytes 3076
  10.7 48.0 %copy-start.24 = (s32[16384]{0:T(1024)S(1)}, s32[16384]{0:T(1024)}, u32[]{:S(2)}) copy-start(s32[16384]{0:T(1024)} %param.16) | copy-start | bytes 196612
  24.3 45.7 %copy-start.3 = (bf16[4,2,64,768]{3,2,1,0:T(8,128)(2,1)}, bf16[4,2,64,768]{3,2,1,0:T(8,128)(2,1)S(1)}, u32[]{:S(2)}) copy-start(bf16[4,2,64,768]{3,2,1,0:T(8,128)(2,1)S(1)} %pad_maximum_fusion.rest_0_) | copy-start | bytes 2359300
  24.3 18.8 %collective-permute-start.14 = (bf16[4,2,64,768]{3,2,1,0:T(8,128)(2,1)S(1)}, bf16[4,2,64,768]{3,2,1,0:T(8,128)(2,1)S(1)}, u32[]{:S(2)}, u32[]{:S(2)}) collective-permute-start(bf16[4,2,64,768]{3,2,1,0:T(8,128)(2,1)S(1)} %pad_maximum_fusion.rest_0_), channel_id=1, source_target_pairs={{0,16},{4,20},{8,24},{12,28},{16,0},{20,4},{24,8},{28,12},{1,17},{... | collective-permute-start | bytes 2359304 | tf_op jit(solution)/shard_map/ppermute | solution.py:21
  25.6 19.5 %collective-permute-start.13 = (bf16[4,2,64,768]{3,2,1,0:T(8,128)(2,1)S(1)}, bf16[4,2,64,768]{3,2,1,0:T(8,128)(2,1)S(1)}, u32[]{:S(2)}, u32[]{:S(2)}) collective-permute-start(bf16[4,2,64,768]{3,2,1,0:T(8,128)(2,1)S(1)} %pad_maximum_fusion.rest_0_), channel_id=1, source_target_pairs={{0,8},{4,12},{8,0},{12,4},{16,24},{20,28},{24,16},{28,20},{1,9},{5... | collective-permute-start | bytes 2359304 | tf_op jit(solution)/shard_map/ppermute | solution.py:21
  26.9 6.1 %collective-permute-start.3 = (bf16[80,128]{1,0:T(8,128)(2,1)}, bf16[80,128]{1,0:T(8,128)(2,1)S(1)}, u32[]{:S(2)}, u32[]{:S(2)}) collective-permute-start(bf16[80,128]{1,0:T(8,128)(2,1)} %get-tuple-element.69), channel_id=1, source_target_pairs={{0,4},{7,3},{4,8},{11,7},{8,12},{15,11},{12,16},{19,15},{16,20},{2... | collective-permute-start | bytes 61448 | tf_op jit(solution)/shard_map/ppermute | solution.py:786
  27.5 10.7 %collective-permute-start.4 = (bf16[80,128]{1,0:T(8,128)(2,1)}, bf16[80,128]{1,0:T(8,128)(2,1)S(1)}, u32[]{:S(2)}, u32[]{:S(2)}) collective-permute-start(bf16[80,128]{1,0:T(8,128)(2,1)} %get-tuple-element.70), channel_id=1, source_target_pairs={{1,4},{6,3},{5,8},{10,7},{9,12},{14,11},{13,16},{18,15},{17,20},{2... | collective-permute-start | bytes 61448 | tf_op jit(solution)/shard_map/ppermute | solution.py:786
  31.3 11.6 %collective-permute-start.5 = (bf16[80,128]{1,0:T(8,128)(2,1)}, bf16[80,128]{1,0:T(8,128)(2,1)S(1)}, u32[]{:S(2)}, u32[]{:S(2)}) collective-permute-start(bf16[80,128]{1,0:T(8,128)(2,1)} %get-tuple-element.71), channel_id=1, source_target_pairs={{2,4},{5,3},{6,8},{9,7},{10,12},{13,11},{14,16},{17,15},{18,20},{2... | collective-permute-start | bytes 61448 | tf_op jit(solution)/shard_map/ppermute | solution.py:786
  33.0 13.4 %collective-permute-start.7 = (bf16[528,128]{1,0:T(8,128)(2,1)}, bf16[528,128]{1,0:T(8,128)(2,1)S(1)}, u32[]{:S(2)}, u32[]{:S(2)}) collective-permute-start(bf16[528,128]{1,0:T(8,128)(2,1)} %get-tuple-element.74), channel_id=1, source_target_pairs={{0,1},{1,0},{2,3},{3,2},{4,5},{5,4},{6,7},{7,6},{8,9},{9,8},{10,11... | collective-permute-start | bytes 405512 | tf_op jit(solution)/shard_map/ppermute | solution.py:21
  38.2 10.2 %collective-permute-start.8 = (bf16[528,128]{1,0:T(8,128)(2,1)}, bf16[528,128]{1,0:T(8,128)(2,1)S(1)}, u32[]{:S(2)}, u32[]{:S(2)}) collective-permute-start(bf16[528,128]{1,0:T(8,128)(2,1)} %get-tuple-element.75), channel_id=1, source_target_pairs={{0,2},{1,3},{2,0},{3,1},{4,6},{5,7},{6,4},{7,5},{8,10},{9,11},{10,... | collective-permute-start | bytes 405512 | tf_op jit(solution)/shard_map/ppermute | solution.py:21
  42.9 8.0 %collective-permute-start.9 = (bf16[528,128]{1,0:T(8,128)(2,1)}, bf16[528,128]{1,0:T(8,128)(2,1)S(1)}, u32[]{:S(2)}, u32[]{:S(2)}) collective-permute-start(bf16[528,128]{1,0:T(8,128)(2,1)} %get-tuple-element.76), channel_id=1, source_target_pairs={{0,3},{1,2},{2,1},{3,0},{4,7},{5,6},{6,5},{7,4},{8,11},{9,10},{10,... | collective-permute-start | bytes 405512 | tf_op jit(solution)/shard_map/ppermute | solution.py:21
  43.2 0.7 collective-permute-start.6
  43.9 14.9 %collective-permute-start.17 = (bf16[4,2,64,768]{3,2,1,0:T(8,128)(2,1)S(1)}, bf16[4,2,64,768]{3,2,1,0:T(8,128)(2,1)S(1)}, u32[]{:S(2)}, u32[]{:S(2)}) collective-permute-start(bf16[4,2,64,768]{3,2,1,0:T(8,128)(2,1)S(1)} %pad_maximum_fusion.rest_0_), channel_id=1, source_target_pairs={{0,4},{4,0},{8,12},{12,8},{16,20},{20,16},{24,28},{28,24},{1,5},{5... | collective-permute-start | bytes 2359304 | tf_op jit(solution)/shard_map/ppermute | solution.py:21
  45.2 10.3 %collective-permute-start.15 = (bf16[2,2,64,768]{3,2,1,0:T(8,128)(2,1)S(1)}, bf16[2,2,64,768]{3,2,1,0:T(8,128)(2,1)}, u32[]{:S(2)}, u32[]{:S(2)}) collective-permute-start(bf16[2,2,64,768]{3,2,1,0:T(8,128)(2,1)S(1)} %slice.44), channel_id=1, source_target_pairs={{0,8},{4,12},{8,0},{12,4},{16,24},{20,28},{24,16},{28,20},{1,9},{5... | collective-permute-start | bytes 1179656 | tf_op jit(solution)/shard_map/ppermute | solution.py:21
  46.4 10.4 %collective-permute-start.16 = (bf16[2,2,64,768]{3,2,1,0:T(8,128)(2,1)S(1)}, bf16[2,2,64,768]{3,2,1,0:T(8,128)(2,1)}, u32[]{:S(2)}, u32[]{:S(2)}) collective-permute-start(bf16[2,2,64,768]{3,2,1,0:T(8,128)(2,1)S(1)} %slice.45), channel_id=1, source_target_pairs={{0,16},{4,20},{8,24},{12,28},{16,0},{20,4},{24,8},{28,12},{1,17},{... | collective-permute-start | bytes 1179656 | tf_op jit(solution)/shard_map/ppermute | solution.py:21
  48.4 20.8 %collective-permute-start.18 = (bf16[4,2,64,768]{3,2,1,0:T(8,128)(2,1)S(1)}, bf16[4,2,64,768]{3,2,1,0:T(8,128)(2,1)}, u32[]{:S(2)}, u32[]{:S(2)}) collective-permute-start(bf16[4,2,64,768]{3,2,1,0:T(8,128)(2,1)S(1)} %collective-permute-done.13.rest_1_), channel_id=1, source_target_pairs={{0,4},{4,0},{8,12},{12,8},{16,20},{20,16},{24,28},{28,24},{1,5},{5... | collective-permute-start | bytes 2359304 | tf_op jit(solution)/shard_map/ppermute | solution.py:21
  50.9 18.2 %collective-permute-start.19 = (bf16[4,2,64,768]{3,2,1,0:T(8,128)(2,1)S(1)}, bf16[4,2,64,768]{3,2,1,0:T(8,128)(2,1)}, u32[]{:S(2)}, u32[]{:S(2)}) collective-permute-start(bf16[4,2,64,768]{3,2,1,0:T(8,128)(2,1)S(1)} %collective-permute-done.14.rest_2_), channel_id=1, source_target_pairs={{0,4},{4,0},{8,12},{12,8},{16,20},{20,16},{24,28},{28,24},{1,5},{5... | collective-permute-start | bytes 2359304 | tf_op jit(solution)/shard_map/ppermute | solution.py:21
  55.5 11.6 %collective-permute-start.20 = (bf16[2,2,64,768]{3,2,1,0:T(8,128)(2,1)}, bf16[2,2,64,768]{3,2,1,0:T(8,128)(2,1)}, u32[]{:S(2)}, u32[]{:S(2)}) collective-permute-start(bf16[2,2,64,768]{3,2,1,0:T(8,128)(2,1)} %collective-permute-done.15.rest_3_), channel_id=1, source_target_pairs={{0,4},{4,0},{8,12},{12,8},{16,20},{20,16},{24,28},{28,24},{1,5},{5... | collective-permute-start | bytes 1179656 | tf_op jit(solution)/shard_map/ppermute | solution.py:21
  56.8 12.0 %collective-permute-start.21 = (bf16[2,2,64,768]{3,2,1,0:T(8,128)(2,1)}, bf16[2,2,64,768]{3,2,1,0:T(8,128)(2,1)}, u32[]{:S(2)}, u32[]{:S(2)}) collective-permute-start(bf16[2,2,64,768]{3,2,1,0:T(8,128)(2,1)} %collective-permute-done.16.rest_4_), channel_id=1, source_target_pairs={{0,4},{4,0},{8,12},{12,8},{16,20},{20,16},{24,28},{28,24},{1,5},{5... | collective-permute-start | bytes 1179656 | tf_op jit(solution)/shard_map/ppermute | solution.py:21
  58.8 53.9 %collective-permute-start = (bf16[64,4224]{1,0:T(8,128)(2,1)}, bf16[64,4224]{1,0:T(8,128)(2,1)}, u32[]{:S(2)}, u32[]{:S(2)}) collective-permute-start(bf16[64,4224]{1,0:T(8,128)(2,1)} %get-tuple-element.66), channel_id=1, source_target_pairs={{0,1},{1,0},{2,3},{3,2},{4,5},{5,4},{6,7},{7,6},{8,9},{9,8},{10,11... | collective-permute-start | bytes 1622024 | tf_op jit(solution)/shard_map/ppermute | solution.py:21
  67.1 45.8 %collective-permute-start.1 = (bf16[64,4224]{1,0:T(8,128)(2,1)}, bf16[64,4224]{1,0:T(8,128)(2,1)}, u32[]{:S(2)}, u32[]{:S(2)}) collective-permute-start(bf16[64,4224]{1,0:T(8,128)(2,1)} %get-tuple-element.67), channel_id=1, source_target_pairs={{0,2},{1,3},{2,0},{3,1},{4,6},{5,7},{6,4},{7,5},{8,10},{9,11},{10,... | collective-permute-start | bytes 1622024 | tf_op jit(solution)/shard_map/ppermute | solution.py:21
  68.8 47.7 %collective-permute-start.2 = (bf16[64,4224]{1,0:T(8,128)(2,1)}, bf16[64,4224]{1,0:T(8,128)(2,1)}, u32[]{:S(2)}, u32[]{:S(2)}) collective-permute-start(bf16[64,4224]{1,0:T(8,128)(2,1)} %get-tuple-element.68), channel_id=1, source_target_pairs={{0,3},{1,2},{2,1},{3,0},{4,7},{5,6},{6,5},{7,4},{8,11},{9,10},{10,... | collective-permute-start | bytes 1622024 | tf_op jit(solution)/shard_map/ppermute | solution.py:21
  109.4 63.4 %collective-permute-start.22 = (bf16[64,4096]{1,0:T(8,128)(2,1)}, bf16[64,4096]{1,0:T(8,128)(2,1)S(1)}, u32[]{:S(2)}, u32[]{:S(2)}) collective-permute-start(bf16[64,4096]{1,0:T(8,128)(2,1)} %get-tuple-element.91), channel_id=1, source_target_pairs={{0,1},{1,0},{2,3},{3,2},{4,5},{5,4},{6,7},{7,6},{8,9},{9,8},{10,11... | collective-permute-start | bytes 1572872 | tf_op jit(solution)/shard_map/ppermute | solution.py:21
  111.2 61.5 %collective-permute-start.23 = (bf16[64,4096]{1,0:T(8,128)(2,1)}, bf16[64,4096]{1,0:T(8,128)(2,1)S(1)}, u32[]{:S(2)}, u32[]{:S(2)}) collective-permute-start(bf16[64,4096]{1,0:T(8,128)(2,1)} %get-tuple-element.92), channel_id=1, source_target_pairs={{0,2},{1,3},{2,0},{3,1},{4,6},{5,7},{6,4},{7,5},{8,10},{9,11},{10,... | collective-permute-start | bytes 1572872 | tf_op jit(solution)/shard_map/ppermute | solution.py:21
  112.7 60.1 %collective-permute-start.24 = (bf16[64,4096]{1,0:T(8,128)(2,1)}, bf16[64,4096]{1,0:T(8,128)(2,1)S(1)}, u32[]{:S(2)}, u32[]{:S(2)}) collective-permute-start(bf16[64,4096]{1,0:T(8,128)(2,1)} %get-tuple-element.93), channel_id=1, source_target_pairs={{0,3},{1,2},{2,1},{3,0},{4,7},{5,6},{6,5},{7,4},{8,11},{9,10},{10,... | collective-permute-start | bytes 1572872 | tf_op jit(solution)/shard_map/ppermute | solution.py:21
  172.8 6.8 %collective-permute-start.28 = (bf16[4,2,256,768]{3,2,1,0:T(8,128)(2,1)}, bf16[4,2,256,768]{3,2,1,0:T(8,128)(2,1)S(1)}, u32[]{:S(2)}, u32[]{:S(2)}) collective-permute-start(bf16[4,2,256,768]{3,2,1,0:T(8,128)(2,1)} %get-tuple-element.103), channel_id=1, source_target_pairs={{0,4},{4,0},{8,12},{12,8},{16,20},{20,16},{24,28},{28,24},{1,5},{5... | collective-permute-start | bytes 9437192 | tf_op jit(solution)/shard_map/ppermute | solution.py:21
  182.5 10.9 %collective-permute-start.29 = (bf16[1,256,768]{2,1,0:T(8,128)(2,1)S(1)}, bf16[1,256,768]{2,1,0:T(8,128)(2,1)S(1)}, u32[]{:S(2)}, u32[]{:S(2)}) collective-permute-start(bf16[1,256,768]{2,1,0:T(8,128)(2,1)S(1)} %get-tuple-element.119), channel_id=1, source_target_pairs={{0,16},{4,20},{8,24},{12,28},{16,0},{20,4},{24,8},{28,12},{1,17},{... | collective-permute-start | bytes 1179656 | tf_op jit(solution)/shard_map/ppermute | solution.py:21
  184.2 10.0 %collective-permute-start.31 = (bf16[1,256,768]{2,1,0:T(8,128)(2,1)S(1)}, bf16[1,256,768]{2,1,0:T(8,128)(2,1)S(1)}, u32[]{:S(2)}, u32[]{:S(2)}) collective-permute-start(bf16[1,256,768]{2,1,0:T(8,128)(2,1)S(1)} %get-tuple-element.118), channel_id=1, source_target_pairs={{0,8},{4,12},{8,0},{12,4},{16,24},{20,28},{24,16},{28,20},{1,9},{5... | collective-permute-start | bytes 1179656 | tf_op jit(solution)/shard_map/ppermute | solution.py:21
  195.3 17.8 %collective-permute-start.30 = (bf16[2,256,768]{2,1,0:T(8,128)(2,1)}, bf16[2,256,768]{2,1,0:T(8,128)(2,1)}, u32[]{:S(2)}, u32[]{:S(2)}) collective-permute-start(bf16[2,256,768]{2,1,0:T(8,128)(2,1)} %pad_maximum_fusion.1), channel_id=1, source_target_pairs={{0,8},{4,12},{8,0},{12,4},{16,24},{20,28},{24,16},{28,20},{1,9},{5... | collective-permute-start | bytes 2359304 | tf_op jit(solution)/shard_map/ppermute | solution.py:21
  196.6 17.5 %collective-permute-start.32 = (bf16[2,256,768]{2,1,0:T(8,128)(2,1)}, bf16[2,256,768]{2,1,0:T(8,128)(2,1)}, u32[]{:S(2)}, u32[]{:S(2)}) collective-permute-start(bf16[2,256,768]{2,1,0:T(8,128)(2,1)} %pad_maximum_fusion.2), channel_id=1, source_target_pairs={{0,16},{4,20},{8,24},{12,28},{16,0},{20,4},{24,8},{28,12},{1,17},{... | collective-permute-start | bytes 2359304 | tf_op jit(solution)/shard_map/ppermute | solution.py:21
  196.9 4.4 %collective-permute-start.25 = (bf16[512,128]{1,0:T(8,128)(2,1)}, bf16[512,128]{1,0:T(8,128)(2,1)S(1)}, u32[]{:S(2)}, u32[]{:S(2)}) collective-permute-start(bf16[512,128]{1,0:T(8,128)(2,1)} %get-tuple-element.99), channel_id=1, source_target_pairs={{0,1},{1,0},{2,3},{3,2},{4,5},{5,4},{6,7},{7,6},{8,9},{9,8},{10,11... | collective-permute-start | bytes 393224 | tf_op jit(solution)/shard_map/ppermute | solution.py:21
  196.9 10.7 %collective-permute-start.26 = (bf16[512,128]{1,0:T(8,128)(2,1)}, bf16[512,128]{1,0:T(8,128)(2,1)S(1)}, u32[]{:S(2)}, u32[]{:S(2)}) collective-permute-start(bf16[512,128]{1,0:T(8,128)(2,1)} %get-tuple-element.100), channel_id=1, source_target_pairs={{0,2},{1,3},{2,0},{3,1},{4,6},{5,7},{6,4},{7,5},{8,10},{9,11},{10,... | collective-permute-start | bytes 393224 | tf_op jit(solution)/shard_map/ppermute | solution.py:21
  199.7 11.0 %collective-permute-start.27 = (bf16[512,128]{1,0:T(8,128)(2,1)S(1)}, bf16[512,128]{1,0:T(8,128)(2,1)S(1)}, u32[]{:S(2)}, u32[]{:S(2)}) collective-permute-start(bf16[512,128]{1,0:T(8,128)(2,1)S(1)} %copy-done.30), channel_id=1, source_target_pairs={{0,3},{1,2},{2,1},{3,0},{4,7},{5,6},{6,5},{7,4},{8,11},{9,10},{10,... | collective-permute-start | bytes 393224 | tf_op jit(solution)/shard_map/ppermute | solution.py:21
  215.7 4.6 %collective-permute-start.33 = (bf16[2,64,768]{2,1,0:T(8,128)(2,1)S(1)}, bf16[2,64,768]{2,1,0:T(8,128)(2,1)S(1)}, u32[]{:S(2)}, u32[]{:S(2)}) collective-permute-start(bf16[2,64,768]{2,1,0:T(8,128)(2,1)S(1)} %get-tuple-element.122), channel_id=1, source_target_pairs={{0,1},{1,0},{2,3},{3,2},{4,5},{5,4},{6,7},{7,6},{8,9},{9,8},{10,11... | collective-permute-start | bytes 589832 | tf_op jit(solution)/shard_map/ppermute | solution.py:21
  215.8 8.8 %collective-permute-start.34 = (bf16[2,64,768]{2,1,0:T(8,128)(2,1)S(1)}, bf16[2,64,768]{2,1,0:T(8,128)(2,1)S(1)}, u32[]{:S(2)}, u32[]{:S(2)}) collective-permute-start(bf16[2,64,768]{2,1,0:T(8,128)(2,1)S(1)} %get-tuple-element.124), channel_id=1, source_target_pairs={{0,2},{1,3},{2,0},{3,1},{4,6},{5,7},{6,4},{7,5},{8,10},{9,11},{10,... | collective-permute-start | bytes 589832 | tf_op jit(solution)/shard_map/ppermute | solution.py:21
  218.1 15.8 %collective-permute-start.35 = (bf16[2,64,768]{2,1,0:T(8,128)(2,1)S(1)}, bf16[2,64,768]{2,1,0:T(8,128)(2,1)S(1)}, u32[]{:S(2)}, u32[]{:S(2)}) collective-permute-start(bf16[2,64,768]{2,1,0:T(8,128)(2,1)S(1)} %get-tuple-element.123), channel_id=1, source_target_pairs={{0,3},{1,2},{2,1},{3,0},{4,7},{5,6},{6,5},{7,4},{8,11},{9,10},{10,... | collective-permute-start | bytes 589832 | tf_op jit(solution)/shard_map/ppermute | solution.py:21
  234.0 4.6 %collective-permute-start.37 = (bf16[2,64,768]{2,1,0:T(8,128)(2,1)S(1)}, bf16[2,64,768]{2,1,0:T(8,128)(2,1)S(1)}, u32[]{:S(2)}, u32[]{:S(2)}) collective-permute-start(bf16[2,64,768]{2,1,0:T(8,128)(2,1)S(1)} %add_add_fusion.rest_0_), channel_id=1, source_target_pairs={{0,16},{4,20},{8,24},{12,28},{16,0},{20,4},{24,8},{28,12},{1,17},{... | collective-permute-start | bytes 589832 | tf_op jit(solution)/shard_map/ppermute | solution.py:21
  234.8 5.8 %collective-permute-start.36 = (bf16[2,64,768]{2,1,0:T(8,128)(2,1)S(1)}, bf16[2,64,768]{2,1,0:T(8,128)(2,1)S(1)}, u32[]{:S(2)}, u32[]{:S(2)}) collective-permute-start(bf16[2,64,768]{2,1,0:T(8,128)(2,1)S(1)} %add_add_fusion.rest_0_), channel_id=1, source_target_pairs={{0,8},{4,12},{8,0},{12,4},{16,24},{20,28},{24,16},{28,20},{1,9},{5... | collective-permute-start | bytes 589832 | tf_op jit(solution)/shard_map/ppermute | solution.py:21
  238.6 7.9 %collective-permute-start.38 = (bf16[1,64,768]{2,1,0:T(8,128)(2,1)S(1)}, bf16[1,64,768]{2,1,0:T(8,128)(2,1)S(1)}, u32[]{:S(2)}, u32[]{:S(2)}) collective-permute-start(bf16[1,64,768]{2,1,0:T(8,128)(2,1)S(1)} %slice.53), channel_id=1, source_target_pairs={{0,8},{4,12},{8,0},{12,4},{16,24},{20,28},{24,16},{28,20},{1,9},{5... | collective-permute-start | bytes 294920 | tf_op jit(solution)/shard_map/ppermute | solution.py:21
  240.7 6.8 %collective-permute-start.39 = (bf16[1,64,768]{2,1,0:T(8,128)(2,1)S(1)}, bf16[1,64,768]{2,1,0:T(8,128)(2,1)S(1)}, u32[]{:S(2)}, u32[]{:S(2)}) collective-permute-start(bf16[1,64,768]{2,1,0:T(8,128)(2,1)S(1)} %slice.54), channel_id=1, source_target_pairs={{0,16},{4,20},{8,24},{12,28},{16,0},{20,4},{24,8},{28,12},{1,17},{... | collective-permute-start | bytes 294920 | tf_op jit(solution)/shard_map/ppermute | solution.py:21
  241.7 7.7 %collective-permute-start.40 = (bf16[2,64,768]{2,1,0:T(8,128)(2,1)S(1)}, bf16[2,64,768]{2,1,0:T(8,128)(2,1)S(1)}, u32[]{:S(2)}, u32[]{:S(2)}) collective-permute-start(bf16[2,64,768]{2,1,0:T(8,128)(2,1)S(1)} %add_add_fusion.rest_0_), channel_id=1, source_target_pairs={{0,4},{4,0},{8,12},{12,8},{16,20},{20,16},{24,28},{28,24},{1,5},{5... | collective-permute-start | bytes 589832 | tf_op jit(solution)/shard_map/ppermute | solution.py:21
  246.0 4.3 %collective-permute-start.41 = (bf16[2,64,768]{2,1,0:T(8,128)(2,1)S(1)}, bf16[2,64,768]{2,1,0:T(8,128)(2,1)S(1)}, u32[]{:S(2)}, u32[]{:S(2)}) collective-permute-start(bf16[2,64,768]{2,1,0:T(8,128)(2,1)S(1)} %collective-permute-done.36.rest_1_), channel_id=1, source_target_pairs={{0,4},{4,0},{8,12},{12,8},{16,20},{20,16},{24,28},{28,24},{1,5},{5... | collective-permute-start | bytes 589832 | tf_op jit(solution)/shard_map/ppermute | solution.py:21
  246.1 4.2 %collective-permute-start.42 = (bf16[2,64,768]{2,1,0:T(8,128)(2,1)S(1)}, bf16[2,64,768]{2,1,0:T(8,128)(2,1)S(1)}, u32[]{:S(2)}, u32[]{:S(2)}) collective-permute-start(bf16[2,64,768]{2,1,0:T(8,128)(2,1)S(1)} %collective-permute-done.37.rest_2_), channel_id=1, source_target_pairs={{0,4},{4,0},{8,12},{12,8},{16,20},{20,16},{24,28},{28,24},{1,5},{5... | collective-permute-start | bytes 589832 | tf_op jit(solution)/shard_map/ppermute | solution.py:21
  246.5 2.9 %collective-permute-start.43 = (bf16[1,64,768]{2,1,0:T(8,128)(2,1)S(1)}, bf16[1,64,768]{2,1,0:T(8,128)(2,1)S(1)}, u32[]{:S(2)}, u32[]{:S(2)}) collective-permute-start(bf16[1,64,768]{2,1,0:T(8,128)(2,1)S(1)} %collective-permute-done.38.rest_3_), channel_id=1, source_target_pairs={{0,4},{4,0},{8,12},{12,8},{16,20},{20,16},{24,28},{28,24},{1,5},{5... | collective-permute-start | bytes 294920 | tf_op jit(solution)/shard_map/ppermute | solution.py:21
  247.5 2.9 %collective-permute-start.44 = (bf16[1,64,768]{2,1,0:T(8,128)(2,1)S(1)}, bf16[1,64,768]{2,1,0:T(8,128)(2,1)S(1)}, u32[]{:S(2)}, u32[]{:S(2)}) collective-permute-start(bf16[1,64,768]{2,1,0:T(8,128)(2,1)S(1)} %collective-permute-done.39.rest_4_), channel_id=1, source_target_pairs={{0,4},{4,0},{8,12},{12,8},{16,20},{20,16},{24,28},{28,24},{1,5},{5... | collective-permute-start | bytes 294920 | tf_op jit(solution)/shard_map/ppermute | solution.py:21
  (32 other events, 413.9 us)

commit v3 on v2

v3 whole, which is shorter than its diff:
```python
import jax
import jax.numpy as jnp
from jax import lax
from jax.experimental import pallas as pl
from jax.experimental.pallas import tpu as pltpu
from jax.sharding import PartitionSpec as P

EPSILON = 1e-06
F32 = jnp.float32
BF16 = jnp.bfloat16
HALO = 8
EARLY = 4
VMEM_BYTES = 60 * 1024 * 1024


def xor_pairs(axis, bit):
    return [(i, i ^ bit) for i in range(lax.axis_size(axis))]


def swap(values, axis, bit):
    return lax.ppermute(values, axis, xor_pairs(axis, bit))


def spread(piece):
    half = piece.shape[0] // 2
    by_x = swap(piece, "tm", 2)
    by_y = swap(piece, "tm", 4)
    far_a = swap(by_y[:half], "tm", 2)
    far_b = swap(by_x[half:], "tm", 4)
    near = [piece, by_x, by_y, far_a, far_b]
    return near + [swap(entry, "tm", 1) for entry in near]


def gather_weights(column, signals):
    by_x = swap(column, "tm", 2)
    by_y = swap(column, "tm", 4)
    by_x, by_y, signals = lax.optimization_barrier((by_x, by_y, signals))
    far_a = swap(by_y[:2], "tm", 2)
    far_b = swap(by_x[2:], "tm", 4)
    near = lax.optimization_barrier([column, by_x, by_y, far_a, far_b])
    return near + [swap(entry, "tm", 1) for entry in near], signals


WEIGHT_PLACES = [(0, 0, 4), (2, 0, 4), (4, 0, 4), (6, 0, 2), (6, 2, 2)]
WEIGHT_PLACES = WEIGHT_PLACES + [(a + 1, first, count) for a, first, count in WEIGHT_PLACES]


SPREAD_PLACES = [(0, 0, 2), (2, 0, 2), (4, 0, 2), (6, 0, 1), (6, 1, 1)]
SPREAD_PLACES = SPREAD_PLACES + [(a + 1, first, count) for a, first, count in SPREAD_PLACES]


def nt(left, right):
    return lax.dot_general(left, right, (((1,), (1,)), ((), ())), preferred_element_type=F32)


def nn(left, right):
    return lax.dot_general(left, right, (((1,), (0,)), ((), ())), preferred_element_type=F32)


def tn(left, right):
    return lax.dot_general(left, right, (((0,), (0,)), ((), ())), preferred_element_type=F32)


def sigmoid(values):
    return 0.5 * jnp.tanh(0.5 * values) + 0.5


def silu_half(half):
    turn = jnp.tanh(half)
    product = half * turn
    return half + product, turn, product


def slope_twice(half, turn, product):
    return (1.0 + turn) + (half - product * turn)


def to_rows(flat, values, target):
    count = values.shape[0] // 16
    for group in range(16):
        start = group * (count + 1)
        flat[start : start + count] = values[group * count : group * count + count]
    for tile in range(count):
        part = flat[pl.ds(tile, 16, stride=count + 1)]
        target[16 * tile : 16 * tile + 16] = part.astype(BF16)


def fill_masks(ids_ref, flat, mask_ref):
    rows = mask_ref.shape[1]
    own = rows - 2 * HALO
    for index, step in enumerate((-1, 1, -2, 2)):
        inside = (ids_ref[16 : 8 + rows] == ids_ref[16 + step : 8 + rows + step]).astype(F32)
        before = (ids_ref[8:16] == ids_ref[8 + step : 16 + step]).astype(F32)
        to_rows(flat, inside[0:own], mask_ref.at[index])
        halo = jnp.concatenate([inside[own : own + 8], before], axis=0)
        mask_ref[index, own:rows] = halo.astype(BF16)


def masked_move(store, target, values, mask_ref, step):
    rows = values.shape[0]
    own = rows - 2 * HALO
    index = {-1: 0, 1: 1, -2: 2, 2: 3}[step]
    place = lax.broadcasted_iota(jnp.int32, (16, values.shape[1]), 0)

    def tile(number):
        return values[16 * number : 16 * number + 16].astype(F32)

    def turned(part, count):
        return pltpu.roll(part, count % 16, 0)

    count = own // 16
    halo = tile(count)
    size = abs(step)
    if step > 0:
        last = {}
        outer = turned(halo, -step)
        for n in range(step):
            inner_part = turned(tile(n), -1)
            last[count - step + n] = jnp.where(place == 15, turned(halo, -1 - n), inner_part)
            outer = jnp.where(place == 16 - step + n, turned(tile(n), n - step), outer)
        kept = (0, own - 16 * size, 16 * size)
    else:
        last = {}
        outer = turned(halo, size)
        for n in range(size):
            source = tile(count - size + n)
            last[n] = jnp.where(place == 0, turned(halo, size - n), turned(source, 1))
            outer = jnp.where(place == n, turned(source, n + 1), outer)
        kept = (16 * size, own, -16 * size)
    last[count] = outer
    wide = values.shape[1] // 128

    def masked(part, first):
        mask = mask_ref[index, first : first + part.shape[0]]
        return part * jnp.concatenate([mask] * wide, axis=1)

    first, end, offset = kept
    store[target, first:end] = masked(values[first + offset : end + offset], first)
    for number, part in last.items():
        store[target, 16 * number : 16 * number + 16] = masked(part.astype(BF16), 16 * number)


def move_far(store, mask_ref):
    masked_move(store, 0, store[16], mask_ref, -2)
    masked_move(store, 25, store[9], mask_ref, 2)


def move_near(store, mask_ref, dilate):
    def before(phase, carry):
        masked_move(store, 1 + phase, store[9 + phase], mask_ref, -1)
        return carry

    def after(phase, carry):
        masked_move(store, 17 + phase, store[9 + phase], mask_ref, 1)
        return carry

    lax.fori_loop(8 - dilate, 8, before, 0)
    lax.fori_loop(0, dilate, after, 0)


def move_each(store, mask_ref, phase, values):
    masked_move(store, 1 + phase, values, mask_ref, -1)
    masked_move(store, 17 + phase, values, mask_ref, 1)


def pack_weights_kernel(
    places, sec_ref, three_ref, mix_ref, skip_ref, bs, bt, bm, bk, gt, gm, gk, out, wide, rows, mats
):
    turn = places[0]
    for q in range(4):
        part = sec_ref[:, :, 128 * q : 128 * q + 128].astype(F32)
        wide[q] = part.reshape(1024, 128)
    rows[...] = jnp.zeros_like(rows)
    rows[0:1, 0:64] = bs[...].astype(F32)
    for index, ref in enumerate((bt, bm, bk, gt, gm, gk)):
        rows[1 + 3 * index : 4 + 3 * index, 0:64] = ref[...].astype(F32)
    columns = jnp.transpose(rows[...])[0:64]
    for b in range(3):
        three = three_ref[b].astype(F32)
        gain = columns[:, 10 + b : 11 + b]
        total = jnp.sum(jnp.sum(three * three, axis=0), axis=1, keepdims=True)
        scale = 0.5 * gain / jnp.sqrt(total + EPSILON)
        for tap in range(3):
            mats[5 * b + tap] = (three[tap] * scale).astype(BF16)
        for index, ref in ((3, mix_ref), (4, skip_ref)):
            part = ref[b].astype(F32)
            gain = columns[:, 3 * index + 4 + b : 3 * index + 5 + b]
            total = jnp.sum(part * part, axis=1, keepdims=True)
            gain = 0.5 * gain if index == 3 else gain
            mats[5 * b + index] = (part * (gain / jnp.sqrt(total + EPSILON))).astype(BF16)
    mats[15, :, 0:128] = columns.astype(BF16)
    mats[15, :, 128:256] = jnp.zeros((64, 128), BF16)
    for tap in range(2):
        for q in range(4):
            part = wide[q, pl.ds(2 * turn + tap, 64, stride=16), :]
            out[tap, :, 128 * q : 128 * q + 128] = part.astype(BF16)
        out[tap, :, 512:768] = mats[2 * turn + tap]


def pack_frames_kernel(places, low, high, signal, cotangent, *rest):
    firsts, seconds = rest[0:4], rest[4:8]
    chan = places[1]
    own = signal.shape[0] // 4
    frames = 8 * own
    count = own // 64
    row = lax.broadcasted_iota(jnp.int32, (16, 128), 0)
    lane = lax.broadcasted_iota(jnp.int32, (64, 128), 1)

    def halo(dest, after, before, edges, is_after):
        last, first = jnp.where(dest == 3, 1, 0), jnp.where(dest == 0, 1, 0)
        after = jnp.where(last == 1, edges[1].astype(F32), after.astype(F32))
        before = jnp.where(first == 1, edges[0].astype(F32), before.astype(F32))
        return jnp.where(is_after, after, before).astype(BF16)

    for k in range(4):
        dest = chan ^ k
        part = signal[pl.ds(pl.multiple_of(dest * own, own), own)]
        firsts[k][0:count] = part.reshape(count, 64, 128)
        after = pl.multiple_of(jnp.minimum(dest + 1, 3) * own, 16)
        before = pl.multiple_of(jnp.maximum(dest * own - 16, 0), 16)
        edges = (low[0:16], high[0:16])
        firsts[k][count] = jnp.zeros((64, 128), BF16)
        firsts[k][count, 0:16] = halo(
            dest, signal[pl.ds(after, 16)], signal[pl.ds(before, 16)], edges, row < HALO
        )
        for q in range(frames // 128):
            lanes = pl.ds(pl.multiple_of(dest * frames + 128 * q, 128), 128)
            part = cotangent[:, lanes]
            if q < EARLY:
                firsts[k][count + 1 + q] = part
            else:
                seconds[k][q - EARLY] = part
        after = pl.multiple_of(jnp.minimum(dest + 1, 3) * frames, 128)
        before = pl.multiple_of(jnp.maximum(dest * frames - 128, 0), 128)
        edges = (low[16:80], high[16:80])
        seconds[k][frames // 128 - EARLY] = halo(
            dest,
            cotangent[:, pl.ds(after, 128)],
            cotangent[:, pl.ds(before, 128)],
            edges,
            lane < 8 * HALO,
        )


def finish_kernel(places, sec_ref, three_ref, mix_ref, skip_ref, gt, gm, gk, stat, *rest):
    pieces = rest[:10]
    sec_out, gain_out, bs, three_out, gt_out, bt, mix_out, gm_out, bm, skip_out, gk_out, bk = rest[10:22]
    wide, rows, mats = rest[22:]
    turn = places[0]
    for ref, (place, first, _) in zip(pieces, SPREAD_PLACES, strict=True):
        pair = 2 * (turn ^ place)
        taps = 1 if place >= 6 else 2
        for tap in range(taps):
            k = pair + tap + first
            part = ref[tap].astype(F32)
            for q in range(4):
                wide[q, pl.ds(k, 64, stride=16), :] = part[:, 128 * q : 128 * q + 128]
            mats[k] = part[:, 512:768]
    aux = mats[15]
    norm, scale = stat[0:1], stat[1:2]
    gains = jnp.concatenate([aux[q : q + 1, 128:256] for q in range(4)], axis=1) / norm
    gain_out[...] = gains
    ratio = gains / norm
    for q in range(4):
        lanes = slice(128 * q, 128 * q + 128)
        part = sec_ref[:, :, lanes].astype(F32).reshape(1024, 128)
        grad = scale[:, lanes] * (wide[q] - ratio[:, lanes] * part)
        sec_out[:, :, lanes] = grad.reshape(64, 16, 128)
    rows[...] = jnp.zeros_like(rows)
    for index, ref in enumerate((gt, gm, gk)):
        rows[3 * index : 3 * index + 3, 0:64] = ref[...].astype(F32)
    columns = jnp.transpose(rows[...])[0:64]
    results = []
    for b in range(3):
        three = three_ref[b].astype(F32)
        norm = jnp.sqrt(jnp.sum(jnp.sum(three * three, axis=0), axis=1, keepdims=True) + EPSILON)
        total = mats[5 * b] * three[0] + mats[5 * b + 1] * three[1] + mats[5 * b + 2] * three[2]
        gain = jnp.sum(total, axis=1, keepdims=True) / norm
        results.append(gain)
        for tap in range(3):
            grad = mats[5 * b + tap] - gain / norm * three[tap]
            three_out[b, tap] = columns[:, b : b + 1] / norm * grad
    for index, (ref, out) in enumerate(((mix_ref, mix_out), (skip_ref, skip_out))):
        for b in range(3):
            part = ref[b].astype(F32)
            grad = mats[5 * b + 3 + index]
            norm = jnp.sqrt(jnp.sum(part * part, axis=1, keepdims=True) + EPSILON)
            gain = jnp.sum(grad * part, axis=1, keepdims=True) / norm
            results.append(gain)
            place = 3 + 3 * index + b
            out[b] = columns[:, place : place + 1] / norm * (grad - gain / norm * part)
    lane = lax.broadcasted_iota(jnp.int32, (64, 128), 1)
    table = jnp.where(lane < 7, aux[:, 0:128], 0.0)
    for index, gain in enumerate(results):
        table = jnp.where(lane == 8 + index, gain, table)
    rows[:, 0:64] = jnp.transpose(table)
    bs[...] = rows[0:1, 0:64]
    bt[...] = rows[1:4, 0:64]
    bm[...] = rows[4:7, 0:64]
    bk[...] = rows[4:7, 0:64]
    gt_out[...] = rows[8:11, 0:64]
    gm_out[...] = rows[11:14, 0:64]
    gk_out[...] = rows[14:17, 0:64]


def weight_copies(places, refs, wsec, wblk, sem, block_sem):
    turn, chan = places[0], places[1]
    copies = []
    for ref, (place, first, _) in zip(refs, WEIGHT_PLACES, strict=True):
        slots = pl.ds(2 * (turn ^ place), 2)
        for k in range(ref.shape[0]):
            rows = pl.ds(pl.multiple_of(64 * (chan ^ (first + k)), 64), 64)
            copies.append(
                pltpu.make_async_copy(
                    ref.at[k, :, :, 0:512], wsec.at[slots, rows, :], sem
                )
            )
            copies.append(
                pltpu.make_async_copy(
                    ref.at[k, :, :, 512:768], wblk.at[slots, rows, :], block_sem
                )
            )
    return copies


def forward_kernel(
    places,
    sig0,
    sig1,
    sig2,
    sig3,
    ids_ref,
    gain_ref,
    *rest,
):
    pieces, rest = rest[:10], rest[10:]
    hid_out, act_out, mix_out, dsi_out = rest[0:4]
    sact_out, mask_out, stat_out = rest[4:7]
    outs = rest[7:11]
    wsec, wblk, cat, bias, wide, turned, flat = rest[11:18]
    hids, mixs, dsis, acts = rest[18:21], rest[21:24], rest[24:27], rest[27:30]
    wsem, ssem = rest[30:]
    chan = places[1]
    rows = sact_out.shape[0]
    own = rows - 2 * HALO
    pitch = own // 2 + 1
    loads = weight_copies(places, pieces, wsec, wblk, wsem, wsem)
    for copy in loads:
        copy.start()
    fill_masks(ids_ref, flat, mask_out)
    for k, ref in enumerate((sig0, sig1, sig2, sig3)):
        lanes = pl.ds(pl.multiple_of(128 * (chan ^ k), 128), 128)
        values = silu_half(0.5 * ref[0 : own // 64].reshape(own, 128).astype(F32))[0]
        to_rows(flat, values, sact_out.at[:, lanes])
        halo = silu_half(0.5 * ref[own // 64, 0:16].astype(F32))[0]
        sact_out[own:rows, lanes] = halo.astype(BF16)
    for copy in loads:
        copy.wait()

    def square(k, total):
        part = wsec[k].astype(F32)
        return total + jnp.sum((part * part).reshape(32, 8, 512), axis=0)

    total = lax.fori_loop(0, 16, square, jnp.zeros((8, 512), F32))
    norm = jnp.sqrt(jnp.sum(total, axis=0, keepdims=True) + EPSILON)
    scale = gain_ref[...] / norm
    stat_out[...] = jnp.concatenate([norm, scale, jnp.zeros((6, 512), F32)], axis=0)
    bias[...] = 0.5 * jnp.transpose(wblk[15].astype(F32))[:16]
    cat[0] = (sact_out[...].astype(F32) * (0.5 * scale)).astype(BF16)
    masked_move(cat, 1, cat[0], mask_out, -1)
    masked_move(cat, 2, cat[0], mask_out, 1)
    saves = []

    def keep(source, out, b):
        copy = pltpu.make_async_copy(source, out.at[b], ssem)
        copy.start()
        saves.append(copy)

    def enter(b, r, half):
        hids[b][r] = half.astype(BF16)
        value = silu_half(half)[0].astype(BF16)
        acts[b][9 + r] = value
        if b == 2:
            move_each(acts[b], mask_out, r, value)

    def phase_rows(values, n):
        return values[n * rows : n * rows + rows]

    def section(q, carry):
        left = jnp.concatenate([cat[0], cat[1 + q // 4]], axis=1)
        right = jnp.concatenate([wsec[q + 4], wsec[lax.rem(q + 12, 16)]], axis=1)
        enter(0, q, nt(left, right) + bias[0:1])
        return carry

    lax.fori_loop(0, 8, section, 0)
    for b in range(3):
        dilate = 3**b
        act, mix, dsi, hid = acts[b], mixs[b], dsis[b], hids[b]
        if b < 2:
            move_near(act, mask_out, dilate)
        else:
            move_far(act, mask_out)
        keep(hid, hid_out, b)
        keep(act.at[9:17], act_out, b)

        def taps(q):
            left = []
            for r in (2 * q, 2 * q + 1):
                parts = [act[9 + r - dilate], act[9 + r], act[9 + r + dilate]]
                left.append(jnp.concatenate(parts, axis=1))
            right = jnp.concatenate([wblk[5 * b], wblk[5 * b + 1], wblk[5 * b + 2]], axis=1)
            inner = nt(jnp.concatenate(left, axis=0), right)
            for n in range(2):
                half = phase_rows(inner, n) + bias[1 + b : 2 + b]
                value, turn, product = silu_half(half)
                mix[2 * q + n] = value.astype(BF16)
                dsi[2 * q + n] = slope_twice(
                    half.astype(BF16), turn.astype(BF16), product.astype(BF16)
                )

        def blend(q):
            left = []
            for r in (2 * q, 2 * q + 1):
                left.append(jnp.concatenate([mix[r], hid[r]], axis=1))
            right = jnp.concatenate([wblk[5 * b + 3], wblk[5 * b + 4]], axis=1)
            total = nt(jnp.concatenate(left, axis=0), right)
            for n in range(2):
                r = 2 * q + n
                after = phase_rows(total, n) + (bias[4 + b : 5 + b] + bias[7 + b : 8 + b])
                if b < 2:
                    enter(b + 1, r, after)
                else:
                    for tile in range(own // 16):
                        part = 2.0 * after[16 * tile : 16 * tile + 16]
                        frames = pl.ds(8 * tile + r, 16, stride=pitch)
                        wide[0, frames, :] = part[:, 0:128]
                        wide[1, frames, :] = part[:, 128:256]

        def both(q, carry):
            blend(q - 1)
            taps(q)
            return carry

        taps(0)
        lax.fori_loop(1, 4, both, 0)
        blend(3)
        keep(mix, mix_out, b)
        keep(dsi, dsi_out, b)

    def turn(q, carry):
        start = pitch * (q // 2) + 128 * lax.rem(q, 2)
        frames = pl.ds(pl.multiple_of(128 * q, 128), 128)
        for half in range(2):
            part = jnp.transpose(wide[half, pl.ds(start, 128), :])
            turned[128 * half : 128 * half + 128, frames] = part.astype(BF16)
        return carry

    lax.fori_loop(0, 8 * own // 128, turn, 0, unroll=4)
    final = []
    for k, out in enumerate(outs):
        part = turned.at[pl.ds(pl.multiple_of(64 * (chan ^ k), 64), 64), :]
        final.append(pltpu.make_async_copy(part, out, wsem))
    for copy in final:
        copy.start()
    for copy in saves + final:
        copy.wait()


def backward_kernel(
    places,
    first0,
    first1,
    first2,
    first3,
    second0,
    second1,
    second2,
    second3,
    sact_ref,
    mask_ref,
    stat_ref,
    hid_in,
    act_in,
    mix_in,
    dsi_in,
    *rest,
):
    pieces, rest = rest[:10], rest[10:]
    even_out, odd_out = rest[0:2]
    sgrads = rest[2:6]
    (wsec, wblk, turned, sigs, wide, grad, inner_a, inner_b, mix, hid, act, dsi) = rest[6:18]
    (acc_one, acc_three, through, sums, staged, wsem, vsem, csem, bsem, osem) = rest[18:]
    pitch = 4 * (sact_ref.shape[0] - 2 * HALO) // 8 + 1
    turn_index, chan = places[0], places[1]
    rows = mask_ref.shape[1]
    own = rows - 2 * HALO

    loads = weight_copies(places, pieces, wsec, wblk, wsem, vsem)
    cots = []
    count = own // 64
    section_loads = []
    pairs = ((first0, second0), (first1, second1), (first2, second2), (first3, second3))
    for k, (one, two) in enumerate(pairs):
        part = pl.ds(pl.multiple_of(64 * (chan ^ k), 64), 64)
        early = one.at[count + 1 : count + 1 + EARLY]
        cots.append(pltpu.make_async_copy(early, turned.at[0:EARLY, part, :], csem))
        late = turned.at[EARLY : 8 * own // 128 + 1, part, :]
        cots.append(pltpu.make_async_copy(two, late, csem))
        section_loads.append(pltpu.make_async_copy(one.at[0:count], sigs.at[k], wsem))

    def kept(b):
        slot = b % 2
        return [
            pltpu.make_async_copy(dsi_in.at[b], dsi.at[slot], bsem.at[slot, 0]),
            pltpu.make_async_copy(mix_in.at[b, :, 0:own], mix.at[slot], bsem.at[slot, 1]),
            pltpu.make_async_copy(hid_in.at[b], hid.at[slot], bsem.at[slot, 2]),
            pltpu.make_async_copy(act_in.at[b, :, 0:own], act.at[slot], bsem.at[slot, 3]),
        ]

    block_loads, section_loads = loads[1::2], loads[0::2] + section_loads
    for copy in cots + block_loads + kept(2) + kept(1) + section_loads:
        copy.start()
    sums[...] = jnp.zeros_like(sums)
    for copy in cots:
        copy.wait()
    def turn(q, carry):
        start = pitch * (q // 2) + 128 * lax.rem(q, 2)
        for half in range(2):
            part = turned[q, 128 * half : 128 * half + 128].astype(F32)
            wide[half, pl.ds(start, 128), :] = jnp.transpose(part)
        return carry

    lax.fori_loop(0, 8 * own // 128, turn, 0, unroll=4)
    turn(8 * own // 128, 0)

    def phases(r, carry):
        for half in range(2):
            lanes = slice(128 * half, 128 * half + 128)
            for tile in range(own // 16):
                part = wide[half, pl.ds(8 * tile + r, 16, stride=pitch), :]
                grad[r, 16 * tile : 16 * tile + 16, lanes] = part.astype(BF16)
            part = wide[half, pl.ds(16 * pitch + r, 16, stride=8), :]
            grad[r, own:rows, lanes] = part.astype(BF16)
        return carry

    lax.fori_loop(0, 8, phases, 0)
    for copy in block_loads:
        copy.wait()

    def own_sum(values):
        return jnp.sum(values[:own].astype(F32).reshape(own // 8, 8, 256), axis=0)

    def two(store, q, count):
        return jnp.concatenate([store[2 * q, 0:count], store[2 * q + 1, 0:count]], axis=0)

    def enter(b, inner, q):
        slot = b % 2
        g = two(grad, q, rows)
        down = nn(g, wblk[5 * b + 3])
        kept_rows = jnp.concatenate([mix[slot, 2 * q], mix[slot, 2 * q + 1]], axis=0)
        hidden = jnp.concatenate([hid[slot, 2 * q, 0:own], hid[slot, 2 * q + 1, 0:own]], axis=0)
        both = jnp.concatenate([kept_rows, hidden], axis=1)
        acc_one[...] += tn(two(grad, q, own), both)
        for n in range(2):
            r = 2 * q + n
            part = down[n * rows : n * rows + rows] * dsi[slot, r].astype(F32)
            part = part.astype(BF16)
            inner[9 + r] = part
            if b == 2:
                move_each(inner, mask_ref, r, part)

    def through_taps(b, inner, q):
        dilate, slot = 3**b, b % 2
        waves = []
        for r in (2 * q, 2 * q + 1):
            parts = [inner[9 + r + dilate], inner[9 + r], inner[9 + r - dilate]]
            waves.append(jnp.concatenate(parts, axis=1))
            sums[1 + b] += own_sum(parts[1])
            sums[4 + b] += own_sum(grad[r])
        deep = nn(jnp.concatenate(waves, axis=0), wblk[5 * b : 5 * b + 3].reshape(768, 256))
        skip = nn(two(grad, q, rows), wblk[5 * b + 4])
        acts = jnp.concatenate([act[slot, 2 * q], act[slot, 2 * q + 1]], axis=0)
        acc_three[...] += tn(jnp.concatenate([wave[:own] for wave in waves], axis=0), acts)
        for n in range(2):
            part = slice(n * rows, n * rows + rows)
            half = hid[slot, 2 * q + n].astype(F32)
            back = skip[part] + slope_twice(half, *silu_half(half)[1:]) * deep[part]
            grad[2 * q + n] = back.astype(BF16)

    def stage_taps(b):
        for tap in range(3):
            part = acc_three[256 * tap : 256 * tap + 256, :]
            staged[5 * b + tap, :, 512:768] = part.astype(BF16)
        acc_three[...] = jnp.zeros_like(acc_three)

    def stage_points(b):
        staged[5 * b + 3, :, 512:768] = acc_one[:, 0:256].astype(BF16)
        staged[5 * b + 4, :, 512:768] = (2.0 * acc_one[:, 256:512]).astype(BF16)
        acc_one[...] = jnp.zeros_like(acc_one)

    def arrive(b, numbers):
        for number in numbers:
            kept(b)[number].wait()

    def taps(r):
        g = grad[r]
        sums[0] += own_sum(g)
        last[r + 4] = g

        @pl.when(r < 4)
        def _():
            masked_move(last, r + 12, grad[r], mask_ref, 1)

        @pl.when(r >= 4)
        def _():
            masked_move(last, r - 4, grad[r], mask_ref, -1)

    acc_one[...] = jnp.zeros_like(acc_one)
    acc_three[...] = jnp.zeros_like(acc_three)
    arrive(2, (0, 1, 2))

    def enter_last(q, carry):
        enter(2, inner_a, q)
        return carry

    lax.fori_loop(0, 4, enter_last, 0)
    stage_points(2)
    move_far(inner_a, mask_ref)
    arrive(2, (3,))
    arrive(1, (0, 1, 2))
    for b, inner, following in ((2, inner_a, inner_b), (1, inner_b, inner_a)):

        def pipelined(q, carry):
            through_taps(b, inner, q)
            enter(b - 1, following, q - 1)
            return carry

        through_taps(b, inner, 0)
        lax.fori_loop(1, 4, pipelined, 0)
        enter(b - 1, following, 3)
        stage_taps(b)
        stage_points(b - 1)
        move_near(following, mask_ref, 3 ** (b - 1))
        if b == 2:
            for copy in kept(0):
                copy.start()
            arrive(1, (3,))
            arrive(0, (0, 1, 2))
        else:
            arrive(0, (3,))
    last = inner_b

    def final(q, carry):
        through_taps(0, inner_a, q)
        return carry

    lax.fori_loop(0, 4, final, 0)
    stage_taps(0)

    def section_taps(r, carry):
        taps(r)
        return carry

    lax.fori_loop(0, 8, section_taps, 0)
    for copy in section_loads:
        copy.wait()
    through[...] = jnp.zeros_like(through)
    sact = sact_ref[0:own]

    def collect(q, carry):
        left = jnp.concatenate([last[2 * q, 0:own], last[2 * q + 1, 0:own]], axis=1)
        through[...] += nn(left, wsec[pl.ds(2 * q, 2)].reshape(512, 512))
        grads = tn(left, sact).astype(BF16)
        staged[2 * q, :, 0:512] = grads[0:256]
        staged[2 * q + 1, :, 0:512] = grads[256:512]
        return carry

    lax.fori_loop(0, 8, collect, 0)
    deep = through[...]
    gains = jnp.sum(sact.astype(F32) * deep, axis=0, keepdims=True)
    through[...] = deep * (0.5 * stat_ref[1:2])
    biases = jnp.concatenate(
        [jnp.sum(sums[index], axis=0, keepdims=True) for index in range(8)]
        + [jnp.zeros((120, 256), F32)],
        axis=0,
    )
    staged[15, :, 512:640] = jnp.transpose(biases).astype(BF16)
    gain_rows = jnp.concatenate(
        [gains[:, 128 * q : 128 * q + 128] for q in range(4)] + [jnp.zeros((60, 128), F32)], axis=0
    ).astype(BF16)
    for part in range(4):
        staged[15, 64 * part : 64 * part + 64, 640:768] = gain_rows

    def finish(pair, carry):
        place = pair ^ turn_index
        source = staged.at[pl.ds(2 * pair, 2)]

        @pl.when(lax.rem(place, 2) == 0)
        def _():
            pltpu.make_async_copy(source, even_out.at[place // 2], osem).start()

        @pl.when(lax.rem(place, 2) == 1)
        def _():
            pltpu.make_async_copy(source, odd_out.at[place // 2], osem).start()

        return carry

    lax.fori_loop(0, 8, finish, 0)
    for k, out in enumerate(sgrads):
        lanes = pl.ds(pl.multiple_of(128 * (chan ^ k), 128), 128)
        half = 0.5 * sigs[k].reshape(own, 128).astype(F32)
        slope = slope_twice(half, *silu_half(half)[1:])
        count = own // 16
        for tile in range(count):
            part = through[16 * tile : 16 * tile + 16, lanes]
            wide[0, pl.ds(tile, 16, stride=count + 1), :] = part
        groups = [wide[0, (count + 1) * n : (count + 1) * n + count, :] for n in range(16)]
        out[...] = (jnp.concatenate(groups, axis=0) * slope).astype(BF16)
    for pair in range(8):
        pltpu.make_async_copy(staged.at[pl.ds(2 * pair, 2)], even_out.at[0], osem).wait()


def shape_of(shape, kind=BF16):
    return jax.ShapeDtypeStruct(shape, kind)


SPEC_VMEM = pl.BlockSpec(memory_space=pltpu.VMEM)
SPEC_ANY = pl.BlockSpec(memory_space=pl.ANY)
SPEC_SMEM = pl.BlockSpec(memory_space=pltpu.SMEM)


def params():
    return pltpu.CompilerParams(vmem_limit_bytes=VMEM_BYTES)


def cost(flops, moved_bytes):
    return pl.CostEstimate(flops=int(flops), bytes_accessed=int(moved_bytes), transcendentals=0)


def run_pack_weights(places, *arrays):
    return pl.pallas_call(
        pack_weights_kernel,
        out_shape=shape_of((2, 64, 768)),
        in_specs=[SPEC_SMEM] + [SPEC_VMEM] * 11,
        out_specs=SPEC_VMEM,
        scratch_shapes=[
            pltpu.VMEM((4, 1024, 128), F32),
            pltpu.VMEM((128, 128), F32),
            pltpu.VMEM((16, 64, 256), BF16),
        ],
        compiler_params=params(),
        cost_estimate=cost(2e7, 3e6),
        name="pack_weights",
    )(places, *arrays)


def run_pack_frames(places, low, high, signal, cotangent):
    own = signal.shape[0] // 4
    return pl.pallas_call(
        pack_frames_kernel,
        out_shape=[shape_of((own // 64 + 1 + EARLY, 64, 128))] * 4
        + [shape_of((8 * own // 128 + 1 - EARLY, 64, 128))] * 4,
        in_specs=[SPEC_SMEM] + [SPEC_VMEM] * 4,
        out_specs=[SPEC_VMEM] * 8,
        compiler_params=params(),
        cost_estimate=cost(1e6, 6e6),
        name="pack_frames",
    )(places, low, high, signal, cotangent)


def run_finish(places, v_section, three, v_mix, v_skip, g_dilated, g_mix, g_skip, stat, pieces):
    small = shape_of((3, 64), F32)
    out_shape = [
        shape_of((64, 16, 512), F32),
        shape_of((1, 512), F32),
        shape_of((1, 64), F32),
        shape_of((3, 3, 64, 256), F32),
        small,
        small,
        shape_of((3, 64, 256), F32),
        small,
        small,
        shape_of((3, 64, 256), F32),
        small,
        small,
    ]
    return pl.pallas_call(
        finish_kernel,
        out_shape=out_shape,
        in_specs=[SPEC_SMEM] + [SPEC_VMEM] * 18,
        out_specs=[SPEC_VMEM] * 12,
        scratch_shapes=[
            pltpu.VMEM((4, 1024, 128), F32),
            pltpu.VMEM((128, 128), F32),
            pltpu.VMEM((16, 64, 256), F32),
        ],
        compiler_params=params(),
        cost_estimate=cost(2e7, 8e6),
        name="finish_weights",
    )(places, v_section, three, v_mix, v_skip, g_dilated, g_mix, g_skip, stat, *pieces)


def run_forward(places, firsts, ids, gain, pieces):
    own = ids.shape[0] - 32
    rows = own + 2 * HALO
    kept = shape_of((3, 8, rows, 256))
    out_shape = [kept] * 4 + [
        shape_of((rows, 512)),
        shape_of((4, rows, 128)),
        shape_of((8, 512), F32),
    ]
    out_shape = out_shape + [shape_of((64, 8 * own))] * 4
    return pl.pallas_call(
        forward_kernel,
        out_shape=out_shape,
        in_specs=[SPEC_SMEM] + [SPEC_VMEM] * 6 + [SPEC_ANY] * 10,
        out_specs=[SPEC_ANY] * 4 + [SPEC_VMEM] * 3 + [SPEC_ANY] * 4,
        scratch_shapes=[
            pltpu.VMEM((16, 256, 512), BF16),
            pltpu.VMEM((16, 256, 256), BF16),
            pltpu.VMEM((3, rows, 512), BF16),
            pltpu.VMEM((16, 256), F32),
            pltpu.VMEM((2, 16 * (own // 2 + 1), 128), F32),
            pltpu.VMEM((256, 8 * own), BF16),
            pltpu.VMEM((own + 16, 128), F32),
        ]
        + [pltpu.VMEM((8, rows, 256), BF16)] * 9
        + [pltpu.VMEM((26, rows, 256), BF16)] * 3
        + [pltpu.SemaphoreType.DMA, pltpu.SemaphoreType.DMA],
        compiler_params=params(),
        cost_estimate=cost(2 * 1245184 * 8 * rows, 50e6),
        name="forward_blocks",
    )(places, *firsts, ids, gain, *pieces)


def run_backward(places, firsts, seconds, sact, masks, stat, kept, pieces):
    rows = sact.shape[0]
    own = rows - 2 * HALO
    return pl.pallas_call(
        backward_kernel,
        out_shape=[shape_of((4, 2, 256, 768))] * 2 + [shape_of((own, 128))] * 4,
        in_specs=[SPEC_SMEM]
        + [SPEC_ANY] * 8
        + [SPEC_VMEM] * 3
        + [SPEC_ANY] * 14,
        out_specs=[SPEC_ANY] * 2 + [SPEC_VMEM] * 4,
        scratch_shapes=[
            pltpu.VMEM((16, 256, 512), BF16),
            pltpu.VMEM((16, 256, 256), BF16),
            pltpu.VMEM((8 * own // 128 + 1, 256, 128), BF16),
            pltpu.VMEM((4, own // 64, 64, 128), BF16),
            pltpu.VMEM((2, 16 * (own // 2 + 1) + 128, 128), F32),
            pltpu.VMEM((8, rows, 256), BF16),
            pltpu.VMEM((26, rows, 256), BF16),
            pltpu.VMEM((26, rows, 256), BF16),
            pltpu.VMEM((2, 8, own, 256), BF16),
            pltpu.VMEM((2, 8, rows, 256), BF16),
            pltpu.VMEM((2, 8, own, 256), BF16),
            pltpu.VMEM((2, 8, rows, 256), BF16),
            pltpu.VMEM((256, 512), F32),
            pltpu.VMEM((768, 256), F32),
            pltpu.VMEM((own, 512), F32),
            pltpu.VMEM((8, 8, 256), F32),
            pltpu.VMEM((16, 256, 768), BF16),
            pltpu.SemaphoreType.DMA,
            pltpu.SemaphoreType.DMA,
            pltpu.SemaphoreType.DMA,
            pltpu.SemaphoreType.DMA((2, 4)),
            pltpu.SemaphoreType.DMA,
        ],
        compiler_params=params(),
        cost_estimate=cost(2 * 2490368 * 8 * rows, 60e6),
        name="backward_blocks",
    )(places, *firsts, *seconds, sact, masks, stat, *kept, *pieces)


def exchange(values, axis, cut):
    me = lax.axis_index(axis)
    parts = [cut(me)]
    for k in (1, 2, 3):
        parts.append(swap(cut(me ^ k), axis, k))
    return parts


def body(
    signal,
    segment_ids,
    v_section,
    g_section,
    b_section,
    v_dilated,
    g_dilated,
    b_dilated,
    v_mix,
    g_mix,
    b_mix,
    v_skip,
    g_skip,
    b_skip,
    cotangent,
):
    tm_index, chan = lax.axis_index("tm"), lax.axis_index("chan")
    tm_size = lax.axis_size("tm")
    turn = tm_index % 8
    places = jnp.stack([turn, chan]).astype(jnp.int32)
    own = signal.shape[0] // 4
    rows = own + 2 * HALO
    start = tm_index * signal.shape[0] + chan * own

    three_v = jnp.transpose(v_dilated, (0, 2, 1, 3))
    piece = run_pack_weights(
        places,
        v_section,
        three_v,
        v_mix,
        v_skip,
        b_section[None],
        b_dilated,
        b_mix,
        b_skip,
        g_dilated,
        g_mix,
        g_skip,
    )
    by_chan = [piece] + [swap(piece, "chan", k) for k in (1, 2, 3)]

    first = jnp.concatenate([signal[:16], cotangent[:, :128]], axis=0)
    final = jnp.concatenate([signal[-16:], cotangent[:, -128:]], axis=0)
    onward = [(i, i + 1) for i in range(tm_size - 1)]
    low = lax.ppermute(final, "tm", onward)
    high = lax.ppermute(first, "tm", [(target, source) for source, target in onward])
    packed = run_pack_frames(places, low, high, signal, cotangent)
    firsts, seconds = list(packed[0:4]), list(packed[4:8])
    by_chan, _ = lax.optimization_barrier((by_chan, packed[0]))
    for k in (1, 2, 3):
        firsts[k] = swap(firsts[k], "chan", k)
        seconds[k] = swap(seconds[k], "chan", k)
    pieces, firsts = gather_weights(jnp.stack(by_chan), firsts)
    firsts, seconds[1:3] = lax.optimization_barrier((firsts, seconds[1:3]))
    padded = jnp.pad(segment_ids, 16, constant_values=-1)
    nearby = lax.dynamic_slice_in_dim(padded, start, own + 32)
    ids = jnp.broadcast_to(nearby[:, None], (own + 32, 128))

    frames = 8 * own
    results = run_forward(places, firsts, ids, g_section[None].astype(F32), pieces)
    kept, sact, masks, stat, outs = results[:4], results[4], results[5], results[6], results[7:]

    outs, seconds = lax.optimization_barrier((list(outs), seconds))
    received = [outs[0]] + [swap(outs[k], "chan", k) for k in (1, 2, 3)]
    results = run_backward(places, firsts, seconds, sact, masks, stat, kept, pieces)
    even, odd, sgrads = results[0], results[1], results[2:]
    odd, received = lax.optimization_barrier((odd, received))
    output = jnp.zeros((64, 4 * frames), BF16)
    for k in range(4):
        output = lax.dynamic_update_slice_in_dim(output, received[k], (chan ^ k) * frames, axis=1)

    quarter = even + swap(odd, "tm", 1)
    far_a = swap(quarter[3, :1], "tm", 2)
    far_b = swap(quarter[3, 1:], "tm", 4)
    for_y = jnp.concatenate([quarter[2, :1] + far_a, quarter[2, 1:]], axis=0)
    for_x = jnp.concatenate([quarter[1, :1], quarter[1, 1:] + far_b], axis=0)
    summed = quarter[0] + swap(for_x, "tm", 2) + swap(for_y, "tm", 4)

    def cut_rows(place):
        return lax.dynamic_slice_in_dim(summed, place * 64, 64, axis=1)

    parts = exchange(summed, "chan", cut_rows)
    mine = parts[0] + parts[1] + parts[2] + parts[3]
    bit = 8
    while bit < tm_size:
        mine = mine + swap(mine, "tm", bit)
        bit = 2 * bit
    gathered = spread(mine)

    received = [sgrads[0]] + [swap(sgrads[k], "chan", k) for k in (1, 2, 3)]
    signal_grad = jnp.zeros((4 * own, 128), BF16)
    for k in range(4):
        signal_grad = lax.dynamic_update_slice_in_dim(
            signal_grad, received[k], (chan ^ k) * own, axis=0
        )
    (sec, gain, bs, three, gt, bt, mix, gm, bm, skip, gk, bk) = run_finish(
        places, v_section, three_v, v_mix, v_skip, g_dilated, g_mix, g_skip, stat, gathered
    )
    return (
        output,
        signal_grad,
        sec,
        gain.reshape(512),
        bs.reshape(64),
        jnp.transpose(three, (0, 2, 1, 3)),
        gt,
        bt,
        mix,
        gm,
        bm,
        skip,
        gk,
        bk,
    )


def solution(mesh):
    return jax.shard_map(
        body,
        mesh=mesh,
        in_specs=(
            P("tm", "chan"),
            P(),
            P("chan", None, None),
            P(),
            P("chan"),
            P(None, "chan", None, None),
            P(None, "chan"),
            P(None, "chan"),
            P(None, "chan", None),
            P(None, "chan"),
            P(None, "chan"),
            P(None, "chan", None),
            P(None, "chan"),
            P(None, "chan"),
            P("chan", "tm"),
        ),
        out_specs=(
            P("chan", "tm"),
            P("tm", "chan"),
            P("chan", None, None),
            P(),
            P("chan"),
            P(None, "chan", None, None),
            P(None, "chan"),
            P(None, "chan"),
            P(None, "chan", None),
            P(None, "chan"),
            P(None, "chan"),
            P(None, "chan", None),
            P(None, "chan"),
            P(None, "chan"),
        ),
        check_vma=False,
    )
```

time: 259 us -> 239 us (0.923)
  Pallas kernels: 108 us -> 80.6 us
  waiting for transfers between devices: 72.1 us -> 88 us
  starting transfers between devices: 65.5 us -> 55.2 us
  local copies, waits for them, and re-layouts: 3.06 us -> 5.82 us
    pallas_call x1, Pallas kernels: 56.1 us -> 40.1 us  [run_backward(): pl.pallas_call(backward_kernel, out_shape=[shape_of((4, 2, 256, 768))] *...]
    ppermute x41, waiting for transfers between devices: 72.1 us -> 84.8 us  [swap(): return lax.ppermute(values, axis, xor_pairs(axis, bit))]
    pallas_call x1, Pallas kernels: 39.3 us -> 27 us  [run_forward(): pl.pallas_call(forward_kernel, out_shape=out_shape, in_specs=[SPEC_SMEM]...]
    ppermute x41, starting transfers between devices: 58.7 us -> 48.8 us  [swap(): return lax.ppermute(values, axis, xor_pairs(axis, bit))]
    ppermute x4 -> x2, waiting for transfers between devices: 0.01 us -> 3.15 us  [the longest x1 3.15 us: body(): lax.ppermute(first, 'tm', [(target, source) for source, target in onward])]
    ppermute x4 -> x2, starting transfers between devices: 6.76 us -> 6.43 us  [the longest x1 4.51 us: body(): low = lax.ppermute(final, 'tm', onward)]
  transfers between devices with their start and end apart: 45 -> 43, of which waited for: 20 -> 24; matrix products, arithmetic and copies ran while one was open for 1% -> 2% of each run, Pallas kernels for 38% -> 30%
where the time goes in v3:
time: 239 us
  waiting for transfers between devices  88 us (37%)
  Pallas kernels  80.6 us (34%)
  starting transfers between devices  55.2 us (23%)
  other arithmetic  7.7 us (3%)
  local copies, waits for them, and re-layouts  5.82 us (2%)
    ppermute x41, waiting for transfers between devices, swap(): return lax.ppermute(values, axis, xor_pairs(axis, bit))  84.8 us
    ppermute x41, starting transfers between devices, swap(): return lax.ppermute(values, axis, xor_pairs(axis, bit))  48.8 us
    pallas_call x1, Pallas kernels, run_backward(): pl.pallas_call(backward_kernel, out_shape=[shape_of((4, 2, 256, 768))] *...  40.1 us
    pallas_call x1, Pallas kernels, run_forward(): pl.pallas_call(forward_kernel, out_shape=out_shape, in_specs=[SPEC_SMEM]...  27 us
    pallas_call x1, Pallas kernels, run_finish(): pl.pallas_call(finish_kernel, out_shape=out_shape, in_specs=[SPEC_SMEM] +...  6.21 us
  transfers between devices with their start and end apart: 43, of which 24 were waited for; matrix products, arithmetic and copies ran while one was open for 2% of the time, Pallas kernels for 30%

profile of v3, /device:TPU:9, one launch (start us, length us, event | category | flops | bytes accessed | tf_op | source)
XLA Modules:
  0.0 238.7 jit_solution(1625044700136048573)
XLA Ops:
  1.3 3.3 %pack_weights.1 = bf16[2,64,768]{2,1,0:T(8,128)(2,1)} custom-call(s32[2]{0:T(128)} %pad_add_fusion.places, bf16[64,16,512]{2,1,0:T(8,128)(2,1)} %sec_ref.3, bf16[3,3,64,256]{3,2,1,0:T(8,128)(2,1)} %bitcast.34, bf16[3,64,256]{2,1,0:T(8,128)(2,1)} %mix_ref.3, bf16[3,64,256]{2,1,0:T(8,128)(2,1)} %skip_ref.3, bf16[1,64]{1,0:T(2,128)(2,1)} %bitcast.41, ...), custom_call_target="tpu_custom_call" | custom-call | flops 20000000 | bytes 3000000 | tf_op jit(solution)/shard_map/pack_weights/pallas_call | solution.py:741
  4.6 2.5 %collective-permute-start.1 = (bf16[2,64,768]{2,1,0:T(8,128)(2,1)}, bf16[2,64,768]{2,1,0:T(8,128)(2,1)S(1)}, u32[]{:S(2)}, u32[]{:S(2)}) collective-permute-start(bf16[2,64,768]{2,1,0:T(8,128)(2,1)} %pack_weights.1), channel_id=1, source_target_pairs={{0,2},{1,3},{2,0},{3,1},{4,6},{5,7},{6,4},{7,5},{8,10},{9,11},{10,... | collective-permute-start | bytes 589832 | tf_op jit(solution)/shard_map/ppermute | solution.py:21
  8.7 4.5 %collective-permute-start.3 = (bf16[80,128]{1,0:T(8,128)(2,1)S(1)}, bf16[80,128]{1,0:T(8,128)(2,1)S(1)}, u32[]{:S(2)}, u32[]{:S(2)}) collective-permute-start(bf16[80,128]{1,0:T(8,128)(2,1)S(1)} %pad_maximum_fusion.3), channel_id=1, source_target_pairs={{0,4},{4,8},{8,12},{12,16},{16,20},{20,24},{24,28},{1,5},{5,9},{9,... | collective-permute-start | bytes 61448 | tf_op jit(solution)/shard_map/ppermute | solution.py:930
  13.2 1.9 collective-permute-start.4
  15.2 3.2 %collective-permute-done.4.high = bf16[80,128]{1,0:T(8,128)(2,1)S(1)} collective-permute-done((bf16[80,128]{1,0:T(8,128)(2,1)S(1)}, bf16[80,128]{1,0:T(8,128)(2,1)S(1)}, u32[]{:S(2)}, u32[]{:S(2)}) %collective-permute-start.4) | collective-permute-done | bytes 20512 | tf_op jit(solution)/shard_map/ppermute | solution.py:931
  19.0 4.0 %pack_frames.1 = (bf16[13,64,128]{2,1,0:T(8,128)(2,1)}, bf16[13,64,128]{2,1,0:T(8,128)(2,1)}, bf16[13,64,128]{2,1,0:T(8,128)(2,1)}, bf16[13,64,128]{2,1,0:T(8,12...) custom-call(s32[2]{0:T(128)} %pad_add_fusion.places, ...), custom_call_target="tpu_custom_call" | custom-call | flops 1000000 | bytes 6000000 | tf_op jit(solution)/shard_map/pack_frames/pallas_call | solution.py:759
  23.0 1.3 collective-permute-done.2
  24.3 1.3 collective-permute-start.5
  25.6 1.2 collective-permute-start.6
  26.9 2.4 %collective-permute-start.8 = (bf16[13,64,128]{2,1,0:T(8,128)(2,1)}, bf16[13,64,128]{2,1,0:T(8,128)(2,1)S(1)}, u32[]{:S(2)}, u32[]{:S(2)}) collective-permute-start(bf16[13,64,128]{2,1,0:T(8,128)(2,1)} %get-tuple-element.91), channel_id=1, source_target_pairs={{0,2},{1,3},{2,0},{3,1},{4,6},{5,7},{6,4},{7,5},{8,10},{9,11},{10,... | collective-permute-start | bytes 638984 | tf_op jit(solution)/shard_map/ppermute | solution.py:21
  29.5 2.6 %collective-permute-done.7.sig1.first1 = bf16[13,64,128]{2,1,0:T(8,128)(2,1)S(1)} collective-permute-done((bf16[13,64,128]{2,1,0:T(8,128)(2,1)}, bf16[13,64,128]{2,1,0:T(8,128)(2,1)S(1)}, u32[]{:S(2)}, u32[]{:S(2)}) %collective-permute-start.7) | collective-permute-done | bytes 213024 | tf_op jit(solution)/shard_map/ppermute | solution.py:21
  32.1 4.6 %collective-permute-done.8.sig2.first2 = bf16[13,64,128]{2,1,0:T(8,128)(2,1)S(1)} collective-permute-done((bf16[13,64,128]{2,1,0:T(8,128)(2,1)}, bf16[13,64,128]{2,1,0:T(8,128)(2,1)S(1)}, u32[]{:S(2)}, u32[]{:S(2)}) %collective-permute-start.8) | collective-permute-done | bytes 213024 | tf_op jit(solution)/shard_map/ppermute | solution.py:21
  36.7 10.0 %collective-permute-done.9.sig3.first3 = bf16[13,64,128]{2,1,0:T(8,128)(2,1)S(1)} collective-permute-done((bf16[13,64,128]{2,1,0:T(8,128)(2,1)}, bf16[13,64,128]{2,1,0:T(8,128)(2,1)S(1)}, u32[]{:S(2)}, u32[]{:S(2)}) %collective-permute-start.9) | collective-permute-done | bytes 213024 | tf_op jit(solution)/shard_map/ppermute | solution.py:21
  47.1 1.3 collective-permute-start.13
  48.4 2.7 %collective-permute-start.11 = (bf16[29,64,128]{2,1,0:T(8,128)(2,1)S(1)}, bf16[29,64,128]{2,1,0:T(8,128)(2,1)}, u32[]{:S(2)}, u32[]{:S(2)}) collective-permute-start(bf16[29,64,128]{2,1,0:T(8,128)(2,1)S(1)} %copy-done.29), channel_id=1, source_target_pairs={{0,2},{1,3},{2,0},{3,1},{4,6},{5,7},{6,4},{7,5},{8,10},{9,11},{10,... | collective-permute-start | bytes 1425416 | tf_op jit(solution)/shard_map/ppermute | solution.py:21
  51.1 3.4 %collective-permute-done.12.rest_3_ = bf16[2,2,64,768]{3,2,1,0:T(8,128)(2,1)} collective-permute-done((bf16[2,2,64,768]{3,2,1,0:T(8,128)(2,1)S(1)}, bf16[2,2,64,768]{3,2,1,0:T(8,128)(2,1)}, u32[]{:S(2)}, u32[]{:S(2)}) %collective-permute-start.12) | collective-permute-done | bytes 393248 | tf_op jit(solution)/shard_map/ppermute | solution.py:21
  54.6 4.2 %collective-permute-start.14 = (bf16[4,2,64,768]{3,2,1,0:T(8,128)(2,1)S(1)}, bf16[4,2,64,768]{3,2,1,0:T(8,128)(2,1)S(1)}, u32[]{:S(2)}, u32[]{:S(2)}) collective-permute-start(bf16[4,2,64,768]{3,2,1,0:T(8,128)(2,1)S(1)} %pad_maximum_fusion.rest_0_), channel_id=1, source_target_pairs={{0,4},{4,0},{8,12},{12,8},{16,20},{20,16},{24,28},{28,24},{1,5},{5... | collective-permute-start | bytes 2359304 | tf_op jit(solution)/shard_map/ppermute | solution.py:21
  59.3 7.4 %collective-permute-done.10.second1 = bf16[29,64,128]{2,1,0:T(8,128)(2,1)} collective-permute-done((bf16[29,64,128]{2,1,0:T(8,128)(2,1)S(1)}, bf16[29,64,128]{2,1,0:T(8,128)(2,1)}, u32[]{:S(2)}, u32[]{:S(2)}) %collective-permute-start.10) | collective-permute-done | bytes 475168 | tf_op jit(solution)/shard_map/ppermute | solution.py:21
  66.7 2.9 %collective-permute-start.17 = (bf16[2,2,64,768]{3,2,1,0:T(8,128)(2,1)}, bf16[2,2,64,768]{3,2,1,0:T(8,128)(2,1)}, u32[]{:S(2)}, u32[]{:S(2)}) collective-permute-start(bf16[2,2,64,768]{3,2,1,0:T(8,128)(2,1)} %collective-permute-done.12.rest_3_), channel_id=1, source_target_pairs={{0,4},{4,0},{8,12},{12,8},{16,20},{20,16},{24,28},{28,24},{1,5},{5... | collective-permute-start | bytes 1179656 | tf_op jit(solution)/shard_map/ppermute | solution.py:21
  69.6 3.6 %collective-permute-start.18 = (bf16[2,2,64,768]{3,2,1,0:T(8,128)(2,1)}, bf16[2,2,64,768]{3,2,1,0:T(8,128)(2,1)}, u32[]{:S(2)}, u32[]{:S(2)}) collective-permute-start(bf16[2,2,64,768]{3,2,1,0:T(8,128)(2,1)} %collective-permute-done.13.rest_4_), channel_id=1, source_target_pairs={{0,4},{4,0},{8,12},{12,8},{16,20},{20,16},{24,28},{28,24},{1,5},{5... | collective-permute-start | bytes 1179656 | tf_op jit(solution)/shard_map/ppermute | solution.py:21
  75.9 27.0 %forward_blocks.1 = (bf16[3,8,528,256]{3,2,1,0:T(8,128)(2,1)}, bf16[3,8,528,256]{3,2,1,0:T(8,128)(2,1)}, bf16[3,8,528,256]{3,2,1,0:T(8,128)(2,1)}, bf16[3,8,528,...) custom-call(s32[2]{0:T(128)} %pad_add_fusion.places, ...), custom_call_target="tpu_custom_call" | custom-call | flops 10519314432 | bytes 50000000 | tf_op jit(solution)/shard_map/forward_blocks/pallas_call | solution.py:813
  102.9 2.7 %collective-permute-start.20 = (bf16[64,4096]{1,0:T(8,128)(2,1)}, bf16[64,4096]{1,0:T(8,128)(2,1)S(1)}, u32[]{:S(2)}, u32[]{:S(2)}) collective-permute-start(bf16[64,4096]{1,0:T(8,128)(2,1)} %get-tuple-element.131), channel_id=1, source_target_pairs={{0,1},{1,0},{2,3},{3,2},{4,5},{5,4},{6,7},{7,6},{8,9},{9,8},{10,11... | collective-permute-start | bytes 1572872 | tf_op jit(solution)/shard_map/ppermute | solution.py:21
  106.1 1.4 collective-permute-start.22
  107.5 40.1 %backward_blocks.1 = (bf16[4,2,256,768]{3,2,1,0:T(8,128)(2,1)}, bf16[4,2,256,768]{3,2,1,0:T(8,128)(2,1)}, bf16[512,128]{1,0:T(8,128)(2,1)}, bf16[512,128]{1,0:T(...) custom-call(s32[2]{0:T(128)} %pad_add_fusion.places, ...), custom_call_target="tpu_custom_call" | custom-call | flops 21038628864 | bytes 60000000 | tf_op jit(solution)/shard_map/backward_blocks/pallas_call | solution.py:839
  147.7 5.6 %collective-permute-done.22 = bf16[64,4096]{1,0:T(8,128)(2,1)S(1)} collective-permute-done((bf16[64,4096]{1,0:T(8,128)(2,1)}, bf16[64,4096]{1,0:T(8,128)(2,1)S(1)}, u32[]{:S(2)}, u32[]{:S(2)}) %collective-permute-start.22) | collective-permute-done | bytes 524320 | tf_op jit(solution)/shard_map/ppermute | solution.py:21
  153.2 1.1 collective-permute-start.26
  154.3 5.5 %collective-permute-done.26 = bf16[4,2,256,768]{3,2,1,0:T(8,128)(2,1)S(1)} collective-permute-done((bf16[4,2,256,768]{3,2,1,0:T(8,128)(2,1)}, bf16[4,2,256,768]{3,2,1,0:T(8,128)(2,1)S(1)}, u32[]{:S(2)}, u32[]{:S(2)}) %collective-permute-start.26) | collective-permute-done | bytes 3145760 | tf_op jit(solution)/shard_map/ppermute | solution.py:21
  159.8 2.8 %add.83 = bf16[4,2,256,768]{3,2,1,0:T(8,128)(2,1)S(1)} add(bf16[4,2,256,768]{3,2,1,0:T(8,128)(2,1)} %get-tuple-element.142, bf16[4,2,256,768]{3,2,1,0:T(8,128)(2,1)S(1)} %collective-permute-done.26) | non-fusion elementwise | flops 1572864 | bytes 9437184 | tf_op jit(solution)/shard_map/add | solution.py:957
  163.6 1.2 collective-permute-start.29
  164.7 8.4 %collective-permute-done.27 = bf16[1,256,768]{2,1,0:T(8,128)(2,1)S(1)} collective-permute-done((bf16[1,256,768]{2,1,0:T(8,128)(2,1)S(1)}, bf16[1,256,768]{2,1,0:T(8,128)(2,1)S(1)}, u32[]{:S(2)}, u32[]{:S(2)}) %collective-permute-start.27) | collective-permute-done | bytes 393248 | tf_op jit(solution)/shard_map/ppermute | solution.py:21
  174.6 1.2 collective-permute-start.28
  177.7 1.3 collective-permute-start.24
  179.0 1.3 collective-permute-start.25
  180.5 1.7 collective-permute-done.23
  182.2 1.1 collective-permute-done.24
  183.3 8.9 %collective-permute-done.25 = bf16[512,128]{1,0:T(8,128)(2,1)S(1)} collective-permute-done((bf16[512,128]{1,0:T(8,128)(2,1)S(1)}, bf16[512,128]{1,0:T(8,128)(2,1)S(1)}, u32[]{:S(2)}, u32[]{:S(2)}) %collective-permute-start.25) | collective-permute-done | bytes 131104 | tf_op jit(solution)/shard_map/ppermute | solution.py:21
  193.0 1.3 collective-permute-done.30
  194.3 1.5 fusion.1
  195.9 1.3 collective-permute-start.32
  197.2 1.3 collective-permute-start.33
  198.8 1.6 collective-permute-done.31
  200.5 3.0 %collective-permute-done.32 = bf16[2,64,768]{2,1,0:T(8,128)(2,1)S(1)} collective-permute-done((bf16[2,64,768]{2,1,0:T(8,128)(2,1)S(1)}, bf16[2,64,768]{2,1,0:T(8,128)(2,1)S(1)}, u32[]{:S(2)}, u32[]{:S(2)}) %collective-permute-start.32) | collective-permute-done | bytes 196640 | tf_op jit(solution)/shard_map/ppermute | solution.py:21
  203.4 11.6 %collective-permute-done.33 = bf16[2,64,768]{2,1,0:T(8,128)(2,1)S(1)} collective-permute-done((bf16[2,64,768]{2,1,0:T(8,128)(2,1)S(1)}, bf16[2,64,768]{2,1,0:T(8,128)(2,1)S(1)}, u32[]{:S(2)}, u32[]{:S(2)}) %collective-permute-start.33) | collective-permute-done | bytes 196640 | tf_op jit(solution)/shard_map/ppermute | solution.py:21
  216.2 3.5 %collective-permute-done.35.rest_2_ = bf16[2,64,768]{2,1,0:T(8,128)(2,1)S(1)} collective-permute-done((bf16[2,64,768]{2,1,0:T(8,128)(2,1)S(1)}, bf16[2,64,768]{2,1,0:T(8,128)(2,1)S(1)}, u32[]{:S(2)}, u32[]{:S(2)}) %collective-permute-start.35) | collective-permute-done | bytes 196640 | tf_op jit(solution)/shard_map/ppermute | solution.py:21
  221.6 4.3 %collective-permute-start.38 = (bf16[2,64,768]{2,1,0:T(8,128)(2,1)S(1)}, bf16[2,64,768]{2,1,0:T(8,128)(2,1)S(1)}, u32[]{:S(2)}, u32[]{:S(2)}) collective-permute-start(bf16[2,64,768]{2,1,0:T(8,128)(2,1)S(1)} %add_add_fusion.rest_0_), channel_id=1, source_target_pairs={{0,4},{4,0},{8,12},{12,8},{16,20},{20,16},{24,28},{28,24},{1,5},{5... | collective-permute-start | bytes 589832 | tf_op jit(solution)/shard_map/ppermute | solution.py:21
  226.4 1.2 collective-permute-start.41
  227.6 2.3 collective-permute-start.42
  232.3 6.2 %finish_weights.1 = (f32[64,16,512]{2,1,0:T(8,128)}, f32[1,512]{1,0:T(1,128)}, f32[1,64]{1,0:T(1,128)}, f32[3,3,64,256]{3,2,1,0:T(8,128)}, f32[3,64]{1,0:T(4,128...) custom-call(s32[2]{0:T(128)} %pad_add_fusion.places, ...), custom_call_target="tpu_custom_call" | custom-call | flops 20000000 | bytes 8000000 | tf_op jit(solution)/shard_map/finish_weights/pallas_call | solution.py:787
  (146 shorter events, 18.9 us)
Async XLA Ops:
  4.6 18.3 %collective-permute-start = (bf16[2,64,768]{2,1,0:T(8,128)(2,1)}, bf16[2,64,768]{2,1,0:T(8,128)(2,1)S(1)}, u32[]{:S(2)}, u32[]{:S(2)}) collective-permute-start(bf16[2,64,768]{2,1,0:T(8,128)(2,1)} %pack_weights.1), channel_id=1, source_target_pairs={{0,1},{1,0},{2,3},{3,2},{4,5},{5,4},{6,7},{7,6},{8,9},{9,8},{10,11... | collective-permute-start | bytes 589832 | tf_op jit(solution)/shard_map/ppermute | solution.py:21
  4.6 18.3 %collective-permute-start.1 = (bf16[2,64,768]{2,1,0:T(8,128)(2,1)}, bf16[2,64,768]{2,1,0:T(8,128)(2,1)S(1)}, u32[]{:S(2)}, u32[]{:S(2)}) collective-permute-start(bf16[2,64,768]{2,1,0:T(8,128)(2,1)} %pack_weights.1), channel_id=1, source_target_pairs={{0,2},{1,3},{2,0},{3,1},{4,6},{5,7},{6,4},{7,5},{8,10},{9,11},{10,... | collective-permute-start | bytes 589832 | tf_op jit(solution)/shard_map/ppermute | solution.py:21
  7.1 17.1 %collective-permute-start.2 = (bf16[2,64,768]{2,1,0:T(8,128)(2,1)}, bf16[2,64,768]{2,1,0:T(8,128)(2,1)S(1)}, u32[]{:S(2)}, u32[]{:S(2)}) collective-permute-start(bf16[2,64,768]{2,1,0:T(8,128)(2,1)} %pack_weights.1), channel_id=1, source_target_pairs={{0,3},{1,2},{2,1},{3,0},{4,7},{5,6},{6,5},{7,4},{8,11},{9,10},{10,... | collective-permute-start | bytes 589832 | tf_op jit(solution)/shard_map/ppermute | solution.py:21
  8.7 6.5 %collective-permute-start.3 = (bf16[80,128]{1,0:T(8,128)(2,1)S(1)}, bf16[80,128]{1,0:T(8,128)(2,1)S(1)}, u32[]{:S(2)}, u32[]{:S(2)}) collective-permute-start(bf16[80,128]{1,0:T(8,128)(2,1)S(1)} %pad_maximum_fusion.3), channel_id=1, source_target_pairs={{0,4},{4,8},{8,12},{12,16},{16,20},{20,24},{24,28},{1,5},{5,9},{9,... | collective-permute-start | bytes 61448 | tf_op jit(solution)/shard_map/ppermute | solution.py:930
  13.2 5.1 %collective-permute-start.4 = (bf16[80,128]{1,0:T(8,128)(2,1)S(1)}, bf16[80,128]{1,0:T(8,128)(2,1)S(1)}, u32[]{:S(2)}, u32[]{:S(2)}) collective-permute-start(bf16[80,128]{1,0:T(8,128)(2,1)S(1)} %pad_maximum_fusion.4), channel_id=1, source_target_pairs={{4,0},{8,4},{12,8},{16,12},{20,16},{24,20},{28,24},{5,1},{9,5},{13... | collective-permute-start | bytes 61448 | tf_op jit(solution)/shard_map/ppermute | solution.py:931
  22.9 50.3 %copy-start.27 = (bf16[512]{0:T(512)(128)(2,1)S(1)}, bf16[512]{0:T(512)(128)(2,1)}, u32[]{:S(2)}) copy-start(bf16[512]{0:T(512)(128)(2,1)} %param.18) | copy-start | bytes 3076
  22.9 50.9 %copy-start.24 = (s32[16384]{0:T(1024)S(1)}, s32[16384]{0:T(1024)}, u32[]{:S(2)}) copy-start(s32[16384]{0:T(1024)} %param.16) | copy-start | bytes 196612
  24.3 51.6 %copy-start.3 = (bf16[4,2,64,768]{3,2,1,0:T(8,128)(2,1)}, bf16[4,2,64,768]{3,2,1,0:T(8,128)(2,1)S(1)}, u32[]{:S(2)}) copy-start(bf16[4,2,64,768]{3,2,1,0:T(8,128)(2,1)S(1)} %pad_maximum_fusion.rest_0_) | copy-start | bytes 2359300
  24.3 22.3 %collective-permute-start.5 = (bf16[4,2,64,768]{3,2,1,0:T(8,128)(2,1)S(1)}, bf16[4,2,64,768]{3,2,1,0:T(8,128)(2,1)S(1)}, u32[]{:S(2)}, u32[]{:S(2)}) collective-permute-start(bf16[4,2,64,768]{3,2,1,0:T(8,128)(2,1)S(1)} %pad_maximum_fusion.rest_0_), channel_id=1, source_target_pairs={{0,8},{4,12},{8,0},{12,4},{16,24},{20,28},{24,16},{28,20},{1,9},{5... | collective-permute-start | bytes 2359304 | tf_op jit(solution)/shard_map/ppermute | solution.py:21
  25.6 21.1 %collective-permute-start.6 = (bf16[4,2,64,768]{3,2,1,0:T(8,128)(2,1)S(1)}, bf16[4,2,64,768]{3,2,1,0:T(8,128)(2,1)S(1)}, u32[]{:S(2)}, u32[]{:S(2)}) collective-permute-start(bf16[4,2,64,768]{3,2,1,0:T(8,128)(2,1)S(1)} %pad_maximum_fusion.rest_0_), channel_id=1, source_target_pairs={{0,16},{4,20},{8,24},{12,28},{16,0},{20,4},{24,8},{28,12},{1,17},{... | collective-permute-start | bytes 2359304 | tf_op jit(solution)/shard_map/ppermute | solution.py:21
  26.9 5.2 %collective-permute-start.7 = (bf16[13,64,128]{2,1,0:T(8,128)(2,1)}, bf16[13,64,128]{2,1,0:T(8,128)(2,1)S(1)}, u32[]{:S(2)}, u32[]{:S(2)}) collective-permute-start(bf16[13,64,128]{2,1,0:T(8,128)(2,1)} %get-tuple-element.90), channel_id=1, source_target_pairs={{0,1},{1,0},{2,3},{3,2},{4,5},{5,4},{6,7},{7,6},{8,9},{9,8},{10,11... | collective-permute-start | bytes 638984 | tf_op jit(solution)/shard_map/ppermute | solution.py:21
  26.9 9.8 %collective-permute-start.8 = (bf16[13,64,128]{2,1,0:T(8,128)(2,1)}, bf16[13,64,128]{2,1,0:T(8,128)(2,1)S(1)}, u32[]{:S(2)}, u32[]{:S(2)}) collective-permute-start(bf16[13,64,128]{2,1,0:T(8,128)(2,1)} %get-tuple-element.91), channel_id=1, source_target_pairs={{0,2},{1,3},{2,0},{3,1},{4,6},{5,7},{6,4},{7,5},{8,10},{9,11},{10,... | collective-permute-start | bytes 638984 | tf_op jit(solution)/shard_map/ppermute | solution.py:21
  29.3 17.4 %collective-permute-start.9 = (bf16[13,64,128]{2,1,0:T(8,128)(2,1)}, bf16[13,64,128]{2,1,0:T(8,128)(2,1)S(1)}, u32[]{:S(2)}, u32[]{:S(2)}) collective-permute-start(bf16[13,64,128]{2,1,0:T(8,128)(2,1)} %get-tuple-element.92), channel_id=1, source_target_pairs={{0,3},{1,2},{2,1},{3,0},{4,7},{5,6},{6,5},{7,4},{8,11},{9,10},{10,... | collective-permute-start | bytes 638984 | tf_op jit(solution)/shard_map/ppermute | solution.py:21
  32.1 43.8 %copy-start.32 = (bf16[13,64,128]{2,1,0:T(8,128)(2,1)}, bf16[13,64,128]{2,1,0:T(8,128)(2,1)S(1)}, u32[]{:S(2)}) copy-start(bf16[13,64,128]{2,1,0:T(8,128)(2,1)S(1)} %collective-permute-done.7.sig1.first1) | copy-start | bytes 638980
  46.7 7.8 %collective-permute-start.12 = (bf16[2,2,64,768]{3,2,1,0:T(8,128)(2,1)S(1)}, bf16[2,2,64,768]{3,2,1,0:T(8,128)(2,1)}, u32[]{:S(2)}, u32[]{:S(2)}) collective-permute-start(bf16[2,2,64,768]{3,2,1,0:T(8,128)(2,1)S(1)} %slice.49), channel_id=1, source_target_pairs={{0,8},{4,12},{8,0},{12,4},{16,24},{20,28},{24,16},{28,20},{1,9},{5... | collective-permute-start | bytes 1179656 | tf_op jit(solution)/shard_map/ppermute | solution.py:21
  47.1 7.5 %collective-permute-start.13 = (bf16[2,2,64,768]{3,2,1,0:T(8,128)(2,1)S(1)}, bf16[2,2,64,768]{3,2,1,0:T(8,128)(2,1)}, u32[]{:S(2)}, u32[]{:S(2)}) collective-permute-start(bf16[2,2,64,768]{3,2,1,0:T(8,128)(2,1)S(1)} %slice.50), channel_id=1, source_target_pairs={{0,16},{4,20},{8,24},{12,28},{16,0},{20,4},{24,8},{28,12},{1,17},{... | collective-permute-start | bytes 1179656 | tf_op jit(solution)/shard_map/ppermute | solution.py:21
  48.4 18.3 %collective-permute-start.10 = (bf16[29,64,128]{2,1,0:T(8,128)(2,1)S(1)}, bf16[29,64,128]{2,1,0:T(8,128)(2,1)}, u32[]{:S(2)}, u32[]{:S(2)}) collective-permute-start(bf16[29,64,128]{2,1,0:T(8,128)(2,1)S(1)} %copy-done.30), channel_id=1, source_target_pairs={{0,1},{1,0},{2,3},{3,2},{4,5},{5,4},{6,7},{7,6},{8,9},{9,8},{10,11... | collective-permute-start | bytes 1425416 | tf_op jit(solution)/shard_map/ppermute | solution.py:21
  48.4 21.3 %collective-permute-start.11 = (bf16[29,64,128]{2,1,0:T(8,128)(2,1)S(1)}, bf16[29,64,128]{2,1,0:T(8,128)(2,1)}, u32[]{:S(2)}, u32[]{:S(2)}) collective-permute-start(bf16[29,64,128]{2,1,0:T(8,128)(2,1)S(1)} %copy-done.29), channel_id=1, source_target_pairs={{0,2},{1,3},{2,0},{3,1},{4,6},{5,7},{6,4},{7,5},{8,10},{9,11},{10,... | collective-permute-start | bytes 1425416 | tf_op jit(solution)/shard_map/ppermute | solution.py:21
  54.6 20.3 %collective-permute-start.14 = (bf16[4,2,64,768]{3,2,1,0:T(8,128)(2,1)S(1)}, bf16[4,2,64,768]{3,2,1,0:T(8,128)(2,1)S(1)}, u32[]{:S(2)}, u32[]{:S(2)}) collective-permute-start(bf16[4,2,64,768]{3,2,1,0:T(8,128)(2,1)S(1)} %pad_maximum_fusion.rest_0_), channel_id=1, source_target_pairs={{0,4},{4,0},{8,12},{12,8},{16,20},{20,16},{24,28},{28,24},{1,5},{5... | collective-permute-start | bytes 2359304 | tf_op jit(solution)/shard_map/ppermute | solution.py:21
  58.8 16.1 %collective-permute-start.15 = (bf16[4,2,64,768]{3,2,1,0:T(8,128)(2,1)S(1)}, bf16[4,2,64,768]{3,2,1,0:T(8,128)(2,1)}, u32[]{:S(2)}, u32[]{:S(2)}) collective-permute-start(bf16[4,2,64,768]{3,2,1,0:T(8,128)(2,1)S(1)} %collective-permute-done.5.rest_1_), channel_id=1, source_target_pairs={{0,4},{4,0},{8,12},{12,8},{16,20},{20,16},{24,28},{28,24},{1,5},{5... | collective-permute-start | bytes 2359304 | tf_op jit(solution)/shard_map/ppermute | solution.py:21
  58.8 16.1 %collective-permute-start.16 = (bf16[4,2,64,768]{3,2,1,0:T(8,128)(2,1)S(1)}, bf16[4,2,64,768]{3,2,1,0:T(8,128)(2,1)}, u32[]{:S(2)}, u32[]{:S(2)}) collective-permute-start(bf16[4,2,64,768]{3,2,1,0:T(8,128)(2,1)S(1)} %collective-permute-done.6.rest_2_), channel_id=1, source_target_pairs={{0,4},{4,0},{8,12},{12,8},{16,20},{20,16},{24,28},{28,24},{1,5},{5... | collective-permute-start | bytes 2359304 | tf_op jit(solution)/shard_map/ppermute | solution.py:21
  66.7 7.2 %collective-permute-start.17 = (bf16[2,2,64,768]{3,2,1,0:T(8,128)(2,1)}, bf16[2,2,64,768]{3,2,1,0:T(8,128)(2,1)}, u32[]{:S(2)}, u32[]{:S(2)}) collective-permute-start(bf16[2,2,64,768]{3,2,1,0:T(8,128)(2,1)} %collective-permute-done.12.rest_3_), channel_id=1, source_target_pairs={{0,4},{4,0},{8,12},{12,8},{16,20},{20,16},{24,28},{28,24},{1,5},{5... | collective-permute-start | bytes 1179656 | tf_op jit(solution)/shard_map/ppermute | solution.py:21
  69.6 5.3 %collective-permute-start.18 = (bf16[2,2,64,768]{3,2,1,0:T(8,128)(2,1)}, bf16[2,2,64,768]{3,2,1,0:T(8,128)(2,1)}, u32[]{:S(2)}, u32[]{:S(2)}) collective-permute-start(bf16[2,2,64,768]{3,2,1,0:T(8,128)(2,1)} %collective-permute-done.13.rest_4_), channel_id=1, source_target_pairs={{0,4},{4,0},{8,12},{12,8},{16,20},{20,16},{24,28},{28,24},{1,5},{5... | collective-permute-start | bytes 1179656 | tf_op jit(solution)/shard_map/ppermute | solution.py:21
  73.9 29.0 %collective-permute-start.19 = (bf16[29,64,128]{2,1,0:T(8,128)(2,1)}, bf16[29,64,128]{2,1,0:T(8,128)(2,1)S(1)}, u32[]{:S(2)}, u32[]{:S(2)}) collective-permute-start(bf16[29,64,128]{2,1,0:T(8,128)(2,1)} %get-tuple-element.117), channel_id=1, source_target_pairs={{0,3},{1,2},{2,1},{3,0},{4,7},{5,6},{6,5},{7,4},{8,11},{9,10},{10,... | collective-permute-start | bytes 1425416 | tf_op jit(solution)/shard_map/ppermute | solution.py:21
  102.9 44.7 %collective-permute-start.20 = (bf16[64,4096]{1,0:T(8,128)(2,1)}, bf16[64,4096]{1,0:T(8,128)(2,1)S(1)}, u32[]{:S(2)}, u32[]{:S(2)}) collective-permute-start(bf16[64,4096]{1,0:T(8,128)(2,1)} %get-tuple-element.131), channel_id=1, source_target_pairs={{0,1},{1,0},{2,3},{3,2},{4,5},{5,4},{6,7},{7,6},{8,9},{9,8},{10,11... | collective-permute-start | bytes 1572872 | tf_op jit(solution)/shard_map/ppermute | solution.py:21
  105.6 42.1 %collective-permute-start.21 = (bf16[64,4096]{1,0:T(8,128)(2,1)}, bf16[64,4096]{1,0:T(8,128)(2,1)S(1)}, u32[]{:S(2)}, u32[]{:S(2)}) collective-permute-start(bf16[64,4096]{1,0:T(8,128)(2,1)} %get-tuple-element.132), channel_id=1, source_target_pairs={{0,2},{1,3},{2,0},{3,1},{4,6},{5,7},{6,4},{7,5},{8,10},{9,11},{10,... | collective-permute-start | bytes 1572872 | tf_op jit(solution)/shard_map/ppermute | solution.py:21
  106.1 47.1 %collective-permute-start.22 = (bf16[64,4096]{1,0:T(8,128)(2,1)}, bf16[64,4096]{1,0:T(8,128)(2,1)S(1)}, u32[]{:S(2)}, u32[]{:S(2)}) collective-permute-start(bf16[64,4096]{1,0:T(8,128)(2,1)} %get-tuple-element.133), channel_id=1, source_target_pairs={{0,3},{1,2},{2,1},{3,0},{4,7},{5,6},{6,5},{7,4},{8,11},{9,10},{10,... | collective-permute-start | bytes 1572872 | tf_op jit(solution)/shard_map/ppermute | solution.py:21
  153.2 6.6 %collective-permute-start.26 = (bf16[4,2,256,768]{3,2,1,0:T(8,128)(2,1)}, bf16[4,2,256,768]{3,2,1,0:T(8,128)(2,1)S(1)}, u32[]{:S(2)}, u32[]{:S(2)}) collective-permute-start(bf16[4,2,256,768]{3,2,1,0:T(8,128)(2,1)} %get-tuple-element.143), channel_id=1, source_target_pairs={{0,4},{4,0},{8,12},{12,8},{16,20},{20,16},{24,28},{28,24},{1,5},{5... | collective-permute-start | bytes 9437192 | tf_op jit(solution)/shard_map/ppermute | solution.py:21
  162.7 10.4 %collective-permute-start.27 = (bf16[1,256,768]{2,1,0:T(8,128)(2,1)S(1)}, bf16[1,256,768]{2,1,0:T(8,128)(2,1)S(1)}, u32[]{:S(2)}, u32[]{:S(2)}) collective-permute-start(bf16[1,256,768]{2,1,0:T(8,128)(2,1)S(1)} %get-tuple-element.159), channel_id=1, source_target_pairs={{0,16},{4,20},{8,24},{12,28},{16,0},{20,4},{24,8},{28,12},{1,17},{... | collective-permute-start | bytes 1179656 | tf_op jit(solution)/shard_map/ppermute | solution.py:21
  163.6 10.0 %collective-permute-start.29 = (bf16[1,256,768]{2,1,0:T(8,128)(2,1)S(1)}, bf16[1,256,768]{2,1,0:T(8,128)(2,1)S(1)}, u32[]{:S(2)}, u32[]{:S(2)}) collective-permute-start(bf16[1,256,768]{2,1,0:T(8,128)(2,1)S(1)} %get-tuple-element.158), channel_id=1, source_target_pairs={{0,8},{4,12},{8,0},{12,4},{16,24},{20,28},{24,16},{28,20},{1,9},{5... | collective-permute-start | bytes 1179656 | tf_op jit(solution)/shard_map/ppermute | solution.py:21
  174.6 17.8 %collective-permute-start.28 = (bf16[2,256,768]{2,1,0:T(8,128)(2,1)}, bf16[2,256,768]{2,1,0:T(8,128)(2,1)}, u32[]{:S(2)}, u32[]{:S(2)}) collective-permute-start(bf16[2,256,768]{2,1,0:T(8,128)(2,1)} %pad_maximum_fusion.1), channel_id=1, source_target_pairs={{0,8},{4,12},{8,0},{12,4},{16,24},{20,28},{24,16},{28,20},{1,9},{5... | collective-permute-start | bytes 2359304 | tf_op jit(solution)/shard_map/ppermute | solution.py:21
  176.8 17.5 %collective-permute-start.30 = (bf16[2,256,768]{2,1,0:T(8,128)(2,1)}, bf16[2,256,768]{2,1,0:T(8,128)(2,1)}, u32[]{:S(2)}, u32[]{:S(2)}) collective-permute-start(bf16[2,256,768]{2,1,0:T(8,128)(2,1)} %pad_maximum_fusion.2), channel_id=1, source_target_pairs={{0,16},{4,20},{8,24},{12,28},{16,0},{20,4},{24,8},{28,12},{1,17},{... | collective-permute-start | bytes 2359304 | tf_op jit(solution)/shard_map/ppermute | solution.py:21
  177.7 4.4 %collective-permute-start.23 = (bf16[512,128]{1,0:T(8,128)(2,1)}, bf16[512,128]{1,0:T(8,128)(2,1)S(1)}, u32[]{:S(2)}, u32[]{:S(2)}) collective-permute-start(bf16[512,128]{1,0:T(8,128)(2,1)} %get-tuple-element.139), channel_id=1, source_target_pairs={{0,1},{1,0},{2,3},{3,2},{4,5},{5,4},{6,7},{7,6},{8,9},{9,8},{10,11... | collective-permute-start | bytes 393224 | tf_op jit(solution)/shard_map/ppermute | solution.py:21
  177.7 5.6 %collective-permute-start.24 = (bf16[512,128]{1,0:T(8,128)(2,1)}, bf16[512,128]{1,0:T(8,128)(2,1)S(1)}, u32[]{:S(2)}, u32[]{:S(2)}) collective-permute-start(bf16[512,128]{1,0:T(8,128)(2,1)} %get-tuple-element.140), channel_id=1, source_target_pairs={{0,2},{1,3},{2,0},{3,1},{4,6},{5,7},{6,4},{7,5},{8,10},{9,11},{10,... | collective-permute-start | bytes 393224 | tf_op jit(solution)/shard_map/ppermute | solution.py:21
  179.0 13.2 %collective-permute-start.25 = (bf16[512,128]{1,0:T(8,128)(2,1)S(1)}, bf16[512,128]{1,0:T(8,128)(2,1)S(1)}, u32[]{:S(2)}, u32[]{:S(2)}) collective-permute-start(bf16[512,128]{1,0:T(8,128)(2,1)S(1)} %copy-done.35), channel_id=1, source_target_pairs={{0,3},{1,2},{2,1},{3,0},{4,7},{5,6},{6,5},{7,4},{8,11},{9,10},{10,... | collective-permute-start | bytes 393224 | tf_op jit(solution)/shard_map/ppermute | solution.py:21
  195.9 4.6 %collective-permute-start.31 = (bf16[2,64,768]{2,1,0:T(8,128)(2,1)S(1)}, bf16[2,64,768]{2,1,0:T(8,128)(2,1)S(1)}, u32[]{:S(2)}, u32[]{:S(2)}) collective-permute-start(bf16[2,64,768]{2,1,0:T(8,128)(2,1)S(1)} %get-tuple-element.164), channel_id=1, source_target_pairs={{0,1},{1,0},{2,3},{3,2},{4,5},{5,4},{6,7},{7,6},{8,9},{9,8},{10,11... | collective-permute-start | bytes 589832 | tf_op jit(solution)/shard_map/ppermute | solution.py:21
  195.9 7.5 %collective-permute-start.32 = (bf16[2,64,768]{2,1,0:T(8,128)(2,1)S(1)}, bf16[2,64,768]{2,1,0:T(8,128)(2,1)S(1)}, u32[]{:S(2)}, u32[]{:S(2)}) collective-permute-start(bf16[2,64,768]{2,1,0:T(8,128)(2,1)S(1)} %get-tuple-element.166), channel_id=1, source_target_pairs={{0,2},{1,3},{2,0},{3,1},{4,6},{5,7},{6,4},{7,5},{8,10},{9,11},{10,... | collective-permute-start | bytes 589832 | tf_op jit(solution)/shard_map/ppermute | solution.py:21
  197.2 17.8 %collective-permute-start.33 = (bf16[2,64,768]{2,1,0:T(8,128)(2,1)S(1)}, bf16[2,64,768]{2,1,0:T(8,128)(2,1)S(1)}, u32[]{:S(2)}, u32[]{:S(2)}) collective-permute-start(bf16[2,64,768]{2,1,0:T(8,128)(2,1)S(1)} %get-tuple-element.165), channel_id=1, source_target_pairs={{0,3},{1,2},{2,1},{3,0},{4,7},{5,6},{6,5},{7,4},{8,11},{9,10},{10,... | collective-permute-start | bytes 589832 | tf_op jit(solution)/shard_map/ppermute | solution.py:21
  198.7 31.2 %copy-start.6 = (bf16[64,4096]{1,0:T(8,128)(2,1)S(1)}, bf16[64,4096]{1,0:T(8,128)(2,1)}, u32[]{:S(2)}) copy-start(bf16[64,4096]{1,0:T(8,128)(2,1)} %copy-done.5) | copy-start | bytes 1572868
  215.2 4.6 %collective-permute-start.35 = (bf16[2,64,768]{2,1,0:T(8,128)(2,1)S(1)}, bf16[2,64,768]{2,1,0:T(8,128)(2,1)S(1)}, u32[]{:S(2)}, u32[]{:S(2)}) collective-permute-start(bf16[2,64,768]{2,1,0:T(8,128)(2,1)S(1)} %add_add_fusion.rest_0_), channel_id=1, source_target_pairs={{0,16},{4,20},{8,24},{12,28},{16,0},{20,4},{24,8},{28,12},{1,17},{... | collective-permute-start | bytes 589832 | tf_op jit(solution)/shard_map/ppermute | solution.py:21
  216.2 4.8 %collective-permute-start.34 = (bf16[2,64,768]{2,1,0:T(8,128)(2,1)S(1)}, bf16[2,64,768]{2,1,0:T(8,128)(2,1)S(1)}, u32[]{:S(2)}, u32[]{:S(2)}) collective-permute-start(bf16[2,64,768]{2,1,0:T(8,128)(2,1)S(1)} %add_add_fusion.rest_0_), channel_id=1, source_target_pairs={{0,8},{4,12},{8,0},{12,4},{16,24},{20,28},{24,16},{28,20},{1,9},{5... | collective-permute-start | bytes 589832 | tf_op jit(solution)/shard_map/ppermute | solution.py:21
  219.8 6.7 %collective-permute-start.36 = (bf16[1,64,768]{2,1,0:T(8,128)(2,1)S(1)}, bf16[1,64,768]{2,1,0:T(8,128)(2,1)S(1)}, u32[]{:S(2)}, u32[]{:S(2)}) collective-permute-start(bf16[1,64,768]{2,1,0:T(8,128)(2,1)S(1)} %slice.67), channel_id=1, source_target_pairs={{0,8},{4,12},{8,0},{12,4},{16,24},{20,28},{24,16},{28,20},{1,9},{5... | collective-permute-start | bytes 294920 | tf_op jit(solution)/shard_map/ppermute | solution.py:21
  221.0 6.6 %collective-permute-start.37 = (bf16[1,64,768]{2,1,0:T(8,128)(2,1)S(1)}, bf16[1,64,768]{2,1,0:T(8,128)(2,1)S(1)}, u32[]{:S(2)}, u32[]{:S(2)}) collective-permute-start(bf16[1,64,768]{2,1,0:T(8,128)(2,1)S(1)} %slice.68), channel_id=1, source_target_pairs={{0,16},{4,20},{8,24},{12,28},{16,0},{20,4},{24,8},{28,12},{1,17},{... | collective-permute-start | bytes 294920 | tf_op jit(solution)/shard_map/ppermute | solution.py:21
  221.6 8.4 %collective-permute-start.38 = (bf16[2,64,768]{2,1,0:T(8,128)(2,1)S(1)}, bf16[2,64,768]{2,1,0:T(8,128)(2,1)S(1)}, u32[]{:S(2)}, u32[]{:S(2)}) collective-permute-start(bf16[2,64,768]{2,1,0:T(8,128)(2,1)S(1)} %add_add_fusion.rest_0_), channel_id=1, source_target_pairs={{0,4},{4,0},{8,12},{12,8},{16,20},{20,16},{24,28},{28,24},{1,5},{5... | collective-permute-start | bytes 589832 | tf_op jit(solution)/shard_map/ppermute | solution.py:21
  225.9 5.0 %collective-permute-start.39 = (bf16[2,64,768]{2,1,0:T(8,128)(2,1)S(1)}, bf16[2,64,768]{2,1,0:T(8,128)(2,1)S(1)}, u32[]{:S(2)}, u32[]{:S(2)}) collective-permute-start(bf16[2,64,768]{2,1,0:T(8,128)(2,1)S(1)} %collective-permute-done.34.rest_1_), channel_id=1, source_target_pairs={{0,4},{4,0},{8,12},{12,8},{16,20},{20,16},{24,28},{28,24},{1,5},{5... | collective-permute-start | bytes 589832 | tf_op jit(solution)/shard_map/ppermute | solution.py:21
  226.0 4.9 %collective-permute-start.40 = (bf16[2,64,768]{2,1,0:T(8,128)(2,1)S(1)}, bf16[2,64,768]{2,1,0:T(8,128)(2,1)S(1)}, u32[]{:S(2)}, u32[]{:S(2)}) collective-permute-start(bf16[2,64,768]{2,1,0:T(8,128)(2,1)S(1)} %collective-permute-done.35.rest_2_), channel_id=1, source_target_pairs={{0,4},{4,0},{8,12},{12,8},{16,20},{20,16},{24,28},{28,24},{1,5},{5... | collective-permute-start | bytes 589832 | tf_op jit(solution)/shard_map/ppermute | solution.py:21
  226.4 3.6 %collective-permute-start.41 = (bf16[1,64,768]{2,1,0:T(8,128)(2,1)S(1)}, bf16[1,64,768]{2,1,0:T(8,128)(2,1)S(1)}, u32[]{:S(2)}, u32[]{:S(2)}) collective-permute-start(bf16[1,64,768]{2,1,0:T(8,128)(2,1)S(1)} %collective-permute-done.36.rest_3_), channel_id=1, source_target_pairs={{0,4},{4,0},{8,12},{12,8},{16,20},{20,16},{24,28},{28,24},{1,5},{5... | collective-permute-start | bytes 294920 | tf_op jit(solution)/shard_map/ppermute | solution.py:21
  227.6 3.2 %collective-permute-start.42 = (bf16[1,64,768]{2,1,0:T(8,128)(2,1)S(1)}, bf16[1,64,768]{2,1,0:T(8,128)(2,1)S(1)}, u32[]{:S(2)}, u32[]{:S(2)}) collective-permute-start(bf16[1,64,768]{2,1,0:T(8,128)(2,1)S(1)} %collective-permute-done.37.rest_4_), channel_id=1, source_target_pairs={{0,4},{4,0},{8,12},{12,8},{16,20},{20,16},{24,28},{28,24},{1,5},{5... | collective-permute-start | bytes 294920 | tf_op jit(solution)/shard_map/ppermute | solution.py:21
  (31 other events, 311.8 us)

commit v4 on v3

--- a/solution.py
+++ b/solution.py
@@ -254,7 +254,7 @@
             k = pair + tap + first
             part = ref[tap].astype(F32)
             for q in range(4):
-                wide[q, pl.ds(k, 64, stride=16), :] = part[:, 128 * q : 128 * q + 128]
+                wide[q, pl.ds(k, 64, stride=17), :] = part[:, 128 * q : 128 * q + 128]
             mats[k] = part[:, 512:768]
     aux = mats[15]
     norm, scale = stat[0:1], stat[1:2]
@@ -263,9 +263,10 @@
     ratio = gains / norm
     for q in range(4):
         lanes = slice(128 * q, 128 * q + 128)
-        part = sec_ref[:, :, lanes].astype(F32).reshape(1024, 128)
-        grad = scale[:, lanes] * (wide[q] - ratio[:, lanes] * part)
-        sec_out[:, :, lanes] = grad.reshape(64, 16, 128)
+        for o in range(64):
+            part = sec_ref[o, :, lanes].astype(F32)
+            grad = wide[q, 17 * o : 17 * o + 16, :] - ratio[:, lanes] * part
+            sec_out[o, :, lanes] = scale[:, lanes] * grad
     rows[...] = jnp.zeros_like(rows)
     for index, ref in enumerate((gt, gm, gk)):
         rows[3 * index : 3 * index + 3, 0:64] = ref[...].astype(F32)
@@ -334,11 +335,11 @@
     *rest,
 ):
     pieces, rest = rest[:10], rest[10:]
-    hid_out, act_out, mix_out, dsi_out = rest[0:4]
+    hid_out, act_out, mix_out, inner_out = rest[0:4]
     sact_out, mask_out, stat_out = rest[4:7]
     outs = rest[7:11]
     wsec, wblk, cat, bias, wide, turned, flat = rest[11:18]
-    hids, mixs, dsis, acts = rest[18:21], rest[21:24], rest[24:27], rest[27:30]
+    hids, mixs, inners, acts = rest[18:21], rest[21:24], rest[24:27], rest[27:30]
     wsem, ssem = rest[30:]
     chan = places[1]
     rows = sact_out.shape[0]
@@ -392,10 +393,10 @@
         enter(0, q, nt(left, right) + bias[0:1])
         return carry
 
-    lax.fori_loop(0, 8, section, 0)
+    lax.fori_loop(0, 8, section, 0, unroll=4)
     for b in range(3):
         dilate = 3**b
-        act, mix, dsi, hid = acts[b], mixs[b], dsis[b], hids[b]
+        act, mix, sum_in, hid = acts[b], mixs[b], inners[b], hids[b]
         if b < 2:
             move_near(act, mask_out, dilate)
         else:
@@ -412,21 +413,18 @@
             inner = nt(jnp.concatenate(left, axis=0), right)
             for n in range(2):
                 half = phase_rows(inner, n) + bias[1 + b : 2 + b]
-                value, turn, product = silu_half(half)
-                mix[2 * q + n] = value.astype(BF16)
-                dsi[2 * q + n] = slope_twice(
-                    half.astype(BF16), turn.astype(BF16), product.astype(BF16)
-                )
+                mix[2 * q + n] = silu_half(half)[0].astype(BF16)
+                sum_in[2 * q + n] = half.astype(BF16)
 
         def blend(q):
             left = []
             for r in (2 * q, 2 * q + 1):
                 left.append(jnp.concatenate([mix[r], hid[r]], axis=1))
             right = jnp.concatenate([wblk[5 * b + 3], wblk[5 * b + 4]], axis=1)
-            total = nt(jnp.concatenate(left, axis=0), right)
+            totals = [nt(part, right) for part in left]
             for n in range(2):
                 r = 2 * q + n
-                after = phase_rows(total, n) + (bias[4 + b : 5 + b] + bias[7 + b : 8 + b])
+                after = totals[n] + (bias[4 + b : 5 + b] + bias[7 + b : 8 + b])
                 if b < 2:
                     enter(b + 1, r, after)
                 else:
@@ -445,7 +443,7 @@
         lax.fori_loop(1, 4, both, 0)
         blend(3)
         keep(mix, mix_out, b)
-        keep(dsi, dsi_out, b)
+        keep(sum_in, inner_out, b)
 
     def turn(q, carry):
         start = pitch * (q // 2) + 128 * lax.rem(q, 2)
@@ -482,14 +480,21 @@
     hid_in,
     act_in,
     mix_in,
-    dsi_in,
+    inner_in,
     *rest,
 ):
     pieces, rest = rest[:10], rest[10:]
-    even_out, odd_out = rest[0:2]
-    sgrads = rest[2:6]
-    (wsec, wblk, turned, sigs, wide, grad, inner_a, inner_b, mix, hid, act, dsi) = rest[6:18]
-    (acc_one, acc_three, through, sums, staged, wsem, vsem, csem, bsem, osem) = rest[18:]
+    sums_out = rest[0:6]
+    sgrads = rest[6:10]
+    targets = [(sums_out[0], 6), (sums_out[1].at[0], 2), (sums_out[1].at[1], 4), (sums_out[2], 0)]
+    targets = targets + [
+        (sums_out[3], 7),
+        (sums_out[4].at[0], 3),
+        (sums_out[4].at[1], 5),
+        (sums_out[5], 1),
+    ]
+    (wsec, wblk, turned, sigs, wide, grad, inner_a, inner_b, mix, hid, act, halves) = rest[10:22]
+    (acc_one, acc_three, through, sums, staged, wsem, vsem, csem, bsem, osem) = rest[22:]
     pitch = 4 * (sact_ref.shape[0] - 2 * HALO) // 8 + 1
     turn_index, chan = places[0], places[1]
     rows = mask_ref.shape[1]
@@ -511,7 +516,7 @@
     def kept(b):
         slot = b % 2
         return [
-            pltpu.make_async_copy(dsi_in.at[b], dsi.at[slot], bsem.at[slot, 0]),
+            pltpu.make_async_copy(inner_in.at[b], halves.at[slot], bsem.at[slot, 0]),
             pltpu.make_async_copy(mix_in.at[b, :, 0:own], mix.at[slot], bsem.at[slot, 1]),
             pltpu.make_async_copy(hid_in.at[b], hid.at[slot], bsem.at[slot, 2]),
             pltpu.make_async_copy(act_in.at[b, :, 0:own], act.at[slot], bsem.at[slot, 3]),
@@ -563,8 +568,9 @@
         acc_one[...] += tn(two(grad, q, own), both)
         for n in range(2):
             r = 2 * q + n
-            part = down[n * rows : n * rows + rows] * dsi[slot, r].astype(F32)
-            part = part.astype(BF16)
+            half = halves[slot, r].astype(F32)
+            slope = slope_twice(half, *silu_half(half)[1:])
+            part = (down[n * rows : n * rows + rows] * slope).astype(BF16)
             inner[9 + r] = part
             if b == 2:
                 move_each(inner, mask_ref, r, part)
@@ -667,12 +673,26 @@
     through[...] = jnp.zeros_like(through)
     sact = sact_ref[0:own]
 
+    def send(pair):
+        place = pair ^ turn_index
+        source = staged.at[pl.ds(2 * pair, 2)]
+        for out, place_of in targets:
+
+            @pl.when(place == place_of)
+            def _(out=out):
+                pltpu.make_async_copy(source, out, osem).start()
+
     def collect(q, carry):
         left = jnp.concatenate([last[2 * q, 0:own], last[2 * q + 1, 0:own]], axis=1)
         through[...] += nn(left, wsec[pl.ds(2 * q, 2)].reshape(512, 512))
         grads = tn(left, sact).astype(BF16)
         staged[2 * q, :, 0:512] = grads[0:256]
         staged[2 * q + 1, :, 0:512] = grads[256:512]
+
+        @pl.when(q < 7)
+        def _():
+            send(q)
+
         return carry
 
     lax.fori_loop(0, 8, collect, 0)
@@ -691,21 +711,7 @@
     for part in range(4):
         staged[15, 64 * part : 64 * part + 64, 640:768] = gain_rows
 
-    def finish(pair, carry):
-        place = pair ^ turn_index
-        source = staged.at[pl.ds(2 * pair, 2)]
-
-        @pl.when(lax.rem(place, 2) == 0)
-        def _():
-            pltpu.make_async_copy(source, even_out.at[place // 2], osem).start()
-
-        @pl.when(lax.rem(place, 2) == 1)
-        def _():
-            pltpu.make_async_copy(source, odd_out.at[place // 2], osem).start()
-
-        return carry
-
-    lax.fori_loop(0, 8, finish, 0)
+    send(7)
     for k, out in enumerate(sgrads):
         lanes = pl.ds(pl.multiple_of(128 * (chan ^ k), 128), 128)
         half = 0.5 * sigs[k].reshape(own, 128).astype(F32)
@@ -717,7 +723,7 @@
         groups = [wide[0, (count + 1) * n : (count + 1) * n + count, :] for n in range(16)]
         out[...] = (jnp.concatenate(groups, axis=0) * slope).astype(BF16)
     for pair in range(8):
-        pltpu.make_async_copy(staged.at[pl.ds(2 * pair, 2)], even_out.at[0], osem).wait()
+        pltpu.make_async_copy(staged.at[pl.ds(2 * pair, 2)], sums_out[0], osem).wait()
 
 
 def shape_of(shape, kind=BF16):
@@ -790,7 +796,7 @@
         in_specs=[SPEC_SMEM] + [SPEC_VMEM] * 18,
         out_specs=[SPEC_VMEM] * 12,
         scratch_shapes=[
-            pltpu.VMEM((4, 1024, 128), F32),
+            pltpu.VMEM((4, 64 * 17, 128), F32),
             pltpu.VMEM((128, 128), F32),
             pltpu.VMEM((16, 64, 256), F32),
         ],
@@ -838,12 +844,18 @@
     own = rows - 2 * HALO
     return pl.pallas_call(
         backward_kernel,
-        out_shape=[shape_of((4, 2, 256, 768))] * 2 + [shape_of((own, 128))] * 4,
+        out_shape=[
+            shape_of((2, 256, 768)),
+            shape_of((2, 2, 256, 768)),
+            shape_of((2, 256, 768)),
+        ]
+        * 2
+        + [shape_of((own, 128))] * 4,
         in_specs=[SPEC_SMEM]
         + [SPEC_ANY] * 8
         + [SPEC_VMEM] * 3
         + [SPEC_ANY] * 14,
-        out_specs=[SPEC_ANY] * 2 + [SPEC_VMEM] * 4,
+        out_specs=[SPEC_ANY] * 6 + [SPEC_VMEM] * 4,
         scratch_shapes=[
             pltpu.VMEM((16, 256, 512), BF16),
             pltpu.VMEM((16, 256, 256), BF16),
@@ -948,28 +960,35 @@
     outs, seconds = lax.optimization_barrier((list(outs), seconds))
     received = [outs[0]] + [swap(outs[k], "chan", k) for k in (1, 2, 3)]
     results = run_backward(places, firsts, seconds, sact, masks, stat, kept, pieces)
-    even, odd, sgrads = results[0], results[1], results[2:]
-    odd, received = lax.optimization_barrier((odd, received))
+    far, sides, here, odd_far, odd_sides, odd_here = results[0:6]
+    sgrads = results[6:]
+    far, sides, here, odd_far, odd_sides, odd_here, sgrads, received = lax.optimization_barrier(
+        (far, sides, here, odd_far, odd_sides, odd_here, list(sgrads), received)
+    )
+
+    def chan_sum(values):
+        def cut_rows(place):
+            return lax.dynamic_slice_in_dim(values, place * 64, 64, axis=1)
+
+        parts = exchange(values, "chan", cut_rows)
+        return parts[0] + parts[1] + parts[2] + parts[3]
+
+    odd_sides = swap(odd_sides, "tm", 1)
+    far = far + swap(odd_far, "tm", 1)
+    odd_here = swap(odd_here, "tm", 1)
     output = jnp.zeros((64, 4 * frames), BF16)
     for k in range(4):
         output = lax.dynamic_update_slice_in_dim(output, received[k], (chan ^ k) * frames, axis=1)
-
-    quarter = even + swap(odd, "tm", 1)
-    far_a = swap(quarter[3, :1], "tm", 2)
-    far_b = swap(quarter[3, 1:], "tm", 4)
-    for_y = jnp.concatenate([quarter[2, :1] + far_a, quarter[2, 1:]], axis=0)
-    for_x = jnp.concatenate([quarter[1, :1], quarter[1, 1:] + far_b], axis=0)
-    summed = quarter[0] + swap(for_x, "tm", 2) + swap(for_y, "tm", 4)
-
-    def cut_rows(place):
-        return lax.dynamic_slice_in_dim(summed, place * 64, 64, axis=1)
-
-    parts = exchange(summed, "chan", cut_rows)
-    mine = parts[0] + parts[1] + parts[2] + parts[3]
+    across = chan_sum(far)
+    for_x, for_y = sides[0] + odd_sides[0], sides[1] + odd_sides[1]
+    summed = (here + odd_here) + swap(for_x, "tm", 2) + swap(for_y, "tm", 4)
+    summed, across = lax.optimization_barrier((summed, across))
+    mine = chan_sum(summed) + swap(across, "tm", 6)
     bit = 8
     while bit < tm_size:
         mine = mine + swap(mine, "tm", bit)
         bit = 2 * bit
+    mine, sgrads = lax.optimization_barrier((mine, sgrads))
     gathered = spread(mine)
 
     received = [sgrads[0]] + [swap(sgrads[k], "chan", k) for k in (1, 2, 3)]

time: 239 us -> 227 us (0.950)
  Pallas kernels: 80.6 us -> 74.2 us
  other arithmetic: 7.7 us -> 3.44 us
  waiting for transfers between devices: 88 us -> 84.5 us
    pallas_call x1, Pallas kernels: 27 us -> 23.4 us  [run_forward(): pl.pallas_call(forward_kernel, out_shape=out_shape, in_specs=[SPEC_SMEM]...]
    ppermute x41 -> x45, waiting for transfers between devices: 84.8 us -> 81.3 us  [swap(): return lax.ppermute(values, axis, xor_pairs(axis, bit))]
    ppermute x41 -> x45, starting transfers between devices: 48.8 us -> 49.4 us  [swap(): return lax.ppermute(values, axis, xor_pairs(axis, bit))]
  transfers between devices with their start and end apart: 43 -> 47, of which waited for: 24 -> 20; matrix products, arithmetic and copies ran while one was open for 2% -> 2% of each run, Pallas kernels for 30% -> 29%
where the time goes in v4:
time: 227 us
  waiting for transfers between devices  84.5 us (37%)
  Pallas kernels  74.2 us (33%)
  starting transfers between devices  55.9 us (25%)
  local copies, waits for them, and re-layouts  7.16 us (3%)
  other arithmetic  3.44 us (2%)
    ppermute x45, waiting for transfers between devices, swap(): return lax.ppermute(values, axis, xor_pairs(axis, bit))  81.3 us
    ppermute x45, starting transfers between devices, swap(): return lax.ppermute(values, axis, xor_pairs(axis, bit))  49.4 us
    pallas_call x1, Pallas kernels, run_backward(): pl.pallas_call(backward_kernel, out_shape=[shape_of((2, 256, 768)), shape...  38.6 us
    pallas_call x1, Pallas kernels, run_forward(): pl.pallas_call(forward_kernel, out_shape=out_shape, in_specs=[SPEC_SMEM]...  23.4 us
    pallas_call x1, Pallas kernels, run_finish(): pl.pallas_call(finish_kernel, out_shape=out_shape, in_specs=[SPEC_SMEM] +...  4.92 us
  transfers between devices with their start and end apart: 47, of which 20 were waited for; matrix products, arithmetic and copies ran while one was open for 2% of the time, Pallas kernels for 29%

profile of v4, /device:TPU:9, one launch (start us, length us, event | category | flops | bytes accessed | tf_op | source)
XLA Modules:
  0.0 226.6 jit_solution(10992681904846816703)
XLA Ops:
  1.3 3.3 %pack_weights.1 = bf16[2,64,768]{2,1,0:T(8,128)(2,1)} custom-call(s32[2]{0:T(128)} %pad_add_fusion.places, bf16[64,16,512]{2,1,0:T(8,128)(2,1)} %sec_ref.3, bf16[3,3,64,256]{3,2,1,0:T(8,128)(2,1)} %bitcast.16, bf16[3,64,256]{2,1,0:T(8,128)(2,1)} %mix_ref.3, bf16[3,64,256]{2,1,0:T(8,128)(2,1)} %skip_ref.3, bf16[1,64]{1,0:T(2,128)(2,1)} %bitcast.23, ...), custom_call_target="tpu_custom_call" | custom-call | flops 20000000 | bytes 3000000 | tf_op jit(solution)/shard_map/pack_weights/pallas_call | solution.py:747
  4.6 2.5 %collective-permute-start.1 = (bf16[2,64,768]{2,1,0:T(8,128)(2,1)}, bf16[2,64,768]{2,1,0:T(8,128)(2,1)S(1)}, u32[]{:S(2)}, u32[]{:S(2)}) collective-permute-start(bf16[2,64,768]{2,1,0:T(8,128)(2,1)} %pack_weights.1), channel_id=1, source_target_pairs={{0,2},{1,3},{2,0},{3,1},{4,6},{5,7},{6,4},{7,5},{8,10},{9,11},{10,... | collective-permute-start | bytes 589832 | tf_op jit(solution)/shard_map/ppermute | solution.py:21
  8.7 4.5 %collective-permute-start.3 = (bf16[80,128]{1,0:T(8,128)(2,1)S(1)}, bf16[80,128]{1,0:T(8,128)(2,1)S(1)}, u32[]{:S(2)}, u32[]{:S(2)}) collective-permute-start(bf16[80,128]{1,0:T(8,128)(2,1)S(1)} %pad_maximum_fusion.1), channel_id=1, source_target_pairs={{0,4},{4,8},{8,12},{12,16},{16,20},{20,24},{24,28},{1,5},{5,9},{9,... | collective-permute-start | bytes 61448 | tf_op jit(solution)/shard_map/ppermute | solution.py:942
  13.2 1.9 collective-permute-start.4
  15.2 3.2 %collective-permute-done.4.high = bf16[80,128]{1,0:T(8,128)(2,1)S(1)} collective-permute-done((bf16[80,128]{1,0:T(8,128)(2,1)S(1)}, bf16[80,128]{1,0:T(8,128)(2,1)S(1)}, u32[]{:S(2)}, u32[]{:S(2)}) %collective-permute-start.4) | collective-permute-done | bytes 20512 | tf_op jit(solution)/shard_map/ppermute | solution.py:943
  18.9 3.9 %pack_frames.1 = (bf16[13,64,128]{2,1,0:T(8,128)(2,1)}, bf16[13,64,128]{2,1,0:T(8,128)(2,1)}, bf16[13,64,128]{2,1,0:T(8,128)(2,1)}, bf16[13,64,128]{2,1,0:T(8,12...) custom-call(s32[2]{0:T(128)} %pad_add_fusion.places, ...), custom_call_target="tpu_custom_call" | custom-call | flops 1000000 | bytes 6000000 | tf_op jit(solution)/shard_map/pack_frames/pallas_call | solution.py:765
  22.9 1.3 collective-permute-done.2
  24.3 1.3 collective-permute-start.5
  25.6 1.2 collective-permute-start.6
  26.8 2.4 %collective-permute-start.8 = (bf16[13,64,128]{2,1,0:T(8,128)(2,1)}, bf16[13,64,128]{2,1,0:T(8,128)(2,1)S(1)}, u32[]{:S(2)}, u32[]{:S(2)}) collective-permute-start(bf16[13,64,128]{2,1,0:T(8,128)(2,1)} %get-tuple-element.111), channel_id=1, source_target_pairs={{0,2},{1,3},{2,0},{3,1},{4,6},{5,7},{6,4},{7,5},{8,10},{9,11},{10,... | collective-permute-start | bytes 638984 | tf_op jit(solution)/shard_map/ppermute | solution.py:21
  29.5 2.6 %collective-permute-done.7.sig1.first1 = bf16[13,64,128]{2,1,0:T(8,128)(2,1)S(1)} collective-permute-done((bf16[13,64,128]{2,1,0:T(8,128)(2,1)}, bf16[13,64,128]{2,1,0:T(8,128)(2,1)S(1)}, u32[]{:S(2)}, u32[]{:S(2)}) %collective-permute-start.7) | collective-permute-done | bytes 213024 | tf_op jit(solution)/shard_map/ppermute | solution.py:21
  32.0 4.6 %collective-permute-done.8.sig2.first2 = bf16[13,64,128]{2,1,0:T(8,128)(2,1)S(1)} collective-permute-done((bf16[13,64,128]{2,1,0:T(8,128)(2,1)}, bf16[13,64,128]{2,1,0:T(8,128)(2,1)S(1)}, u32[]{:S(2)}, u32[]{:S(2)}) %collective-permute-start.8) | collective-permute-done | bytes 213024 | tf_op jit(solution)/shard_map/ppermute | solution.py:21
  36.6 10.0 %collective-permute-done.9.sig3.first3 = bf16[13,64,128]{2,1,0:T(8,128)(2,1)S(1)} collective-permute-done((bf16[13,64,128]{2,1,0:T(8,128)(2,1)}, bf16[13,64,128]{2,1,0:T(8,128)(2,1)S(1)}, u32[]{:S(2)}, u32[]{:S(2)}) %collective-permute-start.9) | collective-permute-done | bytes 213024 | tf_op jit(solution)/shard_map/ppermute | solution.py:21
  47.7 1.3 collective-permute-start.13
  49.0 2.7 %collective-permute-start.11 = (bf16[29,64,128]{2,1,0:T(8,128)(2,1)S(1)}, bf16[29,64,128]{2,1,0:T(8,128)(2,1)}, u32[]{:S(2)}, u32[]{:S(2)}) collective-permute-start(bf16[29,64,128]{2,1,0:T(8,128)(2,1)S(1)} %copy-done.30), channel_id=1, source_target_pairs={{0,2},{1,3},{2,0},{3,1},{4,6},{5,7},{6,4},{7,5},{8,10},{9,11},{10,... | collective-permute-start | bytes 1425416 | tf_op jit(solution)/shard_map/ppermute | solution.py:21
  51.7 3.4 %collective-permute-done.12.rest_3_ = bf16[2,2,64,768]{3,2,1,0:T(8,128)(2,1)S(1)} collective-permute-done((bf16[2,2,64,768]{3,2,1,0:T(8,128)(2,1)S(1)}, bf16[2,2,64,768]{3,2,1,0:T(8,128)(2,1)S(1)}, u32[]{:S(2)}, u32[]{:S(2)}) %collective-permute-start.12) | collective-permute-done | bytes 393248 | tf_op jit(solution)/shard_map/ppermute | solution.py:21
  55.2 4.2 %collective-permute-start.14 = (bf16[4,2,64,768]{3,2,1,0:T(8,128)(2,1)S(1)}, bf16[4,2,64,768]{3,2,1,0:T(8,128)(2,1)}, u32[]{:S(2)}, u32[]{:S(2)}) collective-permute-start(bf16[4,2,64,768]{3,2,1,0:T(8,128)(2,1)S(1)} %pad_maximum_fusion.rest_0_), channel_id=1, source_target_pairs={{0,4},{4,0},{8,12},{12,8},{16,20},{20,16},{24,28},{28,24},{1,5},{5... | collective-permute-start | bytes 2359304 | tf_op jit(solution)/shard_map/ppermute | solution.py:21
  59.9 7.4 %collective-permute-done.10.second1 = bf16[29,64,128]{2,1,0:T(8,128)(2,1)} collective-permute-done((bf16[29,64,128]{2,1,0:T(8,128)(2,1)S(1)}, bf16[29,64,128]{2,1,0:T(8,128)(2,1)}, u32[]{:S(2)}, u32[]{:S(2)}) %collective-permute-start.10) | collective-permute-done | bytes 475168 | tf_op jit(solution)/shard_map/ppermute | solution.py:21
  67.3 2.9 %collective-permute-start.17 = (bf16[2,2,64,768]{3,2,1,0:T(8,128)(2,1)S(1)}, bf16[2,2,64,768]{3,2,1,0:T(8,128)(2,1)S(1)}, u32[]{:S(2)}, u32[]{:S(2)}) collective-permute-start(bf16[2,2,64,768]{3,2,1,0:T(8,128)(2,1)S(1)} %collective-permute-done.12.rest_3_), channel_id=1, source_target_pairs={{0,4},{4,0},{8,12},{12,8},{16,20},{20,16},{24,28},{28,24},{1,5},{5... | collective-permute-start | bytes 1179656 | tf_op jit(solution)/shard_map/ppermute | solution.py:21
  70.2 3.5 %collective-permute-start.18 = (bf16[2,2,64,768]{3,2,1,0:T(8,128)(2,1)}, bf16[2,2,64,768]{3,2,1,0:T(8,128)(2,1)}, u32[]{:S(2)}, u32[]{:S(2)}) collective-permute-start(bf16[2,2,64,768]{3,2,1,0:T(8,128)(2,1)} %collective-permute-done.13.rest_4_), channel_id=1, source_target_pairs={{0,4},{4,0},{8,12},{12,8},{16,20},{20,16},{24,28},{28,24},{1,5},{5... | collective-permute-start | bytes 1179656 | tf_op jit(solution)/shard_map/ppermute | solution.py:21
  74.5 1.0 collective-permute-done.18.rest_9_
  75.5 0.8 broadcast_in_dim.18.ids_ref
  76.4 23.4 %forward_blocks.1 = (bf16[3,8,528,256]{3,2,1,0:T(8,128)(2,1)}, bf16[3,8,528,256]{3,2,1,0:T(8,128)(2,1)}, bf16[3,8,528,256]{3,2,1,0:T(8,128)(2,1)}, bf16[3,8,528,...) custom-call(s32[2]{0:T(128)} %pad_add_fusion.places, ...), custom_call_target="tpu_custom_call" | custom-call | flops 10519314432 | bytes 50000000 | tf_op jit(solution)/shard_map/forward_blocks/pallas_call | solution.py:819
  99.8 2.7 %collective-permute-start.20 = (bf16[64,4096]{1,0:T(8,128)(2,1)}, bf16[64,4096]{1,0:T(8,128)(2,1)S(1)}, u32[]{:S(2)}, u32[]{:S(2)}) collective-permute-start(bf16[64,4096]{1,0:T(8,128)(2,1)} %get-tuple-element.160), channel_id=1, source_target_pairs={{0,1},{1,0},{2,3},{3,2},{4,5},{5,4},{6,7},{7,6},{8,9},{9,8},{10,11... | collective-permute-start | bytes 1572872 | tf_op jit(solution)/shard_map/ppermute | solution.py:21
  102.5 1.3 collective-permute-start.22
  103.8 38.6 %backward_blocks.1 = (bf16[2,256,768]{2,1,0:T(8,128)(2,1)}, bf16[2,2,256,768]{3,2,1,0:T(8,128)(2,1)}, bf16[2,256,768]{2,1,0:T(8,128)(2,1)}, bf16[2,256,768]{2,1,...) custom-call(s32[2]{0:T(128)} %pad_add_fusion.places, ...), custom_call_target="tpu_custom_call" | custom-call | flops 21038628864 | bytes 60000000 | tf_op jit(solution)/shard_map/backward_blocks/pallas_call | solution.py:845
  142.4 7.1 %collective-permute-done.22 = bf16[64,4096]{1,0:T(8,128)(2,1)S(1)} collective-permute-done((bf16[64,4096]{1,0:T(8,128)(2,1)}, bf16[64,4096]{1,0:T(8,128)(2,1)S(1)}, u32[]{:S(2)}, u32[]{:S(2)}) %collective-permute-start.22) | collective-permute-done | bytes 524320 | tf_op jit(solution)/shard_map/ppermute | solution.py:21
  149.5 0.8 copy-done.7
  150.3 1.1 collective-permute-start.24
  151.9 5.0 %collective-permute-done.27 = bf16[2,256,768]{2,1,0:T(8,128)(2,1)} collective-permute-done((bf16[2,256,768]{2,1,0:T(8,128)(2,1)}, bf16[2,256,768]{2,1,0:T(8,128)(2,1)}, u32[]{:S(2)}, u32[]{:S(2)}) %collective-permute-start.27) | collective-permute-done | bytes 786464 | tf_op jit(solution)/shard_map/ppermute | solution.py:21
  156.9 1.6 add.111
  158.8 1.5 collective-permute-start.25
  161.1 1.4 collective-permute-start.29
  162.5 2.4 %collective-permute-done.28 = bf16[2,64,768]{2,1,0:T(8,128)(2,1)S(1)} collective-permute-done((bf16[2,64,768]{2,1,0:T(8,128)(2,1)S(1)}, bf16[2,64,768]{2,1,0:T(8,128)(2,1)S(1)}, u32[]{:S(2)}, u32[]{:S(2)}) %collective-permute-start.28) | collective-permute-done | bytes 196640 | tf_op jit(solution)/shard_map/ppermute | solution.py:21
  165.2 9.2 %collective-permute-done.29 = bf16[2,64,768]{2,1,0:T(8,128)(2,1)S(1)} collective-permute-done((bf16[2,64,768]{2,1,0:T(8,128)(2,1)S(1)}, bf16[2,64,768]{2,1,0:T(8,128)(2,1)S(1)}, u32[]{:S(2)}, u32[]{:S(2)}) %collective-permute-start.29) | collective-permute-done | bytes 196640 | tf_op jit(solution)/shard_map/ppermute | solution.py:21
  174.4 6.7 %collective-permute-done.30 = bf16[2,64,768]{2,1,0:T(8,128)(2,1)S(1)} collective-permute-done((bf16[2,64,768]{2,1,0:T(8,128)(2,1)S(1)}, bf16[2,64,768]{2,1,0:T(8,128)(2,1)S(1)}, u32[]{:S(2)}, u32[]{:S(2)}) %collective-permute-start.30) | collective-permute-done | bytes 196640 | tf_op jit(solution)/shard_map/ppermute | solution.py:21
  181.7 0.8 collective-permute-start.32
  182.5 1.8 collective-permute-start.33
  184.6 2.4 %collective-permute-done.31 = bf16[2,64,768]{2,1,0:T(8,128)(2,1)S(1)} collective-permute-done((bf16[2,64,768]{2,1,0:T(8,128)(2,1)S(1)}, bf16[2,64,768]{2,1,0:T(8,128)(2,1)S(1)}, u32[]{:S(2)}, u32[]{:S(2)}) %collective-permute-start.31) | collective-permute-done | bytes 196640 | tf_op jit(solution)/shard_map/ppermute | solution.py:21
  187.0 2.7 %collective-permute-done.32 = bf16[2,64,768]{2,1,0:T(8,128)(2,1)S(1)} collective-permute-done((bf16[2,64,768]{2,1,0:T(8,128)(2,1)S(1)}, bf16[2,64,768]{2,1,0:T(8,128)(2,1)S(1)}, u32[]{:S(2)}, u32[]{:S(2)}) %collective-permute-start.32) | collective-permute-done | bytes 196640 | tf_op jit(solution)/shard_map/ppermute | solution.py:21
  189.7 11.6 %collective-permute-done.33 = bf16[2,64,768]{2,1,0:T(8,128)(2,1)S(1)} collective-permute-done((bf16[2,64,768]{2,1,0:T(8,128)(2,1)S(1)}, bf16[2,64,768]{2,1,0:T(8,128)(2,1)S(1)}, u32[]{:S(2)}, u32[]{:S(2)}) %collective-permute-start.33) | collective-permute-done | bytes 196640 | tf_op jit(solution)/shard_map/ppermute | solution.py:21
  201.6 0.9 collective-permute-start.39
  203.0 2.2 collective-permute-start.37
  205.4 4.1 %collective-permute-start.42 = (bf16[2,64,768]{2,1,0:T(8,128)(2,1)S(1)}, bf16[2,64,768]{2,1,0:T(8,128)(2,1)S(1)}, u32[]{:S(2)}, u32[]{:S(2)}) collective-permute-start(bf16[2,64,768]{2,1,0:T(8,128)(2,1)S(1)} %add_add_fusion.1.rest_0_), channel_id=1, source_target_pairs={{0,4},{4,0},{8,12},{12,8},{16,20},{20,16},{24,28},{28,24},{1,5},{5... | collective-permute-start | bytes 589832 | tf_op jit(solution)/shard_map/ppermute | solution.py:21
  210.6 3.2 %collective-permute-start.43 = (bf16[2,64,768]{2,1,0:T(8,128)(2,1)S(1)}, bf16[2,64,768]{2,1,0:T(8,128)(2,1)S(1)}, u32[]{:S(2)}, u32[]{:S(2)}) collective-permute-start(bf16[2,64,768]{2,1,0:T(8,128)(2,1)S(1)} %collective-permute-done.38.rest_1_), channel_id=1, source_target_pairs={{0,4},{4,0},{8,12},{12,8},{16,20},{20,16},{24,28},{28,24},{1,5},{5... | collective-permute-start | bytes 589832 | tf_op jit(solution)/shard_map/ppermute | solution.py:21
  213.8 2.8 %collective-permute-done.37 = bf16[512,128]{1,0:T(8,128)(2,1)S(1)} collective-permute-done((bf16[512,128]{1,0:T(8,128)(2,1)S(1)}, bf16[512,128]{1,0:T(8,128)(2,1)S(1)}, u32[]{:S(2)}, u32[]{:S(2)}) %collective-permute-start.37) | collective-permute-done | bytes 131104 | tf_op jit(solution)/shard_map/ppermute | solution.py:21
  216.6 1.3 collective-permute-start.44
  221.5 4.9 %finish_weights.1 = (f32[64,16,512]{2,1,0:T(8,128)}, f32[1,512]{1,0:T(1,128)}, f32[1,64]{1,0:T(1,128)}, f32[3,3,64,256]{3,2,1,0:T(8,128)}, f32[3,64]{1,0:T(4,128...) custom-call(s32[2]{0:T(128)} %pad_add_fusion.places, ...), custom_call_target="tpu_custom_call" | custom-call | flops 20000000 | bytes 8000000 | tf_op jit(solution)/shard_map/finish_weights/pallas_call | solution.py:793
  (163 shorter events, 13.6 us)
Async XLA Ops:
  4.6 18.3 %collective-permute-start = (bf16[2,64,768]{2,1,0:T(8,128)(2,1)}, bf16[2,64,768]{2,1,0:T(8,128)(2,1)S(1)}, u32[]{:S(2)}, u32[]{:S(2)}) collective-permute-start(bf16[2,64,768]{2,1,0:T(8,128)(2,1)} %pack_weights.1), channel_id=1, source_target_pairs={{0,1},{1,0},{2,3},{3,2},{4,5},{5,4},{6,7},{7,6},{8,9},{9,8},{10,11... | collective-permute-start | bytes 589832 | tf_op jit(solution)/shard_map/ppermute | solution.py:21
  4.6 18.3 %collective-permute-start.1 = (bf16[2,64,768]{2,1,0:T(8,128)(2,1)}, bf16[2,64,768]{2,1,0:T(8,128)(2,1)S(1)}, u32[]{:S(2)}, u32[]{:S(2)}) collective-permute-start(bf16[2,64,768]{2,1,0:T(8,128)(2,1)} %pack_weights.1), channel_id=1, source_target_pairs={{0,2},{1,3},{2,0},{3,1},{4,6},{5,7},{6,4},{7,5},{8,10},{9,11},{10,... | collective-permute-start | bytes 589832 | tf_op jit(solution)/shard_map/ppermute | solution.py:21
  7.1 17.1 %collective-permute-start.2 = (bf16[2,64,768]{2,1,0:T(8,128)(2,1)}, bf16[2,64,768]{2,1,0:T(8,128)(2,1)S(1)}, u32[]{:S(2)}, u32[]{:S(2)}) collective-permute-start(bf16[2,64,768]{2,1,0:T(8,128)(2,1)} %pack_weights.1), channel_id=1, source_target_pairs={{0,3},{1,2},{2,1},{3,0},{4,7},{5,6},{6,5},{7,4},{8,11},{9,10},{10,... | collective-permute-start | bytes 589832 | tf_op jit(solution)/shard_map/ppermute | solution.py:21
  8.7 6.5 %collective-permute-start.3 = (bf16[80,128]{1,0:T(8,128)(2,1)S(1)}, bf16[80,128]{1,0:T(8,128)(2,1)S(1)}, u32[]{:S(2)}, u32[]{:S(2)}) collective-permute-start(bf16[80,128]{1,0:T(8,128)(2,1)S(1)} %pad_maximum_fusion.1), channel_id=1, source_target_pairs={{0,4},{4,8},{8,12},{12,16},{16,20},{20,24},{24,28},{1,5},{5,9},{9,... | collective-permute-start | bytes 61448 | tf_op jit(solution)/shard_map/ppermute | solution.py:942
  13.2 5.1 %collective-permute-start.4 = (bf16[80,128]{1,0:T(8,128)(2,1)S(1)}, bf16[80,128]{1,0:T(8,128)(2,1)S(1)}, u32[]{:S(2)}, u32[]{:S(2)}) collective-permute-start(bf16[80,128]{1,0:T(8,128)(2,1)S(1)} %pad_maximum_fusion.2), channel_id=1, source_target_pairs={{4,0},{8,4},{12,8},{16,12},{20,16},{24,20},{28,24},{5,1},{9,5},{13... | collective-permute-start | bytes 61448 | tf_op jit(solution)/shard_map/ppermute | solution.py:943
  24.3 52.0 %copy-start.3 = (bf16[4,2,64,768]{3,2,1,0:T(8,128)(2,1)}, bf16[4,2,64,768]{3,2,1,0:T(8,128)(2,1)S(1)}, u32[]{:S(2)}) copy-start(bf16[4,2,64,768]{3,2,1,0:T(8,128)(2,1)S(1)} %pad_maximum_fusion.rest_0_) | copy-start | bytes 2359300
  24.3 22.3 %collective-permute-start.5 = (bf16[4,2,64,768]{3,2,1,0:T(8,128)(2,1)S(1)}, bf16[4,2,64,768]{3,2,1,0:T(8,128)(2,1)S(1)}, u32[]{:S(2)}, u32[]{:S(2)}) collective-permute-start(bf16[4,2,64,768]{3,2,1,0:T(8,128)(2,1)S(1)} %pad_maximum_fusion.rest_0_), channel_id=1, source_target_pairs={{0,8},{4,12},{8,0},{12,4},{16,24},{20,28},{24,16},{28,20},{1,9},{5... | collective-permute-start | bytes 2359304 | tf_op jit(solution)/shard_map/ppermute | solution.py:21
  25.6 21.7 %collective-permute-start.6 = (bf16[4,2,64,768]{3,2,1,0:T(8,128)(2,1)S(1)}, bf16[4,2,64,768]{3,2,1,0:T(8,128)(2,1)S(1)}, u32[]{:S(2)}, u32[]{:S(2)}) collective-permute-start(bf16[4,2,64,768]{3,2,1,0:T(8,128)(2,1)S(1)} %pad_maximum_fusion.rest_0_), channel_id=1, source_target_pairs={{0,16},{4,20},{8,24},{12,28},{16,0},{20,4},{24,8},{28,12},{1,17},{... | collective-permute-start | bytes 2359304 | tf_op jit(solution)/shard_map/ppermute | solution.py:21
  26.8 5.2 %collective-permute-start.7 = (bf16[13,64,128]{2,1,0:T(8,128)(2,1)}, bf16[13,64,128]{2,1,0:T(8,128)(2,1)S(1)}, u32[]{:S(2)}, u32[]{:S(2)}) collective-permute-start(bf16[13,64,128]{2,1,0:T(8,128)(2,1)} %get-tuple-element.110), channel_id=1, source_target_pairs={{0,1},{1,0},{2,3},{3,2},{4,5},{5,4},{6,7},{7,6},{8,9},{9,8},{10,11... | collective-permute-start | bytes 638984 | tf_op jit(solution)/shard_map/ppermute | solution.py:21
  26.8 9.8 %collective-permute-start.8 = (bf16[13,64,128]{2,1,0:T(8,128)(2,1)}, bf16[13,64,128]{2,1,0:T(8,128)(2,1)S(1)}, u32[]{:S(2)}, u32[]{:S(2)}) collective-permute-start(bf16[13,64,128]{2,1,0:T(8,128)(2,1)} %get-tuple-element.111), channel_id=1, source_target_pairs={{0,2},{1,3},{2,0},{3,1},{4,6},{5,7},{6,4},{7,5},{8,10},{9,11},{10,... | collective-permute-start | bytes 638984 | tf_op jit(solution)/shard_map/ppermute | solution.py:21
  29.3 17.4 %collective-permute-start.9 = (bf16[13,64,128]{2,1,0:T(8,128)(2,1)}, bf16[13,64,128]{2,1,0:T(8,128)(2,1)S(1)}, u32[]{:S(2)}, u32[]{:S(2)}) collective-permute-start(bf16[13,64,128]{2,1,0:T(8,128)(2,1)} %get-tuple-element.112), channel_id=1, source_target_pairs={{0,3},{1,2},{2,1},{3,0},{4,7},{5,6},{6,5},{7,4},{8,11},{9,10},{10,... | collective-permute-start | bytes 638984 | tf_op jit(solution)/shard_map/ppermute | solution.py:21
  47.3 7.8 %collective-permute-start.12 = (bf16[2,2,64,768]{3,2,1,0:T(8,128)(2,1)S(1)}, bf16[2,2,64,768]{3,2,1,0:T(8,128)(2,1)S(1)}, u32[]{:S(2)}, u32[]{:S(2)}) collective-permute-start(bf16[2,2,64,768]{3,2,1,0:T(8,128)(2,1)S(1)} %slice.40), channel_id=1, source_target_pairs={{0,8},{4,12},{8,0},{12,4},{16,24},{20,28},{24,16},{28,20},{1,9},{5... | collective-permute-start | bytes 1179656 | tf_op jit(solution)/shard_map/ppermute | solution.py:21
  47.7 7.5 %collective-permute-start.13 = (bf16[2,2,64,768]{3,2,1,0:T(8,128)(2,1)S(1)}, bf16[2,2,64,768]{3,2,1,0:T(8,128)(2,1)}, u32[]{:S(2)}, u32[]{:S(2)}) collective-permute-start(bf16[2,2,64,768]{3,2,1,0:T(8,128)(2,1)S(1)} %slice.41), channel_id=1, source_target_pairs={{0,16},{4,20},{8,24},{12,28},{16,0},{20,4},{24,8},{28,12},{1,17},{... | collective-permute-start | bytes 1179656 | tf_op jit(solution)/shard_map/ppermute | solution.py:21
  49.0 18.3 %collective-permute-start.10 = (bf16[29,64,128]{2,1,0:T(8,128)(2,1)S(1)}, bf16[29,64,128]{2,1,0:T(8,128)(2,1)}, u32[]{:S(2)}, u32[]{:S(2)}) collective-permute-start(bf16[29,64,128]{2,1,0:T(8,128)(2,1)S(1)} %copy-done.31), channel_id=1, source_target_pairs={{0,1},{1,0},{2,3},{3,2},{4,5},{5,4},{6,7},{7,6},{8,9},{9,8},{10,11... | collective-permute-start | bytes 1425416 | tf_op jit(solution)/shard_map/ppermute | solution.py:21
  49.0 21.3 %collective-permute-start.11 = (bf16[29,64,128]{2,1,0:T(8,128)(2,1)S(1)}, bf16[29,64,128]{2,1,0:T(8,128)(2,1)}, u32[]{:S(2)}, u32[]{:S(2)}) collective-permute-start(bf16[29,64,128]{2,1,0:T(8,128)(2,1)S(1)} %copy-done.30), channel_id=1, source_target_pairs={{0,2},{1,3},{2,0},{3,1},{4,6},{5,7},{6,4},{7,5},{8,10},{9,11},{10,... | collective-permute-start | bytes 1425416 | tf_op jit(solution)/shard_map/ppermute | solution.py:21
  55.2 20.3 %collective-permute-start.14 = (bf16[4,2,64,768]{3,2,1,0:T(8,128)(2,1)S(1)}, bf16[4,2,64,768]{3,2,1,0:T(8,128)(2,1)}, u32[]{:S(2)}, u32[]{:S(2)}) collective-permute-start(bf16[4,2,64,768]{3,2,1,0:T(8,128)(2,1)S(1)} %pad_maximum_fusion.rest_0_), channel_id=1, source_target_pairs={{0,4},{4,0},{8,12},{12,8},{16,20},{20,16},{24,28},{28,24},{1,5},{5... | collective-permute-start | bytes 2359304 | tf_op jit(solution)/shard_map/ppermute | solution.py:21
  59.4 16.1 %collective-permute-start.15 = (bf16[4,2,64,768]{3,2,1,0:T(8,128)(2,1)S(1)}, bf16[4,2,64,768]{3,2,1,0:T(8,128)(2,1)}, u32[]{:S(2)}, u32[]{:S(2)}) collective-permute-start(bf16[4,2,64,768]{3,2,1,0:T(8,128)(2,1)S(1)} %collective-permute-done.5.rest_1_), channel_id=1, source_target_pairs={{0,4},{4,0},{8,12},{12,8},{16,20},{20,16},{24,28},{28,24},{1,5},{5... | collective-permute-start | bytes 2359304 | tf_op jit(solution)/shard_map/ppermute | solution.py:21
  59.4 16.1 %collective-permute-start.16 = (bf16[4,2,64,768]{3,2,1,0:T(8,128)(2,1)S(1)}, bf16[4,2,64,768]{3,2,1,0:T(8,128)(2,1)}, u32[]{:S(2)}, u32[]{:S(2)}) collective-permute-start(bf16[4,2,64,768]{3,2,1,0:T(8,128)(2,1)S(1)} %collective-permute-done.6.rest_2_), channel_id=1, source_target_pairs={{0,4},{4,0},{8,12},{12,8},{16,20},{20,16},{24,28},{28,24},{1,5},{5... | collective-permute-start | bytes 2359304 | tf_op jit(solution)/shard_map/ppermute | solution.py:21
  67.3 7.1 %collective-permute-start.17 = (bf16[2,2,64,768]{3,2,1,0:T(8,128)(2,1)S(1)}, bf16[2,2,64,768]{3,2,1,0:T(8,128)(2,1)S(1)}, u32[]{:S(2)}, u32[]{:S(2)}) collective-permute-start(bf16[2,2,64,768]{3,2,1,0:T(8,128)(2,1)S(1)} %collective-permute-done.12.rest_3_), channel_id=1, source_target_pairs={{0,4},{4,0},{8,12},{12,8},{16,20},{20,16},{24,28},{28,24},{1,5},{5... | collective-permute-start | bytes 1179656 | tf_op jit(solution)/shard_map/ppermute | solution.py:21
  70.2 5.2 %collective-permute-start.18 = (bf16[2,2,64,768]{3,2,1,0:T(8,128)(2,1)}, bf16[2,2,64,768]{3,2,1,0:T(8,128)(2,1)}, u32[]{:S(2)}, u32[]{:S(2)}) collective-permute-start(bf16[2,2,64,768]{3,2,1,0:T(8,128)(2,1)} %collective-permute-done.13.rest_4_), channel_id=1, source_target_pairs={{0,4},{4,0},{8,12},{12,8},{16,20},{20,16},{24,28},{28,24},{1,5},{5... | collective-permute-start | bytes 1179656 | tf_op jit(solution)/shard_map/ppermute | solution.py:21
  74.4 25.4 %collective-permute-start.19 = (bf16[29,64,128]{2,1,0:T(8,128)(2,1)}, bf16[29,64,128]{2,1,0:T(8,128)(2,1)S(1)}, u32[]{:S(2)}, u32[]{:S(2)}) collective-permute-start(bf16[29,64,128]{2,1,0:T(8,128)(2,1)} %get-tuple-element.137), channel_id=1, source_target_pairs={{0,3},{1,2},{2,1},{3,0},{4,7},{5,6},{6,5},{7,4},{8,11},{9,10},{10,... | collective-permute-start | bytes 1425416 | tf_op jit(solution)/shard_map/ppermute | solution.py:21
  99.8 42.5 %collective-permute-start.20 = (bf16[64,4096]{1,0:T(8,128)(2,1)}, bf16[64,4096]{1,0:T(8,128)(2,1)S(1)}, u32[]{:S(2)}, u32[]{:S(2)}) collective-permute-start(bf16[64,4096]{1,0:T(8,128)(2,1)} %get-tuple-element.160), channel_id=1, source_target_pairs={{0,1},{1,0},{2,3},{3,2},{4,5},{5,4},{6,7},{7,6},{8,9},{9,8},{10,11... | collective-permute-start | bytes 1572872 | tf_op jit(solution)/shard_map/ppermute | solution.py:21
  102.5 39.9 %collective-permute-start.21 = (bf16[64,4096]{1,0:T(8,128)(2,1)}, bf16[64,4096]{1,0:T(8,128)(2,1)S(1)}, u32[]{:S(2)}, u32[]{:S(2)}) collective-permute-start(bf16[64,4096]{1,0:T(8,128)(2,1)} %get-tuple-element.161), channel_id=1, source_target_pairs={{0,2},{1,3},{2,0},{3,1},{4,6},{5,7},{6,4},{7,5},{8,10},{9,11},{10,... | collective-permute-start | bytes 1572872 | tf_op jit(solution)/shard_map/ppermute | solution.py:21
  102.5 47.0 %collective-permute-start.22 = (bf16[64,4096]{1,0:T(8,128)(2,1)}, bf16[64,4096]{1,0:T(8,128)(2,1)S(1)}, u32[]{:S(2)}, u32[]{:S(2)}) collective-permute-start(bf16[64,4096]{1,0:T(8,128)(2,1)} %get-tuple-element.162), channel_id=1, source_target_pairs={{0,3},{1,2},{2,1},{3,0},{4,7},{5,6},{6,5},{7,4},{8,11},{9,10},{10,... | collective-permute-start | bytes 1572872 | tf_op jit(solution)/shard_map/ppermute | solution.py:21
  150.3 8.3 %collective-permute-start.24 = (bf16[2,2,256,768]{3,2,1,0:T(8,128)(2,1)}, bf16[2,2,256,768]{3,2,1,0:T(8,128)(2,1)S(1)}, u32[]{:S(2)}, u32[]{:S(2)}) collective-permute-start(bf16[2,2,256,768]{3,2,1,0:T(8,128)(2,1)} %get-tuple-element.170), channel_id=1, source_target_pairs={{0,4},{4,0},{8,12},{12,8},{16,20},{20,16},{24,28},{28,24},{1,5},{5... | collective-permute-start | bytes 4718600 | tf_op jit(solution)/shard_map/ppermute | solution.py:21
  151.4 5.5 %collective-permute-start.27 = (bf16[2,256,768]{2,1,0:T(8,128)(2,1)}, bf16[2,256,768]{2,1,0:T(8,128)(2,1)}, u32[]{:S(2)}, u32[]{:S(2)}) collective-permute-start(bf16[2,256,768]{2,1,0:T(8,128)(2,1)} %get-tuple-element.172), channel_id=1, source_target_pairs={{0,4},{4,0},{8,12},{12,8},{16,20},{20,16},{24,28},{28,24},{1,5},{5... | collective-permute-start | bytes 2359304 | tf_op jit(solution)/shard_map/ppermute | solution.py:21
  151.4 29.9 %collective-permute-start.23 = (bf16[2,256,768]{2,1,0:T(8,128)(2,1)}, bf16[2,256,768]{2,1,0:T(8,128)(2,1)S(1)}, u32[]{:S(2)}, u32[]{:S(2)}) collective-permute-start(bf16[2,256,768]{2,1,0:T(8,128)(2,1)} %get-tuple-element.168), channel_id=1, source_target_pairs={{0,4},{4,0},{8,12},{12,8},{16,20},{20,16},{24,28},{28,24},{1,5},{5... | collective-permute-start | bytes 2359304 | tf_op jit(solution)/shard_map/ppermute | solution.py:21
  158.5 6.4 %collective-permute-start.28 = (bf16[2,64,768]{2,1,0:T(8,128)(2,1)S(1)}, bf16[2,64,768]{2,1,0:T(8,128)(2,1)S(1)}, u32[]{:S(2)}, u32[]{:S(2)}) collective-permute-start(bf16[2,64,768]{2,1,0:T(8,128)(2,1)S(1)} %get-tuple-element.203), channel_id=1, source_target_pairs={{0,1},{1,0},{2,3},{3,2},{4,5},{5,4},{6,7},{7,6},{8,9},{9,8},{10,11... | collective-permute-start | bytes 589832 | tf_op jit(solution)/shard_map/ppermute | solution.py:21
  158.8 22.5 %collective-permute-start.25 = (bf16[2,256,768]{2,1,0:T(8,128)(2,1)S(1)}, bf16[2,256,768]{2,1,0:T(8,128)(2,1)S(1)}, u32[]{:S(2)}, u32[]{:S(2)}) collective-permute-start(bf16[2,256,768]{2,1,0:T(8,128)(2,1)S(1)} %get-tuple-element.196), channel_id=1, source_target_pairs={{0,8},{4,12},{8,0},{12,4},{16,24},{20,28},{24,16},{28,20},{1,9},{5... | collective-permute-start | bytes 2359304 | tf_op jit(solution)/shard_map/ppermute | solution.py:21
  160.3 21.0 %collective-permute-start.26 = (bf16[2,256,768]{2,1,0:T(8,128)(2,1)S(1)}, bf16[2,256,768]{2,1,0:T(8,128)(2,1)S(1)}, u32[]{:S(2)}, u32[]{:S(2)}) collective-permute-start(bf16[2,256,768]{2,1,0:T(8,128)(2,1)S(1)} %get-tuple-element.197), channel_id=1, source_target_pairs={{0,16},{4,20},{8,24},{12,28},{16,0},{20,4},{24,8},{28,12},{1,17},{... | collective-permute-start | bytes 2359304 | tf_op jit(solution)/shard_map/ppermute | solution.py:21
  161.1 13.3 %collective-permute-start.29 = (bf16[2,64,768]{2,1,0:T(8,128)(2,1)S(1)}, bf16[2,64,768]{2,1,0:T(8,128)(2,1)S(1)}, u32[]{:S(2)}, u32[]{:S(2)}) collective-permute-start(bf16[2,64,768]{2,1,0:T(8,128)(2,1)S(1)} %get-tuple-element.205), channel_id=1, source_target_pairs={{0,2},{1,3},{2,0},{3,1},{4,6},{5,7},{6,4},{7,5},{8,10},{9,11},{10,... | collective-permute-start | bytes 589832 | tf_op jit(solution)/shard_map/ppermute | solution.py:21
  165.0 16.2 %collective-permute-start.30 = (bf16[2,64,768]{2,1,0:T(8,128)(2,1)S(1)}, bf16[2,64,768]{2,1,0:T(8,128)(2,1)S(1)}, u32[]{:S(2)}, u32[]{:S(2)}) collective-permute-start(bf16[2,64,768]{2,1,0:T(8,128)(2,1)S(1)} %get-tuple-element.204), channel_id=1, source_target_pairs={{0,3},{1,2},{2,1},{3,0},{4,7},{5,6},{6,5},{7,4},{8,11},{9,10},{10,... | collective-permute-start | bytes 589832 | tf_op jit(solution)/shard_map/ppermute | solution.py:21
  181.6 5.4 %collective-permute-start.31 = (bf16[2,64,768]{2,1,0:T(8,128)(2,1)S(1)}, bf16[2,64,768]{2,1,0:T(8,128)(2,1)S(1)}, u32[]{:S(2)}, u32[]{:S(2)}) collective-permute-start(bf16[2,64,768]{2,1,0:T(8,128)(2,1)S(1)} %get-tuple-element.200), channel_id=1, source_target_pairs={{0,1},{1,0},{2,3},{3,2},{4,5},{5,4},{6,7},{7,6},{8,9},{9,8},{10,11... | collective-permute-start | bytes 589832 | tf_op jit(solution)/shard_map/ppermute | solution.py:21
  181.7 8.1 %collective-permute-start.32 = (bf16[2,64,768]{2,1,0:T(8,128)(2,1)S(1)}, bf16[2,64,768]{2,1,0:T(8,128)(2,1)S(1)}, u32[]{:S(2)}, u32[]{:S(2)}) collective-permute-start(bf16[2,64,768]{2,1,0:T(8,128)(2,1)S(1)} %get-tuple-element.202), channel_id=1, source_target_pairs={{0,2},{1,3},{2,0},{3,1},{4,6},{5,7},{6,4},{7,5},{8,10},{9,11},{10,... | collective-permute-start | bytes 589832 | tf_op jit(solution)/shard_map/ppermute | solution.py:21
  182.5 18.8 %collective-permute-start.33 = (bf16[2,64,768]{2,1,0:T(8,128)(2,1)S(1)}, bf16[2,64,768]{2,1,0:T(8,128)(2,1)S(1)}, u32[]{:S(2)}, u32[]{:S(2)}) collective-permute-start(bf16[2,64,768]{2,1,0:T(8,128)(2,1)S(1)} %get-tuple-element.201), channel_id=1, source_target_pairs={{0,3},{1,2},{2,1},{3,0},{4,7},{5,6},{6,5},{7,4},{8,11},{9,10},{10,... | collective-permute-start | bytes 589832 | tf_op jit(solution)/shard_map/ppermute | solution.py:21
  184.3 17.0 %collective-permute-start.34 = (bf16[2,64,768]{2,1,0:T(8,128)(2,1)S(1)}, bf16[2,64,768]{2,1,0:T(8,128)(2,1)S(1)}, u32[]{:S(2)}, u32[]{:S(2)}) collective-permute-start(bf16[2,64,768]{2,1,0:T(8,128)(2,1)S(1)} %add_add_fusion.2), channel_id=1, source_target_pairs={{0,24},{4,28},{8,16},{12,20},{16,8},{20,12},{24,0},{28,4},{1,25},{... | collective-permute-start | bytes 589832 | tf_op jit(solution)/shard_map/ppermute | solution.py:21
  201.5 3.9 %collective-permute-start.35 = (bf16[512,128]{1,0:T(8,128)(2,1)S(1)}, bf16[512,128]{1,0:T(8,128)(2,1)S(1)}, u32[]{:S(2)}, u32[]{:S(2)}) collective-permute-start(bf16[512,128]{1,0:T(8,128)(2,1)S(1)} %copy-done.40), channel_id=1, source_target_pairs={{0,1},{1,0},{2,3},{3,2},{4,5},{5,4},{6,7},{7,6},{8,9},{9,8},{10,11... | collective-permute-start | bytes 393224 | tf_op jit(solution)/shard_map/ppermute | solution.py:21
  201.6 7.9 %collective-permute-start.39 = (bf16[2,64,768]{2,1,0:T(8,128)(2,1)S(1)}, bf16[2,64,768]{2,1,0:T(8,128)(2,1)S(1)}, u32[]{:S(2)}, u32[]{:S(2)}) collective-permute-start(bf16[2,64,768]{2,1,0:T(8,128)(2,1)S(1)} %add_add_fusion.1.rest_0_), channel_id=1, source_target_pairs={{0,16},{4,20},{8,24},{12,28},{16,0},{20,4},{24,8},{28,12},{1,17},{... | collective-permute-start | bytes 589832 | tf_op jit(solution)/shard_map/ppermute | solution.py:21
  202.6 7.3 %collective-permute-start.38 = (bf16[2,64,768]{2,1,0:T(8,128)(2,1)S(1)}, bf16[2,64,768]{2,1,0:T(8,128)(2,1)S(1)}, u32[]{:S(2)}, u32[]{:S(2)}) collective-permute-start(bf16[2,64,768]{2,1,0:T(8,128)(2,1)S(1)} %add_add_fusion.1.rest_0_), channel_id=1, source_target_pairs={{0,8},{4,12},{8,0},{12,4},{16,24},{20,28},{24,16},{28,20},{1,9},{5... | collective-permute-start | bytes 589832 | tf_op jit(solution)/shard_map/ppermute | solution.py:21
  202.6 8.0 %collective-permute-start.36 = (bf16[512,128]{1,0:T(8,128)(2,1)S(1)}, bf16[512,128]{1,0:T(8,128)(2,1)S(1)}, u32[]{:S(2)}, u32[]{:S(2)}) collective-permute-start(bf16[512,128]{1,0:T(8,128)(2,1)S(1)} %copy-done.39), channel_id=1, source_target_pairs={{0,2},{1,3},{2,0},{3,1},{4,6},{5,7},{6,4},{7,5},{8,10},{9,11},{10,... | collective-permute-start | bytes 393224 | tf_op jit(solution)/shard_map/ppermute | solution.py:21
  203.0 13.6 %collective-permute-start.37 = (bf16[512,128]{1,0:T(8,128)(2,1)S(1)}, bf16[512,128]{1,0:T(8,128)(2,1)S(1)}, u32[]{:S(2)}, u32[]{:S(2)}) collective-permute-start(bf16[512,128]{1,0:T(8,128)(2,1)S(1)} %copy-done.38), channel_id=1, source_target_pairs={{0,3},{1,2},{2,1},{3,0},{4,7},{5,6},{6,5},{7,4},{8,11},{9,10},{10,... | collective-permute-start | bytes 393224 | tf_op jit(solution)/shard_map/ppermute | solution.py:21
  205.4 13.2 %collective-permute-start.42 = (bf16[2,64,768]{2,1,0:T(8,128)(2,1)S(1)}, bf16[2,64,768]{2,1,0:T(8,128)(2,1)S(1)}, u32[]{:S(2)}, u32[]{:S(2)}) collective-permute-start(bf16[2,64,768]{2,1,0:T(8,128)(2,1)S(1)} %add_add_fusion.1.rest_0_), channel_id=1, source_target_pairs={{0,4},{4,0},{8,12},{12,8},{16,20},{20,16},{24,28},{28,24},{1,5},{5... | collective-permute-start | bytes 589832 | tf_op jit(solution)/shard_map/ppermute | solution.py:21
  209.5 8.4 %collective-permute-start.40 = (bf16[1,64,768]{2,1,0:T(8,128)(2,1)S(1)}, bf16[1,64,768]{2,1,0:T(8,128)(2,1)S(1)}, u32[]{:S(2)}, u32[]{:S(2)}) collective-permute-start(bf16[1,64,768]{2,1,0:T(8,128)(2,1)S(1)} %slice.50), channel_id=1, source_target_pairs={{0,8},{4,12},{8,0},{12,4},{16,24},{20,28},{24,16},{28,20},{1,9},{5... | collective-permute-start | bytes 294920 | tf_op jit(solution)/shard_map/ppermute | solution.py:21
  209.9 8.1 %collective-permute-start.41 = (bf16[1,64,768]{2,1,0:T(8,128)(2,1)S(1)}, bf16[1,64,768]{2,1,0:T(8,128)(2,1)S(1)}, u32[]{:S(2)}, u32[]{:S(2)}) collective-permute-start(bf16[1,64,768]{2,1,0:T(8,128)(2,1)S(1)} %slice.51), channel_id=1, source_target_pairs={{0,16},{4,20},{8,24},{12,28},{16,0},{20,4},{24,8},{28,12},{1,17},{... | collective-permute-start | bytes 294920 | tf_op jit(solution)/shard_map/ppermute | solution.py:21
  210.6 8.9 %collective-permute-start.43 = (bf16[2,64,768]{2,1,0:T(8,128)(2,1)S(1)}, bf16[2,64,768]{2,1,0:T(8,128)(2,1)S(1)}, u32[]{:S(2)}, u32[]{:S(2)}) collective-permute-start(bf16[2,64,768]{2,1,0:T(8,128)(2,1)S(1)} %collective-permute-done.38.rest_1_), channel_id=1, source_target_pairs={{0,4},{4,0},{8,12},{12,8},{16,20},{20,16},{24,28},{28,24},{1,5},{5... | collective-permute-start | bytes 589832 | tf_op jit(solution)/shard_map/ppermute | solution.py:21
  216.6 3.5 %collective-permute-start.44 = (bf16[2,64,768]{2,1,0:T(8,128)(2,1)S(1)}, bf16[2,64,768]{2,1,0:T(8,128)(2,1)S(1)}, u32[]{:S(2)}, u32[]{:S(2)}) collective-permute-start(bf16[2,64,768]{2,1,0:T(8,128)(2,1)S(1)} %collective-permute-done.39.rest_2_), channel_id=1, source_target_pairs={{0,4},{4,0},{8,12},{12,8},{16,20},{20,16},{24,28},{28,24},{1,5},{5... | collective-permute-start | bytes 589832 | tf_op jit(solution)/shard_map/ppermute | solution.py:21
  218.0 1.4 collective-permute-start.45
  218.1 1.4 collective-permute-start.46
  (40 other events, 569.4 us)

commit v5 on v4

--- a/solution.py
+++ b/solution.py
@@ -9,7 +9,7 @@
 F32 = jnp.float32
 BF16 = jnp.bfloat16
 HALO = 8
-EARLY = 4
+EARLY = 15
 VMEM_BYTES = 60 * 1024 * 1024
 
 
@@ -22,31 +22,21 @@
 
 
 def spread(piece):
-    half = piece.shape[0] // 2
-    by_x = swap(piece, "tm", 2)
-    by_y = swap(piece, "tm", 4)
-    far_a = swap(by_y[:half], "tm", 2)
-    far_b = swap(by_x[half:], "tm", 4)
-    near = [piece, by_x, by_y, far_a, far_b]
+    near = [piece] + [swap(piece, "tm", place) for place in (2, 4, 6)]
     return near + [swap(entry, "tm", 1) for entry in near]
 
 
 def gather_weights(column, signals):
-    by_x = swap(column, "tm", 2)
-    by_y = swap(column, "tm", 4)
-    by_x, by_y, signals = lax.optimization_barrier((by_x, by_y, signals))
-    far_a = swap(by_y[:2], "tm", 2)
-    far_b = swap(by_x[2:], "tm", 4)
-    near = lax.optimization_barrier([column, by_x, by_y, far_a, far_b])
+    near = [column] + [swap(column, "tm", place) for place in (6, 2, 4)]
+    near, signals = lax.optimization_barrier((near, signals))
     return near + [swap(entry, "tm", 1) for entry in near], signals
 
 
-WEIGHT_PLACES = [(0, 0, 4), (2, 0, 4), (4, 0, 4), (6, 0, 2), (6, 2, 2)]
+WEIGHT_PLACES = [(0, 0, 4), (6, 0, 4), (2, 0, 4), (4, 0, 4)]
 WEIGHT_PLACES = WEIGHT_PLACES + [(a + 1, first, count) for a, first, count in WEIGHT_PLACES]
 
 
-SPREAD_PLACES = [(0, 0, 2), (2, 0, 2), (4, 0, 2), (6, 0, 1), (6, 1, 1)]
-SPREAD_PLACES = SPREAD_PLACES + [(a + 1, first, count) for a, first, count in SPREAD_PLACES]
+SPREAD_PLACES = [0, 2, 4, 6, 1, 3, 5, 7]
 
 
 def nt(left, right):
@@ -243,15 +233,14 @@
 
 
 def finish_kernel(places, sec_ref, three_ref, mix_ref, skip_ref, gt, gm, gk, stat, *rest):
-    pieces = rest[:10]
-    sec_out, gain_out, bs, three_out, gt_out, bt, mix_out, gm_out, bm, skip_out, gk_out, bk = rest[10:22]
-    wide, rows, mats = rest[22:]
+    pieces = rest[:8]
+    sec_out, gain_out, bs, three_out, gt_out, bt, mix_out, gm_out, bm, skip_out, gk_out, bk = rest[8:20]
+    wide, rows, mats = rest[20:]
     turn = places[0]
-    for ref, (place, first, _) in zip(pieces, SPREAD_PLACES, strict=True):
+    for ref, place in zip(pieces, SPREAD_PLACES, strict=True):
         pair = 2 * (turn ^ place)
-        taps = 1 if place >= 6 else 2
-        for tap in range(taps):
-            k = pair + tap + first
+        for tap in range(2):
+            k = pair + tap
             part = ref[tap].astype(F32)
             for q in range(4):
                 wide[q, pl.ds(k, 64, stride=17), :] = part[:, 128 * q : 128 * q + 128]
@@ -306,22 +295,18 @@
 
 def weight_copies(places, refs, wsec, wblk, sem, block_sem):
     turn, chan = places[0], places[1]
-    copies = []
-    for ref, (place, first, _) in zip(refs, WEIGHT_PLACES, strict=True):
+    section, blocks = [], []
+    for index, (ref, (place, _, _)) in enumerate(zip(refs, WEIGHT_PLACES, strict=True)):
         slots = pl.ds(2 * (turn ^ place), 2)
-        for k in range(ref.shape[0]):
-            rows = pl.ds(pl.multiple_of(64 * (chan ^ (first + k)), 64), 64)
-            copies.append(
-                pltpu.make_async_copy(
-                    ref.at[k, :, :, 0:512], wsec.at[slots, rows, :], sem
-                )
-            )
-            copies.append(
-                pltpu.make_async_copy(
-                    ref.at[k, :, :, 512:768], wblk.at[slots, rows, :], block_sem
-                )
-            )
-    return copies
+        copies = []
+        for k in range(4):
+            rows = pl.ds(pl.multiple_of(64 * (chan ^ k), 64), 64)
+            target = wsec.at[slots, rows, :]
+            copies.append(pltpu.make_async_copy(ref.at[k, :, :, 0:512], target, sem.at[index]))
+            target = wblk.at[slots, rows, :]
+            blocks.append(pltpu.make_async_copy(ref.at[k, :, :, 512:768], target, block_sem))
+        section.append(copies)
+    return section, blocks
 
 
 def forward_kernel(
@@ -334,19 +319,19 @@
     gain_ref,
     *rest,
 ):
-    pieces, rest = rest[:10], rest[10:]
+    pieces, rest = rest[:8], rest[8:]
     hid_out, act_out, mix_out, inner_out = rest[0:4]
     sact_out, mask_out, stat_out = rest[4:7]
     outs = rest[7:11]
     wsec, wblk, cat, bias, wide, turned, flat = rest[11:18]
     hids, mixs, inners, acts = rest[18:21], rest[21:24], rest[24:27], rest[27:30]
-    wsem, ssem = rest[30:]
+    wsem, vsem, ssem = rest[30:]
     chan = places[1]
     rows = sact_out.shape[0]
     own = rows - 2 * HALO
     pitch = own // 2 + 1
-    loads = weight_copies(places, pieces, wsec, wblk, wsem, wsem)
-    for copy in loads:
+    section_loads, block_loads = weight_copies(places, pieces, wsec, wblk, wsem, vsem)
+    for copy in sum(section_loads, []) + block_loads:
         copy.start()
     fill_masks(ids_ref, flat, mask_out)
     for k, ref in enumerate((sig0, sig1, sig2, sig3)):
@@ -355,14 +340,15 @@
         to_rows(flat, values, sact_out.at[:, lanes])
         halo = silu_half(0.5 * ref[own // 64, 0:16].astype(F32))[0]
         sact_out[own:rows, lanes] = halo.astype(BF16)
-    for copy in loads:
+    total = jnp.zeros((8, 512), F32)
+    for (place, _, _), copies in zip(WEIGHT_PLACES, section_loads, strict=True):
+        for copy in copies:
+            copy.wait()
+        for tap in range(2):
+            part = wsec[2 * (places[0] ^ place) + tap].astype(F32)
+            total = total + jnp.sum((part * part).reshape(32, 8, 512), axis=0)
+    for copy in block_loads:
         copy.wait()
-
-    def square(k, total):
-        part = wsec[k].astype(F32)
-        return total + jnp.sum((part * part).reshape(32, 8, 512), axis=0)
-
-    total = lax.fori_loop(0, 16, square, jnp.zeros((8, 512), F32))
     norm = jnp.sqrt(jnp.sum(total, axis=0, keepdims=True) + EPSILON)
     scale = gain_ref[...] / norm
     stat_out[...] = jnp.concatenate([norm, scale, jnp.zeros((6, 512), F32)], axis=0)
@@ -457,7 +443,7 @@
     final = []
     for k, out in enumerate(outs):
         part = turned.at[pl.ds(pl.multiple_of(64 * (chan ^ k), 64), 64), :]
-        final.append(pltpu.make_async_copy(part, out, wsem))
+        final.append(pltpu.make_async_copy(part, out, vsem))
     for copy in final:
         copy.start()
     for copy in saves + final:
@@ -483,7 +469,7 @@
     inner_in,
     *rest,
 ):
-    pieces, rest = rest[:10], rest[10:]
+    pieces, rest = rest[:8], rest[8:]
     sums_out = rest[0:6]
     sgrads = rest[6:10]
     targets = [(sums_out[0], 6), (sums_out[1].at[0], 2), (sums_out[1].at[1], 4), (sums_out[2], 0)]
@@ -494,13 +480,13 @@
         (sums_out[5], 1),
     ]
     (wsec, wblk, turned, sigs, wide, grad, inner_a, inner_b, mix, hid, act, halves) = rest[10:22]
-    (acc_one, acc_three, through, sums, staged, wsem, vsem, csem, bsem, osem) = rest[22:]
+    (acc_one, acc_three, through, sums, staged, wsem, vsem, gsem, csem, bsem, osem) = rest[22:]
     pitch = 4 * (sact_ref.shape[0] - 2 * HALO) // 8 + 1
     turn_index, chan = places[0], places[1]
     rows = mask_ref.shape[1]
     own = rows - 2 * HALO
 
-    loads = weight_copies(places, pieces, wsec, wblk, wsem, vsem)
+    section_weights, block_loads = weight_copies(places, pieces, wsec, wblk, wsem, vsem)
     cots = []
     count = own // 64
     section_loads = []
@@ -511,7 +497,7 @@
         cots.append(pltpu.make_async_copy(early, turned.at[0:EARLY, part, :], csem))
         late = turned.at[EARLY : 8 * own // 128 + 1, part, :]
         cots.append(pltpu.make_async_copy(two, late, csem))
-        section_loads.append(pltpu.make_async_copy(one.at[0:count], sigs.at[k], wsem))
+        section_loads.append(pltpu.make_async_copy(one.at[0:count], sigs.at[k], gsem))
 
     def kept(b):
         slot = b % 2
@@ -522,7 +508,7 @@
             pltpu.make_async_copy(act_in.at[b, :, 0:own], act.at[slot], bsem.at[slot, 3]),
         ]
 
-    block_loads, section_loads = loads[1::2], loads[0::2] + section_loads
+    section_loads = sum(section_weights, []) + section_loads
     for copy in cots + block_loads + kept(2) + kept(1) + section_loads:
         copy.start()
     sums[...] = jnp.zeros_like(sums)
@@ -793,7 +779,7 @@
     return pl.pallas_call(
         finish_kernel,
         out_shape=out_shape,
-        in_specs=[SPEC_SMEM] + [SPEC_VMEM] * 18,
+        in_specs=[SPEC_SMEM] + [SPEC_VMEM] * 16,
         out_specs=[SPEC_VMEM] * 12,
         scratch_shapes=[
             pltpu.VMEM((4, 64 * 17, 128), F32),
@@ -819,7 +805,7 @@
     return pl.pallas_call(
         forward_kernel,
         out_shape=out_shape,
-        in_specs=[SPEC_SMEM] + [SPEC_VMEM] * 6 + [SPEC_ANY] * 10,
+        in_specs=[SPEC_SMEM] + [SPEC_VMEM] * 6 + [SPEC_ANY] * 8,
         out_specs=[SPEC_ANY] * 4 + [SPEC_VMEM] * 3 + [SPEC_ANY] * 4,
         scratch_shapes=[
             pltpu.VMEM((16, 256, 512), BF16),
@@ -832,7 +818,7 @@
         ]
         + [pltpu.VMEM((8, rows, 256), BF16)] * 9
         + [pltpu.VMEM((26, rows, 256), BF16)] * 3
-        + [pltpu.SemaphoreType.DMA, pltpu.SemaphoreType.DMA],
+        + [pltpu.SemaphoreType.DMA((8,)), pltpu.SemaphoreType.DMA, pltpu.SemaphoreType.DMA],
         compiler_params=params(),
         cost_estimate=cost(2 * 1245184 * 8 * rows, 50e6),
         name="forward_blocks",
@@ -854,7 +840,7 @@
         in_specs=[SPEC_SMEM]
         + [SPEC_ANY] * 8
         + [SPEC_VMEM] * 3
-        + [SPEC_ANY] * 14,
+        + [SPEC_ANY] * 12,
         out_specs=[SPEC_ANY] * 6 + [SPEC_VMEM] * 4,
         scratch_shapes=[
             pltpu.VMEM((16, 256, 512), BF16),
@@ -874,6 +860,7 @@
             pltpu.VMEM((own, 512), F32),
             pltpu.VMEM((8, 8, 256), F32),
             pltpu.VMEM((16, 256, 768), BF16),
+            pltpu.SemaphoreType.DMA((8,)),
             pltpu.SemaphoreType.DMA,
             pltpu.SemaphoreType.DMA,
             pltpu.SemaphoreType.DMA,
@@ -948,7 +935,6 @@
         firsts[k] = swap(firsts[k], "chan", k)
         seconds[k] = swap(seconds[k], "chan", k)
     pieces, firsts = gather_weights(jnp.stack(by_chan), firsts)
-    firsts, seconds[1:3] = lax.optimization_barrier((firsts, seconds[1:3]))
     padded = jnp.pad(segment_ids, 16, constant_values=-1)
     nearby = lax.dynamic_slice_in_dim(padded, start, own + 32)
     ids = jnp.broadcast_to(nearby[:, None], (own + 32, 128))
@@ -981,6 +967,8 @@
         output = lax.dynamic_update_slice_in_dim(output, received[k], (chan ^ k) * frames, axis=1)
     across = chan_sum(far)
     for_x, for_y = sides[0] + odd_sides[0], sides[1] + odd_sides[1]
+    sgrad_near = swap(sgrads[1], "chan", 1)
+    far, sgrad_near = lax.optimization_barrier((far, sgrad_near))
     summed = (here + odd_here) + swap(for_x, "tm", 2) + swap(for_y, "tm", 4)
     summed, across = lax.optimization_barrier((summed, across))
     mine = chan_sum(summed) + swap(across, "tm", 6)
@@ -988,10 +976,9 @@
     while bit < tm_size:
         mine = mine + swap(mine, "tm", bit)
         bit = 2 * bit
-    mine, sgrads = lax.optimization_barrier((mine, sgrads))
     gathered = spread(mine)
 
-    received = [sgrads[0]] + [swap(sgrads[k], "chan", k) for k in (1, 2, 3)]
+    received = [sgrads[0], sgrad_near, swap(sgrads[2], "chan", 2), swap(sgrads[3], "chan", 3)]
     signal_grad = jnp.zeros((4 * own, 128), BF16)
     for k in range(4):
         signal_grad = lax.dynamic_update_slice_in_dim(

time: 227 us -> 218 us (0.960)
  waiting for transfers between devices: 84.5 us -> 70.9 us
  starting transfers between devices: 55.9 us -> 61.6 us
    ppermute x45 -> x41, waiting for transfers between devices: 81.3 us -> 67.7 us  [swap(): return lax.ppermute(values, axis, xor_pairs(axis, bit))]
    ppermute x45 -> x41, starting transfers between devices: 49.4 us -> 55.1 us  [swap(): return lax.ppermute(values, axis, xor_pairs(axis, bit))]
    unnamed x82 -> x72, local copies, waits for them, and re-layouts: 4.18 us -> 1.73 us
  transfers between devices with their start and end apart: 47 -> 43, of which waited for: 20 -> 14; matrix products, arithmetic and copies ran while one was open for 2% -> 3% of each run, Pallas kernels for 29% -> 30%
where the time goes in v5:
time: 218 us; the launch traced here: 217 us
  Pallas kernels  74.2 us (34%)
  waiting for transfers between devices  70.9 us (33%)
  starting transfers between devices  61.6 us (28%)
  local copies, waits for them, and re-layouts  5.81 us (3%)
  other arithmetic  3.27 us (2%)
    ppermute x41, waiting for transfers between devices, swap(): return lax.ppermute(values, axis, xor_pairs(axis, bit))  67.7 us
    ppermute x41, starting transfers between devices, swap(): return lax.ppermute(values, axis, xor_pairs(axis, bit))  55.1 us
    pallas_call x1, Pallas kernels, run_backward(): pl.pallas_call(backward_kernel, out_shape=[shape_of((2, 256, 768)), shape...  38.7 us
    pallas_call x1, Pallas kernels, run_forward(): pl.pallas_call(forward_kernel, out_shape=out_shape, in_specs=[SPEC_SMEM]...  23.4 us
    pallas_call x1, Pallas kernels, run_finish(): pl.pallas_call(finish_kernel, out_shape=out_shape, in_specs=[SPEC_SMEM] +...  4.92 us
    ppermute x1, starting transfers between devices, body(): low = lax.ppermute(final, 'tm', onward)  4.51 us
  transfers between devices with their start and end apart: 43, of which 14 were waited for; matrix products, arithmetic and copies ran while one was open for 3% of the time, Pallas kernels for 30%

profile of v5, /device:TPU:9, one launch (start us, length us, event | category | flops | bytes accessed | tf_op | source)
XLA Modules:
  0.0 217.2 jit_solution(1038439307674598824)
XLA Ops:
  1.3 3.3 %pack_weights.1 = bf16[2,64,768]{2,1,0:T(8,128)(2,1)} custom-call(s32[2]{0:T(128)} %pad_add_fusion.places, bf16[64,16,512]{2,1,0:T(8,128)(2,1)} %sec_ref.3, bf16[3,3,64,256]{3,2,1,0:T(8,128)(2,1)} %bitcast.16, bf16[3,64,256]{2,1,0:T(8,128)(2,1)} %mix_ref.3, bf16[3,64,256]{2,1,0:T(8,128)(2,1)} %skip_ref.3, bf16[1,64]{1,0:T(2,128)(2,1)} %bitcast.23, ...), custom_call_target="tpu_custom_call" | custom-call | flops 20000000 | bytes 3000000 | tf_op jit(solution)/shard_map/pack_weights/pallas_call | solution.py:733
  4.6 2.5 %collective-permute-start.1 = (bf16[2,64,768]{2,1,0:T(8,128)(2,1)}, bf16[2,64,768]{2,1,0:T(8,128)(2,1)S(1)}, u32[]{:S(2)}, u32[]{:S(2)}) collective-permute-start(bf16[2,64,768]{2,1,0:T(8,128)(2,1)} %pack_weights.1), channel_id=1, source_target_pairs={{0,2},{1,3},{2,0},{3,1},{4,6},{5,7},{6,4},{7,5},{8,10},{9,11},{10,... | collective-permute-start | bytes 589832 | tf_op jit(solution)/shard_map/ppermute | solution.py:21
  7.2 0.7 fusion.2
  8.7 4.5 %collective-permute-start.3 = (bf16[80,128]{1,0:T(8,128)(2,1)S(1)}, bf16[80,128]{1,0:T(8,128)(2,1)S(1)}, u32[]{:S(2)}, u32[]{:S(2)}) collective-permute-start(bf16[80,128]{1,0:T(8,128)(2,1)S(1)} %pad_maximum_fusion.1), channel_id=1, source_target_pairs={{0,4},{4,8},{8,12},{12,16},{16,20},{20,24},{24,28},{1,5},{5,9},{9,... | collective-permute-start | bytes 61448 | tf_op jit(solution)/shard_map/ppermute | solution.py:929
  13.2 2.1 collective-permute-start.4
  15.3 3.2 %collective-permute-done.4.high = bf16[80,128]{1,0:T(8,128)(2,1)S(1)} collective-permute-done((bf16[80,128]{1,0:T(8,128)(2,1)S(1)}, bf16[80,128]{1,0:T(8,128)(2,1)S(1)}, u32[]{:S(2)}, u32[]{:S(2)}) %collective-permute-start.4) | collective-permute-done | bytes 20512 | tf_op jit(solution)/shard_map/ppermute | solution.py:930
  19.1 3.9 %pack_frames.1 = (bf16[24,64,128]{2,1,0:T(8,128)(2,1)}, bf16[24,64,128]{2,1,0:T(8,128)(2,1)}, bf16[24,64,128]{2,1,0:T(8,128)(2,1)}, bf16[24,64,128]{2,1,0:T(8,12...) custom-call(s32[2]{0:T(128)} %pad_add_fusion.places, ...), custom_call_target="tpu_custom_call" | custom-call | flops 1000000 | bytes 6000000 | tf_op jit(solution)/shard_map/pack_frames/pallas_call | solution.py:751
  23.0 1.3 collective-permute-start.10
  24.5 2.1 collective-permute-start.5
  27.0 0.9 collective-permute-start.7
  27.8 3.4 %collective-permute-start.8 = (bf16[24,64,128]{2,1,0:T(8,128)(2,1)}, bf16[24,64,128]{2,1,0:T(8,128)(2,1)S(1)}, u32[]{:S(2)}, u32[]{:S(2)}) collective-permute-start(bf16[24,64,128]{2,1,0:T(8,128)(2,1)} %get-tuple-element.97), channel_id=1, source_target_pairs={{0,1},{1,0},{2,3},{3,2},{4,5},{5,4},{6,7},{7,6},{8,9},{9,8},{10,11... | collective-permute-start | bytes 1179656 | tf_op jit(solution)/shard_map/ppermute | solution.py:21
  31.2 11.2 %collective-permute-done.10.sig3.first3 = bf16[24,64,128]{2,1,0:T(8,128)(2,1)S(1)} collective-permute-done((bf16[24,64,128]{2,1,0:T(8,128)(2,1)}, bf16[24,64,128]{2,1,0:T(8,128)(2,1)S(1)}, u32[]{:S(2)}, u32[]{:S(2)}) %collective-permute-start.10) | collective-permute-done | bytes 393248 | tf_op jit(solution)/shard_map/ppermute | solution.py:21
  42.5 17.5 %collective-permute-done.9.sig2.first2 = bf16[24,64,128]{2,1,0:T(8,128)(2,1)S(1)} collective-permute-done((bf16[24,64,128]{2,1,0:T(8,128)(2,1)}, bf16[24,64,128]{2,1,0:T(8,128)(2,1)S(1)}, u32[]{:S(2)}, u32[]{:S(2)}) %collective-permute-start.9) | collective-permute-done | bytes 393248 | tf_op jit(solution)/shard_map/ppermute | solution.py:21
  60.0 0.7 collective-permute-done.7.rest_3_
  60.8 1.6 collective-permute-start.11
  63.7 3.4 %collective-permute-start.15 = (bf16[18,64,128]{2,1,0:T(8,128)(2,1)}, bf16[18,64,128]{2,1,0:T(8,128)(2,1)S(1)}, u32[]{:S(2)}, u32[]{:S(2)}) collective-permute-start(bf16[18,64,128]{2,1,0:T(8,128)(2,1)} %get-tuple-element.113), channel_id=1, source_target_pairs={{0,1},{1,0},{2,3},{3,2},{4,5},{5,4},{6,7},{7,6},{8,9},{9,8},{10,11... | collective-permute-start | bytes 884744 | tf_op jit(solution)/shard_map/ppermute | solution.py:21
  67.1 2.0 collective-permute-start.17
  69.0 0.8 broadcast_in_dim.18.ids_ref
  69.9 23.4 %forward_blocks.1 = (bf16[3,8,528,256]{3,2,1,0:T(8,128)(2,1)}, bf16[3,8,528,256]{3,2,1,0:T(8,128)(2,1)}, bf16[3,8,528,256]{3,2,1,0:T(8,128)(2,1)}, bf16[3,8,528,...) custom-call(s32[2]{0:T(128)} %pad_add_fusion.places, ...), custom_call_target="tpu_custom_call" | custom-call | flops 10519314432 | bytes 50000000 | tf_op jit(solution)/shard_map/forward_blocks/pallas_call | solution.py:805
  93.3 1.8 collective-permute-done.17.second3
  95.1 1.2 collective-permute-start.18
  96.3 1.5 collective-permute-start.20
  97.8 38.7 %backward_blocks.1 = (bf16[2,256,768]{2,1,0:T(8,128)(2,1)}, bf16[2,2,256,768]{3,2,1,0:T(8,128)(2,1)}, bf16[2,256,768]{2,1,0:T(8,128)(2,1)}, bf16[2,256,768]{2,1,...) custom-call(s32[2]{0:T(128)} %pad_add_fusion.places, ...), custom_call_target="tpu_custom_call" | custom-call | flops 21038628864 | bytes 60000000 | tf_op jit(solution)/shard_map/backward_blocks/pallas_call | solution.py:831
  136.5 5.8 %collective-permute-done.20 = bf16[64,4096]{1,0:T(8,128)(2,1)S(1)} collective-permute-done((bf16[64,4096]{1,0:T(8,128)(2,1)}, bf16[64,4096]{1,0:T(8,128)(2,1)S(1)}, u32[]{:S(2)}, u32[]{:S(2)}) %collective-permute-start.20) | collective-permute-done | bytes 524320 | tf_op jit(solution)/shard_map/ppermute | solution.py:21
  142.2 0.8 copy-done.8
  143.1 2.4 %collective-permute-start.26 = (bf16[2,2,256,768]{3,2,1,0:T(8,128)(2,1)}, bf16[2,2,256,768]{3,2,1,0:T(8,128)(2,1)S(1)}, u32[]{:S(2)}, u32[]{:S(2)}) collective-permute-start(bf16[2,2,256,768]{3,2,1,0:T(8,128)(2,1)} %get-tuple-element.155), channel_id=1, source_target_pairs={{0,4},{4,0},{8,12},{12,8},{16,20},{20,16},{24,28},{28,24},{1,5},{5... | collective-permute-start | bytes 4718600 | tf_op jit(solution)/shard_map/ppermute | solution.py:21
  146.1 1.2 constant_dynamic-update-slice_fusion.7
  147.3 3.6 %collective-permute-done.21 = bf16[2,256,768]{2,1,0:T(8,128)(2,1)} collective-permute-done((bf16[2,256,768]{2,1,0:T(8,128)(2,1)}, bf16[2,256,768]{2,1,0:T(8,128)(2,1)}, u32[]{:S(2)}, u32[]{:S(2)}) %collective-permute-start.21) | collective-permute-done | bytes 786464 | tf_op jit(solution)/shard_map/ppermute | solution.py:21
  151.0 1.3 add.105
  153.2 0.7 collective-permute-start.28
  153.9 1.3 collective-permute-start.30
  155.2 3.6 %collective-permute-done.29 = bf16[2,64,768]{2,1,0:T(8,128)(2,1)S(1)} collective-permute-done((bf16[2,64,768]{2,1,0:T(8,128)(2,1)S(1)}, bf16[2,64,768]{2,1,0:T(8,128)(2,1)S(1)}, u32[]{:S(2)}, u32[]{:S(2)}) %collective-permute-start.29) | collective-permute-done | bytes 196640 | tf_op jit(solution)/shard_map/ppermute | solution.py:21
  158.8 3.9 %collective-permute-done.30 = bf16[2,64,768]{2,1,0:T(8,128)(2,1)S(1)} collective-permute-done((bf16[2,64,768]{2,1,0:T(8,128)(2,1)S(1)}, bf16[2,64,768]{2,1,0:T(8,128)(2,1)S(1)}, u32[]{:S(2)}, u32[]{:S(2)}) %collective-permute-start.30) | collective-permute-done | bytes 196640 | tf_op jit(solution)/shard_map/ppermute | solution.py:21
  162.8 8.0 %collective-permute-start.22 = (bf16[512,128]{1,0:T(8,128)(2,1)S(1)}, bf16[512,128]{1,0:T(8,128)(2,1)S(1)}, u32[]{:S(2)}, u32[]{:S(2)}) collective-permute-start(bf16[512,128]{1,0:T(8,128)(2,1)S(1)} %copy-done.35), channel_id=1, source_target_pairs={{0,1},{1,0},{2,3},{3,2},{4,5},{5,4},{6,7},{7,6},{8,9},{9,8},{10,11... | collective-permute-start | bytes 393224 | tf_op jit(solution)/shard_map/ppermute | solution.py:21
  170.7 3.0 %collective-permute-done.31 = bf16[2,64,768]{2,1,0:T(8,128)(2,1)S(1)} collective-permute-done((bf16[2,64,768]{2,1,0:T(8,128)(2,1)S(1)}, bf16[2,64,768]{2,1,0:T(8,128)(2,1)S(1)}, u32[]{:S(2)}, u32[]{:S(2)}) %collective-permute-start.31) | collective-permute-done | bytes 196640 | tf_op jit(solution)/shard_map/ppermute | solution.py:21
  174.3 0.7 collective-permute-start.33
  175.0 1.9 collective-permute-start.34
  176.9 1.7 collective-permute-start.35
  178.7 0.9 collective-permute-done.32
  179.6 3.1 %collective-permute-start.23 = (bf16[512,128]{1,0:T(8,128)(2,1)S(1)}, bf16[512,128]{1,0:T(8,128)(2,1)S(1)}, u32[]{:S(2)}, u32[]{:S(2)}) collective-permute-start(bf16[512,128]{1,0:T(8,128)(2,1)S(1)} %copy-done.34), channel_id=1, source_target_pairs={{0,2},{1,3},{2,0},{3,1},{4,6},{5,7},{6,4},{7,5},{8,10},{9,11},{10,... | collective-permute-start | bytes 393224 | tf_op jit(solution)/shard_map/ppermute | solution.py:21
  182.7 14.1 %collective-permute-done.34 = bf16[2,64,768]{2,1,0:T(8,128)(2,1)S(1)} collective-permute-done((bf16[2,64,768]{2,1,0:T(8,128)(2,1)S(1)}, bf16[2,64,768]{2,1,0:T(8,128)(2,1)S(1)}, u32[]{:S(2)}, u32[]{:S(2)}) %collective-permute-start.34) | collective-permute-done | bytes 196640 | tf_op jit(solution)/shard_map/ppermute | solution.py:21
  196.9 1.9 collective-permute-start.36
  199.0 1.0 collective-permute-start.38
  200.3 3.2 %collective-permute-start.39 = (bf16[2,64,768]{2,1,0:T(8,128)(2,1)S(1)}, bf16[2,64,768]{2,1,0:T(8,128)(2,1)S(1)}, u32[]{:S(2)}, u32[]{:S(2)}) collective-permute-start(bf16[2,64,768]{2,1,0:T(8,128)(2,1)S(1)} %add_add_fusion.1.rest_0_), channel_id=1, source_target_pairs={{0,4},{4,0},{8,12},{12,8},{16,20},{20,16},{24,28},{28,24},{1,5},{5... | collective-permute-start | bytes 589832 | tf_op jit(solution)/shard_map/ppermute | solution.py:21
  203.5 3.7 %collective-permute-start.40 = (bf16[2,64,768]{2,1,0:T(8,128)(2,1)S(1)}, bf16[2,64,768]{2,1,0:T(8,128)(2,1)S(1)}, u32[]{:S(2)}, u32[]{:S(2)}) collective-permute-start(bf16[2,64,768]{2,1,0:T(8,128)(2,1)S(1)} %collective-permute-done.36.rest_1_), channel_id=1, source_target_pairs={{0,4},{4,0},{8,12},{12,8},{16,20},{20,16},{24,28},{28,24},{1,5},{5... | collective-permute-start | bytes 589832 | tf_op jit(solution)/shard_map/ppermute | solution.py:21
  207.2 3.1 %collective-permute-start.41 = (bf16[2,64,768]{2,1,0:T(8,128)(2,1)S(1)}, bf16[2,64,768]{2,1,0:T(8,128)(2,1)S(1)}, u32[]{:S(2)}, u32[]{:S(2)}) collective-permute-start(bf16[2,64,768]{2,1,0:T(8,128)(2,1)S(1)} %collective-permute-done.37.rest_2_), channel_id=1, source_target_pairs={{0,4},{4,0},{8,12},{12,8},{16,20},{20,16},{24,28},{28,24},{1,5},{5... | collective-permute-start | bytes 589832 | tf_op jit(solution)/shard_map/ppermute | solution.py:21
  210.5 0.9 collective-permute-done.41.rest_6_
  212.1 4.9 %finish_weights.1 = (f32[64,16,512]{2,1,0:T(8,128)}, f32[1,512]{1,0:T(1,128)}, f32[1,64]{1,0:T(1,128)}, f32[3,3,64,256]{3,2,1,0:T(8,128)}, f32[3,64]{1,0:T(4,128...) custom-call(s32[2]{0:T(128)} %pad_add_fusion.places, ...), custom_call_target="tpu_custom_call" | custom-call | flops 20000000 | bytes 8000000 | tf_op jit(solution)/shard_map/finish_weights/pallas_call | solution.py:779
  (141 shorter events, 7.4 us)
Async XLA Ops:
  4.6 19.7 %collective-permute-start = (bf16[2,64,768]{2,1,0:T(8,128)(2,1)}, bf16[2,64,768]{2,1,0:T(8,128)(2,1)S(1)}, u32[]{:S(2)}, u32[]{:S(2)}) collective-permute-start(bf16[2,64,768]{2,1,0:T(8,128)(2,1)} %pack_weights.1), channel_id=1, source_target_pairs={{0,1},{1,0},{2,3},{3,2},{4,5},{5,4},{6,7},{7,6},{8,9},{9,8},{10,11... | collective-permute-start | bytes 589832 | tf_op jit(solution)/shard_map/ppermute | solution.py:21
  4.6 19.7 %collective-permute-start.1 = (bf16[2,64,768]{2,1,0:T(8,128)(2,1)}, bf16[2,64,768]{2,1,0:T(8,128)(2,1)S(1)}, u32[]{:S(2)}, u32[]{:S(2)}) collective-permute-start(bf16[2,64,768]{2,1,0:T(8,128)(2,1)} %pack_weights.1), channel_id=1, source_target_pairs={{0,2},{1,3},{2,0},{3,1},{4,6},{5,7},{6,4},{7,5},{8,10},{9,11},{10,... | collective-permute-start | bytes 589832 | tf_op jit(solution)/shard_map/ppermute | solution.py:21
  7.1 17.3 %collective-permute-start.2 = (bf16[2,64,768]{2,1,0:T(8,128)(2,1)}, bf16[2,64,768]{2,1,0:T(8,128)(2,1)S(1)}, u32[]{:S(2)}, u32[]{:S(2)}) collective-permute-start(bf16[2,64,768]{2,1,0:T(8,128)(2,1)} %pack_weights.1), channel_id=1, source_target_pairs={{0,3},{1,2},{2,1},{3,0},{4,7},{5,6},{6,5},{7,4},{8,11},{9,10},{10,... | collective-permute-start | bytes 589832 | tf_op jit(solution)/shard_map/ppermute | solution.py:21
  8.7 6.6 %collective-permute-start.3 = (bf16[80,128]{1,0:T(8,128)(2,1)S(1)}, bf16[80,128]{1,0:T(8,128)(2,1)S(1)}, u32[]{:S(2)}, u32[]{:S(2)}) collective-permute-start(bf16[80,128]{1,0:T(8,128)(2,1)S(1)} %pad_maximum_fusion.1), channel_id=1, source_target_pairs={{0,4},{4,8},{8,12},{12,16},{16,20},{20,24},{24,28},{1,5},{5,9},{9,... | collective-permute-start | bytes 61448 | tf_op jit(solution)/shard_map/ppermute | solution.py:929
  13.2 49.8 %copy-start.24 = (bf16[512]{0:T(512)(128)(2,1)S(1)}, bf16[512]{0:T(512)(128)(2,1)}, u32[]{:S(2)}) copy-start(bf16[512]{0:T(512)(128)(2,1)} %param.18) | copy-start | bytes 3076
  13.2 50.4 %copy-start.21 = (s32[16384]{0:T(1024)S(1)}, s32[16384]{0:T(1024)}, u32[]{:S(2)}) copy-start(s32[16384]{0:T(1024)} %param.16) | copy-start | bytes 196612
  13.2 5.2 %collective-permute-start.4 = (bf16[80,128]{1,0:T(8,128)(2,1)S(1)}, bf16[80,128]{1,0:T(8,128)(2,1)S(1)}, u32[]{:S(2)}, u32[]{:S(2)}) collective-permute-start(bf16[80,128]{1,0:T(8,128)(2,1)S(1)} %pad_maximum_fusion.2), channel_id=1, source_target_pairs={{4,0},{8,4},{12,8},{16,12},{20,16},{24,20},{28,24},{5,1},{9,5},{13... | collective-permute-start | bytes 61448 | tf_op jit(solution)/shard_map/ppermute | solution.py:930
  23.0 19.4 %collective-permute-start.10 = (bf16[24,64,128]{2,1,0:T(8,128)(2,1)}, bf16[24,64,128]{2,1,0:T(8,128)(2,1)S(1)}, u32[]{:S(2)}, u32[]{:S(2)}) collective-permute-start(bf16[24,64,128]{2,1,0:T(8,128)(2,1)} %get-tuple-element.99), channel_id=1, source_target_pairs={{0,3},{1,2},{2,1},{3,0},{4,7},{5,6},{6,5},{7,4},{8,11},{9,10},{10,... | collective-permute-start | bytes 1179656 | tf_op jit(solution)/shard_map/ppermute | solution.py:21
  24.5 45.4 %copy-start.3 = (bf16[4,2,64,768]{3,2,1,0:T(8,128)(2,1)}, bf16[4,2,64,768]{3,2,1,0:T(8,128)(2,1)S(1)}, u32[]{:S(2)}) copy-start(bf16[4,2,64,768]{3,2,1,0:T(8,128)(2,1)S(1)} %pad_maximum_fusion.rest_0_) | copy-start | bytes 2359300
  24.5 35.6 %collective-permute-start.5 = (bf16[4,2,64,768]{3,2,1,0:T(8,128)(2,1)S(1)}, bf16[4,2,64,768]{3,2,1,0:T(8,128)(2,1)S(1)}, u32[]{:S(2)}, u32[]{:S(2)}) collective-permute-start(bf16[4,2,64,768]{3,2,1,0:T(8,128)(2,1)S(1)} %pad_maximum_fusion.rest_0_), channel_id=1, source_target_pairs={{0,24},{4,28},{8,16},{12,20},{16,8},{20,12},{24,0},{28,4},{1,25},{... | collective-permute-start | bytes 2359304 | tf_op jit(solution)/shard_map/ppermute | solution.py:21
  26.6 33.5 %collective-permute-start.6 = (bf16[4,2,64,768]{3,2,1,0:T(8,128)(2,1)S(1)}, bf16[4,2,64,768]{3,2,1,0:T(8,128)(2,1)S(1)}, u32[]{:S(2)}, u32[]{:S(2)}) collective-permute-start(bf16[4,2,64,768]{3,2,1,0:T(8,128)(2,1)S(1)} %pad_maximum_fusion.rest_0_), channel_id=1, source_target_pairs={{0,8},{4,12},{8,0},{12,4},{16,24},{20,28},{24,16},{28,20},{1,9},{5... | collective-permute-start | bytes 2359304 | tf_op jit(solution)/shard_map/ppermute | solution.py:21
  27.0 33.8 %collective-permute-start.7 = (bf16[4,2,64,768]{3,2,1,0:T(8,128)(2,1)S(1)}, bf16[4,2,64,768]{3,2,1,0:T(8,128)(2,1)S(1)}, u32[]{:S(2)}, u32[]{:S(2)}) collective-permute-start(bf16[4,2,64,768]{3,2,1,0:T(8,128)(2,1)S(1)} %pad_maximum_fusion.rest_0_), channel_id=1, source_target_pairs={{0,16},{4,20},{8,24},{12,28},{16,0},{20,4},{24,8},{28,12},{1,17},{... | collective-permute-start | bytes 2359304 | tf_op jit(solution)/shard_map/ppermute | solution.py:21
  27.8 14.6 %collective-permute-start.8 = (bf16[24,64,128]{2,1,0:T(8,128)(2,1)}, bf16[24,64,128]{2,1,0:T(8,128)(2,1)S(1)}, u32[]{:S(2)}, u32[]{:S(2)}) collective-permute-start(bf16[24,64,128]{2,1,0:T(8,128)(2,1)} %get-tuple-element.97), channel_id=1, source_target_pairs={{0,1},{1,0},{2,3},{3,2},{4,5},{5,4},{6,7},{7,6},{8,9},{9,8},{10,11... | collective-permute-start | bytes 1179656 | tf_op jit(solution)/shard_map/ppermute | solution.py:21
  42.5 17.6 %collective-permute-start.9 = (bf16[24,64,128]{2,1,0:T(8,128)(2,1)}, bf16[24,64,128]{2,1,0:T(8,128)(2,1)S(1)}, u32[]{:S(2)}, u32[]{:S(2)}) collective-permute-start(bf16[24,64,128]{2,1,0:T(8,128)(2,1)} %get-tuple-element.98), channel_id=1, source_target_pairs={{0,2},{1,3},{2,0},{3,1},{4,6},{5,7},{6,4},{7,5},{8,10},{9,11},{10,... | collective-permute-start | bytes 1179656 | tf_op jit(solution)/shard_map/ppermute | solution.py:21
  60.8 6.3 %collective-permute-start.11 = (bf16[4,2,64,768]{3,2,1,0:T(8,128)(2,1)S(1)}, bf16[4,2,64,768]{3,2,1,0:T(8,128)(2,1)}, u32[]{:S(2)}, u32[]{:S(2)}) collective-permute-start(bf16[4,2,64,768]{3,2,1,0:T(8,128)(2,1)S(1)} %pad_maximum_fusion.rest_0_), channel_id=1, source_target_pairs={{0,4},{4,0},{8,12},{12,8},{16,20},{20,16},{24,28},{28,24},{1,5},{5... | collective-permute-start | bytes 2359304 | tf_op jit(solution)/shard_map/ppermute | solution.py:21
  62.4 4.7 %collective-permute-start.12 = (bf16[4,2,64,768]{3,2,1,0:T(8,128)(2,1)S(1)}, bf16[4,2,64,768]{3,2,1,0:T(8,128)(2,1)}, u32[]{:S(2)}, u32[]{:S(2)}) collective-permute-start(bf16[4,2,64,768]{3,2,1,0:T(8,128)(2,1)S(1)} %collective-permute-done.5.rest_1_), channel_id=1, source_target_pairs={{0,4},{4,0},{8,12},{12,8},{16,20},{20,16},{24,28},{28,24},{1,5},{5... | collective-permute-start | bytes 2359304 | tf_op jit(solution)/shard_map/ppermute | solution.py:21
  62.5 6.5 %collective-permute-start.13 = (bf16[4,2,64,768]{3,2,1,0:T(8,128)(2,1)S(1)}, bf16[4,2,64,768]{3,2,1,0:T(8,128)(2,1)}, u32[]{:S(2)}, u32[]{:S(2)}) collective-permute-start(bf16[4,2,64,768]{3,2,1,0:T(8,128)(2,1)S(1)} %collective-permute-done.6.rest_2_), channel_id=1, source_target_pairs={{0,4},{4,0},{8,12},{12,8},{16,20},{20,16},{24,28},{28,24},{1,5},{5... | collective-permute-start | bytes 2359304 | tf_op jit(solution)/shard_map/ppermute | solution.py:21
  62.9 6.1 %collective-permute-start.14 = (bf16[4,2,64,768]{3,2,1,0:T(8,128)(2,1)S(1)}, bf16[4,2,64,768]{3,2,1,0:T(8,128)(2,1)}, u32[]{:S(2)}, u32[]{:S(2)}) collective-permute-start(bf16[4,2,64,768]{3,2,1,0:T(8,128)(2,1)S(1)} %collective-permute-done.7.rest_3_), channel_id=1, source_target_pairs={{0,4},{4,0},{8,12},{12,8},{16,20},{20,16},{24,28},{28,24},{1,5},{5... | collective-permute-start | bytes 2359304 | tf_op jit(solution)/shard_map/ppermute | solution.py:21
  63.7 29.6 %collective-permute-start.15 = (bf16[18,64,128]{2,1,0:T(8,128)(2,1)}, bf16[18,64,128]{2,1,0:T(8,128)(2,1)S(1)}, u32[]{:S(2)}, u32[]{:S(2)}) collective-permute-start(bf16[18,64,128]{2,1,0:T(8,128)(2,1)} %get-tuple-element.113), channel_id=1, source_target_pairs={{0,1},{1,0},{2,3},{3,2},{4,5},{5,4},{6,7},{7,6},{8,9},{9,8},{10,11... | collective-permute-start | bytes 884744 | tf_op jit(solution)/shard_map/ppermute | solution.py:21
  67.1 26.2 %collective-permute-start.16 = (bf16[18,64,128]{2,1,0:T(8,128)(2,1)}, bf16[18,64,128]{2,1,0:T(8,128)(2,1)S(1)}, u32[]{:S(2)}, u32[]{:S(2)}) collective-permute-start(bf16[18,64,128]{2,1,0:T(8,128)(2,1)} %get-tuple-element.114), channel_id=1, source_target_pairs={{0,2},{1,3},{2,0},{3,1},{4,6},{5,7},{6,4},{7,5},{8,10},{9,11},{10,... | collective-permute-start | bytes 884744 | tf_op jit(solution)/shard_map/ppermute | solution.py:21
  67.1 28.0 %collective-permute-start.17 = (bf16[18,64,128]{2,1,0:T(8,128)(2,1)}, bf16[18,64,128]{2,1,0:T(8,128)(2,1)}, u32[]{:S(2)}, u32[]{:S(2)}) collective-permute-start(bf16[18,64,128]{2,1,0:T(8,128)(2,1)} %get-tuple-element.115), channel_id=1, source_target_pairs={{0,3},{1,2},{2,1},{3,0},{4,7},{5,6},{6,5},{7,4},{8,11},{9,10},{10,... | collective-permute-start | bytes 884744 | tf_op jit(solution)/shard_map/ppermute | solution.py:21
  95.1 41.3 %collective-permute-start.18 = (bf16[64,4096]{1,0:T(8,128)(2,1)}, bf16[64,4096]{1,0:T(8,128)(2,1)S(1)}, u32[]{:S(2)}, u32[]{:S(2)}) collective-permute-start(bf16[64,4096]{1,0:T(8,128)(2,1)} %get-tuple-element.138), channel_id=1, source_target_pairs={{0,1},{1,0},{2,3},{3,2},{4,5},{5,4},{6,7},{7,6},{8,9},{9,8},{10,11... | collective-permute-start | bytes 1572872 | tf_op jit(solution)/shard_map/ppermute | solution.py:21
  96.3 40.2 %collective-permute-start.19 = (bf16[64,4096]{1,0:T(8,128)(2,1)}, bf16[64,4096]{1,0:T(8,128)(2,1)S(1)}, u32[]{:S(2)}, u32[]{:S(2)}) collective-permute-start(bf16[64,4096]{1,0:T(8,128)(2,1)} %get-tuple-element.139), channel_id=1, source_target_pairs={{0,2},{1,3},{2,0},{3,1},{4,6},{5,7},{6,4},{7,5},{8,10},{9,11},{10,... | collective-permute-start | bytes 1572872 | tf_op jit(solution)/shard_map/ppermute | solution.py:21
  96.3 45.9 %collective-permute-start.20 = (bf16[64,4096]{1,0:T(8,128)(2,1)}, bf16[64,4096]{1,0:T(8,128)(2,1)S(1)}, u32[]{:S(2)}, u32[]{:S(2)}) collective-permute-start(bf16[64,4096]{1,0:T(8,128)(2,1)} %get-tuple-element.140), channel_id=1, source_target_pairs={{0,3},{1,2},{2,1},{3,0},{4,7},{5,6},{6,5},{7,4},{8,11},{9,10},{10,... | collective-permute-start | bytes 1572872 | tf_op jit(solution)/shard_map/ppermute | solution.py:21
  143.1 9.4 %collective-permute-start.26 = (bf16[2,2,256,768]{3,2,1,0:T(8,128)(2,1)}, bf16[2,2,256,768]{3,2,1,0:T(8,128)(2,1)S(1)}, u32[]{:S(2)}, u32[]{:S(2)}) collective-permute-start(bf16[2,2,256,768]{3,2,1,0:T(8,128)(2,1)} %get-tuple-element.155), channel_id=1, source_target_pairs={{0,4},{4,0},{8,12},{12,8},{16,20},{20,16},{24,28},{28,24},{1,5},{5... | collective-permute-start | bytes 4718600 | tf_op jit(solution)/shard_map/ppermute | solution.py:21
  145.5 5.5 %collective-permute-start.21 = (bf16[2,256,768]{2,1,0:T(8,128)(2,1)}, bf16[2,256,768]{2,1,0:T(8,128)(2,1)}, u32[]{:S(2)}, u32[]{:S(2)}) collective-permute-start(bf16[2,256,768]{2,1,0:T(8,128)(2,1)} %get-tuple-element.147), channel_id=1, source_target_pairs={{0,4},{4,0},{8,12},{12,8},{16,20},{20,16},{24,28},{28,24},{1,5},{5... | collective-permute-start | bytes 2359304 | tf_op jit(solution)/shard_map/ppermute | solution.py:21
  145.5 28.4 %collective-permute-start.25 = (bf16[2,256,768]{2,1,0:T(8,128)(2,1)}, bf16[2,256,768]{2,1,0:T(8,128)(2,1)S(1)}, u32[]{:S(2)}, u32[]{:S(2)}) collective-permute-start(bf16[2,256,768]{2,1,0:T(8,128)(2,1)} %get-tuple-element.153), channel_id=1, source_target_pairs={{0,4},{4,0},{8,12},{12,8},{16,20},{20,16},{24,28},{28,24},{1,5},{5... | collective-permute-start | bytes 2359304 | tf_op jit(solution)/shard_map/ppermute | solution.py:21
  152.4 6.4 %collective-permute-start.29 = (bf16[2,64,768]{2,1,0:T(8,128)(2,1)S(1)}, bf16[2,64,768]{2,1,0:T(8,128)(2,1)S(1)}, u32[]{:S(2)}, u32[]{:S(2)}) collective-permute-start(bf16[2,64,768]{2,1,0:T(8,128)(2,1)S(1)} %get-tuple-element.177), channel_id=1, source_target_pairs={{0,1},{1,0},{2,3},{3,2},{4,5},{5,4},{6,7},{7,6},{8,9},{9,8},{10,11... | collective-permute-start | bytes 589832 | tf_op jit(solution)/shard_map/ppermute | solution.py:21
  152.7 21.2 %collective-permute-start.27 = (bf16[2,256,768]{2,1,0:T(8,128)(2,1)S(1)}, bf16[2,256,768]{2,1,0:T(8,128)(2,1)S(1)}, u32[]{:S(2)}, u32[]{:S(2)}) collective-permute-start(bf16[2,256,768]{2,1,0:T(8,128)(2,1)S(1)} %get-tuple-element.170), channel_id=1, source_target_pairs={{0,8},{4,12},{8,0},{12,4},{16,24},{20,28},{24,16},{28,20},{1,9},{5... | collective-permute-start | bytes 2359304 | tf_op jit(solution)/shard_map/ppermute | solution.py:21
  153.2 20.7 %collective-permute-start.28 = (bf16[2,256,768]{2,1,0:T(8,128)(2,1)S(1)}, bf16[2,256,768]{2,1,0:T(8,128)(2,1)S(1)}, u32[]{:S(2)}, u32[]{:S(2)}) collective-permute-start(bf16[2,256,768]{2,1,0:T(8,128)(2,1)S(1)} %get-tuple-element.171), channel_id=1, source_target_pairs={{0,16},{4,20},{8,24},{12,28},{16,0},{20,4},{24,8},{28,12},{1,17},{... | collective-permute-start | bytes 2359304 | tf_op jit(solution)/shard_map/ppermute | solution.py:21
  153.9 8.8 %collective-permute-start.30 = (bf16[2,64,768]{2,1,0:T(8,128)(2,1)S(1)}, bf16[2,64,768]{2,1,0:T(8,128)(2,1)S(1)}, u32[]{:S(2)}, u32[]{:S(2)}) collective-permute-start(bf16[2,64,768]{2,1,0:T(8,128)(2,1)S(1)} %get-tuple-element.179), channel_id=1, source_target_pairs={{0,2},{1,3},{2,0},{3,1},{4,6},{5,7},{6,4},{7,5},{8,10},{9,11},{10,... | collective-permute-start | bytes 589832 | tf_op jit(solution)/shard_map/ppermute | solution.py:21
  158.8 15.0 %collective-permute-start.31 = (bf16[2,64,768]{2,1,0:T(8,128)(2,1)S(1)}, bf16[2,64,768]{2,1,0:T(8,128)(2,1)S(1)}, u32[]{:S(2)}, u32[]{:S(2)}) collective-permute-start(bf16[2,64,768]{2,1,0:T(8,128)(2,1)S(1)} %get-tuple-element.178), channel_id=1, source_target_pairs={{0,3},{1,2},{2,1},{3,0},{4,7},{5,6},{6,5},{7,4},{8,11},{9,10},{10,... | collective-permute-start | bytes 589832 | tf_op jit(solution)/shard_map/ppermute | solution.py:21
  162.8 37.4 %collective-permute-start.22 = (bf16[512,128]{1,0:T(8,128)(2,1)S(1)}, bf16[512,128]{1,0:T(8,128)(2,1)S(1)}, u32[]{:S(2)}, u32[]{:S(2)}) collective-permute-start(bf16[512,128]{1,0:T(8,128)(2,1)S(1)} %copy-done.35), channel_id=1, source_target_pairs={{0,1},{1,0},{2,3},{3,2},{4,5},{5,4},{6,7},{7,6},{8,9},{9,8},{10,11... | collective-permute-start | bytes 393224 | tf_op jit(solution)/shard_map/ppermute | solution.py:21
  174.1 26.1 %copy-start.33 = (bf16[512,128]{1,0:T(8,128)(2,1)S(1)}, bf16[512,128]{1,0:T(8,128)(2,1)}, u32[]{:S(2)}) copy-start(bf16[512,128]{1,0:T(8,128)(2,1)} %get-tuple-element.151) | copy-start | bytes 393220
  174.2 5.4 %collective-permute-start.32 = (bf16[2,64,768]{2,1,0:T(8,128)(2,1)S(1)}, bf16[2,64,768]{2,1,0:T(8,128)(2,1)S(1)}, u32[]{:S(2)}, u32[]{:S(2)}) collective-permute-start(bf16[2,64,768]{2,1,0:T(8,128)(2,1)S(1)} %get-tuple-element.174), channel_id=1, source_target_pairs={{0,1},{1,0},{2,3},{3,2},{4,5},{5,4},{6,7},{7,6},{8,9},{9,8},{10,11... | collective-permute-start | bytes 589832 | tf_op jit(solution)/shard_map/ppermute | solution.py:21
  174.3 8.4 %collective-permute-start.33 = (bf16[2,64,768]{2,1,0:T(8,128)(2,1)S(1)}, bf16[2,64,768]{2,1,0:T(8,128)(2,1)S(1)}, u32[]{:S(2)}, u32[]{:S(2)}) collective-permute-start(bf16[2,64,768]{2,1,0:T(8,128)(2,1)S(1)} %get-tuple-element.176), channel_id=1, source_target_pairs={{0,2},{1,3},{2,0},{3,1},{4,6},{5,7},{6,4},{7,5},{8,10},{9,11},{10,... | collective-permute-start | bytes 589832 | tf_op jit(solution)/shard_map/ppermute | solution.py:21
  175.0 21.7 %collective-permute-start.34 = (bf16[2,64,768]{2,1,0:T(8,128)(2,1)S(1)}, bf16[2,64,768]{2,1,0:T(8,128)(2,1)S(1)}, u32[]{:S(2)}, u32[]{:S(2)}) collective-permute-start(bf16[2,64,768]{2,1,0:T(8,128)(2,1)S(1)} %get-tuple-element.175), channel_id=1, source_target_pairs={{0,3},{1,2},{2,1},{3,0},{4,7},{5,6},{6,5},{7,4},{8,11},{9,10},{10,... | collective-permute-start | bytes 589832 | tf_op jit(solution)/shard_map/ppermute | solution.py:21
  176.9 19.8 %collective-permute-start.35 = (bf16[2,64,768]{2,1,0:T(8,128)(2,1)S(1)}, bf16[2,64,768]{2,1,0:T(8,128)(2,1)S(1)}, u32[]{:S(2)}, u32[]{:S(2)}) collective-permute-start(bf16[2,64,768]{2,1,0:T(8,128)(2,1)S(1)} %add_add_fusion.2), channel_id=1, source_target_pairs={{0,24},{4,28},{8,16},{12,20},{16,8},{20,12},{24,0},{28,4},{1,25},{... | collective-permute-start | bytes 589832 | tf_op jit(solution)/shard_map/ppermute | solution.py:21
  178.7 38.4 %copy-start = (bf16[64,16384]{1,0:T(8,128)(2,1)}, bf16[64,16384]{1,0:T(8,128)(2,1)S(1)}, u32[]{:S(2)}) copy-start(bf16[64,16384]{1,0:T(8,128)(2,1)S(1)} %constant_dynamic-update-slice_fusion.4) | copy-start | bytes 6291460
  179.6 20.7 %collective-permute-start.23 = (bf16[512,128]{1,0:T(8,128)(2,1)S(1)}, bf16[512,128]{1,0:T(8,128)(2,1)S(1)}, u32[]{:S(2)}, u32[]{:S(2)}) collective-permute-start(bf16[512,128]{1,0:T(8,128)(2,1)S(1)} %copy-done.34), channel_id=1, source_target_pairs={{0,2},{1,3},{2,0},{3,1},{4,6},{5,7},{6,4},{7,5},{8,10},{9,11},{10,... | collective-permute-start | bytes 393224 | tf_op jit(solution)/shard_map/ppermute | solution.py:21
  196.9 6.6 %collective-permute-start.36 = (bf16[2,64,768]{2,1,0:T(8,128)(2,1)S(1)}, bf16[2,64,768]{2,1,0:T(8,128)(2,1)S(1)}, u32[]{:S(2)}, u32[]{:S(2)}) collective-permute-start(bf16[2,64,768]{2,1,0:T(8,128)(2,1)S(1)} %add_add_fusion.1.rest_0_), channel_id=1, source_target_pairs={{0,8},{4,12},{8,0},{12,4},{16,24},{20,28},{24,16},{28,20},{1,9},{5... | collective-permute-start | bytes 589832 | tf_op jit(solution)/shard_map/ppermute | solution.py:21
  198.8 8.4 %collective-permute-start.37 = (bf16[2,64,768]{2,1,0:T(8,128)(2,1)S(1)}, bf16[2,64,768]{2,1,0:T(8,128)(2,1)S(1)}, u32[]{:S(2)}, u32[]{:S(2)}) collective-permute-start(bf16[2,64,768]{2,1,0:T(8,128)(2,1)S(1)} %add_add_fusion.1.rest_0_), channel_id=1, source_target_pairs={{0,16},{4,20},{8,24},{12,28},{16,0},{20,4},{24,8},{28,12},{1,17},{... | collective-permute-start | bytes 589832 | tf_op jit(solution)/shard_map/ppermute | solution.py:21
  199.0 11.3 %collective-permute-start.38 = (bf16[2,64,768]{2,1,0:T(8,128)(2,1)S(1)}, bf16[2,64,768]{2,1,0:T(8,128)(2,1)S(1)}, u32[]{:S(2)}, u32[]{:S(2)}) collective-permute-start(bf16[2,64,768]{2,1,0:T(8,128)(2,1)S(1)} %add_add_fusion.1.rest_0_), channel_id=1, source_target_pairs={{0,24},{4,28},{8,16},{12,20},{16,8},{20,12},{24,0},{28,4},{1,25},{... | collective-permute-start | bytes 589832 | tf_op jit(solution)/shard_map/ppermute | solution.py:21
  200.2 10.2 %collective-permute-start.24 = (bf16[512,128]{1,0:T(8,128)(2,1)S(1)}, bf16[512,128]{1,0:T(8,128)(2,1)S(1)}, u32[]{:S(2)}, u32[]{:S(2)}) collective-permute-start(bf16[512,128]{1,0:T(8,128)(2,1)S(1)} %copy-done.33), channel_id=1, source_target_pairs={{0,3},{1,2},{2,1},{3,0},{4,7},{5,6},{6,5},{7,4},{8,11},{9,10},{10,... | collective-permute-start | bytes 393224 | tf_op jit(solution)/shard_map/ppermute | solution.py:21
  200.3 10.2 %collective-permute-start.39 = (bf16[2,64,768]{2,1,0:T(8,128)(2,1)S(1)}, bf16[2,64,768]{2,1,0:T(8,128)(2,1)S(1)}, u32[]{:S(2)}, u32[]{:S(2)}) collective-permute-start(bf16[2,64,768]{2,1,0:T(8,128)(2,1)S(1)} %add_add_fusion.1.rest_0_), channel_id=1, source_target_pairs={{0,4},{4,0},{8,12},{12,8},{16,20},{20,16},{24,28},{28,24},{1,5},{5... | collective-permute-start | bytes 589832 | tf_op jit(solution)/shard_map/ppermute | solution.py:21
  203.5 7.0 %collective-permute-start.40 = (bf16[2,64,768]{2,1,0:T(8,128)(2,1)S(1)}, bf16[2,64,768]{2,1,0:T(8,128)(2,1)S(1)}, u32[]{:S(2)}, u32[]{:S(2)}) collective-permute-start(bf16[2,64,768]{2,1,0:T(8,128)(2,1)S(1)} %collective-permute-done.36.rest_1_), channel_id=1, source_target_pairs={{0,4},{4,0},{8,12},{12,8},{16,20},{20,16},{24,28},{28,24},{1,5},{5... | collective-permute-start | bytes 589832 | tf_op jit(solution)/shard_map/ppermute | solution.py:21
  207.2 4.2 %collective-permute-start.41 = (bf16[2,64,768]{2,1,0:T(8,128)(2,1)S(1)}, bf16[2,64,768]{2,1,0:T(8,128)(2,1)S(1)}, u32[]{:S(2)}, u32[]{:S(2)}) collective-permute-start(bf16[2,64,768]{2,1,0:T(8,128)(2,1)S(1)} %collective-permute-done.37.rest_2_), channel_id=1, source_target_pairs={{0,4},{4,0},{8,12},{12,8},{16,20},{20,16},{24,28},{28,24},{1,5},{5... | collective-permute-start | bytes 589832 | tf_op jit(solution)/shard_map/ppermute | solution.py:21
  210.3 1.6 collective-permute-start.42
  (31 other events, 243.1 us)

commit v6 on v5

--- a/solution.py
+++ b/solution.py
@@ -37,6 +37,10 @@
 
 
 SPREAD_PLACES = [0, 2, 4, 6, 1, 3, 5, 7]
+
+
+def own_places():
+    return lax.axis_index("tm") % 8, lax.axis_index("chan")
 
 
 def nt(left, right):
@@ -153,10 +157,9 @@
     masked_move(store, 17 + phase, values, mask_ref, 1)
 
 
-def pack_weights_kernel(
-    places, sec_ref, three_ref, mix_ref, skip_ref, bs, bt, bm, bk, gt, gm, gk, out, wide, rows, mats
+def pack_weights_kernel(sec_ref, three_ref, mix_ref, skip_ref, bs, bt, bm, bk, gt, gm, gk, out, wide, rows, mats
 ):
-    turn = places[0]
+    turn, _ = own_places()
     for q in range(4):
         part = sec_ref[:, :, 128 * q : 128 * q + 128].astype(F32)
         wide[q] = part.reshape(1024, 128)
@@ -187,9 +190,9 @@
         out[tap, :, 512:768] = mats[2 * turn + tap]
 
 
-def pack_frames_kernel(places, low, high, signal, cotangent, *rest):
+def pack_frames_kernel(low, high, signal, cotangent, *rest):
     firsts, seconds = rest[0:4], rest[4:8]
-    chan = places[1]
+    _, chan = own_places()
     own = signal.shape[0] // 4
     frames = 8 * own
     count = own // 64
@@ -232,11 +235,11 @@
         )
 
 
-def finish_kernel(places, sec_ref, three_ref, mix_ref, skip_ref, gt, gm, gk, stat, *rest):
+def finish_kernel(sec_ref, three_ref, mix_ref, skip_ref, gt, gm, gk, stat, *rest):
     pieces = rest[:8]
     sec_out, gain_out, bs, three_out, gt_out, bt, mix_out, gm_out, bm, skip_out, gk_out, bk = rest[8:20]
     wide, rows, mats = rest[20:]
-    turn = places[0]
+    turn, _ = own_places()
     for ref, place in zip(pieces, SPREAD_PLACES, strict=True):
         pair = 2 * (turn ^ place)
         for tap in range(2):
@@ -293,8 +296,8 @@
     gk_out[...] = rows[14:17, 0:64]
 
 
-def weight_copies(places, refs, wsec, wblk, sem, block_sem):
-    turn, chan = places[0], places[1]
+def weight_copies(refs, wsec, wblk, sem, block_sem):
+    turn, chan = own_places()
     section, blocks = [], []
     for index, (ref, (place, _, _)) in enumerate(zip(refs, WEIGHT_PLACES, strict=True)):
         slots = pl.ds(2 * (turn ^ place), 2)
@@ -310,7 +313,6 @@
 
 
 def forward_kernel(
-    places,
     sig0,
     sig1,
     sig2,
@@ -326,11 +328,11 @@
     wsec, wblk, cat, bias, wide, turned, flat = rest[11:18]
     hids, mixs, inners, acts = rest[18:21], rest[21:24], rest[24:27], rest[27:30]
     wsem, vsem, ssem = rest[30:]
-    chan = places[1]
+    _, chan = own_places()
     rows = sact_out.shape[0]
     own = rows - 2 * HALO
     pitch = own // 2 + 1
-    section_loads, block_loads = weight_copies(places, pieces, wsec, wblk, wsem, vsem)
+    section_loads, block_loads = weight_copies(pieces, wsec, wblk, wsem, vsem)
     for copy in sum(section_loads, []) + block_loads:
         copy.start()
     fill_masks(ids_ref, flat, mask_out)
@@ -345,7 +347,7 @@
         for copy in copies:
             copy.wait()
         for tap in range(2):
-            part = wsec[2 * (places[0] ^ place) + tap].astype(F32)
+            part = wsec[2 * (own_places()[0] ^ place) + tap].astype(F32)
             total = total + jnp.sum((part * part).reshape(32, 8, 512), axis=0)
     for copy in block_loads:
         copy.wait()
@@ -451,7 +453,6 @@
 
 
 def backward_kernel(
-    places,
     first0,
     first1,
     first2,
@@ -482,11 +483,11 @@
     (wsec, wblk, turned, sigs, wide, grad, inner_a, inner_b, mix, hid, act, halves) = rest[10:22]
     (acc_one, acc_three, through, sums, staged, wsem, vsem, gsem, csem, bsem, osem) = rest[22:]
     pitch = 4 * (sact_ref.shape[0] - 2 * HALO) // 8 + 1
-    turn_index, chan = places[0], places[1]
+    turn_index, chan = own_places()
     rows = mask_ref.shape[1]
     own = rows - 2 * HALO
 
-    section_weights, block_loads = weight_copies(places, pieces, wsec, wblk, wsem, vsem)
+    section_weights, block_loads = weight_copies(pieces, wsec, wblk, wsem, vsem)
     cots = []
     count = own // 64
     section_loads = []
@@ -729,11 +730,11 @@
     return pl.CostEstimate(flops=int(flops), bytes_accessed=int(moved_bytes), transcendentals=0)
 
 
-def run_pack_weights(places, *arrays):
+def run_pack_weights(*arrays):
     return pl.pallas_call(
         pack_weights_kernel,
         out_shape=shape_of((2, 64, 768)),
-        in_specs=[SPEC_SMEM] + [SPEC_VMEM] * 11,
+        in_specs=[SPEC_VMEM] * 11,
         out_specs=SPEC_VMEM,
         scratch_shapes=[
             pltpu.VMEM((4, 1024, 128), F32),
@@ -743,24 +744,24 @@
         compiler_params=params(),
         cost_estimate=cost(2e7, 3e6),
         name="pack_weights",
-    )(places, *arrays)
-
-
-def run_pack_frames(places, low, high, signal, cotangent):
+    )(*arrays)
+
+
+def run_pack_frames(low, high, signal, cotangent):
     own = signal.shape[0] // 4
     return pl.pallas_call(
         pack_frames_kernel,
         out_shape=[shape_of((own // 64 + 1 + EARLY, 64, 128))] * 4
         + [shape_of((8 * own // 128 + 1 - EARLY, 64, 128))] * 4,
-        in_specs=[SPEC_SMEM] + [SPEC_VMEM] * 4,
+        in_specs=[SPEC_VMEM] * 4,
         out_specs=[SPEC_VMEM] * 8,
         compiler_params=params(),
         cost_estimate=cost(1e6, 6e6),
         name="pack_frames",
-    )(places, low, high, signal, cotangent)
-
-
-def run_finish(places, v_section, three, v_mix, v_skip, g_dilated, g_mix, g_skip, stat, pieces):
+    )(low, high, signal, cotangent)
+
+
+def run_finish(v_section, three, v_mix, v_skip, g_dilated, g_mix, g_skip, stat, pieces):
     small = shape_of((3, 64), F32)
     out_shape = [
         shape_of((64, 16, 512), F32),
@@ -779,7 +780,7 @@
     return pl.pallas_call(
         finish_kernel,
         out_shape=out_shape,
-        in_specs=[SPEC_SMEM] + [SPEC_VMEM] * 16,
+        in_specs=[SPEC_VMEM] * 16,
         out_specs=[SPEC_VMEM] * 12,
         scratch_shapes=[
             pltpu.VMEM((4, 64 * 17, 128), F32),
@@ -789,10 +790,10 @@
         compiler_params=params(),
         cost_estimate=cost(2e7, 8e6),
         name="finish_weights",
-    )(places, v_section, three, v_mix, v_skip, g_dilated, g_mix, g_skip, stat, *pieces)
-
-
-def run_forward(places, firsts, ids, gain, pieces):
+    )(v_section, three, v_mix, v_skip, g_dilated, g_mix, g_skip, stat, *pieces)
+
+
+def run_forward(firsts, ids, gain, pieces):
     own = ids.shape[0] - 32
     rows = own + 2 * HALO
     kept = shape_of((3, 8, rows, 256))
@@ -805,7 +806,7 @@
     return pl.pallas_call(
         forward_kernel,
         out_shape=out_shape,
-        in_specs=[SPEC_SMEM] + [SPEC_VMEM] * 6 + [SPEC_ANY] * 8,
+        in_specs=[SPEC_VMEM] * 6 + [SPEC_ANY] * 8,
         out_specs=[SPEC_ANY] * 4 + [SPEC_VMEM] * 3 + [SPEC_ANY] * 4,
         scratch_shapes=[
             pltpu.VMEM((16, 256, 512), BF16),
@@ -822,10 +823,10 @@
         compiler_params=params(),
         cost_estimate=cost(2 * 1245184 * 8 * rows, 50e6),
         name="forward_blocks",
-    )(places, *firsts, ids, gain, *pieces)
-
-
-def run_backward(places, firsts, seconds, sact, masks, stat, kept, pieces):
+    )(*firsts, ids, gain, *pieces)
+
+
+def run_backward(firsts, seconds, sact, masks, stat, kept, pieces):
     rows = sact.shape[0]
     own = rows - 2 * HALO
     return pl.pallas_call(
@@ -837,8 +838,7 @@
         ]
         * 2
         + [shape_of((own, 128))] * 4,
-        in_specs=[SPEC_SMEM]
-        + [SPEC_ANY] * 8
+        in_specs=[SPEC_ANY] * 8
         + [SPEC_VMEM] * 3
         + [SPEC_ANY] * 12,
         out_specs=[SPEC_ANY] * 6 + [SPEC_VMEM] * 4,
@@ -870,7 +870,7 @@
         compiler_params=params(),
         cost_estimate=cost(2 * 2490368 * 8 * rows, 60e6),
         name="backward_blocks",
-    )(places, *firsts, *seconds, sact, masks, stat, *kept, *pieces)
+    )(*firsts, *seconds, sact, masks, stat, *kept, *pieces)
 
 
 def exchange(values, axis, cut):
@@ -901,15 +901,13 @@
     tm_index, chan = lax.axis_index("tm"), lax.axis_index("chan")
     tm_size = lax.axis_size("tm")
     turn = tm_index % 8
-    places = jnp.stack([turn, chan]).astype(jnp.int32)
     own = signal.shape[0] // 4
     rows = own + 2 * HALO
     start = tm_index * signal.shape[0] + chan * own
 
     three_v = jnp.transpose(v_dilated, (0, 2, 1, 3))
     piece = run_pack_weights(
-        places,
-        v_section,
+            v_section,
         three_v,
         v_mix,
         v_skip,
@@ -928,7 +926,7 @@
     onward = [(i, i + 1) for i in range(tm_size - 1)]
     low = lax.ppermute(final, "tm", onward)
     high = lax.ppermute(first, "tm", [(target, source) for source, target in onward])
-    packed = run_pack_frames(places, low, high, signal, cotangent)
+    packed = run_pack_frames(low, high, signal, cotangent)
     firsts, seconds = list(packed[0:4]), list(packed[4:8])
     by_chan, _ = lax.optimization_barrier((by_chan, packed[0]))
     for k in (1, 2, 3):
@@ -940,12 +938,12 @@
     ids = jnp.broadcast_to(nearby[:, None], (own + 32, 128))
 
     frames = 8 * own
-    results = run_forward(places, firsts, ids, g_section[None].astype(F32), pieces)
+    results = run_forward(firsts, ids, g_section[None].astype(F32), pieces)
     kept, sact, masks, stat, outs = results[:4], results[4], results[5], results[6], results[7:]
 
     outs, seconds = lax.optimization_barrier((list(outs), seconds))
     received = [outs[0]] + [swap(outs[k], "chan", k) for k in (1, 2, 3)]
-    results = run_backward(places, firsts, seconds, sact, masks, stat, kept, pieces)
+    results = run_backward(firsts, seconds, sact, masks, stat, kept, pieces)
     far, sides, here, odd_far, odd_sides, odd_here = results[0:6]
     sgrads = results[6:]
     far, sides, here, odd_far, odd_sides, odd_here, sgrads, received = lax.optimization_barrier(
@@ -965,8 +963,9 @@
     output = jnp.zeros((64, 4 * frames), BF16)
     for k in range(4):
         output = lax.dynamic_update_slice_in_dim(output, received[k], (chan ^ k) * frames, axis=1)
+    for_x, for_y = sides[0] + odd_sides[0], sides[1] + odd_sides[1]
+    far, for_x, for_y, odd_here = lax.optimization_barrier((far, for_x, for_y, odd_here))
     across = chan_sum(far)
-    for_x, for_y = sides[0] + odd_sides[0], sides[1] + odd_sides[1]
     sgrad_near = swap(sgrads[1], "chan", 1)
     far, sgrad_near = lax.optimization_barrier((far, sgrad_near))
     summed = (here + odd_here) + swap(for_x, "tm", 2) + swap(for_y, "tm", 4)
@@ -985,7 +984,7 @@
             signal_grad, received[k], (chan ^ k) * own, axis=0
         )
     (sec, gain, bs, three, gt, bt, mix, gm, bm, skip, gk, bk) = run_finish(
-        places, v_section, three_v, v_mix, v_skip, g_dilated, g_mix, g_skip, stat, gathered
+        v_section, three_v, v_mix, v_skip, g_dilated, g_mix, g_skip, stat, gathered
     )
     return (
         output,

time: 218 us -> 214 us (0.982)
  starting transfers between devices: 61.6 us -> 54.4 us
  waiting for transfers between devices: 70.9 us -> 76.2 us
    ppermute x41, starting transfers between devices: 55.1 us -> 47.9 us  [swap(): return lax.ppermute(values, axis, xor_pairs(axis, bit))]
    ppermute x41, waiting for transfers between devices: 67.7 us -> 73 us  [swap(): return lax.ppermute(values, axis, xor_pairs(axis, bit))]
  transfers between devices with their start and end apart: 43 -> 43, of which waited for: 14 -> 16; matrix products, arithmetic and copies ran while one was open for 3% -> 3% of each run, Pallas kernels for 30% -> 31%
where the time goes in v6:
time: 214 us; the launch traced here: 213 us
  waiting for transfers between devices  76.2 us (36%)
  Pallas kernels  74.2 us (35%)
  starting transfers between devices  54.4 us (25%)
  local copies, waits for them, and re-layouts  5.75 us (3%)
    ppermute x41, waiting for transfers between devices, swap(): return lax.ppermute(values, axis, xor_pairs(axis, bit))  73 us
    ppermute x41, starting transfers between devices, swap(): return lax.ppermute(values, axis, xor_pairs(axis, bit))  47.9 us
    pallas_call x1, Pallas kernels, run_backward(): pl.pallas_call(backward_kernel, out_shape=[shape_of((2, 256, 768)), shape...  38.7 us
    pallas_call x1, Pallas kernels, run_forward(): pl.pallas_call(forward_kernel, out_shape=out_shape, in_specs=[SPEC_VMEM]...  23.4 us
    pallas_call x1, Pallas kernels, run_finish(): pl.pallas_call(finish_kernel, out_shape=out_shape, in_specs=[SPEC_VMEM] *...  4.92 us
    ppermute x1, starting transfers between devices, body(): low = lax.ppermute(final, 'tm', onward)  4.51 us
  transfers between devices with their start and end apart: 43, of which 16 were waited for; matrix products, arithmetic and copies ran while one was open for 3% of the time, Pallas kernels for 31%

profile of v6, /device:TPU:9, one launch (start us, length us, event | category | flops | bytes accessed | tf_op | source)
XLA Modules:
  0.0 213.4 jit_solution(8495829706533052947)
XLA Ops:
  0.6 3.3 %pack_weights.1 = bf16[2,64,768]{2,1,0:T(8,128)(2,1)} custom-call(bf16[64,16,512]{2,1,0:T(8,128)(2,1)} %sec_ref.3, bf16[3,3,64,256]{3,2,1,0:T(8,128)(2,1)} %bitcast.14, bf16[3,64,256]{2,1,0:T(8,128)(2,1)} %mix_ref.3, bf16[3,64,256]{2,1,0:T(8,128)(2,1)} %skip_ref.3, bf16[1,64]{1,0:T(2,128)(2,1)} %bitcast.21, bf16[3,64]{1,0:T(4,128)(2,1)} %bt.1, ...), custom_call_target="tpu_custom_call" | custom-call | flops 20000000 | bytes 3000000 | tf_op jit(solution)/shard_map/pack_weights/pallas_call | solution.py:734
  3.9 2.5 %collective-permute-start.1 = (bf16[2,64,768]{2,1,0:T(8,128)(2,1)}, bf16[2,64,768]{2,1,0:T(8,128)(2,1)S(1)}, u32[]{:S(2)}, u32[]{:S(2)}) collective-permute-start(bf16[2,64,768]{2,1,0:T(8,128)(2,1)} %pack_weights.1), channel_id=1, source_target_pairs={{0,2},{1,3},{2,0},{3,1},{4,6},{5,7},{6,4},{7,5},{8,10},{9,11},{10,... | collective-permute-start | bytes 589832 | tf_op jit(solution)/shard_map/ppermute | solution.py:21
  6.6 0.7 fusion.2
  7.3 0.7 fusion.3
  8.0 4.5 %collective-permute-start.3 = (bf16[80,128]{1,0:T(8,128)(2,1)S(1)}, bf16[80,128]{1,0:T(8,128)(2,1)S(1)}, u32[]{:S(2)}, u32[]{:S(2)}) collective-permute-start(bf16[80,128]{1,0:T(8,128)(2,1)S(1)} %pad_maximum_fusion.1), channel_id=1, source_target_pairs={{0,4},{4,8},{8,12},{12,16},{16,20},{20,24},{24,28},{1,5},{5,9},{9,... | collective-permute-start | bytes 61448 | tf_op jit(solution)/shard_map/ppermute | solution.py:927
  12.6 2.1 collective-permute-start.4
  14.7 3.2 %collective-permute-done.4.high = bf16[80,128]{1,0:T(8,128)(2,1)S(1)} collective-permute-done((bf16[80,128]{1,0:T(8,128)(2,1)S(1)}, bf16[80,128]{1,0:T(8,128)(2,1)S(1)}, u32[]{:S(2)}, u32[]{:S(2)}) %collective-permute-start.4) | collective-permute-done | bytes 20512 | tf_op jit(solution)/shard_map/ppermute | solution.py:928
  18.4 3.9 %pack_frames.1 = (bf16[24,64,128]{2,1,0:T(8,128)(2,1)}, bf16[24,64,128]{2,1,0:T(8,128)(2,1)}, bf16[24,64,128]{2,1,0:T(8,128)(2,1)}, bf16[24,64,128]{2,1,0:T(8,12...) custom-call(bf16[80,128]{1,0:T(8,128)(2,1)} %copy-done.22, ...), custom_call_target="tpu_custom_call" | custom-call | flops 1000000 | bytes 6000000 | tf_op jit(solution)/shard_map/pack_frames/pallas_call | solution.py:752
  22.4 1.3 collective-permute-start.10
  23.8 2.1 collective-permute-start.5
  26.3 0.9 collective-permute-start.7
  27.2 3.4 %collective-permute-start.8 = (bf16[24,64,128]{2,1,0:T(8,128)(2,1)}, bf16[24,64,128]{2,1,0:T(8,128)(2,1)S(1)}, u32[]{:S(2)}, u32[]{:S(2)}) collective-permute-start(bf16[24,64,128]{2,1,0:T(8,128)(2,1)} %get-tuple-element.101), channel_id=1, source_target_pairs={{0,1},{1,0},{2,3},{3,2},{4,5},{5,4},{6,7},{7,6},{8,9},{9,8},{10,11... | collective-permute-start | bytes 1179656 | tf_op jit(solution)/shard_map/ppermute | solution.py:21
  30.6 11.2 %collective-permute-done.10.sig3.first3 = bf16[24,64,128]{2,1,0:T(8,128)(2,1)S(1)} collective-permute-done((bf16[24,64,128]{2,1,0:T(8,128)(2,1)}, bf16[24,64,128]{2,1,0:T(8,128)(2,1)S(1)}, u32[]{:S(2)}, u32[]{:S(2)}) %collective-permute-start.10) | collective-permute-done | bytes 393248 | tf_op jit(solution)/shard_map/ppermute | solution.py:21
  41.8 17.5 %collective-permute-done.9.sig2.first2 = bf16[24,64,128]{2,1,0:T(8,128)(2,1)S(1)} collective-permute-done((bf16[24,64,128]{2,1,0:T(8,128)(2,1)}, bf16[24,64,128]{2,1,0:T(8,128)(2,1)S(1)}, u32[]{:S(2)}, u32[]{:S(2)}) %collective-permute-start.9) | collective-permute-done | bytes 393248 | tf_op jit(solution)/shard_map/ppermute | solution.py:21
  59.4 0.7 collective-permute-done.7.rest_3_
  60.1 1.6 collective-permute-start.11
  63.0 3.4 %collective-permute-start.15 = (bf16[18,64,128]{2,1,0:T(8,128)(2,1)}, bf16[18,64,128]{2,1,0:T(8,128)(2,1)S(1)}, u32[]{:S(2)}, u32[]{:S(2)}) collective-permute-start(bf16[18,64,128]{2,1,0:T(8,128)(2,1)} %get-tuple-element.117), channel_id=1, source_target_pairs={{0,1},{1,0},{2,3},{3,2},{4,5},{5,4},{6,7},{7,6},{8,9},{9,8},{10,11... | collective-permute-start | bytes 884744 | tf_op jit(solution)/shard_map/ppermute | solution.py:21
  66.4 2.0 collective-permute-start.17
  68.4 0.8 broadcast_in_dim.18.ids_ref
  69.2 23.4 %forward_blocks.1 = (bf16[3,8,528,256]{3,2,1,0:T(8,128)(2,1)}, bf16[3,8,528,256]{3,2,1,0:T(8,128)(2,1)}, bf16[3,8,528,256]{3,2,1,0:T(8,128)(2,1)}, bf16[3,8,528,...) custom-call(bf16[24,64,128]{2,1,0:T(8,128)(2,1)} %get-tuple-element., ...), custom_call_target="tpu_custom_call" | custom-call | flops 10519314432 | bytes 50000000 | tf_op jit(solution)/shard_map/forward_blocks/pallas_call | solution.py:806
  92.7 1.8 collective-permute-done.17.second3
  94.5 1.2 collective-permute-start.18
  95.6 1.5 collective-permute-start.20
  97.1 38.7 %backward_blocks.1 = (bf16[2,256,768]{2,1,0:T(8,128)(2,1)}, bf16[2,2,256,768]{3,2,1,0:T(8,128)(2,1)}, bf16[2,256,768]{2,1,0:T(8,128)(2,1)}, bf16[2,256,768]{2,1,...) custom-call(bf16[24,64,128]{2,1,0:T(8,128)(2,1)} %get-tuple-element., ...), custom_call_target="tpu_custom_call" | custom-call | flops 21038628864 | bytes 60000000 | tf_op jit(solution)/shard_map/backward_blocks/pallas_call | solution.py:832
  135.8 5.8 %collective-permute-done.20 = bf16[64,4096]{1,0:T(8,128)(2,1)S(1)} collective-permute-done((bf16[64,4096]{1,0:T(8,128)(2,1)}, bf16[64,4096]{1,0:T(8,128)(2,1)S(1)}, u32[]{:S(2)}, u32[]{:S(2)}) %collective-permute-start.20) | collective-permute-done | bytes 524320 | tf_op jit(solution)/shard_map/ppermute | solution.py:21
  141.6 0.8 copy-done.8
  142.4 2.4 %collective-permute-start.22 = (bf16[2,2,256,768]{3,2,1,0:T(8,128)(2,1)}, bf16[2,2,256,768]{3,2,1,0:T(8,128)(2,1)S(1)}, u32[]{:S(2)}, u32[]{:S(2)}) collective-permute-start(bf16[2,2,256,768]{3,2,1,0:T(8,128)(2,1)} %get-tuple-element.153), channel_id=1, source_target_pairs={{0,4},{4,0},{8,12},{12,8},{16,20},{20,16},{24,28},{28,24},{1,5},{5... | collective-permute-start | bytes 4718600 | tf_op jit(solution)/shard_map/ppermute | solution.py:21
  145.4 1.2 constant_dynamic-update-slice_fusion.7
  146.7 2.4 %collective-permute-done.21 = bf16[2,256,768]{2,1,0:T(8,128)(2,1)S(1)} collective-permute-done((bf16[2,256,768]{2,1,0:T(8,128)(2,1)}, bf16[2,256,768]{2,1,0:T(8,128)(2,1)S(1)}, u32[]{:S(2)}, u32[]{:S(2)}) %collective-permute-start.21) | collective-permute-done | bytes 786464 | tf_op jit(solution)/shard_map/ppermute | solution.py:21
  149.6 0.7 collective-permute-done.23
  151.4 1.3 collective-permute-start.30
  152.7 1.3 collective-permute-start.31
  154.1 3.1 %collective-permute-done.29 = bf16[2,64,768]{2,1,0:T(8,128)(2,1)S(1)} collective-permute-done((bf16[2,64,768]{2,1,0:T(8,128)(2,1)S(1)}, bf16[2,64,768]{2,1,0:T(8,128)(2,1)S(1)}, u32[]{:S(2)}, u32[]{:S(2)}) %collective-permute-start.29) | collective-permute-done | bytes 196640 | tf_op jit(solution)/shard_map/ppermute | solution.py:21
  157.2 2.7 %collective-permute-start.24 = (bf16[512,128]{1,0:T(8,128)(2,1)S(1)}, bf16[512,128]{1,0:T(8,128)(2,1)S(1)}, u32[]{:S(2)}, u32[]{:S(2)}) collective-permute-start(bf16[512,128]{1,0:T(8,128)(2,1)S(1)} %copy-done.35), channel_id=1, source_target_pairs={{0,1},{1,0},{2,3},{3,2},{4,5},{5,4},{6,7},{7,6},{8,9},{9,8},{10,11... | collective-permute-start | bytes 393224 | tf_op jit(solution)/shard_map/ppermute | solution.py:21
  159.9 1.1 collective-permute-done.30
  161.0 9.8 %collective-permute-done.31 = bf16[2,64,768]{2,1,0:T(8,128)(2,1)S(1)} collective-permute-done((bf16[2,64,768]{2,1,0:T(8,128)(2,1)S(1)}, bf16[2,64,768]{2,1,0:T(8,128)(2,1)S(1)}, u32[]{:S(2)}, u32[]{:S(2)}) %collective-permute-start.31) | collective-permute-done | bytes 196640 | tf_op jit(solution)/shard_map/ppermute | solution.py:21
  171.3 1.0 collective-permute-start.33
  172.3 1.6 collective-permute-start.34
  174.0 1.5 collective-permute-start.35
  176.5 2.6 %collective-permute-done.33 = bf16[2,64,768]{2,1,0:T(8,128)(2,1)S(1)} collective-permute-done((bf16[2,64,768]{2,1,0:T(8,128)(2,1)S(1)}, bf16[2,64,768]{2,1,0:T(8,128)(2,1)S(1)}, u32[]{:S(2)}, u32[]{:S(2)}) %collective-permute-start.33) | collective-permute-done | bytes 196640 | tf_op jit(solution)/shard_map/ppermute | solution.py:21
  179.1 14.4 %collective-permute-done.34 = bf16[2,64,768]{2,1,0:T(8,128)(2,1)S(1)} collective-permute-done((bf16[2,64,768]{2,1,0:T(8,128)(2,1)S(1)}, bf16[2,64,768]{2,1,0:T(8,128)(2,1)S(1)}, u32[]{:S(2)}, u32[]{:S(2)}) %collective-permute-start.34) | collective-permute-done | bytes 196640 | tf_op jit(solution)/shard_map/ppermute | solution.py:21
  193.7 1.4 collective-permute-start.36
  195.5 0.9 collective-permute-start.38
  196.7 5.6 %collective-permute-start.39 = (bf16[2,64,768]{2,1,0:T(8,128)(2,1)S(1)}, bf16[2,64,768]{2,1,0:T(8,128)(2,1)S(1)}, u32[]{:S(2)}, u32[]{:S(2)}) collective-permute-start(bf16[2,64,768]{2,1,0:T(8,128)(2,1)S(1)} %add_add_fusion.1.rest_0_), channel_id=1, source_target_pairs={{0,4},{4,0},{8,12},{12,8},{16,20},{20,16},{24,28},{28,24},{1,5},{5... | collective-permute-start | bytes 589832 | tf_op jit(solution)/shard_map/ppermute | solution.py:21
  202.3 1.3 collective-permute-start.40
  203.6 3.0 %collective-permute-start.41 = (bf16[2,64,768]{2,1,0:T(8,128)(2,1)S(1)}, bf16[2,64,768]{2,1,0:T(8,128)(2,1)S(1)}, u32[]{:S(2)}, u32[]{:S(2)}) collective-permute-start(bf16[2,64,768]{2,1,0:T(8,128)(2,1)S(1)} %collective-permute-done.37.rest_2_), channel_id=1, source_target_pairs={{0,4},{4,0},{8,12},{12,8},{16,20},{20,16},{24,28},{28,24},{1,5},{5... | collective-permute-start | bytes 589832 | tf_op jit(solution)/shard_map/ppermute | solution.py:21
  206.8 0.9 collective-permute-done.41.rest_6_
  208.3 4.9 %finish_weights.1 = (f32[64,16,512]{2,1,0:T(8,128)}, f32[1,512]{1,0:T(1,128)}, f32[1,64]{1,0:T(1,128)}, f32[3,3,64,256]{3,2,1,0:T(8,128)}, f32[3,64]{1,0:T(4,128...) custom-call(bf16[64,16,512]{2,1,0:T(8,128)(2,1)} %sec_ref.3, ...), custom_call_target="tpu_custom_call" | custom-call | flops 20000000 | bytes 8000000 | tf_op jit(solution)/shard_map/finish_weights/pallas_call | solution.py:780
  (140 shorter events, 8.0 us)
Async XLA Ops:
  3.9 19.7 %collective-permute-start = (bf16[2,64,768]{2,1,0:T(8,128)(2,1)}, bf16[2,64,768]{2,1,0:T(8,128)(2,1)S(1)}, u32[]{:S(2)}, u32[]{:S(2)}) collective-permute-start(bf16[2,64,768]{2,1,0:T(8,128)(2,1)} %pack_weights.1), channel_id=1, source_target_pairs={{0,1},{1,0},{2,3},{3,2},{4,5},{5,4},{6,7},{7,6},{8,9},{9,8},{10,11... | collective-permute-start | bytes 589832 | tf_op jit(solution)/shard_map/ppermute | solution.py:21
  3.9 19.7 %collective-permute-start.1 = (bf16[2,64,768]{2,1,0:T(8,128)(2,1)}, bf16[2,64,768]{2,1,0:T(8,128)(2,1)S(1)}, u32[]{:S(2)}, u32[]{:S(2)}) collective-permute-start(bf16[2,64,768]{2,1,0:T(8,128)(2,1)} %pack_weights.1), channel_id=1, source_target_pairs={{0,2},{1,3},{2,0},{3,1},{4,6},{5,7},{6,4},{7,5},{8,10},{9,11},{10,... | collective-permute-start | bytes 589832 | tf_op jit(solution)/shard_map/ppermute | solution.py:21
  6.4 17.3 %collective-permute-start.2 = (bf16[2,64,768]{2,1,0:T(8,128)(2,1)}, bf16[2,64,768]{2,1,0:T(8,128)(2,1)S(1)}, u32[]{:S(2)}, u32[]{:S(2)}) collective-permute-start(bf16[2,64,768]{2,1,0:T(8,128)(2,1)} %pack_weights.1), channel_id=1, source_target_pairs={{0,3},{1,2},{2,1},{3,0},{4,7},{5,6},{6,5},{7,4},{8,11},{9,10},{10,... | collective-permute-start | bytes 589832 | tf_op jit(solution)/shard_map/ppermute | solution.py:21
  8.0 6.6 %collective-permute-start.3 = (bf16[80,128]{1,0:T(8,128)(2,1)S(1)}, bf16[80,128]{1,0:T(8,128)(2,1)S(1)}, u32[]{:S(2)}, u32[]{:S(2)}) collective-permute-start(bf16[80,128]{1,0:T(8,128)(2,1)S(1)} %pad_maximum_fusion.1), channel_id=1, source_target_pairs={{0,4},{4,8},{8,12},{12,16},{16,20},{20,24},{24,28},{1,5},{5,9},{9,... | collective-permute-start | bytes 61448 | tf_op jit(solution)/shard_map/ppermute | solution.py:927
  12.6 49.8 %copy-start.24 = (bf16[512]{0:T(512)(128)(2,1)S(1)}, bf16[512]{0:T(512)(128)(2,1)}, u32[]{:S(2)}) copy-start(bf16[512]{0:T(512)(128)(2,1)} %param.18) | copy-start | bytes 3076
  12.6 50.4 %copy-start.21 = (s32[16384]{0:T(1024)S(1)}, s32[16384]{0:T(1024)}, u32[]{:S(2)}) copy-start(s32[16384]{0:T(1024)} %param.16) | copy-start | bytes 196612
  12.6 5.2 %collective-permute-start.4 = (bf16[80,128]{1,0:T(8,128)(2,1)S(1)}, bf16[80,128]{1,0:T(8,128)(2,1)S(1)}, u32[]{:S(2)}, u32[]{:S(2)}) collective-permute-start(bf16[80,128]{1,0:T(8,128)(2,1)S(1)} %pad_maximum_fusion.2), channel_id=1, source_target_pairs={{4,0},{8,4},{12,8},{16,12},{20,16},{24,20},{28,24},{5,1},{9,5},{13... | collective-permute-start | bytes 61448 | tf_op jit(solution)/shard_map/ppermute | solution.py:928
  22.4 19.4 %collective-permute-start.10 = (bf16[24,64,128]{2,1,0:T(8,128)(2,1)}, bf16[24,64,128]{2,1,0:T(8,128)(2,1)S(1)}, u32[]{:S(2)}, u32[]{:S(2)}) collective-permute-start(bf16[24,64,128]{2,1,0:T(8,128)(2,1)} %get-tuple-element.103), channel_id=1, source_target_pairs={{0,3},{1,2},{2,1},{3,0},{4,7},{5,6},{6,5},{7,4},{8,11},{9,10},{10,... | collective-permute-start | bytes 1179656 | tf_op jit(solution)/shard_map/ppermute | solution.py:21
  23.8 45.4 %copy-start.3 = (bf16[4,2,64,768]{3,2,1,0:T(8,128)(2,1)}, bf16[4,2,64,768]{3,2,1,0:T(8,128)(2,1)S(1)}, u32[]{:S(2)}) copy-start(bf16[4,2,64,768]{3,2,1,0:T(8,128)(2,1)S(1)} %pad_maximum_fusion.rest_0_) | copy-start | bytes 2359300
  23.8 35.6 %collective-permute-start.5 = (bf16[4,2,64,768]{3,2,1,0:T(8,128)(2,1)S(1)}, bf16[4,2,64,768]{3,2,1,0:T(8,128)(2,1)S(1)}, u32[]{:S(2)}, u32[]{:S(2)}) collective-permute-start(bf16[4,2,64,768]{3,2,1,0:T(8,128)(2,1)S(1)} %pad_maximum_fusion.rest_0_), channel_id=1, source_target_pairs={{0,24},{4,28},{8,16},{12,20},{16,8},{20,12},{24,0},{28,4},{1,25},{... | collective-permute-start | bytes 2359304 | tf_op jit(solution)/shard_map/ppermute | solution.py:21
  25.9 33.5 %collective-permute-start.6 = (bf16[4,2,64,768]{3,2,1,0:T(8,128)(2,1)S(1)}, bf16[4,2,64,768]{3,2,1,0:T(8,128)(2,1)S(1)}, u32[]{:S(2)}, u32[]{:S(2)}) collective-permute-start(bf16[4,2,64,768]{3,2,1,0:T(8,128)(2,1)S(1)} %pad_maximum_fusion.rest_0_), channel_id=1, source_target_pairs={{0,8},{4,12},{8,0},{12,4},{16,24},{20,28},{24,16},{28,20},{1,9},{5... | collective-permute-start | bytes 2359304 | tf_op jit(solution)/shard_map/ppermute | solution.py:21
  26.3 33.8 %collective-permute-start.7 = (bf16[4,2,64,768]{3,2,1,0:T(8,128)(2,1)S(1)}, bf16[4,2,64,768]{3,2,1,0:T(8,128)(2,1)S(1)}, u32[]{:S(2)}, u32[]{:S(2)}) collective-permute-start(bf16[4,2,64,768]{3,2,1,0:T(8,128)(2,1)S(1)} %pad_maximum_fusion.rest_0_), channel_id=1, source_target_pairs={{0,16},{4,20},{8,24},{12,28},{16,0},{20,4},{24,8},{28,12},{1,17},{... | collective-permute-start | bytes 2359304 | tf_op jit(solution)/shard_map/ppermute | solution.py:21
  27.2 14.6 %collective-permute-start.8 = (bf16[24,64,128]{2,1,0:T(8,128)(2,1)}, bf16[24,64,128]{2,1,0:T(8,128)(2,1)S(1)}, u32[]{:S(2)}, u32[]{:S(2)}) collective-permute-start(bf16[24,64,128]{2,1,0:T(8,128)(2,1)} %get-tuple-element.101), channel_id=1, source_target_pairs={{0,1},{1,0},{2,3},{3,2},{4,5},{5,4},{6,7},{7,6},{8,9},{9,8},{10,11... | collective-permute-start | bytes 1179656 | tf_op jit(solution)/shard_map/ppermute | solution.py:21
  41.8 17.6 %collective-permute-start.9 = (bf16[24,64,128]{2,1,0:T(8,128)(2,1)}, bf16[24,64,128]{2,1,0:T(8,128)(2,1)S(1)}, u32[]{:S(2)}, u32[]{:S(2)}) collective-permute-start(bf16[24,64,128]{2,1,0:T(8,128)(2,1)} %get-tuple-element.102), channel_id=1, source_target_pairs={{0,2},{1,3},{2,0},{3,1},{4,6},{5,7},{6,4},{7,5},{8,10},{9,11},{10,... | collective-permute-start | bytes 1179656 | tf_op jit(solution)/shard_map/ppermute | solution.py:21
  60.1 6.3 %collective-permute-start.11 = (bf16[4,2,64,768]{3,2,1,0:T(8,128)(2,1)S(1)}, bf16[4,2,64,768]{3,2,1,0:T(8,128)(2,1)}, u32[]{:S(2)}, u32[]{:S(2)}) collective-permute-start(bf16[4,2,64,768]{3,2,1,0:T(8,128)(2,1)S(1)} %pad_maximum_fusion.rest_0_), channel_id=1, source_target_pairs={{0,4},{4,0},{8,12},{12,8},{16,20},{20,16},{24,28},{28,24},{1,5},{5... | collective-permute-start | bytes 2359304 | tf_op jit(solution)/shard_map/ppermute | solution.py:21
  61.8 4.7 %collective-permute-start.12 = (bf16[4,2,64,768]{3,2,1,0:T(8,128)(2,1)S(1)}, bf16[4,2,64,768]{3,2,1,0:T(8,128)(2,1)}, u32[]{:S(2)}, u32[]{:S(2)}) collective-permute-start(bf16[4,2,64,768]{3,2,1,0:T(8,128)(2,1)S(1)} %collective-permute-done.5.rest_1_), channel_id=1, source_target_pairs={{0,4},{4,0},{8,12},{12,8},{16,20},{20,16},{24,28},{28,24},{1,5},{5... | collective-permute-start | bytes 2359304 | tf_op jit(solution)/shard_map/ppermute | solution.py:21
  61.8 6.5 %collective-permute-start.13 = (bf16[4,2,64,768]{3,2,1,0:T(8,128)(2,1)S(1)}, bf16[4,2,64,768]{3,2,1,0:T(8,128)(2,1)}, u32[]{:S(2)}, u32[]{:S(2)}) collective-permute-start(bf16[4,2,64,768]{3,2,1,0:T(8,128)(2,1)S(1)} %collective-permute-done.6.rest_2_), channel_id=1, source_target_pairs={{0,4},{4,0},{8,12},{12,8},{16,20},{20,16},{24,28},{28,24},{1,5},{5... | collective-permute-start | bytes 2359304 | tf_op jit(solution)/shard_map/ppermute | solution.py:21
  62.3 6.1 %collective-permute-start.14 = (bf16[4,2,64,768]{3,2,1,0:T(8,128)(2,1)S(1)}, bf16[4,2,64,768]{3,2,1,0:T(8,128)(2,1)}, u32[]{:S(2)}, u32[]{:S(2)}) collective-permute-start(bf16[4,2,64,768]{3,2,1,0:T(8,128)(2,1)S(1)} %collective-permute-done.7.rest_3_), channel_id=1, source_target_pairs={{0,4},{4,0},{8,12},{12,8},{16,20},{20,16},{24,28},{28,24},{1,5},{5... | collective-permute-start | bytes 2359304 | tf_op jit(solution)/shard_map/ppermute | solution.py:21
  63.0 29.6 %collective-permute-start.15 = (bf16[18,64,128]{2,1,0:T(8,128)(2,1)}, bf16[18,64,128]{2,1,0:T(8,128)(2,1)S(1)}, u32[]{:S(2)}, u32[]{:S(2)}) collective-permute-start(bf16[18,64,128]{2,1,0:T(8,128)(2,1)} %get-tuple-element.117), channel_id=1, source_target_pairs={{0,1},{1,0},{2,3},{3,2},{4,5},{5,4},{6,7},{7,6},{8,9},{9,8},{10,11... | collective-permute-start | bytes 884744 | tf_op jit(solution)/shard_map/ppermute | solution.py:21
  66.4 26.2 %collective-permute-start.16 = (bf16[18,64,128]{2,1,0:T(8,128)(2,1)}, bf16[18,64,128]{2,1,0:T(8,128)(2,1)S(1)}, u32[]{:S(2)}, u32[]{:S(2)}) collective-permute-start(bf16[18,64,128]{2,1,0:T(8,128)(2,1)} %get-tuple-element.118), channel_id=1, source_target_pairs={{0,2},{1,3},{2,0},{3,1},{4,6},{5,7},{6,4},{7,5},{8,10},{9,11},{10,... | collective-permute-start | bytes 884744 | tf_op jit(solution)/shard_map/ppermute | solution.py:21
  66.4 28.0 %collective-permute-start.17 = (bf16[18,64,128]{2,1,0:T(8,128)(2,1)}, bf16[18,64,128]{2,1,0:T(8,128)(2,1)}, u32[]{:S(2)}, u32[]{:S(2)}) collective-permute-start(bf16[18,64,128]{2,1,0:T(8,128)(2,1)} %get-tuple-element.119), channel_id=1, source_target_pairs={{0,3},{1,2},{2,1},{3,0},{4,7},{5,6},{6,5},{7,4},{8,11},{9,10},{10,... | collective-permute-start | bytes 884744 | tf_op jit(solution)/shard_map/ppermute | solution.py:21
  94.5 41.3 %collective-permute-start.18 = (bf16[64,4096]{1,0:T(8,128)(2,1)}, bf16[64,4096]{1,0:T(8,128)(2,1)S(1)}, u32[]{:S(2)}, u32[]{:S(2)}) collective-permute-start(bf16[64,4096]{1,0:T(8,128)(2,1)} %get-tuple-element.142), channel_id=1, source_target_pairs={{0,1},{1,0},{2,3},{3,2},{4,5},{5,4},{6,7},{7,6},{8,9},{9,8},{10,11... | collective-permute-start | bytes 1572872 | tf_op jit(solution)/shard_map/ppermute | solution.py:21
  95.6 40.2 %collective-permute-start.19 = (bf16[64,4096]{1,0:T(8,128)(2,1)}, bf16[64,4096]{1,0:T(8,128)(2,1)S(1)}, u32[]{:S(2)}, u32[]{:S(2)}) collective-permute-start(bf16[64,4096]{1,0:T(8,128)(2,1)} %get-tuple-element.143), channel_id=1, source_target_pairs={{0,2},{1,3},{2,0},{3,1},{4,6},{5,7},{6,4},{7,5},{8,10},{9,11},{10,... | collective-permute-start | bytes 1572872 | tf_op jit(solution)/shard_map/ppermute | solution.py:21
  95.6 46.0 %collective-permute-start.20 = (bf16[64,4096]{1,0:T(8,128)(2,1)}, bf16[64,4096]{1,0:T(8,128)(2,1)S(1)}, u32[]{:S(2)}, u32[]{:S(2)}) collective-permute-start(bf16[64,4096]{1,0:T(8,128)(2,1)} %get-tuple-element.144), channel_id=1, source_target_pairs={{0,3},{1,2},{2,1},{3,0},{4,7},{5,6},{6,5},{7,4},{8,11},{9,10},{10,... | collective-permute-start | bytes 1572872 | tf_op jit(solution)/shard_map/ppermute | solution.py:21
  142.4 6.9 %collective-permute-start.22 = (bf16[2,2,256,768]{3,2,1,0:T(8,128)(2,1)}, bf16[2,2,256,768]{3,2,1,0:T(8,128)(2,1)S(1)}, u32[]{:S(2)}, u32[]{:S(2)}) collective-permute-start(bf16[2,2,256,768]{3,2,1,0:T(8,128)(2,1)} %get-tuple-element.153), channel_id=1, source_target_pairs={{0,4},{4,0},{8,12},{12,8},{16,20},{20,16},{24,28},{28,24},{1,5},{5... | collective-permute-start | bytes 4718600 | tf_op jit(solution)/shard_map/ppermute | solution.py:21
  144.8 4.4 %collective-permute-start.21 = (bf16[2,256,768]{2,1,0:T(8,128)(2,1)}, bf16[2,256,768]{2,1,0:T(8,128)(2,1)S(1)}, u32[]{:S(2)}, u32[]{:S(2)}) collective-permute-start(bf16[2,256,768]{2,1,0:T(8,128)(2,1)} %get-tuple-element.151), channel_id=1, source_target_pairs={{0,4},{4,0},{8,12},{12,8},{16,20},{20,16},{24,28},{28,24},{1,5},{5... | collective-permute-start | bytes 2359304 | tf_op jit(solution)/shard_map/ppermute | solution.py:21
  144.8 5.4 %collective-permute-start.23 = (bf16[2,256,768]{2,1,0:T(8,128)(2,1)}, bf16[2,256,768]{2,1,0:T(8,128)(2,1)S(1)}, u32[]{:S(2)}, u32[]{:S(2)}) collective-permute-start(bf16[2,256,768]{2,1,0:T(8,128)(2,1)} %get-tuple-element.154), channel_id=1, source_target_pairs={{0,4},{4,0},{8,12},{12,8},{16,20},{20,16},{24,28},{28,24},{1,5},{5... | collective-permute-start | bytes 2359304 | tf_op jit(solution)/shard_map/ppermute | solution.py:21
  150.2 20.7 %collective-permute-start.27 = (bf16[2,256,768]{2,1,0:T(8,128)(2,1)S(1)}, bf16[2,256,768]{2,1,0:T(8,128)(2,1)S(1)}, u32[]{:S(2)}, u32[]{:S(2)}) collective-permute-start(bf16[2,256,768]{2,1,0:T(8,128)(2,1)S(1)} %get-tuple-element.162), channel_id=1, source_target_pairs={{0,8},{4,12},{8,0},{12,4},{16,24},{20,28},{24,16},{28,20},{1,9},{5... | collective-permute-start | bytes 2359304 | tf_op jit(solution)/shard_map/ppermute | solution.py:21
  150.7 20.3 %collective-permute-start.28 = (bf16[2,256,768]{2,1,0:T(8,128)(2,1)S(1)}, bf16[2,256,768]{2,1,0:T(8,128)(2,1)S(1)}, u32[]{:S(2)}, u32[]{:S(2)}) collective-permute-start(bf16[2,256,768]{2,1,0:T(8,128)(2,1)S(1)} %get-tuple-element.163), channel_id=1, source_target_pairs={{0,16},{4,20},{8,24},{12,28},{16,0},{20,4},{24,8},{28,12},{1,17},{... | collective-permute-start | bytes 2359304 | tf_op jit(solution)/shard_map/ppermute | solution.py:21
  151.3 5.9 %collective-permute-start.29 = (bf16[2,64,768]{2,1,0:T(8,128)(2,1)S(1)}, bf16[2,64,768]{2,1,0:T(8,128)(2,1)S(1)}, u32[]{:S(2)}, u32[]{:S(2)}) collective-permute-start(bf16[2,64,768]{2,1,0:T(8,128)(2,1)S(1)} %get-tuple-element.185), channel_id=1, source_target_pairs={{0,1},{1,0},{2,3},{3,2},{4,5},{5,4},{6,7},{7,6},{8,9},{9,8},{10,11... | collective-permute-start | bytes 589832 | tf_op jit(solution)/shard_map/ppermute | solution.py:21
  151.4 9.6 %collective-permute-start.30 = (bf16[2,64,768]{2,1,0:T(8,128)(2,1)S(1)}, bf16[2,64,768]{2,1,0:T(8,128)(2,1)S(1)}, u32[]{:S(2)}, u32[]{:S(2)}) collective-permute-start(bf16[2,64,768]{2,1,0:T(8,128)(2,1)S(1)} %get-tuple-element.187), channel_id=1, source_target_pairs={{0,2},{1,3},{2,0},{3,1},{4,6},{5,7},{6,4},{7,5},{8,10},{9,11},{10,... | collective-permute-start | bytes 589832 | tf_op jit(solution)/shard_map/ppermute | solution.py:21
  152.7 18.1 %collective-permute-start.31 = (bf16[2,64,768]{2,1,0:T(8,128)(2,1)S(1)}, bf16[2,64,768]{2,1,0:T(8,128)(2,1)S(1)}, u32[]{:S(2)}, u32[]{:S(2)}) collective-permute-start(bf16[2,64,768]{2,1,0:T(8,128)(2,1)S(1)} %get-tuple-element.186), channel_id=1, source_target_pairs={{0,3},{1,2},{2,1},{3,0},{4,7},{5,6},{6,5},{7,4},{8,11},{9,10},{10,... | collective-permute-start | bytes 589832 | tf_op jit(solution)/shard_map/ppermute | solution.py:21
  157.2 39.3 %collective-permute-start.24 = (bf16[512,128]{1,0:T(8,128)(2,1)S(1)}, bf16[512,128]{1,0:T(8,128)(2,1)S(1)}, u32[]{:S(2)}, u32[]{:S(2)}) collective-permute-start(bf16[512,128]{1,0:T(8,128)(2,1)S(1)} %copy-done.35), channel_id=1, source_target_pairs={{0,1},{1,0},{2,3},{3,2},{4,5},{5,4},{6,7},{7,6},{8,9},{9,8},{10,11... | collective-permute-start | bytes 393224 | tf_op jit(solution)/shard_map/ppermute | solution.py:21
  171.2 25.4 %copy-start.33 = (bf16[512,128]{1,0:T(8,128)(2,1)S(1)}, bf16[512,128]{1,0:T(8,128)(2,1)}, u32[]{:S(2)}) copy-start(bf16[512,128]{1,0:T(8,128)(2,1)} %get-tuple-element.159) | copy-start | bytes 393220
  171.2 4.6 %collective-permute-start.32 = (bf16[2,64,768]{2,1,0:T(8,128)(2,1)S(1)}, bf16[2,64,768]{2,1,0:T(8,128)(2,1)S(1)}, u32[]{:S(2)}, u32[]{:S(2)}) collective-permute-start(bf16[2,64,768]{2,1,0:T(8,128)(2,1)S(1)} %get-tuple-element.182), channel_id=1, source_target_pairs={{0,1},{1,0},{2,3},{3,2},{4,5},{5,4},{6,7},{7,6},{8,9},{9,8},{10,11... | collective-permute-start | bytes 589832 | tf_op jit(solution)/shard_map/ppermute | solution.py:21
  171.3 7.8 %collective-permute-start.33 = (bf16[2,64,768]{2,1,0:T(8,128)(2,1)S(1)}, bf16[2,64,768]{2,1,0:T(8,128)(2,1)S(1)}, u32[]{:S(2)}, u32[]{:S(2)}) collective-permute-start(bf16[2,64,768]{2,1,0:T(8,128)(2,1)S(1)} %get-tuple-element.184), channel_id=1, source_target_pairs={{0,2},{1,3},{2,0},{3,1},{4,6},{5,7},{6,4},{7,5},{8,10},{9,11},{10,... | collective-permute-start | bytes 589832 | tf_op jit(solution)/shard_map/ppermute | solution.py:21
  172.3 21.2 %collective-permute-start.34 = (bf16[2,64,768]{2,1,0:T(8,128)(2,1)S(1)}, bf16[2,64,768]{2,1,0:T(8,128)(2,1)S(1)}, u32[]{:S(2)}, u32[]{:S(2)}) collective-permute-start(bf16[2,64,768]{2,1,0:T(8,128)(2,1)S(1)} %get-tuple-element.183), channel_id=1, source_target_pairs={{0,3},{1,2},{2,1},{3,0},{4,7},{5,6},{6,5},{7,4},{8,11},{9,10},{10,... | collective-permute-start | bytes 589832 | tf_op jit(solution)/shard_map/ppermute | solution.py:21
  174.0 19.6 %collective-permute-start.35 = (bf16[2,64,768]{2,1,0:T(8,128)(2,1)S(1)}, bf16[2,64,768]{2,1,0:T(8,128)(2,1)S(1)}, u32[]{:S(2)}, u32[]{:S(2)}) collective-permute-start(bf16[2,64,768]{2,1,0:T(8,128)(2,1)S(1)} %add_add_fusion.2), channel_id=1, source_target_pairs={{0,24},{4,28},{8,16},{12,20},{16,8},{20,12},{24,0},{28,4},{1,25},{... | collective-permute-start | bytes 589832 | tf_op jit(solution)/shard_map/ppermute | solution.py:21
  175.5 37.7 %copy-start = (bf16[64,16384]{1,0:T(8,128)(2,1)}, bf16[64,16384]{1,0:T(8,128)(2,1)S(1)}, u32[]{:S(2)}) copy-start(bf16[64,16384]{1,0:T(8,128)(2,1)S(1)} %constant_dynamic-update-slice_fusion.4) | copy-start | bytes 6291460
  175.8 20.8 %collective-permute-start.25 = (bf16[512,128]{1,0:T(8,128)(2,1)S(1)}, bf16[512,128]{1,0:T(8,128)(2,1)S(1)}, u32[]{:S(2)}, u32[]{:S(2)}) collective-permute-start(bf16[512,128]{1,0:T(8,128)(2,1)S(1)} %copy-done.34), channel_id=1, source_target_pairs={{0,2},{1,3},{2,0},{3,1},{4,6},{5,7},{6,4},{7,5},{8,10},{9,11},{10,... | collective-permute-start | bytes 393224 | tf_op jit(solution)/shard_map/ppermute | solution.py:21
  193.7 8.6 %collective-permute-start.36 = (bf16[2,64,768]{2,1,0:T(8,128)(2,1)S(1)}, bf16[2,64,768]{2,1,0:T(8,128)(2,1)S(1)}, u32[]{:S(2)}, u32[]{:S(2)}) collective-permute-start(bf16[2,64,768]{2,1,0:T(8,128)(2,1)S(1)} %add_add_fusion.1.rest_0_), channel_id=1, source_target_pairs={{0,8},{4,12},{8,0},{12,4},{16,24},{20,28},{24,16},{28,20},{1,9},{5... | collective-permute-start | bytes 589832 | tf_op jit(solution)/shard_map/ppermute | solution.py:21
  195.1 8.5 %collective-permute-start.37 = (bf16[2,64,768]{2,1,0:T(8,128)(2,1)S(1)}, bf16[2,64,768]{2,1,0:T(8,128)(2,1)S(1)}, u32[]{:S(2)}, u32[]{:S(2)}) collective-permute-start(bf16[2,64,768]{2,1,0:T(8,128)(2,1)S(1)} %add_add_fusion.1.rest_0_), channel_id=1, source_target_pairs={{0,16},{4,20},{8,24},{12,28},{16,0},{20,4},{24,8},{28,12},{1,17},{... | collective-permute-start | bytes 589832 | tf_op jit(solution)/shard_map/ppermute | solution.py:21
  195.5 11.1 %collective-permute-start.38 = (bf16[2,64,768]{2,1,0:T(8,128)(2,1)S(1)}, bf16[2,64,768]{2,1,0:T(8,128)(2,1)S(1)}, u32[]{:S(2)}, u32[]{:S(2)}) collective-permute-start(bf16[2,64,768]{2,1,0:T(8,128)(2,1)S(1)} %add_add_fusion.1.rest_0_), channel_id=1, source_target_pairs={{0,24},{4,28},{8,16},{12,20},{16,8},{20,12},{24,0},{28,4},{1,25},{... | collective-permute-start | bytes 589832 | tf_op jit(solution)/shard_map/ppermute | solution.py:21
  196.5 10.2 %collective-permute-start.26 = (bf16[512,128]{1,0:T(8,128)(2,1)S(1)}, bf16[512,128]{1,0:T(8,128)(2,1)S(1)}, u32[]{:S(2)}, u32[]{:S(2)}) collective-permute-start(bf16[512,128]{1,0:T(8,128)(2,1)S(1)} %copy-done.33), channel_id=1, source_target_pairs={{0,3},{1,2},{2,1},{3,0},{4,7},{5,6},{6,5},{7,4},{8,11},{9,10},{10,... | collective-permute-start | bytes 393224 | tf_op jit(solution)/shard_map/ppermute | solution.py:21
  196.7 10.1 %collective-permute-start.39 = (bf16[2,64,768]{2,1,0:T(8,128)(2,1)S(1)}, bf16[2,64,768]{2,1,0:T(8,128)(2,1)S(1)}, u32[]{:S(2)}, u32[]{:S(2)}) collective-permute-start(bf16[2,64,768]{2,1,0:T(8,128)(2,1)S(1)} %add_add_fusion.1.rest_0_), channel_id=1, source_target_pairs={{0,4},{4,0},{8,12},{12,8},{16,20},{20,16},{24,28},{28,24},{1,5},{5... | collective-permute-start | bytes 589832 | tf_op jit(solution)/shard_map/ppermute | solution.py:21
  202.3 4.5 %collective-permute-start.40 = (bf16[2,64,768]{2,1,0:T(8,128)(2,1)S(1)}, bf16[2,64,768]{2,1,0:T(8,128)(2,1)S(1)}, u32[]{:S(2)}, u32[]{:S(2)}) collective-permute-start(bf16[2,64,768]{2,1,0:T(8,128)(2,1)S(1)} %collective-permute-done.36.rest_1_), channel_id=1, source_target_pairs={{0,4},{4,0},{8,12},{12,8},{16,20},{20,16},{24,28},{28,24},{1,5},{5... | collective-permute-start | bytes 589832 | tf_op jit(solution)/shard_map/ppermute | solution.py:21
  203.6 4.1 %collective-permute-start.41 = (bf16[2,64,768]{2,1,0:T(8,128)(2,1)S(1)}, bf16[2,64,768]{2,1,0:T(8,128)(2,1)S(1)}, u32[]{:S(2)}, u32[]{:S(2)}) collective-permute-start(bf16[2,64,768]{2,1,0:T(8,128)(2,1)S(1)} %collective-permute-done.37.rest_2_), channel_id=1, source_target_pairs={{0,4},{4,0},{8,12},{12,8},{16,20},{20,16},{24,28},{28,24},{1,5},{5... | collective-permute-start | bytes 589832 | tf_op jit(solution)/shard_map/ppermute | solution.py:21
  206.6 1.6 collective-permute-start.42
  (31 other events, 230.5 us)

commit v7 on v6

--- a/solution.py
+++ b/solution.py
@@ -195,7 +195,6 @@
     _, chan = own_places()
     own = signal.shape[0] // 4
     frames = 8 * own
-    count = own // 64
     row = lax.broadcasted_iota(jnp.int32, (16, 128), 0)
     lane = lax.broadcasted_iota(jnp.int32, (64, 128), 1)
 
@@ -208,19 +207,18 @@
     for k in range(4):
         dest = chan ^ k
         part = signal[pl.ds(pl.multiple_of(dest * own, own), own)]
-        firsts[k][0:count] = part.reshape(count, 64, 128)
+        firsts[k][0:own] = part
         after = pl.multiple_of(jnp.minimum(dest + 1, 3) * own, 16)
         before = pl.multiple_of(jnp.maximum(dest * own - 16, 0), 16)
         edges = (low[0:16], high[0:16])
-        firsts[k][count] = jnp.zeros((64, 128), BF16)
-        firsts[k][count, 0:16] = halo(
+        firsts[k][own : own + 16] = halo(
             dest, signal[pl.ds(after, 16)], signal[pl.ds(before, 16)], edges, row < HALO
         )
         for q in range(frames // 128):
             lanes = pl.ds(pl.multiple_of(dest * frames + 128 * q, 128), 128)
             part = cotangent[:, lanes]
             if q < EARLY:
-                firsts[k][count + 1 + q] = part
+                firsts[k][own + 16 + 64 * q : own + 80 + 64 * q] = part
             else:
                 seconds[k][q - EARLY] = part
         after = pl.multiple_of(jnp.minimum(dest + 1, 3) * frames, 128)
@@ -338,9 +336,9 @@
     fill_masks(ids_ref, flat, mask_out)
     for k, ref in enumerate((sig0, sig1, sig2, sig3)):
         lanes = pl.ds(pl.multiple_of(128 * (chan ^ k), 128), 128)
-        values = silu_half(0.5 * ref[0 : own // 64].reshape(own, 128).astype(F32))[0]
+        values = silu_half(0.5 * ref[0:own].astype(F32))[0]
         to_rows(flat, values, sact_out.at[:, lanes])
-        halo = silu_half(0.5 * ref[own // 64, 0:16].astype(F32))[0]
+        halo = silu_half(0.5 * ref[own : own + 16].astype(F32))[0]
         sact_out[own:rows, lanes] = halo.astype(BF16)
     total = jnp.zeros((8, 512), F32)
     for (place, _, _), copies in zip(WEIGHT_PLACES, section_loads, strict=True):
@@ -352,7 +350,7 @@
     for copy in block_loads:
         copy.wait()
     norm = jnp.sqrt(jnp.sum(total, axis=0, keepdims=True) + EPSILON)
-    scale = gain_ref[...] / norm
+    scale = gain_ref[...].astype(F32) / norm
     stat_out[...] = jnp.concatenate([norm, scale, jnp.zeros((6, 512), F32)], axis=0)
     bias[...] = 0.5 * jnp.transpose(wblk[15].astype(F32))[:16]
     cat[0] = (sact_out[...].astype(F32) * (0.5 * scale)).astype(BF16)
@@ -489,16 +487,16 @@
 
     section_weights, block_loads = weight_copies(pieces, wsec, wblk, wsem, vsem)
     cots = []
-    count = own // 64
     section_loads = []
     pairs = ((first0, second0), (first1, second1), (first2, second2), (first3, second3))
     for k, (one, two) in enumerate(pairs):
         part = pl.ds(pl.multiple_of(64 * (chan ^ k), 64), 64)
-        early = one.at[count + 1 : count + 1 + EARLY]
-        cots.append(pltpu.make_async_copy(early, turned.at[0:EARLY, part, :], csem))
+        for q in range(EARLY):
+            early = one.at[own + 16 + 64 * q : own + 80 + 64 * q]
+            cots.append(pltpu.make_async_copy(early, turned.at[q, part, :], csem))
         late = turned.at[EARLY : 8 * own // 128 + 1, part, :]
         cots.append(pltpu.make_async_copy(two, late, csem))
-        section_loads.append(pltpu.make_async_copy(one.at[0:count], sigs.at[k], gsem))
+        section_loads.append(pltpu.make_async_copy(one.at[0:own], sigs.at[k], gsem))
 
     def kept(b):
         slot = b % 2
@@ -701,7 +699,7 @@
     send(7)
     for k, out in enumerate(sgrads):
         lanes = pl.ds(pl.multiple_of(128 * (chan ^ k), 128), 128)
-        half = 0.5 * sigs[k].reshape(own, 128).astype(F32)
+        half = 0.5 * sigs[k].astype(F32)
         slope = slope_twice(half, *silu_half(half)[1:])
         count = own // 16
         for tile in range(count):
@@ -751,7 +749,7 @@
     own = signal.shape[0] // 4
     return pl.pallas_call(
         pack_frames_kernel,
-        out_shape=[shape_of((own // 64 + 1 + EARLY, 64, 128))] * 4
+        out_shape=[shape_of((own + 16 + 64 * EARLY, 128))] * 4
         + [shape_of((8 * own // 128 + 1 - EARLY, 64, 128))] * 4,
         in_specs=[SPEC_VMEM] * 4,
         out_specs=[SPEC_VMEM] * 8,
@@ -846,7 +844,7 @@
             pltpu.VMEM((16, 256, 512), BF16),
             pltpu.VMEM((16, 256, 256), BF16),
             pltpu.VMEM((8 * own // 128 + 1, 256, 128), BF16),
-            pltpu.VMEM((4, own // 64, 64, 128), BF16),
+            pltpu.VMEM((4, own, 128), BF16),
             pltpu.VMEM((2, 16 * (own // 2 + 1) + 128, 128), F32),
             pltpu.VMEM((8, rows, 256), BF16),
             pltpu.VMEM((26, rows, 256), BF16),
@@ -938,7 +936,7 @@
     ids = jnp.broadcast_to(nearby[:, None], (own + 32, 128))
 
     frames = 8 * own
-    results = run_forward(firsts, ids, g_section[None].astype(F32), pieces)
+    results = run_forward(firsts, ids, g_section[None], pieces)
     kept, sact, masks, stat, outs = results[:4], results[4], results[5], results[6], results[7:]
 
     outs, seconds = lax.optimization_barrier((list(outs), seconds))

time: 214 us -> 215 us (level)
  transfers between devices with their start and end apart: 43 -> 43, of which waited for: 16 -> 18; matrix products, arithmetic and copies ran while one was open for 3% -> 3% of each run, Pallas kernels for 31% -> 31%
where the time goes in v7:
time: 215 us; the launch traced here: 214 us
  waiting for transfers between devices  78.2 us (36%)
  Pallas kernels  74.2 us (35%)
  starting transfers between devices  52.9 us (25%)
  local copies, waits for them, and re-layouts  6.31 us (3%)
    ppermute x41, waiting for transfers between devices, swap(): return lax.ppermute(values, axis, xor_pairs(axis, bit))  75.1 us
    ppermute x41, starting transfers between devices, swap(): return lax.ppermute(values, axis, xor_pairs(axis, bit))  46.3 us
    pallas_call x1, Pallas kernels, run_backward(): pl.pallas_call(backward_kernel, out_shape=[shape_of((2, 256, 768)), shape...  38.7 us
    pallas_call x1, Pallas kernels, run_forward(): pl.pallas_call(forward_kernel, out_shape=out_shape, in_specs=[SPEC_VMEM]...  23.3 us
    pallas_call x1, Pallas kernels, run_finish(): pl.pallas_call(finish_kernel, out_shape=out_shape, in_specs=[SPEC_VMEM] *...  4.92 us
    ppermute x1, starting transfers between devices, body(): low = lax.ppermute(final, 'tm', onward)  4.51 us
  transfers between devices with their start and end apart: 43, of which 18 were waited for; matrix products, arithmetic and copies ran while one was open for 3% of the time, Pallas kernels for 31%

profile of v7, /device:TPU:9, one launch (start us, length us, event | category | flops | bytes accessed | tf_op | source)
XLA Modules:
  0.0 213.8 jit_solution(11993620245393753703)
XLA Ops:
  0.6 3.3 %pack_weights.1 = bf16[2,64,768]{2,1,0:T(8,128)(2,1)} custom-call(bf16[64,16,512]{2,1,0:T(8,128)(2,1)} %sec_ref.3, bf16[3,3,64,256]{3,2,1,0:T(8,128)(2,1)} %bitcast.13, bf16[3,64,256]{2,1,0:T(8,128)(2,1)} %mix_ref.3, bf16[3,64,256]{2,1,0:T(8,128)(2,1)} %skip_ref.3, bf16[1,64]{1,0:T(2,128)(2,1)} %bitcast.19, bf16[3,64]{1,0:T(4,128)(2,1)} %bt.1, ...), custom_call_target="tpu_custom_call" | custom-call | flops 20000000 | bytes 3000000 | tf_op jit(solution)/shard_map/pack_weights/pallas_call | solution.py:732
  3.9 2.5 %collective-permute-start.1 = (bf16[2,64,768]{2,1,0:T(8,128)(2,1)}, bf16[2,64,768]{2,1,0:T(8,128)(2,1)S(1)}, u32[]{:S(2)}, u32[]{:S(2)}) collective-permute-start(bf16[2,64,768]{2,1,0:T(8,128)(2,1)} %pack_weights.1), channel_id=1, source_target_pairs={{0,2},{1,3},{2,0},{3,1},{4,6},{5,7},{6,4},{7,5},{8,10},{9,11},{10,... | collective-permute-start | bytes 589832 | tf_op jit(solution)/shard_map/ppermute | solution.py:21
  6.6 0.7 fusion.2
  7.3 0.7 fusion.3
  8.0 4.5 %collective-permute-start.3 = (bf16[80,128]{1,0:T(8,128)(2,1)S(1)}, bf16[80,128]{1,0:T(8,128)(2,1)S(1)}, u32[]{:S(2)}, u32[]{:S(2)}) collective-permute-start(bf16[80,128]{1,0:T(8,128)(2,1)S(1)} %pad_maximum_fusion.1), channel_id=1, source_target_pairs={{0,4},{4,8},{8,12},{12,16},{16,20},{20,24},{24,28},{1,5},{5,9},{9,... | collective-permute-start | bytes 61448 | tf_op jit(solution)/shard_map/ppermute | solution.py:925
  12.6 2.1 collective-permute-start.4
  14.7 3.2 %collective-permute-done.4.high = bf16[80,128]{1,0:T(8,128)(2,1)S(1)} collective-permute-done((bf16[80,128]{1,0:T(8,128)(2,1)S(1)}, bf16[80,128]{1,0:T(8,128)(2,1)S(1)}, u32[]{:S(2)}, u32[]{:S(2)}) %collective-permute-start.4) | collective-permute-done | bytes 20512 | tf_op jit(solution)/shard_map/ppermute | solution.py:926
  18.4 3.9 %pack_frames.1 = (bf16[1488,128]{1,0:T(8,128)(2,1)}, bf16[1488,128]{1,0:T(8,128)(2,1)}, bf16[1488,128]{1,0:T(8,128)(2,1)}, bf16[1488,128]{1,0:T(8,128)(2,1)}, bf...) custom-call(bf16[80,128]{1,0:T(8,128)(2,1)} %copy-done.22, ...), custom_call_target="tpu_custom_call" | custom-call | flops 1000000 | bytes 6000000 | tf_op jit(solution)/shard_map/pack_frames/pallas_call | solution.py:750
  22.4 1.2 collective-permute-done.2
  23.7 2.2 %collective-permute-start.5 = (bf16[4,2,64,768]{3,2,1,0:T(8,128)(2,1)S(1)}, bf16[4,2,64,768]{3,2,1,0:T(8,128)(2,1)S(1)}, u32[]{:S(2)}, u32[]{:S(2)}) collective-permute-start(bf16[4,2,64,768]{3,2,1,0:T(8,128)(2,1)S(1)} %pad_maximum_fusion.rest_0_), channel_id=1, source_target_pairs={{0,24},{4,28},{8,16},{12,20},{16,8},{20,12},{24,0},{28,4},{1,25},{... | collective-permute-start | bytes 2359304 | tf_op jit(solution)/shard_map/ppermute | solution.py:21
  26.4 1.3 collective-permute-start.10
  27.6 2.9 %collective-permute-start.8 = (bf16[1488,128]{1,0:T(8,128)(2,1)}, bf16[1488,128]{1,0:T(8,128)(2,1)S(1)}, u32[]{:S(2)}, u32[]{:S(2)}) collective-permute-start(bf16[1488,128]{1,0:T(8,128)(2,1)} %get-tuple-element.101), channel_id=1, source_target_pairs={{0,1},{1,0},{2,3},{3,2},{4,5},{5,4},{6,7},{7,6},{8,9},{9,8},{10,11... | collective-permute-start | bytes 1142792 | tf_op jit(solution)/shard_map/ppermute | solution.py:21
  30.6 13.4 %collective-permute-done.10.sig3.first3 = bf16[1488,128]{1,0:T(8,128)(2,1)S(1)} collective-permute-done((bf16[1488,128]{1,0:T(8,128)(2,1)}, bf16[1488,128]{1,0:T(8,128)(2,1)S(1)}, u32[]{:S(2)}, u32[]{:S(2)}) %collective-permute-start.10) | collective-permute-done | bytes 380960 | tf_op jit(solution)/shard_map/ppermute | solution.py:21
  43.9 4.3 %collective-permute-done.8.sig1.first1 = bf16[1488,128]{1,0:T(8,128)(2,1)S(1)} collective-permute-done((bf16[1488,128]{1,0:T(8,128)(2,1)}, bf16[1488,128]{1,0:T(8,128)(2,1)S(1)}, u32[]{:S(2)}, u32[]{:S(2)}) %collective-permute-start.8) | collective-permute-done | bytes 380960 | tf_op jit(solution)/shard_map/ppermute | solution.py:21
  48.3 10.6 %collective-permute-done.9.sig2.first2 = bf16[1488,128]{1,0:T(8,128)(2,1)S(1)} collective-permute-done((bf16[1488,128]{1,0:T(8,128)(2,1)}, bf16[1488,128]{1,0:T(8,128)(2,1)S(1)}, u32[]{:S(2)}, u32[]{:S(2)}) %collective-permute-start.9) | collective-permute-done | bytes 380960 | tf_op jit(solution)/shard_map/ppermute | solution.py:21
  58.9 2.0 collective-permute-done.7.rest_3_
  60.9 0.7 collective-permute-start.11
  62.9 2.3 %collective-permute-start.15 = (bf16[18,64,128]{2,1,0:T(8,128)(2,1)}, bf16[18,64,128]{2,1,0:T(8,128)(2,1)S(1)}, u32[]{:S(2)}, u32[]{:S(2)}) collective-permute-start(bf16[18,64,128]{2,1,0:T(8,128)(2,1)} %get-tuple-element.117), channel_id=1, source_target_pairs={{0,1},{1,0},{2,3},{3,2},{4,5},{5,4},{6,7},{7,6},{8,9},{9,8},{10,11... | collective-permute-start | bytes 884744 | tf_op jit(solution)/shard_map/ppermute | solution.py:21
  65.2 1.5 collective-permute-start.16
  67.2 0.8 broadcast_in_dim.20.ids_ref
  68.0 23.3 %forward_blocks.1 = (bf16[3,8,528,256]{3,2,1,0:T(8,128)(2,1)}, bf16[3,8,528,256]{3,2,1,0:T(8,128)(2,1)}, bf16[3,8,528,256]{3,2,1,0:T(8,128)(2,1)}, bf16[3,8,528,...) custom-call(bf16[1488,128]{1,0:T(8,128)(2,1)} %get-tuple-element.104, ...), custom_call_target="tpu_custom_call" | custom-call | flops 10519314432 | bytes 50000000 | tf_op jit(solution)/shard_map/forward_blocks/pallas_call | solution.py:804
  91.4 1.8 collective-permute-done.17.second3
  93.3 1.0 collective-permute-start.18
  94.3 1.2 collective-permute-start.19
  95.9 38.7 %backward_blocks.1 = (bf16[2,256,768]{2,1,0:T(8,128)(2,1)}, bf16[2,2,256,768]{3,2,1,0:T(8,128)(2,1)}, bf16[2,256,768]{2,1,0:T(8,128)(2,1)}, bf16[2,256,768]{2,1,...) custom-call(bf16[1488,128]{1,0:T(8,128)(2,1)} %get-tuple-element.104, ...), custom_call_target="tpu_custom_call" | custom-call | flops 21038628864 | bytes 60000000 | tf_op jit(solution)/shard_map/backward_blocks/pallas_call | solution.py:830
  134.6 5.7 %collective-permute-done.20 = bf16[64,4096]{1,0:T(8,128)(2,1)S(1)} collective-permute-done((bf16[64,4096]{1,0:T(8,128)(2,1)}, bf16[64,4096]{1,0:T(8,128)(2,1)S(1)}, u32[]{:S(2)}, u32[]{:S(2)}) %collective-permute-start.20) | collective-permute-done | bytes 524320 | tf_op jit(solution)/shard_map/ppermute | solution.py:21
  140.4 0.8 copy-done.8
  141.2 2.4 %collective-permute-start.22 = (bf16[2,2,256,768]{3,2,1,0:T(8,128)(2,1)}, bf16[2,2,256,768]{3,2,1,0:T(8,128)(2,1)S(1)}, u32[]{:S(2)}, u32[]{:S(2)}) collective-permute-start(bf16[2,2,256,768]{3,2,1,0:T(8,128)(2,1)} %get-tuple-element.153), channel_id=1, source_target_pairs={{0,4},{4,0},{8,12},{12,8},{16,20},{20,16},{24,28},{28,24},{1,5},{5... | collective-permute-start | bytes 4718600 | tf_op jit(solution)/shard_map/ppermute | solution.py:21
  144.2 1.2 constant_dynamic-update-slice_fusion.7
  145.5 2.4 %collective-permute-done.21 = bf16[2,256,768]{2,1,0:T(8,128)(2,1)S(1)} collective-permute-done((bf16[2,256,768]{2,1,0:T(8,128)(2,1)}, bf16[2,256,768]{2,1,0:T(8,128)(2,1)S(1)}, u32[]{:S(2)}, u32[]{:S(2)}) %collective-permute-start.21) | collective-permute-done | bytes 786464 | tf_op jit(solution)/shard_map/ppermute | solution.py:21
  149.0 1.4 collective-permute-start.27
  150.4 1.7 collective-permute-start.28
  152.2 2.5 %collective-permute-start.30 = (bf16[2,64,768]{2,1,0:T(8,128)(2,1)S(1)}, bf16[2,64,768]{2,1,0:T(8,128)(2,1)S(1)}, u32[]{:S(2)}, u32[]{:S(2)}) collective-permute-start(bf16[2,64,768]{2,1,0:T(8,128)(2,1)S(1)} %get-tuple-element.187), channel_id=1, source_target_pairs={{0,2},{1,3},{2,0},{3,1},{4,6},{5,7},{6,4},{7,5},{8,10},{9,11},{10,... | collective-permute-start | bytes 589832 | tf_op jit(solution)/shard_map/ppermute | solution.py:21
  154.9 3.4 %collective-permute-done.29 = bf16[2,64,768]{2,1,0:T(8,128)(2,1)S(1)} collective-permute-done((bf16[2,64,768]{2,1,0:T(8,128)(2,1)S(1)}, bf16[2,64,768]{2,1,0:T(8,128)(2,1)S(1)}, u32[]{:S(2)}, u32[]{:S(2)}) %collective-permute-start.29) | collective-permute-done | bytes 196640 | tf_op jit(solution)/shard_map/ppermute | solution.py:21
  158.3 2.5 %collective-permute-start.24 = (bf16[512,128]{1,0:T(8,128)(2,1)S(1)}, bf16[512,128]{1,0:T(8,128)(2,1)S(1)}, u32[]{:S(2)}, u32[]{:S(2)}) collective-permute-start(bf16[512,128]{1,0:T(8,128)(2,1)S(1)} %copy-done.34), channel_id=1, source_target_pairs={{0,1},{1,0},{2,3},{3,2},{4,5},{5,4},{6,7},{7,6},{8,9},{9,8},{10,11... | collective-permute-start | bytes 393224 | tf_op jit(solution)/shard_map/ppermute | solution.py:21
  160.8 2.2 %collective-permute-done.30 = bf16[2,64,768]{2,1,0:T(8,128)(2,1)S(1)} collective-permute-done((bf16[2,64,768]{2,1,0:T(8,128)(2,1)S(1)}, bf16[2,64,768]{2,1,0:T(8,128)(2,1)S(1)}, u32[]{:S(2)}, u32[]{:S(2)}) %collective-permute-start.30) | collective-permute-done | bytes 196640 | tf_op jit(solution)/shard_map/ppermute | solution.py:21
  163.0 8.4 %collective-permute-done.31 = bf16[2,64,768]{2,1,0:T(8,128)(2,1)S(1)} collective-permute-done((bf16[2,64,768]{2,1,0:T(8,128)(2,1)S(1)}, bf16[2,64,768]{2,1,0:T(8,128)(2,1)S(1)}, u32[]{:S(2)}, u32[]{:S(2)}) %collective-permute-start.31) | collective-permute-done | bytes 196640 | tf_op jit(solution)/shard_map/ppermute | solution.py:21
  171.8 2.6 %collective-permute-start.33 = (bf16[2,64,768]{2,1,0:T(8,128)(2,1)S(1)}, bf16[2,64,768]{2,1,0:T(8,128)(2,1)S(1)}, u32[]{:S(2)}, u32[]{:S(2)}) collective-permute-start(bf16[2,64,768]{2,1,0:T(8,128)(2,1)S(1)} %get-tuple-element.184), channel_id=1, source_target_pairs={{0,2},{1,3},{2,0},{3,1},{4,6},{5,7},{6,4},{7,5},{8,10},{9,11},{10,... | collective-permute-start | bytes 589832 | tf_op jit(solution)/shard_map/ppermute | solution.py:21
  174.5 1.8 collective-permute-done.32
  176.3 1.1 collective-permute-start.25
  177.5 4.1 %collective-permute-done.33 = bf16[2,64,768]{2,1,0:T(8,128)(2,1)S(1)} collective-permute-done((bf16[2,64,768]{2,1,0:T(8,128)(2,1)S(1)}, bf16[2,64,768]{2,1,0:T(8,128)(2,1)S(1)}, u32[]{:S(2)}, u32[]{:S(2)}) %collective-permute-start.33) | collective-permute-done | bytes 196640 | tf_op jit(solution)/shard_map/ppermute | solution.py:21
  181.6 11.5 %collective-permute-done.34 = bf16[2,64,768]{2,1,0:T(8,128)(2,1)S(1)} collective-permute-done((bf16[2,64,768]{2,1,0:T(8,128)(2,1)S(1)}, bf16[2,64,768]{2,1,0:T(8,128)(2,1)S(1)}, u32[]{:S(2)}, u32[]{:S(2)}) %collective-permute-start.34) | collective-permute-done | bytes 196640 | tf_op jit(solution)/shard_map/ppermute | solution.py:21
  193.8 2.2 %collective-permute-start.38 = (bf16[2,64,768]{2,1,0:T(8,128)(2,1)S(1)}, bf16[2,64,768]{2,1,0:T(8,128)(2,1)S(1)}, u32[]{:S(2)}, u32[]{:S(2)}) collective-permute-start(bf16[2,64,768]{2,1,0:T(8,128)(2,1)S(1)} %add_add_fusion.1.rest_0_), channel_id=1, source_target_pairs={{0,24},{4,28},{8,16},{12,20},{16,8},{20,12},{24,0},{28,4},{1,25},{... | collective-permute-start | bytes 589832 | tf_op jit(solution)/shard_map/ppermute | solution.py:21
  196.1 2.3 %collective-permute-start.26 = (bf16[512,128]{1,0:T(8,128)(2,1)S(1)}, bf16[512,128]{1,0:T(8,128)(2,1)S(1)}, u32[]{:S(2)}, u32[]{:S(2)}) collective-permute-start(bf16[512,128]{1,0:T(8,128)(2,1)S(1)} %copy-done.32), channel_id=1, source_target_pairs={{0,3},{1,2},{2,1},{3,0},{4,7},{5,6},{6,5},{7,4},{8,11},{9,10},{10,... | collective-permute-start | bytes 393224 | tf_op jit(solution)/shard_map/ppermute | solution.py:21
  198.4 5.9 %collective-permute-start.39 = (bf16[2,64,768]{2,1,0:T(8,128)(2,1)S(1)}, bf16[2,64,768]{2,1,0:T(8,128)(2,1)S(1)}, u32[]{:S(2)}, u32[]{:S(2)}) collective-permute-start(bf16[2,64,768]{2,1,0:T(8,128)(2,1)S(1)} %add_add_fusion.1.rest_0_), channel_id=1, source_target_pairs={{0,4},{4,0},{8,12},{12,8},{16,20},{20,16},{24,28},{28,24},{1,5},{5... | collective-permute-start | bytes 589832 | tf_op jit(solution)/shard_map/ppermute | solution.py:21
  204.5 2.4 %collective-permute-start.41 = (bf16[2,64,768]{2,1,0:T(8,128)(2,1)S(1)}, bf16[2,64,768]{2,1,0:T(8,128)(2,1)S(1)}, u32[]{:S(2)}, u32[]{:S(2)}) collective-permute-start(bf16[2,64,768]{2,1,0:T(8,128)(2,1)S(1)} %collective-permute-done.37.rest_2_), channel_id=1, source_target_pairs={{0,4},{4,0},{8,12},{12,8},{16,20},{20,16},{24,28},{28,24},{1,5},{5... | collective-permute-start | bytes 589832 | tf_op jit(solution)/shard_map/ppermute | solution.py:21
  207.2 0.9 collective-permute-done.41.rest_6_
  208.7 4.9 %finish_weights.1 = (f32[64,16,512]{2,1,0:T(8,128)}, f32[1,512]{1,0:T(1,128)}, f32[1,64]{1,0:T(1,128)}, f32[3,3,64,256]{3,2,1,0:T(8,128)}, f32[3,64]{1,0:T(4,128...) custom-call(bf16[64,16,512]{2,1,0:T(8,128)(2,1)} %sec_ref.3, ...), custom_call_target="tpu_custom_call" | custom-call | flops 20000000 | bytes 8000000 | tf_op jit(solution)/shard_map/finish_weights/pallas_call | solution.py:778
  (138 shorter events, 8.0 us)
Async XLA Ops:
  3.9 18.4 %collective-permute-start = (bf16[2,64,768]{2,1,0:T(8,128)(2,1)}, bf16[2,64,768]{2,1,0:T(8,128)(2,1)S(1)}, u32[]{:S(2)}, u32[]{:S(2)}) collective-permute-start(bf16[2,64,768]{2,1,0:T(8,128)(2,1)} %pack_weights.1), channel_id=1, source_target_pairs={{0,1},{1,0},{2,3},{3,2},{4,5},{5,4},{6,7},{7,6},{8,9},{9,8},{10,11... | collective-permute-start | bytes 589832 | tf_op jit(solution)/shard_map/ppermute | solution.py:21
  3.9 18.4 %collective-permute-start.1 = (bf16[2,64,768]{2,1,0:T(8,128)(2,1)}, bf16[2,64,768]{2,1,0:T(8,128)(2,1)S(1)}, u32[]{:S(2)}, u32[]{:S(2)}) collective-permute-start(bf16[2,64,768]{2,1,0:T(8,128)(2,1)} %pack_weights.1), channel_id=1, source_target_pairs={{0,2},{1,3},{2,0},{3,1},{4,6},{5,7},{6,4},{7,5},{8,10},{9,11},{10,... | collective-permute-start | bytes 589832 | tf_op jit(solution)/shard_map/ppermute | solution.py:21
  6.4 17.1 %collective-permute-start.2 = (bf16[2,64,768]{2,1,0:T(8,128)(2,1)}, bf16[2,64,768]{2,1,0:T(8,128)(2,1)S(1)}, u32[]{:S(2)}, u32[]{:S(2)}) collective-permute-start(bf16[2,64,768]{2,1,0:T(8,128)(2,1)} %pack_weights.1), channel_id=1, source_target_pairs={{0,3},{1,2},{2,1},{3,0},{4,7},{5,6},{6,5},{7,4},{8,11},{9,10},{10,... | collective-permute-start | bytes 589832 | tf_op jit(solution)/shard_map/ppermute | solution.py:21
  8.0 6.6 %collective-permute-start.3 = (bf16[80,128]{1,0:T(8,128)(2,1)S(1)}, bf16[80,128]{1,0:T(8,128)(2,1)S(1)}, u32[]{:S(2)}, u32[]{:S(2)}) collective-permute-start(bf16[80,128]{1,0:T(8,128)(2,1)S(1)} %pad_maximum_fusion.1), channel_id=1, source_target_pairs={{0,4},{4,8},{8,12},{12,16},{16,20},{20,24},{24,28},{1,5},{5,9},{9,... | collective-permute-start | bytes 61448 | tf_op jit(solution)/shard_map/ppermute | solution.py:925
  12.6 49.7 %copy-start.24 = (bf16[512]{0:T(512)(128)(2,1)S(1)}, bf16[512]{0:T(512)(128)(2,1)}, u32[]{:S(2)}) copy-start(bf16[512]{0:T(512)(128)(2,1)} %param.18) | copy-start | bytes 3076
  12.6 50.3 %copy-start.21 = (s32[16384]{0:T(1024)S(1)}, s32[16384]{0:T(1024)}, u32[]{:S(2)}) copy-start(s32[16384]{0:T(1024)} %param.16) | copy-start | bytes 196612
  12.6 5.2 %collective-permute-start.4 = (bf16[80,128]{1,0:T(8,128)(2,1)S(1)}, bf16[80,128]{1,0:T(8,128)(2,1)S(1)}, u32[]{:S(2)}, u32[]{:S(2)}) collective-permute-start(bf16[80,128]{1,0:T(8,128)(2,1)S(1)} %pad_maximum_fusion.2), channel_id=1, source_target_pairs={{4,0},{8,4},{12,8},{16,12},{20,16},{24,20},{28,24},{5,1},{9,5},{13... | collective-permute-start | bytes 61448 | tf_op jit(solution)/shard_map/ppermute | solution.py:926
  23.7 44.4 %copy-start.3 = (bf16[4,2,64,768]{3,2,1,0:T(8,128)(2,1)}, bf16[4,2,64,768]{3,2,1,0:T(8,128)(2,1)S(1)}, u32[]{:S(2)}) copy-start(bf16[4,2,64,768]{3,2,1,0:T(8,128)(2,1)S(1)} %pad_maximum_fusion.rest_0_) | copy-start | bytes 2359300
  23.7 35.2 %collective-permute-start.5 = (bf16[4,2,64,768]{3,2,1,0:T(8,128)(2,1)S(1)}, bf16[4,2,64,768]{3,2,1,0:T(8,128)(2,1)S(1)}, u32[]{:S(2)}, u32[]{:S(2)}) collective-permute-start(bf16[4,2,64,768]{3,2,1,0:T(8,128)(2,1)S(1)} %pad_maximum_fusion.rest_0_), channel_id=1, source_target_pairs={{0,24},{4,28},{8,16},{12,20},{16,8},{20,12},{24,0},{28,4},{1,25},{... | collective-permute-start | bytes 2359304 | tf_op jit(solution)/shard_map/ppermute | solution.py:21
  25.9 33.0 %collective-permute-start.6 = (bf16[4,2,64,768]{3,2,1,0:T(8,128)(2,1)S(1)}, bf16[4,2,64,768]{3,2,1,0:T(8,128)(2,1)S(1)}, u32[]{:S(2)}, u32[]{:S(2)}) collective-permute-start(bf16[4,2,64,768]{3,2,1,0:T(8,128)(2,1)S(1)} %pad_maximum_fusion.rest_0_), channel_id=1, source_target_pairs={{0,8},{4,12},{8,0},{12,4},{16,24},{20,28},{24,16},{28,20},{1,9},{5... | collective-permute-start | bytes 2359304 | tf_op jit(solution)/shard_map/ppermute | solution.py:21
  26.2 34.8 %collective-permute-start.7 = (bf16[4,2,64,768]{3,2,1,0:T(8,128)(2,1)S(1)}, bf16[4,2,64,768]{3,2,1,0:T(8,128)(2,1)S(1)}, u32[]{:S(2)}, u32[]{:S(2)}) collective-permute-start(bf16[4,2,64,768]{3,2,1,0:T(8,128)(2,1)S(1)} %pad_maximum_fusion.rest_0_), channel_id=1, source_target_pairs={{0,16},{4,20},{8,24},{12,28},{16,0},{20,4},{24,8},{28,12},{1,17},{... | collective-permute-start | bytes 2359304 | tf_op jit(solution)/shard_map/ppermute | solution.py:21
  26.4 17.6 %collective-permute-start.10 = (bf16[1488,128]{1,0:T(8,128)(2,1)}, bf16[1488,128]{1,0:T(8,128)(2,1)S(1)}, u32[]{:S(2)}, u32[]{:S(2)}) collective-permute-start(bf16[1488,128]{1,0:T(8,128)(2,1)} %get-tuple-element.103), channel_id=1, source_target_pairs={{0,3},{1,2},{2,1},{3,0},{4,7},{5,6},{6,5},{7,4},{8,11},{9,10},{10,... | collective-permute-start | bytes 1142792 | tf_op jit(solution)/shard_map/ppermute | solution.py:21
  27.6 20.6 %collective-permute-start.8 = (bf16[1488,128]{1,0:T(8,128)(2,1)}, bf16[1488,128]{1,0:T(8,128)(2,1)S(1)}, u32[]{:S(2)}, u32[]{:S(2)}) collective-permute-start(bf16[1488,128]{1,0:T(8,128)(2,1)} %get-tuple-element.101), channel_id=1, source_target_pairs={{0,1},{1,0},{2,3},{3,2},{4,5},{5,4},{6,7},{7,6},{8,9},{9,8},{10,11... | collective-permute-start | bytes 1142792 | tf_op jit(solution)/shard_map/ppermute | solution.py:21
  43.9 15.0 %collective-permute-start.9 = (bf16[1488,128]{1,0:T(8,128)(2,1)}, bf16[1488,128]{1,0:T(8,128)(2,1)S(1)}, u32[]{:S(2)}, u32[]{:S(2)}) collective-permute-start(bf16[1488,128]{1,0:T(8,128)(2,1)} %get-tuple-element.102), channel_id=1, source_target_pairs={{0,2},{1,3},{2,0},{3,1},{4,6},{5,7},{6,4},{7,5},{8,10},{9,11},{10,... | collective-permute-start | bytes 1142792 | tf_op jit(solution)/shard_map/ppermute | solution.py:21
  60.9 4.3 %collective-permute-start.11 = (bf16[4,2,64,768]{3,2,1,0:T(8,128)(2,1)S(1)}, bf16[4,2,64,768]{3,2,1,0:T(8,128)(2,1)}, u32[]{:S(2)}, u32[]{:S(2)}) collective-permute-start(bf16[4,2,64,768]{3,2,1,0:T(8,128)(2,1)S(1)} %pad_maximum_fusion.rest_0_), channel_id=1, source_target_pairs={{0,4},{4,0},{8,12},{12,8},{16,20},{20,16},{24,28},{28,24},{1,5},{5... | collective-permute-start | bytes 2359304 | tf_op jit(solution)/shard_map/ppermute | solution.py:21
  61.7 5.0 %collective-permute-start.12 = (bf16[4,2,64,768]{3,2,1,0:T(8,128)(2,1)S(1)}, bf16[4,2,64,768]{3,2,1,0:T(8,128)(2,1)}, u32[]{:S(2)}, u32[]{:S(2)}) collective-permute-start(bf16[4,2,64,768]{3,2,1,0:T(8,128)(2,1)S(1)} %collective-permute-done.5.rest_1_), channel_id=1, source_target_pairs={{0,4},{4,0},{8,12},{12,8},{16,20},{20,16},{24,28},{28,24},{1,5},{5... | collective-permute-start | bytes 2359304 | tf_op jit(solution)/shard_map/ppermute | solution.py:21
  61.7 5.4 %collective-permute-start.13 = (bf16[4,2,64,768]{3,2,1,0:T(8,128)(2,1)S(1)}, bf16[4,2,64,768]{3,2,1,0:T(8,128)(2,1)}, u32[]{:S(2)}, u32[]{:S(2)}) collective-permute-start(bf16[4,2,64,768]{3,2,1,0:T(8,128)(2,1)S(1)} %collective-permute-done.6.rest_2_), channel_id=1, source_target_pairs={{0,4},{4,0},{8,12},{12,8},{16,20},{20,16},{24,28},{28,24},{1,5},{5... | collective-permute-start | bytes 2359304 | tf_op jit(solution)/shard_map/ppermute | solution.py:21
  62.2 5.0 %collective-permute-start.14 = (bf16[4,2,64,768]{3,2,1,0:T(8,128)(2,1)S(1)}, bf16[4,2,64,768]{3,2,1,0:T(8,128)(2,1)}, u32[]{:S(2)}, u32[]{:S(2)}) collective-permute-start(bf16[4,2,64,768]{3,2,1,0:T(8,128)(2,1)S(1)} %collective-permute-done.7.rest_3_), channel_id=1, source_target_pairs={{0,4},{4,0},{8,12},{12,8},{16,20},{20,16},{24,28},{28,24},{1,5},{5... | collective-permute-start | bytes 2359304 | tf_op jit(solution)/shard_map/ppermute | solution.py:21
  62.9 28.4 %collective-permute-start.15 = (bf16[18,64,128]{2,1,0:T(8,128)(2,1)}, bf16[18,64,128]{2,1,0:T(8,128)(2,1)S(1)}, u32[]{:S(2)}, u32[]{:S(2)}) collective-permute-start(bf16[18,64,128]{2,1,0:T(8,128)(2,1)} %get-tuple-element.117), channel_id=1, source_target_pairs={{0,1},{1,0},{2,3},{3,2},{4,5},{5,4},{6,7},{7,6},{8,9},{9,8},{10,11... | collective-permute-start | bytes 884744 | tf_op jit(solution)/shard_map/ppermute | solution.py:21
  65.2 26.2 %collective-permute-start.16 = (bf16[18,64,128]{2,1,0:T(8,128)(2,1)}, bf16[18,64,128]{2,1,0:T(8,128)(2,1)}, u32[]{:S(2)}, u32[]{:S(2)}) collective-permute-start(bf16[18,64,128]{2,1,0:T(8,128)(2,1)} %get-tuple-element.118), channel_id=1, source_target_pairs={{0,2},{1,3},{2,0},{3,1},{4,6},{5,7},{6,4},{7,5},{8,10},{9,11},{10,... | collective-permute-start | bytes 884744 | tf_op jit(solution)/shard_map/ppermute | solution.py:21
  66.7 26.5 %collective-permute-start.17 = (bf16[18,64,128]{2,1,0:T(8,128)(2,1)}, bf16[18,64,128]{2,1,0:T(8,128)(2,1)}, u32[]{:S(2)}, u32[]{:S(2)}) collective-permute-start(bf16[18,64,128]{2,1,0:T(8,128)(2,1)} %get-tuple-element.119), channel_id=1, source_target_pairs={{0,3},{1,2},{2,1},{3,0},{4,7},{5,6},{6,5},{7,4},{8,11},{9,10},{10,... | collective-permute-start | bytes 884744 | tf_op jit(solution)/shard_map/ppermute | solution.py:21
  93.3 41.4 %collective-permute-start.18 = (bf16[64,4096]{1,0:T(8,128)(2,1)}, bf16[64,4096]{1,0:T(8,128)(2,1)S(1)}, u32[]{:S(2)}, u32[]{:S(2)}) collective-permute-start(bf16[64,4096]{1,0:T(8,128)(2,1)} %get-tuple-element.142), channel_id=1, source_target_pairs={{0,1},{1,0},{2,3},{3,2},{4,5},{5,4},{6,7},{7,6},{8,9},{9,8},{10,11... | collective-permute-start | bytes 1572872 | tf_op jit(solution)/shard_map/ppermute | solution.py:21
  94.3 40.4 %collective-permute-start.19 = (bf16[64,4096]{1,0:T(8,128)(2,1)}, bf16[64,4096]{1,0:T(8,128)(2,1)S(1)}, u32[]{:S(2)}, u32[]{:S(2)}) collective-permute-start(bf16[64,4096]{1,0:T(8,128)(2,1)} %get-tuple-element.143), channel_id=1, source_target_pairs={{0,2},{1,3},{2,0},{3,1},{4,6},{5,7},{6,4},{7,5},{8,10},{9,11},{10,... | collective-permute-start | bytes 1572872 | tf_op jit(solution)/shard_map/ppermute | solution.py:21
  95.4 44.9 %collective-permute-start.20 = (bf16[64,4096]{1,0:T(8,128)(2,1)}, bf16[64,4096]{1,0:T(8,128)(2,1)S(1)}, u32[]{:S(2)}, u32[]{:S(2)}) collective-permute-start(bf16[64,4096]{1,0:T(8,128)(2,1)} %get-tuple-element.144), channel_id=1, source_target_pairs={{0,3},{1,2},{2,1},{3,0},{4,7},{5,6},{6,5},{7,4},{8,11},{9,10},{10,... | collective-permute-start | bytes 1572872 | tf_op jit(solution)/shard_map/ppermute | solution.py:21
  141.2 6.9 %collective-permute-start.22 = (bf16[2,2,256,768]{3,2,1,0:T(8,128)(2,1)}, bf16[2,2,256,768]{3,2,1,0:T(8,128)(2,1)S(1)}, u32[]{:S(2)}, u32[]{:S(2)}) collective-permute-start(bf16[2,2,256,768]{3,2,1,0:T(8,128)(2,1)} %get-tuple-element.153), channel_id=1, source_target_pairs={{0,4},{4,0},{8,12},{12,8},{16,20},{20,16},{24,28},{28,24},{1,5},{5... | collective-permute-start | bytes 4718600 | tf_op jit(solution)/shard_map/ppermute | solution.py:21
  143.5 4.4 %collective-permute-start.21 = (bf16[2,256,768]{2,1,0:T(8,128)(2,1)}, bf16[2,256,768]{2,1,0:T(8,128)(2,1)S(1)}, u32[]{:S(2)}, u32[]{:S(2)}) collective-permute-start(bf16[2,256,768]{2,1,0:T(8,128)(2,1)} %get-tuple-element.151), channel_id=1, source_target_pairs={{0,4},{4,0},{8,12},{12,8},{16,20},{20,16},{24,28},{28,24},{1,5},{5... | collective-permute-start | bytes 2359304 | tf_op jit(solution)/shard_map/ppermute | solution.py:21
  143.6 5.4 %collective-permute-start.23 = (bf16[2,256,768]{2,1,0:T(8,128)(2,1)}, bf16[2,256,768]{2,1,0:T(8,128)(2,1)S(1)}, u32[]{:S(2)}, u32[]{:S(2)}) collective-permute-start(bf16[2,256,768]{2,1,0:T(8,128)(2,1)} %get-tuple-element.154), channel_id=1, source_target_pairs={{0,4},{4,0},{8,12},{12,8},{16,20},{20,16},{24,28},{28,24},{1,5},{5... | collective-permute-start | bytes 2359304 | tf_op jit(solution)/shard_map/ppermute | solution.py:21
  149.0 22.4 %collective-permute-start.27 = (bf16[2,256,768]{2,1,0:T(8,128)(2,1)S(1)}, bf16[2,256,768]{2,1,0:T(8,128)(2,1)S(1)}, u32[]{:S(2)}, u32[]{:S(2)}) collective-permute-start(bf16[2,256,768]{2,1,0:T(8,128)(2,1)S(1)} %get-tuple-element.162), channel_id=1, source_target_pairs={{0,8},{4,12},{8,0},{12,4},{16,24},{20,28},{24,16},{28,20},{1,9},{5... | collective-permute-start | bytes 2359304 | tf_op jit(solution)/shard_map/ppermute | solution.py:21
  150.4 21.1 %collective-permute-start.28 = (bf16[2,256,768]{2,1,0:T(8,128)(2,1)S(1)}, bf16[2,256,768]{2,1,0:T(8,128)(2,1)S(1)}, u32[]{:S(2)}, u32[]{:S(2)}) collective-permute-start(bf16[2,256,768]{2,1,0:T(8,128)(2,1)S(1)} %get-tuple-element.163), channel_id=1, source_target_pairs={{0,16},{4,20},{8,24},{12,28},{16,0},{20,4},{24,8},{28,12},{1,17},{... | collective-permute-start | bytes 2359304 | tf_op jit(solution)/shard_map/ppermute | solution.py:21
  152.1 6.2 %collective-permute-start.29 = (bf16[2,64,768]{2,1,0:T(8,128)(2,1)S(1)}, bf16[2,64,768]{2,1,0:T(8,128)(2,1)S(1)}, u32[]{:S(2)}, u32[]{:S(2)}) collective-permute-start(bf16[2,64,768]{2,1,0:T(8,128)(2,1)S(1)} %get-tuple-element.185), channel_id=1, source_target_pairs={{0,1},{1,0},{2,3},{3,2},{4,5},{5,4},{6,7},{7,6},{8,9},{9,8},{10,11... | collective-permute-start | bytes 589832 | tf_op jit(solution)/shard_map/ppermute | solution.py:21
  152.2 10.7 %collective-permute-start.30 = (bf16[2,64,768]{2,1,0:T(8,128)(2,1)S(1)}, bf16[2,64,768]{2,1,0:T(8,128)(2,1)S(1)}, u32[]{:S(2)}, u32[]{:S(2)}) collective-permute-start(bf16[2,64,768]{2,1,0:T(8,128)(2,1)S(1)} %get-tuple-element.187), channel_id=1, source_target_pairs={{0,2},{1,3},{2,0},{3,1},{4,6},{5,7},{6,4},{7,5},{8,10},{9,11},{10,... | collective-permute-start | bytes 589832 | tf_op jit(solution)/shard_map/ppermute | solution.py:21
  154.7 16.6 %collective-permute-start.31 = (bf16[2,64,768]{2,1,0:T(8,128)(2,1)S(1)}, bf16[2,64,768]{2,1,0:T(8,128)(2,1)S(1)}, u32[]{:S(2)}, u32[]{:S(2)}) collective-permute-start(bf16[2,64,768]{2,1,0:T(8,128)(2,1)S(1)} %get-tuple-element.186), channel_id=1, source_target_pairs={{0,3},{1,2},{2,1},{3,0},{4,7},{5,6},{6,5},{7,4},{8,11},{9,10},{10,... | collective-permute-start | bytes 589832 | tf_op jit(solution)/shard_map/ppermute | solution.py:21
  158.3 37.8 %collective-permute-start.24 = (bf16[512,128]{1,0:T(8,128)(2,1)S(1)}, bf16[512,128]{1,0:T(8,128)(2,1)S(1)}, u32[]{:S(2)}, u32[]{:S(2)}) collective-permute-start(bf16[512,128]{1,0:T(8,128)(2,1)S(1)} %copy-done.34), channel_id=1, source_target_pairs={{0,1},{1,0},{2,3},{3,2},{4,5},{5,4},{6,7},{7,6},{8,9},{9,8},{10,11... | collective-permute-start | bytes 393224 | tf_op jit(solution)/shard_map/ppermute | solution.py:21
  171.7 24.4 %copy-start.32 = (bf16[512,128]{1,0:T(8,128)(2,1)S(1)}, bf16[512,128]{1,0:T(8,128)(2,1)}, u32[]{:S(2)}) copy-start(bf16[512,128]{1,0:T(8,128)(2,1)} %get-tuple-element.159) | copy-start | bytes 393220
  171.8 4.6 %collective-permute-start.32 = (bf16[2,64,768]{2,1,0:T(8,128)(2,1)S(1)}, bf16[2,64,768]{2,1,0:T(8,128)(2,1)S(1)}, u32[]{:S(2)}, u32[]{:S(2)}) collective-permute-start(bf16[2,64,768]{2,1,0:T(8,128)(2,1)S(1)} %get-tuple-element.182), channel_id=1, source_target_pairs={{0,1},{1,0},{2,3},{3,2},{4,5},{5,4},{6,7},{7,6},{8,9},{9,8},{10,11... | collective-permute-start | bytes 589832 | tf_op jit(solution)/shard_map/ppermute | solution.py:21
  171.8 9.7 %collective-permute-start.33 = (bf16[2,64,768]{2,1,0:T(8,128)(2,1)S(1)}, bf16[2,64,768]{2,1,0:T(8,128)(2,1)S(1)}, u32[]{:S(2)}, u32[]{:S(2)}) collective-permute-start(bf16[2,64,768]{2,1,0:T(8,128)(2,1)S(1)} %get-tuple-element.184), channel_id=1, source_target_pairs={{0,2},{1,3},{2,0},{3,1},{4,6},{5,7},{6,4},{7,5},{8,10},{9,11},{10,... | collective-permute-start | bytes 589832 | tf_op jit(solution)/shard_map/ppermute | solution.py:21
  174.4 18.7 %collective-permute-start.34 = (bf16[2,64,768]{2,1,0:T(8,128)(2,1)S(1)}, bf16[2,64,768]{2,1,0:T(8,128)(2,1)S(1)}, u32[]{:S(2)}, u32[]{:S(2)}) collective-permute-start(bf16[2,64,768]{2,1,0:T(8,128)(2,1)S(1)} %get-tuple-element.183), channel_id=1, source_target_pairs={{0,3},{1,2},{2,1},{3,0},{4,7},{5,6},{6,5},{7,4},{8,11},{9,10},{10,... | collective-permute-start | bytes 589832 | tf_op jit(solution)/shard_map/ppermute | solution.py:21
  174.5 18.6 %collective-permute-start.35 = (bf16[2,64,768]{2,1,0:T(8,128)(2,1)S(1)}, bf16[2,64,768]{2,1,0:T(8,128)(2,1)S(1)}, u32[]{:S(2)}, u32[]{:S(2)}) collective-permute-start(bf16[2,64,768]{2,1,0:T(8,128)(2,1)S(1)} %add_add_fusion.2), channel_id=1, source_target_pairs={{0,24},{4,28},{8,16},{12,20},{16,8},{20,12},{24,0},{28,4},{1,25},{... | collective-permute-start | bytes 589832 | tf_op jit(solution)/shard_map/ppermute | solution.py:21
  174.5 39.1 %copy-start = (bf16[64,16384]{1,0:T(8,128)(2,1)}, bf16[64,16384]{1,0:T(8,128)(2,1)S(1)}, u32[]{:S(2)}) copy-start(bf16[64,16384]{1,0:T(8,128)(2,1)S(1)} %constant_dynamic-update-slice_fusion.4) | copy-start | bytes 6291460
  176.3 22.0 %collective-permute-start.25 = (bf16[512,128]{1,0:T(8,128)(2,1)S(1)}, bf16[512,128]{1,0:T(8,128)(2,1)S(1)}, u32[]{:S(2)}, u32[]{:S(2)}) collective-permute-start(bf16[512,128]{1,0:T(8,128)(2,1)S(1)} %copy-done.33), channel_id=1, source_target_pairs={{0,2},{1,3},{2,0},{3,1},{4,6},{5,7},{6,4},{7,5},{8,10},{9,11},{10,... | collective-permute-start | bytes 393224 | tf_op jit(solution)/shard_map/ppermute | solution.py:21
  193.2 11.1 %collective-permute-start.36 = (bf16[2,64,768]{2,1,0:T(8,128)(2,1)S(1)}, bf16[2,64,768]{2,1,0:T(8,128)(2,1)S(1)}, u32[]{:S(2)}, u32[]{:S(2)}) collective-permute-start(bf16[2,64,768]{2,1,0:T(8,128)(2,1)S(1)} %add_add_fusion.1.rest_0_), channel_id=1, source_target_pairs={{0,8},{4,12},{8,0},{12,4},{16,24},{20,28},{24,16},{28,20},{1,9},{5... | collective-permute-start | bytes 589832 | tf_op jit(solution)/shard_map/ppermute | solution.py:21
  193.3 11.2 %collective-permute-start.37 = (bf16[2,64,768]{2,1,0:T(8,128)(2,1)S(1)}, bf16[2,64,768]{2,1,0:T(8,128)(2,1)S(1)}, u32[]{:S(2)}, u32[]{:S(2)}) collective-permute-start(bf16[2,64,768]{2,1,0:T(8,128)(2,1)S(1)} %add_add_fusion.1.rest_0_), channel_id=1, source_target_pairs={{0,16},{4,20},{8,24},{12,28},{16,0},{20,4},{24,8},{28,12},{1,17},{... | collective-permute-start | bytes 589832 | tf_op jit(solution)/shard_map/ppermute | solution.py:21
  193.8 13.2 %collective-permute-start.38 = (bf16[2,64,768]{2,1,0:T(8,128)(2,1)S(1)}, bf16[2,64,768]{2,1,0:T(8,128)(2,1)S(1)}, u32[]{:S(2)}, u32[]{:S(2)}) collective-permute-start(bf16[2,64,768]{2,1,0:T(8,128)(2,1)S(1)} %add_add_fusion.1.rest_0_), channel_id=1, source_target_pairs={{0,24},{4,28},{8,16},{12,20},{16,8},{20,12},{24,0},{28,4},{1,25},{... | collective-permute-start | bytes 589832 | tf_op jit(solution)/shard_map/ppermute | solution.py:21
  196.1 11.0 %collective-permute-start.26 = (bf16[512,128]{1,0:T(8,128)(2,1)S(1)}, bf16[512,128]{1,0:T(8,128)(2,1)S(1)}, u32[]{:S(2)}, u32[]{:S(2)}) collective-permute-start(bf16[512,128]{1,0:T(8,128)(2,1)S(1)} %copy-done.32), channel_id=1, source_target_pairs={{0,3},{1,2},{2,1},{3,0},{4,7},{5,6},{6,5},{7,4},{8,11},{9,10},{10,... | collective-permute-start | bytes 393224 | tf_op jit(solution)/shard_map/ppermute | solution.py:21
  198.4 8.7 %collective-permute-start.39 = (bf16[2,64,768]{2,1,0:T(8,128)(2,1)S(1)}, bf16[2,64,768]{2,1,0:T(8,128)(2,1)S(1)}, u32[]{:S(2)}, u32[]{:S(2)}) collective-permute-start(bf16[2,64,768]{2,1,0:T(8,128)(2,1)S(1)} %add_add_fusion.1.rest_0_), channel_id=1, source_target_pairs={{0,4},{4,0},{8,12},{12,8},{16,20},{20,16},{24,28},{28,24},{1,5},{5... | collective-permute-start | bytes 589832 | tf_op jit(solution)/shard_map/ppermute | solution.py:21
  204.3 2.9 %collective-permute-start.40 = (bf16[2,64,768]{2,1,0:T(8,128)(2,1)S(1)}, bf16[2,64,768]{2,1,0:T(8,128)(2,1)S(1)}, u32[]{:S(2)}, u32[]{:S(2)}) collective-permute-start(bf16[2,64,768]{2,1,0:T(8,128)(2,1)S(1)} %collective-permute-done.36.rest_1_), channel_id=1, source_target_pairs={{0,4},{4,0},{8,12},{12,8},{16,20},{20,16},{24,28},{28,24},{1,5},{5... | collective-permute-start | bytes 589832 | tf_op jit(solution)/shard_map/ppermute | solution.py:21
  204.5 3.5 %collective-permute-start.41 = (bf16[2,64,768]{2,1,0:T(8,128)(2,1)S(1)}, bf16[2,64,768]{2,1,0:T(8,128)(2,1)S(1)}, u32[]{:S(2)}, u32[]{:S(2)}) collective-permute-start(bf16[2,64,768]{2,1,0:T(8,128)(2,1)S(1)} %collective-permute-done.37.rest_2_), channel_id=1, source_target_pairs={{0,4},{4,0},{8,12},{12,8},{16,20},{20,16},{24,28},{28,24},{1,5},{5... | collective-permute-start | bytes 589832 | tf_op jit(solution)/shard_map/ppermute | solution.py:21
  207.0 1.6 collective-permute-start.42
  (30 other events, 218.9 us)
